TPU v7x, 32 devices: a whole 2x2x4 slice. The times are simulated.
32 devices in a mesh: groups: 2 (over y), seq: 4 (over z), chan: 2 (over x), sub: 2 (over core).
Axes of the slice: x: 2, y: 2, z: 4, core: 2. Of those that a mesh axis runs over, the one named last changes fastest.
Arguments:
- features: bfloat16 [3, 4096, 2048], P(None, ('chan', 'sub'), ('groups', 'seq')), parts along dimension 2, may hold values from -6 to 6
- dout: bfloat16 [4096, 2048], P(('chan', 'sub'), ('groups', 'seq')), parts along dimension 1, may hold values from -6 to 6
- filters: bfloat16 [4096, 1024], P(('chan', 'sub'), 'seq'), may hold values from -0.1875 to 0.1875
- taps: float32 [3, 3, 4096], P(None, None, ('chan', 'sub')), may hold values from -3.5 to 3.5
- skip: float32 [4096], P(('chan', 'sub')), may hold values from -4 to 4
- lengths: int32 [32], P('groups'), parts along dimension 0, may hold values from 1 to 256, 1024 in all
Outputs:
- out: bfloat16 [4096, 2048], P(('chan', 'sub'), ('groups', 'seq')), parts along dimension 1
- dfeatures: bfloat16 [3, 4096, 2048], P(None, ('chan', 'sub'), ('groups', 'seq')), parts along dimension 2
There are 2 independent parts, one for each index of `groups`. A program takes and returns all parts, laid end to end along the dimension named above; an argument that names none is the same for every part. Nothing has to cross between parts.
Inputs may be any that keep to these rules, and one draw needn't show every extreme that they name: The lengths of one part sum to 1024, and the longest genome has exactly 256 positions.
All inputs are finite; a program needn't handle non-finite values.
Results may differ from a plain program's by a relative error of at most 0.01.
Values may be sent and summed in bfloat16 or wider, within the bound.
No kernel may reach another device: no remote copies, remote signals or barrier semaphores. Data moves between devices by JAX's collectives and lax.ppermute only.
A program may use at most 64 MiB of HBM per device.

v0:
```python
import jax
import jax.numpy as jnp
from jax import lax
from jax.sharding import PartitionSpec as P

HIGHEST = lax.Precision.HIGHEST
TWO_PI = 6.283185307179586


def shifted(value, axis, steps):
    count = lax.axis_size(axis)
    leading, last = (max(0, -steps), min(count, count - steps))
    return lax.ppermute(value, axis, [(source, source + steps) for source in range(leading, last)])


def genome_offsets(lengths, positions):
    ends_at = jnp.cumsum(lengths, dtype=jnp.int32)
    before = (ends_at[None, :] <= positions[:, None]).astype(jnp.int32)
    return positions - jnp.sum(before * lengths[None, :], axis=1, dtype=jnp.int32)


def short_forward(extended, taps_local, offsets):
    span_rows = offsets.shape[0]
    count = taps_local.shape[1]
    result = jnp.zeros(extended.shape[:2] + (span_rows,), jnp.float32)
    for tap_index in range(count):
        begin = count - 1 - tap_index
        window = extended[:, :, begin : begin + span_rows].astype(jnp.float32)
        keep_mask = (offsets >= tap_index).astype(jnp.float32)
        result = result + taps_local[:, tap_index, :, None] * window * keep_mask[None, None, :]
    return result


def short_backward(grads_ext, taps_local, offsets_ext):
    count = taps_local.shape[1]
    span_rows = offsets_ext.shape[0] - (count - 1)
    result = jnp.zeros(grads_ext.shape[:2] + (span_rows,), jnp.float32)
    for tap_index in range(count):
        window = grads_ext[:, :, tap_index : tap_index + span_rows]
        keep_mask = (offsets_ext[tap_index : tap_index + span_rows] >= tap_index).astype(
            jnp.float32
        )
        result = result + taps_local[:, tap_index, :, None] * window * keep_mask[None, None, :]
    return result


def dft_table(rows_n, cols_n, period):
    row_ids = jnp.arange(rows_n, dtype=jnp.int32)
    col_ids = jnp.arange(cols_n, dtype=jnp.int32)
    phase = row_ids[:, None] * col_ids[None, :] % period
    angles = phase.astype(jnp.float32) * (-TWO_PI / period)
    return (jnp.cos(angles), jnp.sin(angles))


def forward_transform(signal, tables):
    (row_re, row_im), (twid_re, twid_im), (col_re, col_im) = tables
    half_rows = signal.shape[1] // 128
    blocks_in = signal.reshape(signal.shape[0], half_rows, 128)
    part_re = jnp.einsum("kn,cnm->ckm", row_re[:, :half_rows], blocks_in, precision=HIGHEST)
    part_im = jnp.einsum("kn,cnm->ckm", row_im[:, :half_rows], blocks_in, precision=HIGHEST)
    turned_re = part_re * twid_re - part_im * twid_im
    turned_im = part_re * twid_im + part_im * twid_re
    spec_re = jnp.einsum("ckn,nm->ckm", turned_re, col_re, precision=HIGHEST) - jnp.einsum(
        "ckn,nm->ckm", turned_im, col_im, precision=HIGHEST
    )
    spec_im = jnp.einsum("ckn,nm->ckm", turned_re, col_im, precision=HIGHEST) + jnp.einsum(
        "ckn,nm->ckm", turned_im, col_re, precision=HIGHEST
    )
    return (spec_re, spec_im)


def inverse_transform(spec_re, spec_im, tables):
    (row_re, row_im), (twid_re, twid_im), (col_re, col_im) = tables
    rows_n = spec_re.shape[1]
    half_rows = rows_n // 2
    mid_re = jnp.einsum("ckn,nm->ckm", spec_re, col_re, precision=HIGHEST) + jnp.einsum(
        "ckn,nm->ckm", spec_im, col_im, precision=HIGHEST
    )
    mid_im = jnp.einsum("ckn,nm->ckm", spec_im, col_re, precision=HIGHEST) - jnp.einsum(
        "ckn,nm->ckm", spec_re, col_im, precision=HIGHEST
    )
    back_re = mid_re * twid_re + mid_im * twid_im
    back_im = mid_im * twid_re - mid_re * twid_im
    signal = jnp.einsum("nk,ckm->cnm", row_re[:half_rows], back_re, precision=HIGHEST) + jnp.einsum(
        "nk,ckm->cnm", row_im[:half_rows], back_im, precision=HIGHEST
    )
    return signal.reshape(signal.shape[0], half_rows * 128) * (1.0 / (rows_n * 128))


def long_filter(filt, mixed_in, grad_in, skip_part):
    rows_n = 2 * mixed_in.shape[1] // 128
    tables = (
        dft_table(rows_n, rows_n, rows_n),
        dft_table(rows_n, 128, rows_n * 128),
        dft_table(128, 128, 128),
    )
    mixed_f = mixed_in.astype(jnp.float32)
    grad_f = grad_in.astype(jnp.float32)
    filt_re, filt_im = forward_transform(filt.astype(jnp.float32), tables)
    mix_re, mix_im = forward_transform(mixed_f, tables)
    grad_re, grad_im = forward_transform(grad_f, tables)
    conv_out = inverse_transform(
        filt_re * mix_re - filt_im * mix_im, filt_re * mix_im + filt_im * mix_re, tables
    )
    corr_out = inverse_transform(
        filt_re * grad_re + filt_im * grad_im, filt_re * grad_im - filt_im * grad_re, tables
    )
    y_out = (conv_out + skip_part[:, None] * mixed_f).astype(jnp.bfloat16)
    dmixed = (corr_out + skip_part[:, None] * grad_f).astype(jnp.bfloat16)
    return (y_out, dmixed)


def to_channels(stacked):
    return lax.all_to_all(stacked, "seq", split_axis=1, concat_axis=2, tiled=True)


def to_sequence(stacked):
    return lax.all_to_all(stacked, "seq", split_axis=2, concat_axis=1, tiled=True)


def local(features, dout, filters, taps, skip, lengths):
    blocks = lax.axis_size("seq")
    seq_rank = lax.axis_index("seq")
    span_rows = features.shape[2]
    channels_here = features.shape[1]
    chan_part = channels_here // blocks
    count = taps.shape[1]
    margin = count - 1
    rim = shifted(features[:, :, span_rows - margin :], "seq", 1)
    extended = jnp.concatenate([rim, features], axis=2)
    first_pos = seq_rank * span_rows
    offsets = genome_offsets(lengths, first_pos + jnp.arange(span_rows, dtype=jnp.int32))
    filtered = short_forward(extended, taps, offsets).astype(jnp.bfloat16)
    query_side = filtered[0].astype(jnp.float32)
    key_side = filtered[1].astype(jnp.float32)
    value_side = filtered[2].astype(jnp.float32)
    dout_f = dout.astype(jnp.float32)
    mixed = (key_side * value_side).astype(jnp.bfloat16)
    grad_in = (dout_f * query_side).astype(jnp.bfloat16)
    moved = to_channels(jnp.stack([mixed, grad_in, filters]))
    skip_part = lax.dynamic_slice_in_dim(skip, seq_rank * chan_part, chan_part, 0)
    y_out, dmixed = long_filter(moved[2], moved[0], moved[1], skip_part)
    returned = to_sequence(jnp.stack([y_out, dmixed]))
    y_here = returned[0].astype(jnp.float32)
    dmixed_here = returned[1].astype(jnp.float32)
    out = (query_side * y_here).astype(jnp.bfloat16)
    grads = jnp.stack([dout_f * y_here, dmixed_here * value_side, dmixed_here * key_side])
    ahead = shifted(grads[:, :, :margin], "seq", -1)
    grads_ext = jnp.concatenate([grads, ahead], axis=2)
    offsets_ext = genome_offsets(
        lengths, first_pos + jnp.arange(span_rows + margin, dtype=jnp.int32)
    )
    dfeatures = short_backward(grads_ext, taps, offsets_ext).astype(jnp.bfloat16)
    return (out, dfeatures)


def solution(mesh):
    in_specs = (
        P(None, ("chan", "sub"), ("groups", "seq")),
        P(("chan", "sub"), ("groups", "seq")),
        P(("chan", "sub"), "seq"),
        P(None, None, ("chan", "sub")),
        P(("chan", "sub")),
        P("groups"),
    )
    out_specs = (P(("chan", "sub"), ("groups", "seq")), P(None, ("chan", "sub"), ("groups", "seq")))
    return jax.shard_map(local, mesh=mesh, in_specs=in_specs, out_specs=out_specs, check_vma=False)
```

profile of v0, /device:TPU:0, one launch (start us, length us, event | category | flops | bytes accessed | tf_op | source)
XLA Modules:
  0.0 219.6 jit_solution(16636428036014913479)
XLA Ops:
  2.5 4.9 %collective-permute-start = (bf16[3,1024,2]{1,2,0:T(2,128)(2,1)S(1)}, bf16[3,1024,2]{1,2,0:T(2,128)(2,1)S(1)}, u32[]{:S(2)}, u32[]{:S(2)}) collective-permute-start(bf16[3,1024,2]{1,2,0:T(2,128)(2,1)S(1)} %copy.272), channel_id=1, source_target_pairs={{0,4},{4,8},{8,12},{1,5},{5,9},{9,13},{2,6},{6,10},{10,14},{3,7},{... | collective-permute-start | bytes 36872 | tf_op jit(solution)/shard_map/ppermute | solution.py:13
  9.2 3.0 %add_convert_fusion = bf16[3,1024,256]{2,1,0:T(8,128)(2,1)S(1)} fusion(bf16[3,1024,256]{2,1,0:T(8,128)(2,1)S(1)} %copy-done.8, bf16[3,1024,2]{2,1,0:T(8,128)(2,1)S(1)} %copy.207, f32[256]{0:T(256)S(1)} %get-tuple-element.39, f32[3,1024]{1,0:T(4,128)S(1)} %get-tuple-element.40, f32[256]{0:T(256)S(1)} %get-tuple-element.38, ...), kind=kLoop, calls=%fused_computation.9 | loop fusion | flops 14155776 | bytes 3197952 | tf_op jit(solution)/shard_map/convert_element_type | solution.py:133
  13.9 2.7 %copy.208 = bf16[3,1024,256]{2,0,1:T(4,128)(2,1)} copy(bf16[3,1024,256]{2,1,0:T(8,128)(2,1)S(1)} %pad_maximum_fusion.3) | data formatting | bytes 3145728 | tf_op jit(solution)/shard_map/stack | solution.py:140
  16.6 5.7 %all-to-all-start = ((bf16[3,1024,256]{2,0,1:T(4,128)(2,1)}), bf16[3,1024,256]{2,0,1:T(4,128)(2,1)S(1)}, u32[]{:S(2)}, u32[]{:S(2)}) async-start(bf16[3,1024,256]{2,0,1:T(4,128)(2,1)} %copy.208), calls=%async_computation | async-start | bytes 4194304 | tf_op jit(solution)/shard_map/all_to_all | solution.py:114
  23.3 45.9 %all-to-all-done = bf16[3,1024,256]{2,0,1:T(4,128)(2,1)S(1)} async-done(((bf16[3,1024,256]{2,0,1:T(4,128)(2,1)}), bf16[3,1024,256]{2,0,1:T(4,128)(2,1)S(1)}, u32[]{:S(2)}, u32[]{:S(2)}) %all-to-all-start) | async-done | bytes 1572896 | tf_op jit(solution)/shard_map/all_to_all | solution.py:114
  84.2 4.4 %fusion.7 = (f32[256,16,128]{2,1,0:T(8,128)S(1)}, f32[256,16,128]{2,1,0:T(8,128)S(1)}, f32[256,16,128]{2,1,0:T(8,128)S(1)}, f32[256,16,128]{2,1,0:T(8,128)S(1)},...) fusion(f32[256,128,16]{1,2,0:T(8,128)S(1)} %fusion.194, f32[16,128]{1,0:T(8,128)S(1)} %get-tuple-element.42, ...), kind=kOutput, calls=%fused_computation.20 | convolution fusion | flops 59768832 | bytes 23613440 | tf_op jit(solution)/shard_map/kn,cnm->ckm/dot_general | solution.py:60
  88.7 2.5 %fusion.51 = f32[256,16,128]{2,0,1:T(8,128)S(1)} fusion(f32[256,16,128]{2,1,0:T(8,128)S(1)} %get-tuple-element.7), kind=kOutput, calls=%fused_computation.74 | convolution fusion | flops 805535744 | bytes 4194304 | tf_op jit(solution)/shard_map/ckn,nm->ckm/dot_general | solution.py:66
  91.2 2.8 %fusion.53 = f32[256,16,128]{2,0,1:T(8,128)S(1)} fusion(f32[256,16,128]{2,1,0:T(8,128)S(1)} %get-tuple-element.7), kind=kOutput, calls=%fused_computation.76 | convolution fusion | flops 805535744 | bytes 4194304 | tf_op jit(solution)/shard_map/ckn,nm->ckm/dot_general | solution.py:63
  94.0 2.5 %fusion.43 = f32[256,16,128]{2,0,1:T(8,128)S(1)} fusion(f32[256,16,128]{2,1,0:T(8,128)S(1)} %get-tuple-element.28), kind=kOutput, calls=%fused_computation.66 | convolution fusion | flops 805535744 | bytes 4194304 | tf_op jit(solution)/shard_map/ckn,nm->ckm/dot_general | solution.py:66
  96.5 2.6 %fusion.45 = f32[256,16,128]{2,0,1:T(8,128)S(1)} fusion(f32[256,16,128]{2,1,0:T(8,128)S(1)} %get-tuple-element.28), kind=kOutput, calls=%fused_computation.68 | convolution fusion | flops 805535744 | bytes 4194304 | tf_op jit(solution)/shard_map/ckn,nm->ckm/dot_general | solution.py:63
  99.1 2.5 %fusion.59 = f32[256,16,128]{2,0,1:T(8,128)S(1)} fusion(f32[256,16,128]{2,1,0:T(8,128)S(1)} %get-tuple-element.30), kind=kOutput, calls=%fused_computation.82 | convolution fusion | flops 805535744 | bytes 4194304 | tf_op jit(solution)/shard_map/ckn,nm->ckm/dot_general | solution.py:66
  101.6 3.0 %fusion.61 = f32[256,16,128]{2,0,1:T(8,128)S(1)} fusion(f32[256,16,128]{2,1,0:T(8,128)S(1)} %get-tuple-element.30), kind=kOutput, calls=%fused_computation.84 | convolution fusion | flops 805535744 | bytes 4194304 | tf_op jit(solution)/shard_map/ckn,nm->ckm/dot_general | solution.py:63
  104.6 2.6 %fusion.73 = f32[256,16,128]{2,0,1:T(8,128)S(1)} fusion(f32[256,16,128]{2,0,1:T(8,128)S(1)} %fusion.53, f32[256,16,128]{2,1,0:T(8,128)S(1)} %get-tuple-element.6), kind=kOutput, calls=%fused_computation.92 | convolution fusion | flops 806060032 | bytes 6291456 | tf_op jit(solution)/shard_map/ckn,nm->ckm/dot_general | solution.py:63
  107.2 2.6 %fusion.76 = f32[256,16,128]{2,0,1:T(8,128)S(1)} fusion(f32[256,16,128]{2,0,1:T(8,128)S(1)} %fusion.51, f32[256,16,128]{2,1,0:T(8,128)S(1)} %get-tuple-element.6), kind=kOutput, calls=%fused_computation.93 | convolution fusion | flops 806060032 | bytes 6291456 | tf_op jit(solution)/shard_map/ckn,nm->ckm/dot_general | solution.py:66
  109.8 2.6 %fusion.79 = f32[256,16,128]{2,0,1:T(8,128)S(1)} fusion(f32[256,16,128]{2,0,1:T(8,128)S(1)} %fusion.45, f32[256,16,128]{2,1,0:T(8,128)S(1)} %get-tuple-element.29), kind=kOutput, calls=%fused_computation.94 | convolution fusion | flops 806060032 | bytes 6291456 | tf_op jit(solution)/shard_map/ckn,nm->ckm/dot_general | solution.py:63
  112.4 2.6 %fusion.82 = f32[256,16,128]{2,0,1:T(8,128)S(1)} fusion(f32[256,16,128]{2,0,1:T(8,128)S(1)} %fusion.43, f32[256,16,128]{2,1,0:T(8,128)S(1)} %get-tuple-element.29), kind=kOutput, calls=%fused_computation.95 | convolution fusion | flops 806060032 | bytes 6291456 | tf_op jit(solution)/shard_map/ckn,nm->ckm/dot_general | solution.py:66
  115.0 2.7 %fusion.67 = f32[256,16,128]{2,0,1:T(8,128)S(1)} fusion(f32[256,16,128]{2,0,1:T(8,128)S(1)} %fusion.61, f32[256,16,128]{2,1,0:T(8,128)S(1)} %get-tuple-element.31), kind=kOutput, calls=%fused_computation.90 | convolution fusion | flops 806060032 | bytes 6291456 | tf_op jit(solution)/shard_map/ckn,nm->ckm/dot_general | solution.py:63
  117.8 3.5 %multiply_subtract_fusion.1 = (f32[256,16,128]{2,0,1:T(8,128)S(1)}, f32[256,16,128]{2,0,1:T(8,128)S(1)}, f32[256,16,128]{2,0,1:T(8,128)S(1)}, f32[256,16,128]{2,0,1:T(8,128)S(1)}) fusion(f32[256,16,128]{2,0,1:T(8,128)S(1)} %fusion.76, f32[256,16,128]{2,0,1:T(8,128)S(1)} %fusion.67, f32[256,16,128]{2,0,1:T(8,128)S(1)} %fusion.73, ...), kind=kOutput, calls=%fused_computation.49 | convolution fusion | flops 812351488 | bytes 23068672 | tf_op jit(solution)/shard_map/ckn,nm->ckm/dot_general | solution.py:66
  121.3 3.2 %fusion.35 = f32[256,16,128]{2,1,0:T(8,128)S(1)} fusion(f32[256,16,128]{2,0,1:T(8,128)S(1)} %get-tuple-element.3), kind=kOutput, calls=%fused_computation.58 | convolution fusion | flops 805535744 | bytes 4194304 | tf_op jit(solution)/shard_map/ckn,nm->ckm/dot_general | solution.py:79
  124.5 3.2 %fusion.37 = f32[256,16,128]{2,1,0:T(8,128)S(1)} fusion(f32[256,16,128]{2,0,1:T(8,128)S(1)} %get-tuple-element.3), kind=kOutput, calls=%fused_computation.60 | convolution fusion | flops 805535744 | bytes 4194304 | tf_op jit(solution)/shard_map/ckn,nm->ckm/dot_general | solution.py:76
  127.7 4.6 %fusion.27 = f32[256,16,128]{2,1,0:T(8,128)} fusion(f32[256,16,128]{2,0,1:T(8,128)S(1)} %get-tuple-element.12), kind=kOutput, calls=%fused_computation.50 | convolution fusion | flops 805535744 | bytes 4194304 | tf_op jit(solution)/shard_map/ckn,nm->ckm/dot_general | solution.py:79
  132.3 4.4 %fusion.29 = f32[256,16,128]{2,1,0:T(8,128)} fusion(f32[256,16,128]{2,0,1:T(8,128)S(1)} %get-tuple-element.12), kind=kOutput, calls=%fused_computation.52 | convolution fusion | flops 805535744 | bytes 4194304 | tf_op jit(solution)/shard_map/ckn,nm->ckm/dot_general | solution.py:76
  139.1 3.2 %fusion.88 = f32[256,16,128]{2,1,0:T(8,128)S(1)} fusion(f32[256,16,128]{2,1,0:T(8,128)S(1)} %fusion.35, f32[256,16,128]{2,0,1:T(8,128)S(1)} %get-tuple-element.2), kind=kOutput, calls=%fused_computation.97 | convolution fusion | flops 806060032 | bytes 6291456 | tf_op jit(solution)/shard_map/ckn,nm->ckm/dot_general | solution.py:79
  142.3 3.6 %fusion.85 = f32[256,16,128]{2,1,0:T(8,128)S(1)} fusion(f32[256,16,128]{2,1,0:T(8,128)S(1)} %fusion.37, f32[256,16,128]{2,0,1:T(8,128)S(1)} %get-tuple-element.2), kind=kOutput, calls=%fused_computation.96 | convolution fusion | flops 806060032 | bytes 6291456 | tf_op jit(solution)/shard_map/ckn,nm->ckm/dot_general | solution.py:76
  152.2 5.0 %fusion.94 = f32[256,16,128]{2,1,0:T(8,128)S(1)} fusion(f32[256,16,128]{2,1,0:T(8,128)} %fusion.27, f32[256,16,128]{2,0,1:T(8,128)S(1)} %get-tuple-element.13), kind=kOutput, calls=%fused_computation.99 | convolution fusion | flops 806060032 | bytes 6291456 | tf_op jit(solution)/shard_map/ckn,nm->ckm/dot_general | solution.py:79
  157.2 3.2 %fusion.91 = f32[256,16,128]{2,1,0:T(8,128)S(1)} fusion(f32[256,16,128]{2,1,0:T(8,128)S(1)} %copy-done.2, f32[256,16,128]{2,0,1:T(8,128)S(1)} %get-tuple-element.13), kind=kOutput, calls=%fused_computation.98 | convolution fusion | flops 806060032 | bytes 6291456 | tf_op jit(solution)/shard_map/ckn,nm->ckm/dot_general | solution.py:76
  161.9 2.6 %fusion.107 = f32[256,8,128]{2,1,0:T(8,128)} fusion(f32[256,128,8]{1,2,0:T(8,128)S(1)} %fusion.11, f32[256,16,128]{2,1,0:T(8,128)S(1)} %fusion.94, f32[256,16,128]{2,1,0:T(8,128)S(1)} %fusion.91, f32[16,128]{1,0:T(8,128)S(1)} %get-tuple-element.42, f32[16,128]{1,0:T(8,128)S(1)} %get-tuple-element.43, f32[16,16]{0,1:T(8,128)S(1)} %fusion.192), kind=kOutput, calls=%fused_computation.106 | convolution fusion | flops 52428800 | bytes 6308864 | tf_op jit(solution)/shard_map/nk,ckm->cnm/dot_general | solution.py:84
  164.5 2.5 %mul.900 = f32[1,256,1024]{2,1,0:T(8,128)} reshape(f32[256,8,128]{2,1,0:T(8,128)} %fusion.107) | data formatting | bytes 2097152 | tf_op jit(solution)/shard_map/mul | solution.py:87
  170.6 3.5 %all-to-all-start.1 = ((bf16[2,256,1024]{1,0,2:T(2,128)(2,1)}), bf16[2,256,1024]{1,0,2:T(2,128)(2,1)S(1)}, u32[]{:S(2)}, u32[]{:S(2)}) async-start(bf16[2,256,1024]{1,0,2:T(2,128)(2,1)} %copy.245), calls=%async_computation.1 | async-start | bytes 2097152 | tf_op jit(solution)/shard_map/all_to_all | solution.py:118
  174.3 25.1 %all-to-all-done.1 = bf16[2,256,1024]{1,0,2:T(2,128)(2,1)S(1)} async-done(((bf16[2,256,1024]{1,0,2:T(2,128)(2,1)}), bf16[2,256,1024]{1,0,2:T(2,128)(2,1)S(1)}, u32[]{:S(2)}, u32[]{:S(2)}) %all-to-all-start.1) | async-done | bytes 1048608 | tf_op jit(solution)/shard_map/all_to_all | solution.py:118
  207.7 4.4 %collective-permute-done.1 = f32[3,1024,2]{1,0,2:T(4,128)S(1)} collective-permute-done((f32[3,1024,2]{1,0,2:T(4,128)S(1)}, f32[3,1024,2]{1,0,2:T(4,128)S(1)}, u32[]{:S(2)}, u32[]{:S(2)}) %collective-permute-start.1) | collective-permute-done | bytes 24608 | tf_op jit(solution)/shard_map/ppermute | solution.py:13
  215.5 3.9 %fusion.2 = bf16[3,1024,256]{2,1,0:T(8,128)(2,1)} fusion(f32[3,1024,258]{2,1,0:T(8,128)S(1)} %pad_maximum_fusion, f32[256]{0:T(256)S(1)} %get-tuple-element.33, f32[256]{0:T(256)S(1)} %get-tuple-element.34, f32[256]{0:T(256)S(1)} %get-tuple-element.32, f32[3,1024]{1,0:T(4,128)S(1)} %get-tuple-element.40, f32[3,1024]{1,0:T(4,128)S(1)} %get-tuple-element.41, ...), kind=kLoop, calls=%fused_computation.4 | loop fusion | flops 8650752 | bytes 11049984 | tf_op jit(solution)/shard_map/convert_element_type | solution.py:153
  (86 shorter events, 46.5 us)
Async XLA Ops:
  0.6 8.6 %copy-start.8 = (bf16[3,1024,256]{2,1,0:T(8,128)(2,1)S(1)}, bf16[3,1024,256]{2,1,0:T(8,128)(2,1)}, u32[]{:S(2)}) copy-start(bf16[3,1024,256]{2,1,0:T(8,128)(2,1)} %param.6) | copy-start | bytes 4718596
  0.6 6.8 %copy-start.14 = (s32[16]{0:T(128)S(1)}, s32[16]{0:T(128)}, u32[]{:S(2)}) copy-start(s32[16]{0:T(128)} %param.11) | copy-start | bytes 196
  0.6 7.0 %copy-start.13 = (f32[3,3,1024]{2,1,0:T(4,128)S(1)}, f32[3,3,1024]{2,1,0:T(4,128)}, u32[]{:S(2)}) copy-start(f32[3,3,1024]{2,1,0:T(4,128)} %param.9) | copy-start | bytes 110596
  2.5 6.3 %collective-permute-start = (bf16[3,1024,2]{1,2,0:T(2,128)(2,1)S(1)}, bf16[3,1024,2]{1,2,0:T(2,128)(2,1)S(1)}, u32[]{:S(2)}, u32[]{:S(2)}) collective-permute-start(bf16[3,1024,2]{1,2,0:T(2,128)(2,1)S(1)} %copy.272), channel_id=1, source_target_pairs={{0,4},{4,8},{8,12},{1,5},{5,9},{9,13},{2,6},{6,10},{10,14},{3,7},{... | collective-permute-start | bytes 36872 | tf_op jit(solution)/shard_map/ppermute | solution.py:13
  9.2 4.2 %copy-start.10 = (bf16[1024,256]{1,0:T(8,128)(2,1)S(1)}, bf16[1024,256]{1,0:T(8,128)(2,1)}, u32[]{:S(2)}) copy-start(bf16[1024,256]{1,0:T(8,128)(2,1)} %param.7) | copy-start | bytes 1572868
  12.3 1.1 copy-start
  12.3 1.4 copy-start.12
  16.6 52.6 %all-to-all-start = ((bf16[3,1024,256]{2,0,1:T(4,128)(2,1)}), bf16[3,1024,256]{2,0,1:T(4,128)(2,1)S(1)}, u32[]{:S(2)}, u32[]{:S(2)}) async-start(bf16[3,1024,256]{2,0,1:T(4,128)(2,1)} %copy.208), calls=%async_computation | async-start | bytes 4194304 | tf_op jit(solution)/shard_map/all_to_all | solution.py:114
  75.6 4.7 %copy-start.9 = (bf16[1,256,4,256]{3,1,2,0:T(8,128)(2,1)S(1)}, bf16[1,256,4,256]{3,1,2,0:T(8,128)(2,1)}, u32[]{:S(2)}) copy-start(bf16[1,256,4,256]{3,1,2,0:T(8,128)(2,1)} %get-tuple-element.19) | copy-start | bytes 1572868
  82.6 1.6 copy-start.3
  132.3 4.4 %copy-start.5 = (f32[1,4,32,8,256]{4,3,2,1,0:T(8,128)S(1)}, f32[1,4,32,8,256]{4,3,2,1,0:T(8,128)}, u32[]{:S(2)}) copy-start(f32[1,4,32,8,256]{4,3,2,1,0:T(8,128)} %get-tuple-element.16) | copy-start | bytes 3145732
  136.7 1.2 copy-start.4
  152.2 5.0 %copy-start.2 = (f32[256,16,128]{2,1,0:T(8,128)S(1)}, f32[256,16,128]{2,1,0:T(8,128)}, u32[]{:S(2)}) copy-start(f32[256,16,128]{2,1,0:T(8,128)} %fusion.29) | copy-start | bytes 6291460
  164.5 2.5 %copy-start.6 = (f32[1,4,32,8,256]{4,3,1,2,0:T(8,128)S(1)}, f32[1,4,32,8,256]{4,3,1,2,0:T(8,128)}, u32[]{:S(2)}) copy-start(f32[1,4,32,8,256]{4,3,1,2,0:T(8,128)} %copy.274) | copy-start | bytes 3145732
  164.5 2.5 %copy-start.7 = (f32[1,256,1024]{2,1,0:T(8,128)S(1)}, f32[1,256,1024]{2,1,0:T(8,128)}, u32[]{:S(2)}) copy-start(f32[1,256,1024]{2,1,0:T(8,128)} %mul.883) | copy-start | bytes 3145732
  170.6 28.7 %all-to-all-start.1 = ((bf16[2,256,1024]{1,0,2:T(2,128)(2,1)}), bf16[2,256,1024]{1,0,2:T(2,128)(2,1)S(1)}, u32[]{:S(2)}, u32[]{:S(2)}) async-start(bf16[2,256,1024]{1,0,2:T(2,128)(2,1)} %copy.245), calls=%async_computation.1 | async-start | bytes 2097152 | tf_op jit(solution)/shard_map/all_to_all | solution.py:118
  200.1 1.4 copy-start.1
  200.2 1.6 copy-start.11
  206.3 5.8 %collective-permute-start.1 = (f32[3,1024,2]{1,0,2:T(4,128)S(1)}, f32[3,1024,2]{1,0,2:T(4,128)S(1)}, u32[]{:S(2)}, u32[]{:S(2)}) collective-permute-start(f32[3,1024,2]{1,0,2:T(4,128)S(1)} %copy.247), channel_id=1, source_target_pairs={{4,0},{8,4},{12,8},{5,1},{9,5},{13,9},{6,2},{10,6},{14,10},{7,3},{... | collective-permute-start | bytes 73736 | tf_op jit(solution)/shard_map/ppermute | solution.py:13
where the time goes:
time: 223 us; the launch traced here: 220 us
  matrix products  84.5 us (38%)
  waiting for transfers between devices  76.4 us (34%)
  local copies, waits for them, and re-layouts  27.4 us (12%)
  starting transfers between devices  15.5 us (7%)
  other arithmetic  14.5 us (7%)
    all_to_all x1, waiting for transfers between devices, to_channels(): lax.all_to_all(stacked, 'seq', split_axis=1, concat_axis=2, tiled=True)  45.9 us
    all_to_all x1, waiting for transfers between devices, to_sequence(): lax.all_to_all(stacked, 'seq', split_axis=2, concat_axis=1, tiled=True)  25.1 us
    dot_general x3, matrix products, forward_transform(): jnp.einsum('ckn,nm->ckm', turned_re, col_im, precision=HIGHEST)  8.84 us
    dot_general x3, matrix products, forward_transform(): jnp.einsum('ckn,nm->ckm', turned_im, col_im, precision=HIGHEST)  8.28 us
    dot_general x2, matrix products, inverse_transform(): jnp.einsum('ckn,nm->ckm', spec_re, col_im, precision=HIGHEST)  8.19 us
    dot_general x3, matrix products, forward_transform(): jnp.einsum('ckn,nm->ckm', turned_re, col_re, precision=HIGHEST)  7.87 us
    dot_general x3, matrix products, forward_transform(): jnp.einsum('kn,cnm->ckm', row_im[:, :half_rows], blocks_in, precision=HIG...  7.82 us
    dot_general x2, matrix products, inverse_transform(): jnp.einsum('ckn,nm->ckm', spec_im, col_re, precision=HIGHEST)  7.78 us
  transfers between devices with their start and end apart: 4, of which 4 were waited for; matrix products, arithmetic and copies ran while one was open for 1% of the time, Pallas kernels for 0%

commit v1 on v0

v1 whole, which is shorter than its diff:
```python
import functools
import math

import jax
import jax.numpy as jnp
import numpy as np
from jax import lax
from jax.experimental import pallas as pl
from jax.experimental.pallas import tpu as pltpu
from jax.sharding import PartitionSpec as P

BF16 = jnp.bfloat16
F32 = jnp.float32
VMEM_LIMIT = 48 * 1024 * 1024
WHOLE = pl.BlockSpec(memory_space=pltpu.VMEM)
SCALARS = pl.BlockSpec(memory_space=pltpu.SMEM)


def split_bf16(table):
    high = table.astype(np.float32).astype(BF16)
    low = (table - high.astype(np.float64)).astype(np.float32).astype(BF16)
    return high, low


def block_tables(span):
    freq = np.concatenate([np.arange(0, span, 2), np.arange(1, span, 2)])
    angle = np.pi * (2 * freq[None, :] + 1) * np.arange(span)[:, None] / (2 * span)
    forward = np.concatenate([np.cos(angle), -np.sin(angle)], axis=1)
    inverse = np.concatenate([np.cos(angle), -np.sin(angle)], axis=1).T / span
    return split_bf16(forward) + split_bf16(inverse)


def dot(a, b):
    return jnp.dot(a, b, preferred_element_type=F32)


def call(body, outs, scratch=(), in_specs=None, grid=None, out_specs=None, aliases=None, cost=None):
    return pl.pallas_call(
        body,
        out_shape=outs,
        in_specs=in_specs,
        out_specs=out_specs,
        grid=grid or (),
        scratch_shapes=scratch,
        input_output_aliases=aliases or {},
        compiler_params=pltpu.CompilerParams(vmem_limit_bytes=VMEM_LIMIT),
        cost_estimate=cost,
    )


def estimate(flops, moved):
    return pl.CostEstimate(flops=int(flops), bytes_accessed=int(moved), transcendentals=0)


def offsets_row(lengths_ref, first, span, ahead):
    position = lax.broadcasted_iota(jnp.int32, (8, span), 1) + (first + ahead)

    def step(genome, carry):
        end, start = carry
        end = end + lengths_ref[genome]
        return end, jnp.where(position >= end, end, start)

    begin = (jnp.int32(0), jnp.zeros((8, span), jnp.int32))
    _, start = lax.fori_loop(0, lengths_ref.shape[0], step, begin)
    return position, position - start


def pack_body(parts, rank_ref, tail_ref, filt_ref, taps_ref, skip_ref, halo_ref, cols_ref, *rest):
    filt_out, rows_ref, halo_rows = rest[:parts], rest[parts], rest[parts + 1]
    rank = rank_ref[0]
    size = filt_out[0].shape[0]
    for step in range(parts):
        begin = pl.multiple_of(jnp.bitwise_xor(rank, step) * size, size)
        filt_out[step][...] = filt_ref[pl.ds(begin, size), :]
    halo_rows[...] = jnp.zeros(halo_rows.shape, F32)
    for which in range(3):
        turned = tail_ref[which].astype(F32).T
        halo_rows[2 * which : 2 * which + 2, :] = turned[-2:, :]
    halo_ref[...] = halo_rows[...].astype(BF16)
    rows_ref[...] = jnp.zeros(rows_ref.shape, F32)
    for which in range(3):
        rows_ref[3 * which : 3 * which + 3, :] = taps_ref[which]
    rows_ref[9:10, :] = skip_ref[...]
    cols_ref[...] = rows_ref[...].T


def pack(rank, features, filters, taps, skip, parts):
    _, channels, span = features.shape
    size = channels // parts
    outs = [
        jax.ShapeDtypeStruct((16, channels), BF16),
        jax.ShapeDtypeStruct((channels, 16), F32),
    ] + [jax.ShapeDtypeStruct((size, span), BF16)] * parts
    tail = pl.BlockSpec((3, channels, 128), lambda step: (0, 0, span // 128 - 1))
    found = call(
        functools.partial(pack_body, parts),
        outs,
        scratch=[pltpu.VMEM((16, channels), F32), pltpu.VMEM((16, channels), F32)],
        grid=(1,),
        in_specs=[SCALARS, tail, WHOLE, WHOLE, WHOLE],
        out_specs=[WHOLE] * len(outs),
        cost=estimate(0, 3 * channels * span * 2),
    )(rank, features, filters, taps, skip.reshape(1, channels))
    return found[0], found[1], found[2:]


def gate_body(parts, chunks, rank_ref, lengths_ref, feat_ref, dout_ref, halo_ref, cols_ref, qkv_ref, *rest):
    sent, edge = rest[: parts * chunks], rest[-1]
    rank = rank_ref[0]
    _, channels, span = feat_ref.shape
    rows = channels // parts // chunks
    group = min(32, rows)
    _, offset = offsets_row(lengths_ref, rank * span, span, 0)
    keep = [(offset[0:1, :] >= j).astype(F32) for j in (1, 2)]
    lane = lax.broadcasted_iota(jnp.int32, (group, span), 1)
    edge[...] = halo_ref[...].astype(F32).T
    for step in range(parts):
        for chunk in range(chunks):
            out = sent[step * chunks + chunk]
            base = (jnp.bitwise_xor(rank, step) * chunks + chunk) * rows

            def tile(index, _, base=base, out=out):
                place = pl.ds(pl.multiple_of(base + index * group, group), group)
                local_place = pl.ds(pl.multiple_of(index * group, group), group)
                cols = cols_ref[place, :]
                ends = edge[place, :]
                filtered = []
                for which in range(3):
                    here = feat_ref[which, place, :].astype(F32)
                    two_back = ends[:, 2 * which : 2 * which + 1]
                    one_back = ends[:, 2 * which + 1 : 2 * which + 2]
                    back = jnp.where(lane == 0, one_back, pltpu.roll(here, 1, 1))
                    twice = jnp.where(lane == 0, two_back, jnp.where(lane == 1, one_back, pltpu.roll(here, 2, 1)))
                    total = cols[:, 3 * which : 3 * which + 1] * here
                    total = total + cols[:, 3 * which + 1 : 3 * which + 2] * back * keep[0]
                    total = total + cols[:, 3 * which + 2 : 3 * which + 3] * twice * keep[1]
                    rounded = total.astype(BF16)
                    qkv_ref[which, place, :] = rounded
                    filtered.append(rounded.astype(F32))
                out[0, local_place, :] = (filtered[1] * filtered[2]).astype(BF16)
                out[1, local_place, :] = (dout_ref[place, :].astype(F32) * filtered[0]).astype(BF16)
                return 0

            lax.fori_loop(0, rows // group, tile, 0)


def gate(rank, lengths, features, dout, halo, cols, parts, chunks):
    _, channels, span = features.shape
    rows = channels // parts // chunks
    outs = [jax.ShapeDtypeStruct(features.shape, BF16)]
    outs += [jax.ShapeDtypeStruct((2, rows, span), BF16)] * (parts * chunks)
    found = call(
        functools.partial(gate_body, parts, chunks),
        outs,
        scratch=[pltpu.VMEM((channels, 16), F32)],
        in_specs=[SCALARS, SCALARS, WHOLE, WHOLE, WHOLE, WHOLE],
        out_specs=[WHOLE] * len(outs),
        cost=estimate(30 * channels * span, 9 * channels * span * 2),
    )(rank, lengths, features, dout, halo, cols)
    return found[0], [found[1 + step * chunks : 1 + (step + 1) * chunks] for step in range(parts)]


def conv_body(parts, rank_ref, cols_ref, fhi_ref, flo_ref, ihi_ref, ilo_ref, *rest):
    filt_in, moved_in = rest[:parts], rest[parts : 2 * parts]
    outs = rest[2 * parts : 3 * parts]
    raw, spec, high, low, back = rest[3 * parts :]
    rank = rank_ref[0]
    rows, span = filt_in[0].shape
    half = span // 2
    block = parts * rows
    for step in range(parts):
        slot = jnp.bitwise_xor(rank, step) * rows
        for kind in range(3):
            value = filt_in[step][...] if kind == 0 else moved_in[step][kind - 1]
            raw[pl.ds(pl.multiple_of(kind * block + slot, rows), rows), :] = value

    def forward(kind, _):
        place = pl.ds(pl.multiple_of(kind * block, block), block)
        value = raw[place, :]
        spec[place, :] = dot(value, fhi_ref[...]) + dot(value, flo_ref[...])
        return 0

    lax.fori_loop(0, 3, forward, 0)
    group = min(16, rows)

    def loop(count, body, init):
        if parts <= 4:
            for k in range(count):
                init = body(k, init)
            return init
        return lax.fori_loop(0, count, body, init)

    def products(index, _):
        def read(kind, k):
            begin = kind * block + k * rows + index * group
            place = pl.ds(pl.multiple_of(begin, group), group)
            return spec[place, :span], spec[place, span:]

        def store(kind, k, re, im):
            begin = kind * block + k * rows + index * group
            place = pl.ds(pl.multiple_of(begin, group), group)
            for begin_lane, part in ((0, re), (span, im)):
                top = part.astype(BF16)
                high[place, begin_lane : begin_lane + span] = top
                low[place, begin_lane : begin_lane + span] = (part - top.astype(F32)).astype(BF16)

        zero = jnp.zeros((group, span), F32)

        def turn(re, im):
            return (
                jnp.concatenate([-im[:, :half], im[:, half:]], axis=1),
                jnp.concatenate([re[:, :half], -re[:, half:]], axis=1),
            )

        before = None
        for place in range(parts):

            def add(k, total, place=place):
                f_re, f_im = read(0, k)
                m_re, m_im = read(1, place - k)
                return (total[0] + f_re * m_re - f_im * m_im, total[1] + f_re * m_im + f_im * m_re)

            re, im = loop(place + 1, add, (zero, zero))
            if before is None:
                store(0, place, re, im)
            else:
                t_re, t_im = turn(*before)
                store(0, place, re + t_re, im + t_im)
            before = (re, im)
        before = None
        for place in range(parts - 1, -1, -1):

            def add_conj(k, total, place=place):
                f_re, f_im = read(0, k)
                g_re, g_im = read(2, place + k)
                return (total[0] + f_re * g_re + f_im * g_im, total[1] + f_re * g_im - f_im * g_re)

            re, im = loop(parts - place, add_conj, (zero, zero))
            if before is None:
                store(1, place, re, im)
            else:
                t_re, t_im = turn(*before)
                store(1, place, re - t_re, im - t_im)
            before = (re, im)
        return 0

    lax.fori_loop(0, rows // group, products, 0)

    def inverse(kind, _):
        place = pl.ds(pl.multiple_of(kind * block, block), block)
        top = high[place, :]
        back[place, :] = dot(top, ihi_ref[...]) + dot(top, ilo_ref[...]) + dot(low[place, :], ihi_ref[...])
        return 0

    lax.fori_loop(0, 2, inverse, 0)
    skip = cols_ref[:, 9:10]
    for step in range(parts):
        slot = jnp.bitwise_xor(rank, step) * rows
        for kind in range(2):
            value = back[pl.ds(pl.multiple_of(kind * block + slot, rows), rows), :]
            direct = raw[pl.ds(pl.multiple_of((kind + 1) * block + slot, rows), rows), :].astype(F32)
            outs[step][kind] = (value + skip * direct).astype(BF16)


def conv(rank, cols, filt, moved, tables, chunk, chunks):
    parts = len(filt)
    _, rows, span = moved[0].shape
    block = parts * rows
    outs = [jax.ShapeDtypeStruct((2, rows, span), BF16)] * parts
    cols_spec = pl.BlockSpec((rows, 16), lambda step, rank_ref: (rank_ref[0] * chunks + chunk, 0))
    filt_spec = pl.BlockSpec((rows, span), lambda step, rank_ref: (chunk, 0))

    def fixed(shape):
        return pl.BlockSpec(shape, lambda step, rank_ref: (0,) * len(shape))

    in_specs = [cols_spec] + [fixed(t.shape) for t in tables] + [filt_spec] * parts + [fixed(moved[0].shape)] * parts
    flops = 2 * block * span * 2 * span * 12
    return pl.pallas_call(
        functools.partial(conv_body, parts),
        out_shape=outs,
        grid_spec=pltpu.PrefetchScalarGridSpec(
            num_scalar_prefetch=1,
            grid=(1,),
            in_specs=in_specs,
            out_specs=[fixed((2, rows, span))] * parts,
            scratch_shapes=[
                pltpu.VMEM((3 * block, span), BF16),
                pltpu.VMEM((3 * block, 2 * span), F32),
                pltpu.VMEM((2 * block, 2 * span), BF16),
                pltpu.VMEM((2 * block, 2 * span), BF16),
                pltpu.VMEM((2 * block, span), F32),
            ],
        ),
        compiler_params=pltpu.CompilerParams(vmem_limit_bytes=VMEM_LIMIT),
        cost_estimate=estimate(flops, 5 * block * span * 2),
    )(rank, cols, *tables, *filt, *moved)


def first_body(parts, chunk, chunks, rank_ref, qkv_ref, dout_ref, *rest):
    slots, out_ref, grads = rest[:parts], rest[parts], rest[parts + 1]
    rank = rank_ref[0]
    _, rows, lanes = slots[0].shape
    for step in range(parts):
        owner = jnp.bitwise_xor(rank, step)
        place = pl.ds(pl.multiple_of((owner * chunks + chunk) * rows, rows), rows)
        here = pl.ds(pl.multiple_of(owner * rows, rows), rows)
        y_out = slots[step][0].astype(F32)
        dmixed = slots[step][1].astype(F32)
        grads[0, here, :] = dout_ref[place, :].astype(F32) * y_out
        grads[1, here, :] = dmixed * qkv_ref[2, place, :].astype(F32)
        grads[2, here, :] = dmixed * qkv_ref[1, place, :].astype(F32)
    out_ref[...] = jnp.zeros(out_ref.shape, F32)
    for which in range(3):
        out_ref[2 * which : 2 * which + 2, :] = grads[which].T[0:2, :]


def first_grads(rank, qkv, dout, slots, chunk, chunks):
    parts = len(slots)
    _, rows, span = slots[0].shape
    channels = dout.shape[0]
    return call(
        functools.partial(first_body, parts, chunk, chunks),
        jax.ShapeDtypeStruct((8, parts * rows), F32),
        scratch=[pltpu.VMEM((3, parts * rows, 128), F32)],
        grid=(1,),
        in_specs=[
            SCALARS,
            pl.BlockSpec((3, channels, 128), lambda step: (0, 0, 0)),
            pl.BlockSpec((channels, 128), lambda step: (0, 0)),
        ]
        + [pl.BlockSpec((2, rows, 128), lambda step: (0, 0, 0))] * parts,
        out_specs=WHOLE,
        cost=estimate(0, 3 * channels * 128 * 2),
    )(rank, qkv, dout, *slots)


def final_body(parts, chunk, rank_ref, lengths_ref, qkv_ref, dout_ref, cols_ref, ahead_ref, *rest):
    slots = rest[:parts]
    out_ref, dfeat_ref, edge, moved = rest[-4:]
    rank = rank_ref[0]
    step = pl.program_id(0)
    _, rows, span = slots[0].shape

    @pl.when(step == 0)
    def _():
        edge[...] = ahead_ref[...].T

    for k in range(parts):

        @pl.when(step == k)
        def _(k=k):
            moved[...] = slots[k][...]

    owner = jnp.bitwise_xor(rank, step)
    group = min(32, rows)
    lane = lax.broadcasted_iota(jnp.int32, (group, span), 1)
    keep = []
    for j in (1, 2):
        position, offset = offsets_row(lengths_ref, rank * span, span, j)
        inside = (position < parts * span) & (offset >= j)
        keep.append(inside[0:1, :].astype(F32))

    def tile(index, _):
        place = pl.ds(pl.multiple_of(index * group, group), group)
        ends = edge[pl.ds(pl.multiple_of(owner * rows + index * group, group), group), :]
        cols = cols_ref[place, :]
        y_out = moved[0, place, :].astype(F32)
        dmixed = moved[1, place, :].astype(F32)
        out_ref[place, :] = (qkv_ref[0, place, :].astype(F32) * y_out).astype(BF16)
        grads = (
            dout_ref[place, :].astype(F32) * y_out,
            dmixed * qkv_ref[2, place, :].astype(F32),
            dmixed * qkv_ref[1, place, :].astype(F32),
        )
        for which in range(3):
            here = grads[which]
            first = ends[:, 2 * which : 2 * which + 1]
            second = ends[:, 2 * which + 1 : 2 * which + 2]
            next_one = jnp.where(lane == span - 1, first, pltpu.roll(here, span - 1, 1))
            next_two = jnp.where(
                lane == span - 1, second, jnp.where(lane == span - 2, first, pltpu.roll(here, span - 2, 1))
            )
            total = cols[:, 3 * which : 3 * which + 1] * here
            total = total + cols[:, 3 * which + 1 : 3 * which + 2] * next_one * keep[0]
            total = total + cols[:, 3 * which + 2 : 3 * which + 3] * next_two * keep[1]
            dfeat_ref[which, place, :] = total.astype(BF16)
        return 0

    lax.fori_loop(0, rows // group, tile, 0)


def final(rank, lengths, qkv, dout, cols, ahead, slots, chunk, chunks, earlier):
    parts = len(slots)
    _, rows, span = slots[0].shape
    channels = dout.shape[0]

    def block(step, rank_ref, lengths_ref):
        return jnp.bitwise_xor(rank_ref[0], step) * chunks + chunk

    def wide(step, *refs):
        return (0, block(step, *refs), 0)

    def flat(step, *refs):
        return (block(step, *refs), 0)

    def fixed(shape):
        return pl.BlockSpec(shape, lambda step, *refs: (0,) * len(shape))

    in_specs = [
        pl.BlockSpec((3, rows, span), wide),
        pl.BlockSpec((rows, span), flat),
        pl.BlockSpec((rows, 16), flat),
        fixed(ahead.shape),
    ] + [fixed(slots[0].shape)] * parts
    operands = [qkv, dout, cols, ahead, *slots]
    aliases = {}
    if earlier is not None:
        aliases = {2 + len(operands): 0, 3 + len(operands): 1}
        in_specs = in_specs + [pl.BlockSpec(memory_space=pl.ANY)] * 2
        operands = operands + list(earlier)
    return pl.pallas_call(
        functools.partial(final_body, parts, chunk),
        out_shape=[
            jax.ShapeDtypeStruct((channels, span), BF16),
            jax.ShapeDtypeStruct((3, channels, span), BF16),
        ],
        grid_spec=pltpu.PrefetchScalarGridSpec(
            num_scalar_prefetch=2,
            grid=(parts,),
            in_specs=in_specs,
            out_specs=[pl.BlockSpec((rows, span), flat), pl.BlockSpec((3, rows, span), wide)],
            scratch_shapes=[pltpu.VMEM((parts * rows, 8), F32), pltpu.VMEM((2, rows, span), BF16)],
        ),
        input_output_aliases=aliases,
        compiler_params=pltpu.CompilerParams(vmem_limit_bytes=VMEM_LIMIT),
        cost_estimate=estimate(40 * parts * rows * span, 10 * parts * rows * span * 2),
    )(rank, lengths, *operands)


def swap(value, step, parts):
    return lax.ppermute(value, "seq", [(source, source ^ step) for source in range(parts)])


def around(value, steps, parts):
    return lax.ppermute(value, "seq", [(source, (source + steps) % parts) for source in range(parts)])


def local(features, dout, filters, taps, skip, lengths):
    parts = lax.axis_size("seq")
    _, channels, span = features.shape
    chunks = 2 if channels // parts % 32 == 0 else 1
    rank = lax.axis_index("seq").astype(jnp.int32).reshape(1)
    tables = [jnp.asarray(t) for t in block_tables(span)]

    halo, cols, filt = pack(rank, features, filters, taps, skip, parts)
    halo = around(halo, 1, parts)
    filt = [filt[0]] + [swap(filt[step], step, parts) for step in range(1, parts)]
    qkv, sent = gate(rank, lengths, features, dout, halo, cols, parts, chunks)
    arrived = [
        [sent[0][c]] + [swap(sent[step][c], step, parts) for step in range(1, parts)] for c in range(chunks)
    ]
    done = None
    for c in range(chunks):
        back = conv(rank, cols, filt, arrived[c], tables, c, chunks)
        slots = [back[0]] + [swap(back[step], step, parts) for step in range(1, parts)]
        ahead = around(first_grads(rank, qkv, dout, slots, c, chunks), -1, parts)
        done = final(rank, lengths, qkv, dout, cols, ahead, slots, c, chunks, done)
    return tuple(done)


def solution(mesh):
    in_specs = (
        P(None, ("chan", "sub"), ("groups", "seq")),
        P(("chan", "sub"), ("groups", "seq")),
        P(("chan", "sub"), "seq"),
        P(None, None, ("chan", "sub")),
        P(("chan", "sub")),
        P("groups"),
    )
    out_specs = (P(("chan", "sub"), ("groups", "seq")), P(None, ("chan", "sub"), ("groups", "seq")))
    return jax.shard_map(local, mesh=mesh, in_specs=in_specs, out_specs=out_specs, check_vma=False)
```

time: 223 us -> 83.1 us (0.37); the launches traced: 220 us -> 82.8 us
  matrix products: 84.5 us -> 0 us
  waiting for transfers between devices: 76.4 us -> 12.8 us
  Pallas kernels: 0 us -> 27.6 us
  local copies, waits for them, and re-layouts: 27.4 us -> 4.02 us
  starting transfers between devices: 15.5 us -> 37.7 us
  other arithmetic: 14.5 us -> 0 us
    dot_general x30 -> x0, matrix products: 84.5 us -> none  [the longest x3 8.84 us: forward_transform(): jnp.einsum('ckn,nm->ckm', turned_re, col_im, precision=HIGHEST)]
    all_to_all x2 -> x0, waiting for transfers between devices: 71 us -> none  [the longest x1 45.9 us: to_channels(): lax.all_to_all(stacked, 'seq', split_axis=1, concat_axis=2, tiled=True)]
    ppermute x2 -> x18, starting transfers between devices: 6.22 us -> 37.7 us  [the longest x15 30.8 us: swap(): lax.ppermute(value, 'seq', [(source, source ^ step) for source in range(p...]
    pallas_call x0 -> x8, Pallas kernels: none -> 27.6 us  [the longest x2 11.9 us: final(): pl.pallas_call(functools.partial(final_body, parts, chunk), out_shape=[ja...]
    all_to_all x2 -> x0, starting transfers between devices: 9.25 us -> none  [the longest x1 5.73 us: to_channels(): lax.all_to_all(stacked, 'seq', split_axis=1, concat_axis=2, tiled=True)]
    convert_element_type x6 -> x0, other arithmetic: 8.64 us -> none  [the longest x1 3.92 us: local(): short_backward(grads_ext, taps, offsets_ext).astype(jnp.bfloat16)]
    ppermute x2 -> x18, waiting for transfers between devices: 5.39 us -> 12.8 us  [the longest x15 10.8 us: swap(): lax.ppermute(value, 'seq', [(source, source ^ step) for source in range(p...]
    slice x8 -> x0, local copies, waits for them, and re-layouts: 6.3 us -> none  [the longest x2 3.27 us: local(): ahead = shifted(grads[:, :, :margin], 'seq', -1)]
  transfers between devices with their start and end apart: 4 -> 18, of which waited for: 4 -> 4; matrix products, arithmetic and copies ran while one was open for 1% -> 0% of each run, Pallas kernels for 0% -> 26%
where the time goes in v1:
time: 83.1 us; the launch traced here: 82.8 us
  starting transfers between devices  37.7 us (45%)
  Pallas kernels  27.6 us (33%)
  waiting for transfers between devices  12.8 us (15%)
  local copies, waits for them, and re-layouts  4.02 us (5%)
    ppermute x15, starting transfers between devices, swap(): lax.ppermute(value, 'seq', [(source, source ^ step) for source in range(p...  30.8 us
    pallas_call x2, Pallas kernels, final(): pl.pallas_call(functools.partial(final_body, parts, chunk), out_shape=[ja...  11.9 us
    ppermute x15, waiting for transfers between devices, swap(): lax.ppermute(value, 'seq', [(source, source ^ step) for source in range(p...  10.8 us
    pallas_call x2, Pallas kernels, conv(): pl.pallas_call(functools.partial(conv_body, parts), out_shape=outs, grid_...  7.45 us
    ppermute x3, starting transfers between devices, around(): lax.ppermute(value, 'seq', [(source, (source + steps) % parts) for source...  6.88 us
    pallas_call x1, Pallas kernels, gate(): call(functools.partial(gate_body, parts, chunks), outs, scratch=[pltpu.VM...  6.75 us
    unnamed x20, local copies, waits for them, and re-layouts  4.02 us
    ppermute x3, waiting for transfers between devices, around(): lax.ppermute(value, 'seq', [(source, (source + steps) % parts) for source...  1.96 us
  transfers between devices with their start and end apart: 18, of which 4 were waited for; matrix products, arithmetic and copies ran while one was open for 0% of the time, Pallas kernels for 26%

profile of v1, /device:TPU:0, one launch (start us, length us, event | category | flops | bytes accessed | tf_op | source)
XLA Modules:
  0.0 82.8 jit_solution(8686412368426537427)
XLA Ops:
  0.7 1.5 %copy-done.1 = bf16[3,1024,256]{2,1,0:T(8,128)(2,1)S(1)} copy-done((bf16[3,1024,256]{2,1,0:T(8,128)(2,1)S(1)}, bf16[3,1024,256]{2,1,0:T(8,128)(2,1)}, u32[]{:S(2)}) %copy-start.1) | copy-done | bytes 1572888
  2.1 1.0 %copy-done.2 = bf16[1024,256]{1,0:T(8,128)(2,1)S(1)} copy-done((bf16[1024,256]{1,0:T(8,128)(2,1)S(1)}, bf16[1024,256]{1,0:T(8,128)(2,1)}, u32[]{:S(2)}) %copy-start.2) | copy-done | bytes 524312
  3.2 0.8 copy-done.3
  4.0 0.7 copy-done.5
  4.6 0.5 shard_map.113
  5.1 3.1 %collective-permute-start.1 = (bf16[256,256]{1,0:T(8,128)(2,1)S(1)}, bf16[256,256]{1,0:T(8,128)(2,1)S(1)}, u32[]{:S(2)}, u32[]{:S(2)}) collective-permute-start(bf16[256,256]{1,0:T(8,128)(2,1)S(1)} %get-tuple-element.31), channel_id=1, source_target_pairs={{0,4},{4,0},{8,12},{12,8},{1,5},{5,1},{9,13},{13,9},{2,6},{6,2},{1... | collective-permute-start | bytes 393224 | tf_op jit(solution)/shard_map/ppermute | solution.py:441
  8.3 3.0 %collective-permute-start.2 = (bf16[256,256]{1,0:T(8,128)(2,1)S(1)}, bf16[256,256]{1,0:T(8,128)(2,1)S(1)}, u32[]{:S(2)}, u32[]{:S(2)}) collective-permute-start(bf16[256,256]{1,0:T(8,128)(2,1)S(1)} %get-tuple-element.32), channel_id=1, source_target_pairs={{0,8},{4,12},{8,0},{12,4},{1,9},{5,13},{9,1},{13,5},{2,10},{6,14},... | collective-permute-start | bytes 393224 | tf_op jit(solution)/shard_map/ppermute | solution.py:441
  11.3 2.5 %collective-permute-start.3 = (bf16[256,256]{1,0:T(8,128)(2,1)S(1)}, bf16[256,256]{1,0:T(8,128)(2,1)S(1)}, u32[]{:S(2)}, u32[]{:S(2)}) collective-permute-start(bf16[256,256]{1,0:T(8,128)(2,1)S(1)} %get-tuple-element.33), channel_id=1, source_target_pairs={{0,12},{4,8},{8,4},{12,0},{1,13},{5,9},{9,5},{13,1},{2,14},{6,10},... | collective-permute-start | bytes 393224 | tf_op jit(solution)/shard_map/ppermute | solution.py:441
  13.8 2.0 %collective-permute-done.halo_ref = bf16[16,1024]{1,0:T(8,128)(2,1)S(1)} collective-permute-done((bf16[16,1024]{1,0:T(8,128)(2,1)S(1)}, bf16[16,1024]{1,0:T(8,128)(2,1)S(1)}, u32[]{:S(2)}, u32[]{:S(2)}) %collective-permute-start) | collective-permute-done | bytes 32800 | tf_op jit(solution)/shard_map/ppermute | solution.py:445
  15.7 6.8 %shard_map.114 = (bf16[3,1024,256]{2,1,0:T(8,128)(2,1)S(1)}, bf16[2,128,256]{2,1,0:T(8,128)(2,1)S(1)}, bf16[2,128,256]{2,1,0:T(8,128)(2,1)S(1)}, bf16[2,128,256]...) custom-call(s32[1]{0:T(128)} %bitcast.rank_ref, ...), custom_call_target="tpu_custom_call" | custom-call | flops 7864320 | bytes 4718592 | tf_op jit(solution)/shard_map/pallas_call | solution.py:152
  22.5 0.1 collective-permute-start.11
  22.6 1.9 %collective-permute-start.12 = (bf16[2,128,256]{2,1,0:T(8,128)(2,1)S(1)}, bf16[2,128,256]{2,1,0:T(8,128)(2,1)S(1)}, u32[]{:S(2)}, u32[]{:S(2)}) collective-permute-start(bf16[2,128,256]{2,1,0:T(8,128)(2,1)S(1)} %get-tuple-element.44), channel_id=1, source_target_pairs={{0,8},{4,12},{8,0},{12,4},{1,9},{5,13},{9,1},{13,5},{2,10},{6,14},... | collective-permute-start | bytes 393224 | tf_op jit(solution)/shard_map/ppermute | solution.py:441
  24.5 2.4 %collective-permute-start.13 = (bf16[2,128,256]{2,1,0:T(8,128)(2,1)S(1)}, bf16[2,128,256]{2,1,0:T(8,128)(2,1)S(1)}, u32[]{:S(2)}, u32[]{:S(2)}) collective-permute-start(bf16[2,128,256]{2,1,0:T(8,128)(2,1)S(1)} %get-tuple-element.45), channel_id=1, source_target_pairs={{0,12},{4,8},{8,4},{12,0},{1,13},{5,9},{9,5},{13,1},{2,14},{6,10},... | collective-permute-start | bytes 393224 | tf_op jit(solution)/shard_map/ppermute | solution.py:441
  26.9 1.9 %collective-permute-start.5 = (bf16[2,128,256]{2,1,0:T(8,128)(2,1)S(1)}, bf16[2,128,256]{2,1,0:T(8,128)(2,1)S(1)}, u32[]{:S(2)}, u32[]{:S(2)}) collective-permute-start(bf16[2,128,256]{2,1,0:T(8,128)(2,1)S(1)} %get-tuple-element.36), channel_id=1, source_target_pairs={{0,8},{4,12},{8,0},{12,4},{1,9},{5,13},{9,1},{13,5},{2,10},{6,14},... | collective-permute-start | bytes 393224 | tf_op jit(solution)/shard_map/ppermute | solution.py:441
  28.9 2.0 %collective-permute-done.11.rest_5_ = bf16[2,128,256]{2,1,0:T(8,128)(2,1)S(1)} collective-permute-done((bf16[2,128,256]{2,1,0:T(8,128)(2,1)S(1)}, bf16[2,128,256]{2,1,0:T(8,128)(2,1)S(1)}, u32[]{:S(2)}, u32[]{:S(2)}) %collective-permute-start.11) | collective-permute-done | bytes 131104 | tf_op jit(solution)/shard_map/ppermute | solution.py:441
  30.8 1.4 %collective-permute-start.6 = (bf16[2,128,256]{2,1,0:T(8,128)(2,1)S(1)}, bf16[2,128,256]{2,1,0:T(8,128)(2,1)S(1)}, u32[]{:S(2)}, u32[]{:S(2)}) collective-permute-start(bf16[2,128,256]{2,1,0:T(8,128)(2,1)S(1)} %get-tuple-element.37), channel_id=1, source_target_pairs={{0,12},{4,8},{8,4},{12,0},{1,13},{5,9},{9,5},{13,1},{2,14},{6,10},... | collective-permute-start | bytes 393224 | tf_op jit(solution)/shard_map/ppermute | solution.py:441
  32.2 3.5 %collective-permute-done.12.rest_6_ = bf16[2,128,256]{2,1,0:T(8,128)(2,1)S(1)} collective-permute-done((bf16[2,128,256]{2,1,0:T(8,128)(2,1)S(1)}, bf16[2,128,256]{2,1,0:T(8,128)(2,1)S(1)}, u32[]{:S(2)}, u32[]{:S(2)}) %collective-permute-start.12) | collective-permute-done | bytes 131104 | tf_op jit(solution)/shard_map/ppermute | solution.py:441
  35.8 3.7 %shard_map.117 = (bf16[2,128,256]{2,1,0:T(8,128)(2,1)S(1)}, bf16[2,128,256]{2,1,0:T(8,128)(2,1)S(1)}, bf16[2,128,256]{2,1,0:T(8,128)(2,1)S(1)}, bf16[2,128,256]{2,1,0:T(8,128)(2,1)S(1)}) custom-call(s32[1]{0:T(128)} %bitcast.rank_ref, f32[1024,16]{1,0:T(8,128)S(1)} %get-tuple-element.28.cols_ref, bf16[256,512]{1,0:T(8,128)(2,1)S(1)} %copy-done.9, ...), custom_call_target="tpu_custom_call" | custom-call | flops 1610612736 | bytes 1310720 | tf_op jit(solution)/shard_map/pallas_call | solution.py:278
  39.5 7.4 %collective-permute-start.14 = (bf16[2,128,256]{2,1,0:T(8,128)(2,1)S(1)}, bf16[2,128,256]{2,1,0:T(8,128)(2,1)S(1)}, u32[]{:S(2)}, u32[]{:S(2)}) collective-permute-start(bf16[2,128,256]{2,1,0:T(8,128)(2,1)S(1)} %get-tuple-element.47), channel_id=1, source_target_pairs={{0,4},{4,0},{8,12},{12,8},{1,5},{5,1},{9,13},{13,9},{2,6},{6,2},{1... | collective-permute-start | bytes 393224 | tf_op jit(solution)/shard_map/ppermute | solution.py:441
  46.9 0.4 collective-permute-start.15
  47.3 2.1 %collective-permute-start.16 = (bf16[2,128,256]{2,1,0:T(8,128)(2,1)S(1)}, bf16[2,128,256]{2,1,0:T(8,128)(2,1)S(1)}, u32[]{:S(2)}, u32[]{:S(2)}) collective-permute-start(bf16[2,128,256]{2,1,0:T(8,128)(2,1)S(1)} %get-tuple-element.49), channel_id=1, source_target_pairs={{0,12},{4,8},{8,4},{12,0},{1,13},{5,9},{9,5},{13,1},{2,14},{6,10},... | collective-permute-start | bytes 393224 | tf_op jit(solution)/shard_map/ppermute | solution.py:441
  49.4 3.7 %shard_map.115 = (bf16[2,128,256]{2,1,0:T(8,128)(2,1)S(1)}, bf16[2,128,256]{2,1,0:T(8,128)(2,1)S(1)}, bf16[2,128,256]{2,1,0:T(8,128)(2,1)S(1)}, bf16[2,128,256]{2,1,0:T(8,128)(2,1)S(1)}) custom-call(s32[1]{0:T(128)} %bitcast.rank_ref, f32[1024,16]{1,0:T(8,128)S(1)} %get-tuple-element.28.cols_ref, bf16[256,512]{1,0:T(8,128)(2,1)S(1)} %copy-done.9, ...), custom_call_target="tpu_custom_call" | custom-call | flops 1610612736 | bytes 1310720 | tf_op jit(solution)/shard_map/pallas_call | solution.py:278
  53.1 2.2 %collective-permute-start.7 = (bf16[2,128,256]{2,1,0:T(8,128)(2,1)S(1)}, bf16[2,128,256]{2,1,0:T(8,128)(2,1)S(1)}, u32[]{:S(2)}, u32[]{:S(2)}) collective-permute-start(bf16[2,128,256]{2,1,0:T(8,128)(2,1)S(1)} %get-tuple-element.39), channel_id=1, source_target_pairs={{0,4},{4,0},{8,12},{12,8},{1,5},{5,1},{9,13},{13,9},{2,6},{6,2},{1... | collective-permute-start | bytes 393224 | tf_op jit(solution)/shard_map/ppermute | solution.py:441
  55.3 0.4 collective-permute-start.8
  55.7 2.1 %collective-permute-start.9 = (bf16[2,128,256]{2,1,0:T(8,128)(2,1)S(1)}, bf16[2,128,256]{2,1,0:T(8,128)(2,1)S(1)}, u32[]{:S(2)}, u32[]{:S(2)}) collective-permute-start(bf16[2,128,256]{2,1,0:T(8,128)(2,1)S(1)} %get-tuple-element.41), channel_id=1, source_target_pairs={{0,12},{4,8},{8,4},{12,0},{1,13},{5,9},{9,5},{13,1},{2,14},{6,10},... | collective-permute-start | bytes 393224 | tf_op jit(solution)/shard_map/ppermute | solution.py:441
  57.8 0.5 shard_map.118
  58.3 3.9 %collective-permute-start.17 = (f32[8,512]{1,0:T(8,128)S(1)}, f32[8,512]{1,0:T(8,128)S(1)}, u32[]{:S(2)}, u32[]{:S(2)}) collective-permute-start(f32[8,512]{1,0:T(8,128)S(1)} %shard_map.118), channel_id=1, source_target_pairs={{0,12},{4,0},{8,4},{12,8},{1,13},{5,1},{9,5},{13,9},{2,14},{6,2},{... | collective-permute-start | bytes 49160 | tf_op jit(solution)/shard_map/ppermute | solution.py:445
  62.2 5.3 %collective-permute-done.8.rest_2_ = bf16[2,128,256]{2,1,0:T(8,128)(2,1)S(1)} collective-permute-done((bf16[2,128,256]{2,1,0:T(8,128)(2,1)S(1)}, bf16[2,128,256]{2,1,0:T(8,128)(2,1)S(1)}, u32[]{:S(2)}, u32[]{:S(2)}) %collective-permute-start.8) | collective-permute-done | bytes 131104 | tf_op jit(solution)/shard_map/ppermute | solution.py:441
  67.6 0.5 shard_map.116
  68.1 2.9 %collective-permute-start.10 = (f32[8,512]{1,0:T(8,128)S(1)}, f32[8,512]{1,0:T(8,128)S(1)}, u32[]{:S(2)}, u32[]{:S(2)}) collective-permute-start(f32[8,512]{1,0:T(8,128)S(1)} %shard_map.116), channel_id=1, source_target_pairs={{0,12},{4,0},{8,4},{12,8},{1,13},{5,1},{9,5},{13,9},{2,14},{6,2},{... | collective-permute-start | bytes 49160 | tf_op jit(solution)/shard_map/ppermute | solution.py:445
  71.0 5.9 %shard_map.119 = (bf16[1024,256]{1,0:T(8,128)(2,1)}, bf16[3,1024,256]{2,1,0:T(8,128)(2,1)}) custom-call(s32[1]{0:T(128)} %bitcast.rank_ref, s32[16]{0:T(128)S(1)} %copy-done.4, bf16[3,1024,256]{2,1,0:T(8,128)(2,1)S(1)} %get-tuple-element.29.qkv_ref, bf16[1024,256]{1,0:T(8,128)(2,1)S(1)} %copy-done, f32[1024,16]{1,0:T(8,128)S(1)} %get-tuple-element.28.cols_ref, ...), custom_call_target="tpu_custom_call" | custom-call | flops 5242880 | bytes 2621440 | tf_op jit(solution)/shard_map/pallas_call | solution.py:421
  76.9 5.9 %shard_map.120 = (bf16[1024,256]{1,0:T(8,128)(2,1)}, bf16[3,1024,256]{2,1,0:T(8,128)(2,1)}) custom-call(s32[1]{0:T(128)} %bitcast.rank_ref, s32[16]{0:T(128)S(1)} %copy-done.4, bf16[3,1024,256]{2,1,0:T(8,128)(2,1)S(1)} %get-tuple-element.29.qkv_ref, bf16[1024,256]{1,0:T(8,128)(2,1)S(1)} %copy-done, ...), custom_call_target="tpu_custom_call", output_to_operand_aliasing={{0}: (10, {}), {1}: (11, {})} | custom-call | flops 5242880 | bytes 2621440 | tf_op jit(solution)/shard_map/pallas_call | solution.py:421
  (32 shorter events, 0.1 us)
Async XLA Ops:
  0.6 15.1 %copy-start = (bf16[1024,256]{1,0:T(8,128)(2,1)S(1)}, bf16[1024,256]{1,0:T(8,128)(2,1)}, u32[]{:S(2)}) copy-start(bf16[1024,256]{1,0:T(8,128)(2,1)} %dout_ref.9) | copy-start | bytes 1572868
  0.6 1.5 %copy-start.1 = (bf16[3,1024,256]{2,1,0:T(8,128)(2,1)S(1)}, bf16[3,1024,256]{2,1,0:T(8,128)(2,1)}, u32[]{:S(2)}) copy-start(bf16[3,1024,256]{2,1,0:T(8,128)(2,1)} %feat_ref.1) | copy-start | bytes 4718596
  2.1 1.0 %copy-start.2 = (bf16[1024,256]{1,0:T(8,128)(2,1)S(1)}, bf16[1024,256]{1,0:T(8,128)(2,1)}, u32[]{:S(2)}) copy-start(bf16[1024,256]{1,0:T(8,128)(2,1)} %filt_ref.1) | copy-start | bytes 1572868
  3.2 0.8 copy-start.3
  4.0 0.7 copy-start.5
  4.6 11.1 %copy-start.4 = (s32[16]{0:T(128)S(1)}, s32[16]{0:T(128)}, u32[]{:S(2)}) copy-start(s32[16]{0:T(128)} %lengths_ref.5) | copy-start | bytes 196
  5.1 30.7 %copy-start.6 = (bf16[512,256]{1,0:T(8,128)(2,1)S(1)}, bf16[512,256]{1,0:T(8,128)(2,1)}, u32[]{:S(2)}) copy-start(bf16[512,256]{1,0:T(8,128)(2,1)} %constant.16.clone.ilo_ref) | copy-start | bytes 786436
  5.1 30.7 %copy-start.7 = (bf16[512,256]{1,0:T(8,128)(2,1)S(1)}, bf16[512,256]{1,0:T(8,128)(2,1)}, u32[]{:S(2)}) copy-start(bf16[512,256]{1,0:T(8,128)(2,1)} %constant.15.clone.ihi_ref) | copy-start | bytes 786436
  5.1 30.7 %copy-start.8 = (bf16[256,512]{1,0:T(8,128)(2,1)S(1)}, bf16[256,512]{1,0:T(8,128)(2,1)}, u32[]{:S(2)}) copy-start(bf16[256,512]{1,0:T(8,128)(2,1)} %constant.14.clone.flo_ref) | copy-start | bytes 786436
  5.1 30.7 %copy-start.9 = (bf16[256,512]{1,0:T(8,128)(2,1)S(1)}, bf16[256,512]{1,0:T(8,128)(2,1)}, u32[]{:S(2)}) copy-start(bf16[256,512]{1,0:T(8,128)(2,1)} %constant.13.clone.fhi_ref) | copy-start | bytes 786436
  5.1 19.3 %collective-permute-start.1 = (bf16[256,256]{1,0:T(8,128)(2,1)S(1)}, bf16[256,256]{1,0:T(8,128)(2,1)S(1)}, u32[]{:S(2)}, u32[]{:S(2)}) collective-permute-start(bf16[256,256]{1,0:T(8,128)(2,1)S(1)} %get-tuple-element.31), channel_id=1, source_target_pairs={{0,4},{4,0},{8,12},{12,8},{1,5},{5,1},{9,13},{13,9},{2,6},{6,2},{1... | collective-permute-start | bytes 393224 | tf_op jit(solution)/shard_map/ppermute | solution.py:441
  8.2 7.5 %collective-permute-start = (bf16[16,1024]{1,0:T(8,128)(2,1)S(1)}, bf16[16,1024]{1,0:T(8,128)(2,1)S(1)}, u32[]{:S(2)}, u32[]{:S(2)}) collective-permute-start(bf16[16,1024]{1,0:T(8,128)(2,1)S(1)} %get-tuple-element.27), channel_id=1, source_target_pairs={{0,4},{4,8},{8,12},{12,0},{1,5},{5,9},{9,13},{13,1},{2,6},{6,10},{... | collective-permute-start | bytes 98312 | tf_op jit(solution)/shard_map/ppermute | solution.py:445
  8.3 18.6 %collective-permute-start.2 = (bf16[256,256]{1,0:T(8,128)(2,1)S(1)}, bf16[256,256]{1,0:T(8,128)(2,1)S(1)}, u32[]{:S(2)}, u32[]{:S(2)}) collective-permute-start(bf16[256,256]{1,0:T(8,128)(2,1)S(1)} %get-tuple-element.32), channel_id=1, source_target_pairs={{0,8},{4,12},{8,0},{12,4},{1,9},{5,13},{9,1},{13,5},{2,10},{6,14},... | collective-permute-start | bytes 393224 | tf_op jit(solution)/shard_map/ppermute | solution.py:441
  11.3 15.7 %collective-permute-start.3 = (bf16[256,256]{1,0:T(8,128)(2,1)S(1)}, bf16[256,256]{1,0:T(8,128)(2,1)S(1)}, u32[]{:S(2)}, u32[]{:S(2)}) collective-permute-start(bf16[256,256]{1,0:T(8,128)(2,1)S(1)} %get-tuple-element.33), channel_id=1, source_target_pairs={{0,12},{4,8},{8,4},{12,0},{1,13},{5,9},{9,5},{13,1},{2,14},{6,10},... | collective-permute-start | bytes 393224 | tf_op jit(solution)/shard_map/ppermute | solution.py:441
  22.5 8.4 %collective-permute-start.11 = (bf16[2,128,256]{2,1,0:T(8,128)(2,1)S(1)}, bf16[2,128,256]{2,1,0:T(8,128)(2,1)S(1)}, u32[]{:S(2)}, u32[]{:S(2)}) collective-permute-start(bf16[2,128,256]{2,1,0:T(8,128)(2,1)S(1)} %get-tuple-element.43), channel_id=1, source_target_pairs={{0,4},{4,0},{8,12},{12,8},{1,5},{5,1},{9,13},{13,9},{2,6},{6,2},{1... | collective-permute-start | bytes 393224 | tf_op jit(solution)/shard_map/ppermute | solution.py:441
  22.6 13.2 %collective-permute-start.12 = (bf16[2,128,256]{2,1,0:T(8,128)(2,1)S(1)}, bf16[2,128,256]{2,1,0:T(8,128)(2,1)S(1)}, u32[]{:S(2)}, u32[]{:S(2)}) collective-permute-start(bf16[2,128,256]{2,1,0:T(8,128)(2,1)S(1)} %get-tuple-element.44), channel_id=1, source_target_pairs={{0,8},{4,12},{8,0},{12,4},{1,9},{5,13},{9,1},{13,5},{2,10},{6,14},... | collective-permute-start | bytes 393224 | tf_op jit(solution)/shard_map/ppermute | solution.py:441
  24.5 11.3 %collective-permute-start.13 = (bf16[2,128,256]{2,1,0:T(8,128)(2,1)S(1)}, bf16[2,128,256]{2,1,0:T(8,128)(2,1)S(1)}, u32[]{:S(2)}, u32[]{:S(2)}) collective-permute-start(bf16[2,128,256]{2,1,0:T(8,128)(2,1)S(1)} %get-tuple-element.45), channel_id=1, source_target_pairs={{0,12},{4,8},{8,4},{12,0},{1,13},{5,9},{9,5},{13,1},{2,14},{6,10},... | collective-permute-start | bytes 393224 | tf_op jit(solution)/shard_map/ppermute | solution.py:441
  26.9 20.4 %collective-permute-start.4 = (bf16[2,128,256]{2,1,0:T(8,128)(2,1)S(1)}, bf16[2,128,256]{2,1,0:T(8,128)(2,1)S(1)}, u32[]{:S(2)}, u32[]{:S(2)}) collective-permute-start(bf16[2,128,256]{2,1,0:T(8,128)(2,1)S(1)} %get-tuple-element.35), channel_id=1, source_target_pairs={{0,4},{4,0},{8,12},{12,8},{1,5},{5,1},{9,13},{13,9},{2,6},{6,2},{1... | collective-permute-start | bytes 393224 | tf_op jit(solution)/shard_map/ppermute | solution.py:441
  26.9 22.4 %collective-permute-start.5 = (bf16[2,128,256]{2,1,0:T(8,128)(2,1)S(1)}, bf16[2,128,256]{2,1,0:T(8,128)(2,1)S(1)}, u32[]{:S(2)}, u32[]{:S(2)}) collective-permute-start(bf16[2,128,256]{2,1,0:T(8,128)(2,1)S(1)} %get-tuple-element.36), channel_id=1, source_target_pairs={{0,8},{4,12},{8,0},{12,4},{1,9},{5,13},{9,1},{13,5},{2,10},{6,14},... | collective-permute-start | bytes 393224 | tf_op jit(solution)/shard_map/ppermute | solution.py:441
  30.8 18.5 %collective-permute-start.6 = (bf16[2,128,256]{2,1,0:T(8,128)(2,1)S(1)}, bf16[2,128,256]{2,1,0:T(8,128)(2,1)S(1)}, u32[]{:S(2)}, u32[]{:S(2)}) collective-permute-start(bf16[2,128,256]{2,1,0:T(8,128)(2,1)S(1)} %get-tuple-element.37), channel_id=1, source_target_pairs={{0,12},{4,8},{8,4},{12,0},{1,13},{5,9},{9,5},{13,1},{2,14},{6,10},... | collective-permute-start | bytes 393224 | tf_op jit(solution)/shard_map/ppermute | solution.py:441
  39.5 16.1 %collective-permute-start.14 = (bf16[2,128,256]{2,1,0:T(8,128)(2,1)S(1)}, bf16[2,128,256]{2,1,0:T(8,128)(2,1)S(1)}, u32[]{:S(2)}, u32[]{:S(2)}) collective-permute-start(bf16[2,128,256]{2,1,0:T(8,128)(2,1)S(1)} %get-tuple-element.47), channel_id=1, source_target_pairs={{0,4},{4,0},{8,12},{12,8},{1,5},{5,1},{9,13},{13,9},{2,6},{6,2},{1... | collective-permute-start | bytes 393224 | tf_op jit(solution)/shard_map/ppermute | solution.py:441
  46.9 10.8 %collective-permute-start.15 = (bf16[2,128,256]{2,1,0:T(8,128)(2,1)S(1)}, bf16[2,128,256]{2,1,0:T(8,128)(2,1)S(1)}, u32[]{:S(2)}, u32[]{:S(2)}) collective-permute-start(bf16[2,128,256]{2,1,0:T(8,128)(2,1)S(1)} %get-tuple-element.48), channel_id=1, source_target_pairs={{0,8},{4,12},{8,0},{12,4},{1,9},{5,13},{9,1},{13,5},{2,10},{6,14},... | collective-permute-start | bytes 393224 | tf_op jit(solution)/shard_map/ppermute | solution.py:441
  47.3 10.5 %collective-permute-start.16 = (bf16[2,128,256]{2,1,0:T(8,128)(2,1)S(1)}, bf16[2,128,256]{2,1,0:T(8,128)(2,1)S(1)}, u32[]{:S(2)}, u32[]{:S(2)}) collective-permute-start(bf16[2,128,256]{2,1,0:T(8,128)(2,1)S(1)} %get-tuple-element.49), channel_id=1, source_target_pairs={{0,12},{4,8},{8,4},{12,0},{1,13},{5,9},{9,5},{13,1},{2,14},{6,10},... | collective-permute-start | bytes 393224 | tf_op jit(solution)/shard_map/ppermute | solution.py:441
  53.1 9.1 %collective-permute-start.7 = (bf16[2,128,256]{2,1,0:T(8,128)(2,1)S(1)}, bf16[2,128,256]{2,1,0:T(8,128)(2,1)S(1)}, u32[]{:S(2)}, u32[]{:S(2)}) collective-permute-start(bf16[2,128,256]{2,1,0:T(8,128)(2,1)S(1)} %get-tuple-element.39), channel_id=1, source_target_pairs={{0,4},{4,0},{8,12},{12,8},{1,5},{5,1},{9,13},{13,9},{2,6},{6,2},{1... | collective-permute-start | bytes 393224 | tf_op jit(solution)/shard_map/ppermute | solution.py:441
  55.3 12.2 %collective-permute-start.8 = (bf16[2,128,256]{2,1,0:T(8,128)(2,1)S(1)}, bf16[2,128,256]{2,1,0:T(8,128)(2,1)S(1)}, u32[]{:S(2)}, u32[]{:S(2)}) collective-permute-start(bf16[2,128,256]{2,1,0:T(8,128)(2,1)S(1)} %get-tuple-element.40), channel_id=1, source_target_pairs={{0,8},{4,12},{8,0},{12,4},{1,9},{5,13},{9,1},{13,5},{2,10},{6,14},... | collective-permute-start | bytes 393224 | tf_op jit(solution)/shard_map/ppermute | solution.py:441
  55.7 11.9 %collective-permute-start.9 = (bf16[2,128,256]{2,1,0:T(8,128)(2,1)S(1)}, bf16[2,128,256]{2,1,0:T(8,128)(2,1)S(1)}, u32[]{:S(2)}, u32[]{:S(2)}) collective-permute-start(bf16[2,128,256]{2,1,0:T(8,128)(2,1)S(1)} %get-tuple-element.41), channel_id=1, source_target_pairs={{0,12},{4,8},{8,4},{12,0},{1,13},{5,9},{9,5},{13,1},{2,14},{6,10},... | collective-permute-start | bytes 393224 | tf_op jit(solution)/shard_map/ppermute | solution.py:441
  58.3 12.7 %collective-permute-start.17 = (f32[8,512]{1,0:T(8,128)S(1)}, f32[8,512]{1,0:T(8,128)S(1)}, u32[]{:S(2)}, u32[]{:S(2)}) collective-permute-start(f32[8,512]{1,0:T(8,128)S(1)} %shard_map.118), channel_id=1, source_target_pairs={{0,12},{4,0},{8,4},{12,8},{1,13},{5,1},{9,5},{13,9},{2,14},{6,2},{... | collective-permute-start | bytes 49160 | tf_op jit(solution)/shard_map/ppermute | solution.py:445
  68.1 8.8 %collective-permute-start.10 = (f32[8,512]{1,0:T(8,128)S(1)}, f32[8,512]{1,0:T(8,128)S(1)}, u32[]{:S(2)}, u32[]{:S(2)}) collective-permute-start(f32[8,512]{1,0:T(8,128)S(1)} %shard_map.116), channel_id=1, source_target_pairs={{0,12},{4,0},{8,4},{12,8},{1,13},{5,1},{9,5},{13,9},{2,14},{6,2},{... | collective-permute-start | bytes 49160 | tf_op jit(solution)/shard_map/ppermute | solution.py:445

commit v2 on v0

v2 whole, which is shorter than its diff:
```python
import functools
import math

import jax
import jax.numpy as jnp
import numpy as np
from jax import lax
from jax.experimental import pallas as pl
from jax.experimental.pallas import tpu as pltpu
from jax.sharding import PartitionSpec as P

BF16 = jnp.bfloat16
F32 = jnp.float32
VMEM_LIMIT = 48 * 1024 * 1024
WHOLE = pl.BlockSpec(memory_space=pltpu.VMEM)
SCALARS = pl.BlockSpec(memory_space=pltpu.SMEM)


def split_bf16(table):
    high = table.astype(np.float32).astype(BF16)
    low = (table - high.astype(np.float64)).astype(np.float32).astype(BF16)
    return high, low


def block_tables(span):
    freq = np.concatenate([np.arange(0, span, 2), np.arange(1, span, 2)])
    angle = np.pi * (2 * freq[None, :] + 1) * np.arange(span)[:, None] / (2 * span)
    forward = np.concatenate([np.cos(angle), -np.sin(angle)], axis=1)
    inverse = np.concatenate([np.cos(angle), -np.sin(angle)], axis=1).T / span
    return split_bf16(forward) + split_bf16(inverse)


def dot(a, b):
    return jnp.dot(a, b, preferred_element_type=F32)


def call(body, outs, scratch=(), in_specs=None, grid=None, out_specs=None, aliases=None, cost=None):
    return pl.pallas_call(
        body,
        out_shape=outs,
        in_specs=in_specs,
        out_specs=out_specs,
        grid=grid or (),
        scratch_shapes=scratch,
        input_output_aliases=aliases or {},
        compiler_params=pltpu.CompilerParams(vmem_limit_bytes=VMEM_LIMIT),
        cost_estimate=cost,
    )


def estimate(flops, moved):
    return pl.CostEstimate(flops=int(flops), bytes_accessed=int(moved), transcendentals=0)


def offsets_row(lengths_ref, first, span, ahead):
    position = lax.broadcasted_iota(jnp.int32, (8, span), 1) + (first + ahead)

    def step(genome, carry):
        end, start = carry
        end = end + lengths_ref[genome]
        return end, jnp.where(position >= end, end, start)

    begin = (jnp.int32(0), jnp.zeros((8, span), jnp.int32))
    _, start = lax.fori_loop(0, lengths_ref.shape[0], step, begin)
    return position, position - start


def masks_body(parts, rank_ref, lengths_ref, out_ref):
    _, span = out_ref.shape
    first = (rank_ref[0]) * span
    out_ref[...] = jnp.zeros(out_ref.shape, F32)
    _, offset = offsets_row(lengths_ref, first, span, 0)
    for j in (1, 2):
        out_ref[j - 1 : j, :] = (offset[0:1, :] >= j).astype(F32)
        position, later = offsets_row(lengths_ref, first, span, j)
        inside = (position < parts * span) & (later >= j)
        out_ref[1 + j : 2 + j, :] = inside[0:1, :].astype(F32)


def masks(place, lengths, parts, span):
    return call(
        functools.partial(masks_body, parts),
        jax.ShapeDtypeStruct((8, span), F32),
        in_specs=[SCALARS, SCALARS],
        out_specs=WHOLE,
        cost=estimate(0, 8192),
    )(place, lengths)


class Layout:
    def __init__(self, parts, channels, span):
        self.parts, self.channels, self.span = parts, channels, span
        self.half = parts // 2
        self.size = channels // self.half
        self.sub = self.size // 2


def fixed(shape):
    return pl.BlockSpec(shape, lambda *args: (0,) * len(shape))


def streamed(body, layout, place, operands, in_specs, outs, out_specs, scratch, grid, cost):
    return pl.pallas_call(
        functools.partial(body, layout),
        out_shape=outs,
        grid_spec=pltpu.PrefetchScalarGridSpec(
            num_scalar_prefetch=1,
            grid=grid,
            in_specs=in_specs,
            out_specs=out_specs,
            scratch_shapes=scratch,
        ),
        compiler_params=pltpu.CompilerParams(vmem_limit_bytes=VMEM_LIMIT),
        cost_estimate=cost,
    )(place, *operands)


def sides(place_ref, layout):
    rank = place_ref[0]
    return rank // layout.half, rank % layout.half


def sub_block(layout):
    def block(step, place_ref):
        _, own = sides(place_ref, layout)
        return jnp.bitwise_xor(own, step // 2) * 2 + step % 2

    return block


def pack_body(layout, place_ref, tail_ref, filt_ref, taps_ref, skip_ref, halo_ref, cols_ref, *rest):
    filt_out, turned = rest[: layout.half], rest[layout.half]
    _, own = sides(place_ref, layout)
    group = place_ref[1]
    for step in range(layout.half):
        begin = (jnp.bitwise_xor(own, step) * 2 + group) * layout.sub
        filt_out[step][...] = filt_ref[pl.ds(pl.multiple_of(begin, layout.sub), layout.sub), :]
    turned[...] = jnp.zeros(turned.shape, F32)
    for which in range(3):
        turned[2 * which : 2 * which + 2, :] = tail_ref[which].astype(F32).T[-2:, :]
    halo_ref[...] = turned[...].astype(BF16)
    turned[...] = jnp.zeros(turned.shape, F32)
    for which in range(3):
        turned[3 * which : 3 * which + 3, :] = taps_ref[which]
    turned[9:10, :] = skip_ref[...]
    cols_ref[...] = turned[...].T


def pack(layout, place, features, filters, taps, skip):
    channels, span = layout.channels, layout.span
    shapes = [((16, channels), BF16), ((channels, 16), F32)] + [((layout.sub, span), BF16)] * layout.half
    found = streamed(
        pack_body,
        layout,
        place,
        (features, filters, taps, skip.reshape(1, channels)),
        [
            pl.BlockSpec((3, channels, 128), lambda step, place_ref: (0, 0, span // 128 - 1)),
            fixed(filters.shape),
            fixed(taps.shape),
            fixed((1, channels)),
        ],
        [jax.ShapeDtypeStruct(*s) for s in shapes],
        [fixed(s[0]) for s in shapes],
        [pltpu.VMEM((16, channels), F32)],
        (1,),
        estimate(0, 3 * channels * span * 2),
    )
    return found[0], found[1], found[2:]


def gate_body(layout, place_ref, feat_ref, dout_ref, halo_ref, cols_ref, keep_ref, qkv_ref, *rest):
    half, rows, span = layout.half, layout.sub, layout.span
    inner, cross = rest[:half], rest[half : 2 * half]
    edge, made = rest[2 * half :]
    side, own = sides(place_ref, layout)
    step = pl.program_id(0)
    turn, sub = step // 2, step % 2
    base = sub_block(layout)(step, place_ref) * rows
    group = min(32, rows)

    @pl.when(step == 0)
    def _():
        edge[...] = halo_ref[...].astype(F32).T

    keep = keep_ref[0:1, :], keep_ref[1:2, :]
    lane = lax.broadcasted_iota(jnp.int32, (group, span), 1)

    def tile(index, _):
        here = pl.ds(pl.multiple_of(index * group, group), group)
        cols = cols_ref[here, :]
        ends = edge[pl.ds(pl.multiple_of(base + index * group, group), group), :]
        filtered = []
        for which in range(3):
            value = feat_ref[which, here, :].astype(F32)
            two_back = ends[:, 2 * which : 2 * which + 1]
            one_back = ends[:, 2 * which + 1 : 2 * which + 2]
            back = jnp.where(lane == 0, one_back, pltpu.roll(value, 1, 1))
            twice = jnp.where(lane == 0, two_back, jnp.where(lane == 1, one_back, pltpu.roll(value, 2, 1)))
            total = cols[:, 3 * which : 3 * which + 1] * value
            total = total + cols[:, 3 * which + 1 : 3 * which + 2] * back * keep[0]
            total = total + cols[:, 3 * which + 2 : 3 * which + 3] * twice * keep[1]
            rounded = total.astype(BF16)
            qkv_ref[which, here, :] = rounded
            filtered.append(rounded.astype(F32))
        made[0, here, :] = (filtered[1] * filtered[2]).astype(BF16)
        made[1, here, :] = (dout_ref[here, :].astype(F32) * filtered[0]).astype(BF16)
        return 0

    lax.fori_loop(0, rows // group, tile, 0, unroll=min(4, rows // group))
    for k in range(half):

        @pl.when(turn == k)
        def _(k=k):
            inner[k][:, pl.ds(pl.multiple_of(sub * rows, rows), rows), :] = made[...]

        @pl.when((turn == k) & (sub == side))
        def _(k=k):
            cross[k][...] = made[side]


def gate(layout, place, features, dout, halo, cols, keep):
    half, rows, span, channels = layout.half, layout.sub, layout.span, layout.channels
    block = sub_block(layout)
    wide = pl.BlockSpec((3, rows, span), lambda *a: (0, block(*a), 0))
    flat = pl.BlockSpec((rows, span), lambda *a: (block(*a), 0))
    columns = pl.BlockSpec((rows, 16), lambda *a: (block(*a), 0))
    shapes = [(2, layout.size, span)] * half + [(rows, span)] * half
    found = streamed(
        gate_body,
        layout,
        place,
        (features, dout, halo, cols, keep),
        [wide, flat, fixed(halo.shape), columns, fixed(keep.shape)],
        [jax.ShapeDtypeStruct(features.shape, BF16)] + [jax.ShapeDtypeStruct(s, BF16) for s in shapes],
        [wide] + [fixed(s) for s in shapes],
        [pltpu.VMEM((channels, 16), F32), pltpu.VMEM((2, rows, span), BF16)],
        (layout.parts,),
        estimate(30 * channels * span, 9 * channels * span * 2),
    )
    return found[0], found[1 : 1 + half], found[1 + half :]


def loop(count, body, init):
    if count <= 4:
        for k in range(count):
            init = body(k, init)
        return init
    return lax.fori_loop(0, count, body, init)


def add_product(total, f, x):
    return (total[0] + f[0] * x[0] - f[1] * x[1], total[1] + f[0] * x[1] + f[1] * x[0])


def add_conjugate(total, f, x):
    return (total[0] + f[0] * x[0] + f[1] * x[1], total[1] + f[0] * x[1] - f[1] * x[0])


def turned_sum(spectrum, neighbour, sign):
    half = spectrum[0].shape[1] // 2
    parts = []
    for lanes, flip in ((slice(0, half), sign), (slice(half, None), -sign)):
        n_re, n_im = neighbour[0][:, lanes], neighbour[1][:, lanes]
        s_re, s_im = spectrum[0][:, lanes], spectrum[1][:, lanes]
        parts.append((s_re - n_im, s_im + n_re) if flip > 0 else (s_re + n_im, s_im - n_re))
    return tuple(jnp.concatenate([p[k] for p in parts], axis=1) for k in range(2))


def forward(raw, spec, begin, target, rows, fhi_ref, flo_ref):
    value = raw[pl.ds(pl.multiple_of(begin, 16), rows), :]
    spec[pl.ds(pl.multiple_of(target, 16), rows), :] = dot(value, fhi_ref[...]) + dot(value, flo_ref[...])


def inverse(high, low, back, begin, rows, ihi_ref, ilo_ref):
    place = pl.ds(pl.multiple_of(begin, 16), rows)
    top = high[place, :]
    back[place, :] = dot(top, ihi_ref[...]) + dot(top, ilo_ref[...]) + dot(low[place, :], ihi_ref[...])


def spectrum_at(spec, begin, group, span):
    place = pl.ds(pl.multiple_of(begin, group), group)
    return spec[place, :span], spec[place, span:]


def store_split(high, low, begin, value, group, span):
    place = pl.ds(pl.multiple_of(begin, group), group)
    for lanes, part in ((slice(0, span), value[0]), (slice(span, 2 * span), value[1])):
        top = part.astype(BF16)
        high[place, lanes] = top
        low[place, lanes] = (part - top.astype(F32)).astype(BF16)


def own_body(layout, place_ref, cols_ref, fhi_ref, flo_ref, ihi_ref, ilo_ref, filt_ref, other_ref, *rest):
    parts, half, size, sub, span = layout.parts, layout.half, layout.size, layout.sub, layout.span
    filt_in, rest = rest[: parts - 1], rest[parts - 1 :]
    inner, returned, later = rest[:half], rest[half : 2 * half], rest[2 * half : 3 * half]
    raw, spec, high, low, back = rest[3 * half :]
    side, own = sides(place_ref, layout)
    rank, carried = place_ref[0], place_ref[1]
    kind_rows = half * size
    signals = parts * size

    def rows_at(begin, count):
        return pl.ds(pl.multiple_of(begin, sub), count)

    raw[rows_at(rank * size, size), :] = filt_ref[...]
    for step in range(1, parts):
        begin = jnp.bitwise_xor(rank, step) * size
        raw[rows_at(begin + carried * sub, sub), :] = filt_in[step - 1][...]
        raw[rows_at(begin + (1 - carried) * sub, sub), :] = other_ref[(step - 1) * sub : step * sub, :]
    for step in range(half):
        for kind in range(2):
            begin = signals + kind * kind_rows + jnp.bitwise_xor(own, step) * size
            raw[rows_at(begin, size), :] = inner[step][kind]

    def transform(index, _):
        kind, part = index // half, index % half
        begin = jnp.where(kind == 0, 0, signals + (kind - 1) * kind_rows) + part * size
        forward(raw, spec, begin, index * size, size, fhi_ref, flo_ref)
        return 0

    lax.fori_loop(0, 3 * half, transform, 0)
    group = 16
    zero = (jnp.zeros((group, span), F32),) * 2

    def products(index, _):
        def read(kind, k):
            return spectrum_at(spec, (kind * half + k) * size + index * group, group, span)

        def store(kind, k, value):
            store_split(high, low, (kind * half + k) * size + index * group, value, group, span)

        before = None
        for place in range(half):
            total = loop(place + 1, lambda k, t, p=place: add_product(t, read(0, k), read(1, p - k)), zero)
            store(0, place, total if before is None else turned_sum(total, before, 1))
            before = total
        before = None
        for place in range(half - 1, -1, -1):
            total = loop(half - place, lambda k, t, p=place: add_conjugate(t, read(0, k), read(2, p + k)), zero)
            store(1, place, total if before is None else turned_sum(total, before, -1))
            before = total
        return 0

    lax.fori_loop(0, size // group, products, 0)

    def restore(index, _):
        inverse(high, low, back, index * size, size, ihi_ref, ilo_ref)
        return 0

    lax.fori_loop(0, 2 * half, restore, 0)

    def result(kind, cls, part):
        begin = kind * kind_rows + part * size + cls * sub
        direct = raw[rows_at(signals + begin, sub), :].astype(F32)
        skip = cols_ref[rows_at(cls * sub, sub), 9:10]
        return back[rows_at(begin, sub), :] + skip * direct

    for step in range(half):
        part = jnp.bitwise_xor(own, step)
        returned[step][0] = result(side, 0, part).astype(BF16)
        returned[step][1] = result(side, 1, part).astype(BF16)
        returned[step][2] = result(1 - side, side, part).astype(BF16)
        later[step][...] = result(1 - side, 1 - side, part)


def own_half(layout, place, cols, tables, filters, other, filt, inner):
    half, size, sub, span, parts = layout.half, layout.size, layout.sub, layout.span, layout.parts
    own_class = lambda step, place_ref: (sides(place_ref, layout)[1], 0)
    shapes = [((3, sub, span), BF16)] * half + [((sub, span), F32)] * half
    rows = 3 * half * size
    found = streamed(
        own_body,
        layout,
        place,
        (cols, *tables, filters, other, *filt, *inner),
        [pl.BlockSpec((size, 16), own_class)]
        + [fixed(t.shape) for t in tables]
        + [pl.BlockSpec((size, span), own_class), fixed(other.shape)]
        + [fixed((sub, span))] * (parts - 1)
        + [fixed((2, size, span))] * half,
        [jax.ShapeDtypeStruct(*s) for s in shapes],
        [fixed(s[0]) for s in shapes],
        [
            pltpu.VMEM(((parts + 2 * half) * size, span), BF16),
            pltpu.VMEM((rows, 2 * span), F32),
            pltpu.VMEM((2 * half * size, 2 * span), BF16),
            pltpu.VMEM((2 * half * size, 2 * span), BF16),
            pltpu.VMEM((2 * half * size, span), F32),
        ],
        (1,),
        estimate(2 * rows * span * 2 * span * 4, 7 * half * size * span * 2),
    )
    return found[:half], found[half:]


def cross_body(arriving, layout, place_ref, fhi_ref, flo_ref, ihi_ref, ilo_ref, filt_ref, other_ref, *rest):
    parts, half, sub, span = layout.parts, layout.half, layout.sub, layout.span
    filt_in, rest = rest[: parts - 1], rest[parts - 1 :]
    signal, rest = rest[:half], rest[half:]
    partial, rest = (rest[:half], rest[half:]) if arriving else (None, rest)
    outs = rest[:half]
    raw, spec, high, low, back = rest[half:]
    side, own = sides(place_ref, layout)
    rank, carried = place_ref[0], place_ref[1]
    main = 1 - side
    block = parts * sub

    def rows_at(begin, count):
        return pl.ds(pl.multiple_of(begin, sub), count)

    raw[rows_at(rank * sub, sub), :] = filt_ref[...]
    for step in range(1, parts):
        place = rows_at(jnp.bitwise_xor(rank, step) * sub, sub)
        raw[place, :] = jnp.where(carried == main, filt_in[step - 1][...], other_ref[(step - 1) * sub : step * sub, :])
    for step in range(half):
        value = signal[step][...]
        raw[rows_at(block + jnp.bitwise_xor(own, step) * sub, sub), :] = value.reshape(sub, span)
    count = (parts + half) * sub
    chunk = math.gcd(count, 512)
    lax.fori_loop(
        0, count // chunk, lambda k, _: forward(raw, spec, k * chunk, k * chunk, chunk, fhi_ref, flo_ref) or 0, 0
    )
    group = 16
    zero = (jnp.zeros((group, span), F32),) * 2
    from_first = side == (1 if arriving else 0)

    def products(index, ahead):
        def filt(k):
            return spectrum_at(spec, k * sub + index * group, group, span)

        def sig(k):
            return spectrum_at(spec, block + k * sub + index * group, group, span)

        before = None
        if ahead:
            for place in range(half - 1, parts):
                total = loop(half, lambda k, t, p=place: add_product(t, filt(p - k), sig(k)), zero)
                if before is not None:
                    value = turned_sum(total, before, 1)
                    store_split(high, low, (place - half) * sub + index * group, value, group, span)
                before = total
        else:
            for place in range(half, -1, -1):
                total = loop(half, lambda k, t, p=place: add_conjugate(t, filt(half + k - p), sig(k)), zero)
                if before is not None:
                    value = turned_sum(total, before, -1)
                    store_split(high, low, place * sub + index * group, value, group, span)
                before = total
        return 0

    @pl.when(from_first)
    def _():
        lax.fori_loop(0, sub // group, lambda k, _: products(k, True), 0)

    @pl.when(jnp.logical_not(from_first))
    def _():
        lax.fori_loop(0, sub // group, lambda k, _: products(k, False), 0)

    inverse(high, low, back, 0, half * sub, ihi_ref, ilo_ref)
    for step in range(half):
        value = back[rows_at(jnp.bitwise_xor(own, step) * sub, sub), :]
        if arriving:
            value = value + partial[step][...]
        outs[step][...] = value.astype(BF16)


def cross_half(layout, place, tables, filters, other, filt, signal, partial):
    half, sub, span, parts = layout.half, layout.sub, layout.span, layout.parts
    arriving = partial is not None

    def main_class(step, place_ref):
        side, own = sides(place_ref, layout)
        return (own * 2 + 1 - side, 0)

    def main_signal(step, place_ref):
        side, own = sides(place_ref, layout)
        return (side, 1 - side, 0)

    signal_spec = fixed((sub, span)) if arriving else pl.BlockSpec((1, sub, span), main_signal)
    rows = (parts + half) * sub
    return streamed(
        functools.partial(cross_body, arriving),
        layout,
        place,
        (*tables, filters, other, *filt, *signal, *(partial or ())),
        [fixed(t.shape) for t in tables]
        + [pl.BlockSpec((sub, span), main_class), fixed(other.shape)]
        + [fixed((sub, span))] * (parts - 1)
        + [signal_spec] * half
        + [fixed((sub, span))] * (half if arriving else 0),
        [jax.ShapeDtypeStruct((sub, span), BF16)] * half,
        [fixed((sub, span))] * half,
        [
            pltpu.VMEM((rows, span), BF16),
            pltpu.VMEM((rows, 2 * span), F32),
            pltpu.VMEM((half * sub, 2 * span), BF16),
            pltpu.VMEM((half * sub, 2 * span), BF16),
            pltpu.VMEM((half * sub, span), F32),
        ],
        (1,),
        estimate(2 * rows * span * 2 * span * 3, 10 * half * sub * span * 2),
    )


def gather_results(layout, side, sub, returned, completed, crossed, which):
    plain = returned[sub].astype(F32)
    summed = (returned[2].astype(F32) + crossed[...].astype(F32)).astype(BF16).astype(F32)
    mixed = jnp.where(sub == side, summed, completed[...].astype(F32))
    return jnp.where(side == 0, plain, mixed), jnp.where(side == 0, mixed, plain)


def first_body(layout, place_ref, qkv_ref, dout_ref, *rest):
    half, sub = layout.half, layout.sub
    returned, completed, crossed = rest[:half], rest[half : 2 * half], rest[2 * half : 3 * half]
    out_ref, grads = rest[3 * half :]
    side, own = sides(place_ref, layout)
    for step in range(half):
        for part in range(2):
            begin = (jnp.bitwise_xor(own, step) * 2 + part) * sub
            place = pl.ds(pl.multiple_of(begin, sub), sub)
            y_out, dmixed = gather_results(
                layout, side, part, returned[step], completed[step], crossed[step], None
            )
            grads[0, place, :] = dout_ref[place, :].astype(F32) * y_out
            grads[1, place, :] = dmixed * qkv_ref[2, place, :].astype(F32)
            grads[2, place, :] = dmixed * qkv_ref[1, place, :].astype(F32)
    out_ref[...] = jnp.zeros(out_ref.shape, F32)
    for which in range(3):
        out_ref[2 * which : 2 * which + 2, :] = grads[which].T[0:2, :]


def first_grads(layout, place, qkv, dout, returned, completed, crossed):
    half, sub, channels = layout.half, layout.sub, layout.channels
    return streamed(
        first_body,
        layout,
        place,
        (qkv, dout, *returned, *completed, *crossed),
        [fixed((3, channels, 128)), fixed((channels, 128))]
        + [fixed((3, sub, 128))] * half
        + [fixed((sub, 128))] * (2 * half),
        jax.ShapeDtypeStruct((8, channels), F32),
        fixed((8, channels)),
        [pltpu.VMEM((3, channels, 128), F32)],
        (1,),
        estimate(0, 3 * channels * 128 * 2),
    )


def final_body(layout, place_ref, qkv_ref, dout_ref, cols_ref, ahead_ref, keep_ref, *rest):
    half, rows, span = layout.half, layout.sub, layout.span
    returned, completed, crossed = rest[:half], rest[half : 2 * half], rest[2 * half : 3 * half]
    out_ref, dfeat_ref, edge, moved = rest[3 * half :]
    side, own = sides(place_ref, layout)
    step = pl.program_id(0)
    turn, sub = step // 2, step % 2
    base = sub_block(layout)(step, place_ref) * rows

    @pl.when(step == 0)
    def _():
        edge[...] = ahead_ref[...].T

    for k in range(half):

        @pl.when(turn == k)
        def _(k=k):
            moved[side] = returned[k][sub]

        @pl.when((turn == k) & (sub == side))
        def _(k=k):
            moved[1 - side] = (returned[k][2].astype(F32) + crossed[k][...].astype(F32)).astype(BF16)

        @pl.when((turn == k) & (sub != side))
        def _(k=k):
            moved[1 - side] = completed[k][...]

    group = min(32, rows)
    lane = lax.broadcasted_iota(jnp.int32, (group, span), 1)
    keep = keep_ref[2:3, :], keep_ref[3:4, :]

    def tile(index, _):
        here = pl.ds(pl.multiple_of(index * group, group), group)
        ends = edge[pl.ds(pl.multiple_of(base + index * group, group), group), :]
        cols = cols_ref[here, :]
        y_out = moved[0, here, :].astype(F32)
        dmixed = moved[1, here, :].astype(F32)
        out_ref[here, :] = (qkv_ref[0, here, :].astype(F32) * y_out).astype(BF16)
        grads = (
            dout_ref[here, :].astype(F32) * y_out,
            dmixed * qkv_ref[2, here, :].astype(F32),
            dmixed * qkv_ref[1, here, :].astype(F32),
        )
        for which in range(3):
            value = grads[which]
            first = ends[:, 2 * which : 2 * which + 1]
            second = ends[:, 2 * which + 1 : 2 * which + 2]
            next_one = jnp.where(lane == span - 1, first, pltpu.roll(value, span - 1, 1))
            next_two = jnp.where(
                lane == span - 1, second, jnp.where(lane == span - 2, first, pltpu.roll(value, span - 2, 1))
            )
            total = cols[:, 3 * which : 3 * which + 1] * value
            total = total + cols[:, 3 * which + 1 : 3 * which + 2] * next_one * keep[0]
            total = total + cols[:, 3 * which + 2 : 3 * which + 3] * next_two * keep[1]
            dfeat_ref[which, here, :] = total.astype(BF16)
        return 0

    lax.fori_loop(0, rows // group, tile, 0, unroll=min(4, rows // group))


def final(layout, place, qkv, dout, cols, ahead, keep, returned, completed, crossed):
    half, rows, span, channels = layout.half, layout.sub, layout.span, layout.channels
    block = sub_block(layout)
    wide = pl.BlockSpec((3, rows, span), lambda *a: (0, block(*a), 0))
    flat = pl.BlockSpec((rows, span), lambda *a: (block(*a), 0))
    columns = pl.BlockSpec((rows, 16), lambda *a: (block(*a), 0))
    return streamed(
        final_body,
        layout,
        place,
        (qkv, dout, cols, ahead, keep, *returned, *completed, *crossed),
        [wide, flat, columns, fixed(ahead.shape), fixed(keep.shape)]
        + [fixed((3, rows, span))] * half
        + [fixed((rows, span))] * (2 * half),
        [jax.ShapeDtypeStruct((channels, span), BF16), jax.ShapeDtypeStruct((3, channels, span), BF16)],
        [flat, wide],
        [pltpu.VMEM((channels, 8), F32), pltpu.VMEM((2, rows, span), BF16)],
        (layout.parts,),
        estimate(40 * channels * span, 10 * channels * span * 2),
    )


def swap(value, step, parts, axis="seq"):
    return lax.ppermute(value, axis, [(source, source ^ step) for source in range(parts)])


def around(value, steps, parts):
    return lax.ppermute(value, "seq", [(source, (source + steps) % parts) for source in range(parts)])


def local(features, dout, filters, taps, skip, lengths):
    parts = lax.axis_size("seq")
    _, channels, span = features.shape
    layout = Layout(parts, channels, span)
    half = layout.half
    place = jnp.stack([lax.axis_index("seq"), lax.axis_index("groups")]).astype(jnp.int32)
    tables = [jnp.asarray(t) for t in block_tables(span)]

    halo, cols, filt_out = pack(layout, place, features, filters, taps, skip)
    halo = around(halo, 1, parts)
    filt = [swap(filt_out[step % half], step, parts) for step in range(1, parts)]
    other = swap(jnp.concatenate(filt, axis=0), 1, 2, "groups")
    keep = masks(place, lengths, parts, span)
    qkv, inner, cross = gate(layout, place, features, dout, halo, cols, keep)
    inner = [inner[0]] + [swap(inner[step], step, parts) for step in range(1, half)]
    cross = [swap(cross[step], step + half, parts) for step in range(half)]

    sent = cross_half(layout, place, tables, filters, other, filt, inner, None)
    crossed = [swap(sent[step], step + half, parts) for step in range(half)]
    returned, later = own_half(layout, place, cols, tables, filters, other, filt, inner)
    returned = [returned[0]] + [swap(returned[step], step, parts) for step in range(1, half)]
    completed = cross_half(layout, place, tables, filters, other, filt, cross, later)
    completed = [completed[0]] + [swap(completed[step], step, parts) for step in range(1, half)]

    ahead = around(first_grads(layout, place, qkv, dout, returned, completed, crossed), -1, parts)
    return tuple(final(layout, place, qkv, dout, cols, ahead, keep, returned, completed, crossed))


def solution(mesh):
    in_specs = (
        P(None, ("chan", "sub"), ("groups", "seq")),
        P(("chan", "sub"), ("groups", "seq")),
        P(("chan", "sub"), "seq"),
        P(None, None, ("chan", "sub")),
        P(("chan", "sub")),
        P("groups"),
    )
    out_specs = (P(("chan", "sub"), ("groups", "seq")), P(None, ("chan", "sub"), ("groups", "seq")))
    return jax.shard_map(local, mesh=mesh, in_specs=in_specs, out_specs=out_specs, check_vma=False)
```

time: 223 us -> 91.1 us (0.41); the launches traced: 220 us -> 90.8 us
  matrix products: 84.5 us -> 0 us
  waiting for transfers between devices: 76.4 us -> 35 us
  Pallas kernels: 0 us -> 30.5 us
  local copies, waits for them, and re-layouts: 27.4 us -> 3.97 us
  other arithmetic: 14.5 us -> 0.1 us
  starting transfers between devices: 15.5 us -> 20.4 us
    dot_general x30 -> x0, matrix products: 84.5 us -> none  [the longest x3 8.84 us: forward_transform(): jnp.einsum('ckn,nm->ckm', turned_re, col_im, precision=HIGHEST)]
    all_to_all x2 -> x0, waiting for transfers between devices: 71 us -> none  [the longest x1 45.9 us: to_channels(): lax.all_to_all(stacked, 'seq', split_axis=1, concat_axis=2, tiled=True)]
    pallas_call x0 -> x8, Pallas kernels: none -> 30.5 us  [the longest x7 29.7 us: streamed(): pl.pallas_call(functools.partial(body, layout), out_shape=outs, grid_spec...]
    ppermute x2 -> x13, waiting for transfers between devices: 5.39 us -> 35 us  [the longest x11 24.9 us: swap(): lax.ppermute(value, axis, [(source, source ^ step) for source in range(pa...]
    ppermute x2 -> x13, starting transfers between devices: 6.22 us -> 20.4 us  [the longest x11 18 us: swap(): lax.ppermute(value, axis, [(source, source ^ step) for source in range(pa...]
    all_to_all x2 -> x0, starting transfers between devices: 9.25 us -> none  [the longest x1 5.73 us: to_channels(): lax.all_to_all(stacked, 'seq', split_axis=1, concat_axis=2, tiled=True)]
    convert_element_type x6 -> x0, other arithmetic: 8.64 us -> none  [the longest x1 3.92 us: local(): short_backward(grads_ext, taps, offsets_ext).astype(jnp.bfloat16)]
    slice x8 -> x0, local copies, waits for them, and re-layouts: 6.3 us -> none  [the longest x2 3.27 us: local(): ahead = shifted(grads[:, :, :margin], 'seq', -1)]
  transfers between devices with their start and end apart: 4 -> 13, of which waited for: 4 -> 9; matrix products, arithmetic and copies ran while one was open for 1% -> 0% of each run, Pallas kernels for 0% -> 14%
where the time goes in v2:
time: 91.1 us; the launch traced here: 90.8 us
  waiting for transfers between devices  35 us (38%)
  Pallas kernels  30.5 us (33%)
  starting transfers between devices  20.4 us (22%)
  local copies, waits for them, and re-layouts  3.97 us (4%)
    pallas_call x7, Pallas kernels, streamed(): pl.pallas_call(functools.partial(body, layout), out_shape=outs, grid_spec...  29.7 us
    ppermute x11, waiting for transfers between devices, swap(): lax.ppermute(value, axis, [(source, source ^ step) for source in range(pa...  24.9 us
    ppermute x11, starting transfers between devices, swap(): lax.ppermute(value, axis, [(source, source ^ step) for source in range(pa...  18 us
    ppermute x2, waiting for transfers between devices, around(): lax.ppermute(value, 'seq', [(source, (source + steps) % parts) for source...  10.1 us
    unnamed x24, local copies, waits for them, and re-layouts  3.97 us
    ppermute x2, starting transfers between devices, around(): lax.ppermute(value, 'seq', [(source, (source + steps) % parts) for source...  2.46 us
  transfers between devices with their start and end apart: 13, of which 9 were waited for; matrix products, arithmetic and copies ran while one was open for 0% of the time, Pallas kernels for 14%

profile of v2, /device:TPU:0, one launch (start us, length us, event | category | flops | bytes accessed | tf_op | source)
XLA Modules:
  0.0 90.8 jit_solution(12759150758667723589)
XLA Ops:
  0.7 1.4 %copy-done = bf16[3,1024,256]{2,1,0:T(8,128)(2,1)S(1)} copy-done((bf16[3,1024,256]{2,1,0:T(8,128)(2,1)S(1)}, bf16[3,1024,256]{2,1,0:T(8,128)(2,1)}, u32[]{:S(2)}) %copy-start) | copy-done | bytes 1572888
  2.1 1.0 %copy-done.3 = bf16[1024,256]{1,0:T(8,128)(2,1)S(1)} copy-done((bf16[1024,256]{1,0:T(8,128)(2,1)S(1)}, bf16[1024,256]{1,0:T(8,128)(2,1)}, u32[]{:S(2)}) %copy-start.3) | copy-done | bytes 524312
  3.2 0.8 copy-done.5
  4.0 0.7 copy-done.6
  4.7 1.0 %shard_map.113 = (bf16[16,1024]{1,0:T(8,128)(2,1)S(1)}, f32[1024,16]{1,0:T(8,128)S(1)}, bf16[256,256]{1,0:T(8,128)(2,1)S(1)}, bf16[256,256]{1,0:T(8,128)(2,1)S(1)}) custom-call(s32[2]{0:T(128)S(1)} %pad_add_fusion.place_ref.rank_ref, bf16[3,1024,256]{2,1,0:T(8,128)(2,1)S(1)} %copy-done, bf16[1024,256]{1,0:T(8,128)(2,1)S(1)} %copy-done.3, ...), custom_call_target="tpu_custom_call" | custom-call | bytes 1572864 | tf_op jit(solution)/shard_map/pallas_call | solution.py:103
  5.7 4.1 %collective-permute-start.2 = (bf16[256,256]{1,0:T(8,128)(2,1)S(1)}, bf16[256,256]{1,0:T(8,128)(2,1)S(1)}, u32[]{:S(2)}, u32[]{:S(2)}) collective-permute-start(bf16[256,256]{1,0:T(8,128)(2,1)S(1)} %get-tuple-element.23), channel_id=1, source_target_pairs={{0,8},{4,12},{8,0},{12,4},{1,9},{5,13},{9,1},{13,5},{2,10},{6,14},... | collective-permute-start | bytes 393224 | tf_op jit(solution)/shard_map/ppermute | solution.py:635
  9.8 1.3 %collective-permute-start.3 = (bf16[256,256]{1,0:T(8,128)(2,1)S(1)}, bf16[256,256]{1,0:T(8,128)(2,1)S(1)}, u32[]{:S(2)}, u32[]{:S(2)}) collective-permute-start(bf16[256,256]{1,0:T(8,128)(2,1)S(1)} %get-tuple-element.22), channel_id=1, source_target_pairs={{0,12},{4,8},{8,4},{12,0},{1,13},{5,9},{9,5},{13,1},{2,14},{6,10},... | collective-permute-start | bytes 393224 | tf_op jit(solution)/shard_map/ppermute | solution.py:635
  11.4 1.8 %collective-permute-start = (bf16[16,1024]{1,0:T(8,128)(2,1)S(1)}, bf16[16,1024]{1,0:T(8,128)(2,1)S(1)}, u32[]{:S(2)}, u32[]{:S(2)}) collective-permute-start(bf16[16,1024]{1,0:T(8,128)(2,1)S(1)} %get-tuple-element.19), channel_id=1, source_target_pairs={{0,4},{4,8},{8,12},{12,0},{1,5},{5,9},{9,13},{13,1},{2,6},{6,10},{... | collective-permute-start | bytes 98312 | tf_op jit(solution)/shard_map/ppermute | solution.py:639
  13.2 0.9 shard_map.114.keep_ref
  14.0 6.8 %collective-permute-done.halo_ref = bf16[16,1024]{1,0:T(8,128)(2,1)S(1)} collective-permute-done((bf16[16,1024]{1,0:T(8,128)(2,1)S(1)}, bf16[16,1024]{1,0:T(8,128)(2,1)S(1)}, u32[]{:S(2)}, u32[]{:S(2)}) %collective-permute-start) | collective-permute-done | bytes 32800 | tf_op jit(solution)/shard_map/ppermute | solution.py:639
  20.9 5.8 %shard_map.115 = (bf16[3,1024,256]{2,1,0:T(8,128)(2,1)S(1)}, bf16[2,512,256]{2,1,0:T(8,128)(2,1)S(1)}, bf16[2,512,256]{2,1,0:T(8,128)(2,1)S(1)}, bf16[256,256]{1,0:T(8,128)(2,1)S(1)}, bf16[256,256]{1,0:T(8,128)(2,1)S(1)}) custom-call(s32[2]{0:T(128)S(1)} %pad_add_fusion.place_ref.rank_ref, bf16[3,1024,256]{2,1,0:T(8,128)(2,1)S(1)} %copy-done.1, ...), custom_call_target="tpu_custom_call" | custom-call | flops 7864320 | bytes 4718592 | tf_op jit(solution)/shard_map/pallas_call | solution.py:103
  26.7 2.4 %collective-permute-start.5 = (bf16[2,512,256]{2,1,0:T(8,128)(2,1)S(1)}, bf16[2,512,256]{2,1,0:T(8,128)(2,1)S(1)}, u32[]{:S(2)}, u32[]{:S(2)}) collective-permute-start(bf16[2,512,256]{2,1,0:T(8,128)(2,1)S(1)} %get-tuple-element.25), channel_id=1, source_target_pairs={{0,4},{4,0},{8,12},{12,8},{1,5},{5,1},{9,13},{13,9},{2,6},{6,2},{1... | collective-permute-start | bytes 1572872 | tf_op jit(solution)/shard_map/ppermute | solution.py:635
  29.2 1.6 %collective-permute-start.4 = (bf16[768,256]{1,0:T(8,128)(2,1)S(1)}, bf16[768,256]{1,0:T(8,128)(2,1)S(1)}, u32[]{:S(2)}, u32[]{:S(2)}) collective-permute-start(bf16[768,256]{1,0:T(8,128)(2,1)S(1)} %pad_maximum_fusion), channel_id=1, source_target_pairs={{0,16},{16,0},{1,17},{17,1},{2,18},{18,2},{3,19},{19,3},{4,20},{20... | collective-permute-start | bytes 1179656 | tf_op jit(solution)/shard_map/ppermute | solution.py:635
  30.8 9.2 %collective-permute-done.4.other_ref = bf16[768,256]{1,0:T(8,128)(2,1)S(1)} collective-permute-done((bf16[768,256]{1,0:T(8,128)(2,1)S(1)}, bf16[768,256]{1,0:T(8,128)(2,1)S(1)}, u32[]{:S(2)}, u32[]{:S(2)}) %collective-permute-start.4) | collective-permute-done | bytes 393248 | tf_op jit(solution)/shard_map/ppermute | solution.py:635
  40.0 1.2 %collective-permute-done.5.rest_4_ = bf16[2,512,256]{2,1,0:T(8,128)(2,1)S(1)} collective-permute-done((bf16[2,512,256]{2,1,0:T(8,128)(2,1)S(1)}, bf16[2,512,256]{2,1,0:T(8,128)(2,1)S(1)}, u32[]{:S(2)}, u32[]{:S(2)}) %collective-permute-start.5) | collective-permute-done | bytes 524320 | tf_op jit(solution)/shard_map/ppermute | solution.py:635
  41.3 7.5 %shard_map.116 = (bf16[3,256,256]{2,1,0:T(8,128)(2,1)S(1)}, bf16[3,256,256]{2,1,0:T(8,128)(2,1)S(1)}, f32[256,256]{1,0:T(8,128)S(1)}, f32[256,256]{1,0:T(8,128)S(1)}) custom-call(s32[2]{0:T(128)S(1)} %pad_add_fusion.place_ref.rank_ref, f32[1024,16]{1,0:T(8,128)S(1)} %get-tuple-element.20.cols_ref, bf16[256,512]{1,0:T(8,128)(2,1)S(1)} %copy-done.11, ...), custom_call_target="tpu_custom_call" | custom-call | flops 3221225472 | bytes 3670016 | tf_op jit(solution)/shard_map/pallas_call | solution.py:103
  48.7 1.8 %collective-permute-start.6 = (bf16[3,256,256]{2,1,0:T(8,128)(2,1)S(1)}, bf16[3,256,256]{2,1,0:T(8,128)(2,1)S(1)}, u32[]{:S(2)}, u32[]{:S(2)}) collective-permute-start(bf16[3,256,256]{2,1,0:T(8,128)(2,1)S(1)} %get-tuple-element.27), channel_id=1, source_target_pairs={{0,4},{4,0},{8,12},{12,8},{1,5},{5,1},{9,13},{13,9},{2,6},{6,2},{1... | collective-permute-start | bytes 1179656 | tf_op jit(solution)/shard_map/ppermute | solution.py:635
  50.6 2.2 %collective-permute-start.7 = (bf16[256,256]{1,0:T(8,128)(2,1)S(1)}, bf16[256,256]{1,0:T(8,128)(2,1)S(1)}, u32[]{:S(2)}, u32[]{:S(2)}) collective-permute-start(bf16[256,256]{1,0:T(8,128)(2,1)S(1)} %get-tuple-element.28), channel_id=1, source_target_pairs={{0,8},{4,12},{8,0},{12,4},{1,9},{5,13},{9,1},{13,5},{2,10},{6,14},... | collective-permute-start | bytes 393224 | tf_op jit(solution)/shard_map/ppermute | solution.py:635
  52.8 1.2 %collective-permute-start.8 = (bf16[256,256]{1,0:T(8,128)(2,1)S(1)}, bf16[256,256]{1,0:T(8,128)(2,1)S(1)}, u32[]{:S(2)}, u32[]{:S(2)}) collective-permute-start(bf16[256,256]{1,0:T(8,128)(2,1)S(1)} %get-tuple-element.29), channel_id=1, source_target_pairs={{0,12},{4,8},{8,4},{12,0},{1,13},{5,9},{9,5},{13,1},{2,14},{6,10},... | collective-permute-start | bytes 393224 | tf_op jit(solution)/shard_map/ppermute | solution.py:635
  53.9 3.2 %shard_map.118 = (bf16[256,256]{1,0:T(8,128)(2,1)S(1)}, bf16[256,256]{1,0:T(8,128)(2,1)S(1)}) custom-call(s32[2]{0:T(128)S(1)} %pad_add_fusion.place_ref.rank_ref, bf16[256,512]{1,0:T(8,128)(2,1)S(1)} %copy-done.11, bf16[256,512]{1,0:T(8,128)(2,1)S(1)} %copy-done.10, bf16[512,256]{1,0:T(8,128)(2,1)S(1)} %copy-done.9, bf16[512,256]{1,0:T(8,128)(2,1)S(1)} %copy-done.8, ...), custom_call_target="tpu_custom_call" | custom-call | flops 1207959552 | bytes 2621440 | tf_op jit(solution)/shard_map/pallas_call | solution.py:103
  57.1 2.1 %collective-permute-start.10 = (bf16[256,256]{1,0:T(8,128)(2,1)S(1)}, bf16[256,256]{1,0:T(8,128)(2,1)S(1)}, u32[]{:S(2)}, u32[]{:S(2)}) collective-permute-start(bf16[256,256]{1,0:T(8,128)(2,1)S(1)} %get-tuple-element.34), channel_id=1, source_target_pairs={{0,8},{4,12},{8,0},{12,4},{1,9},{5,13},{9,1},{13,5},{2,10},{6,14},... | collective-permute-start | bytes 393224 | tf_op jit(solution)/shard_map/ppermute | solution.py:635
  59.2 0.9 %collective-permute-start.11 = (bf16[256,256]{1,0:T(8,128)(2,1)S(1)}, bf16[256,256]{1,0:T(8,128)(2,1)S(1)}, u32[]{:S(2)}, u32[]{:S(2)}) collective-permute-start(bf16[256,256]{1,0:T(8,128)(2,1)S(1)} %get-tuple-element.35), channel_id=1, source_target_pairs={{0,12},{4,8},{8,4},{12,0},{1,13},{5,9},{9,5},{13,1},{2,14},{6,10},... | collective-permute-start | bytes 393224 | tf_op jit(solution)/shard_map/ppermute | solution.py:635
  60.1 2.8 %collective-permute-done.7.rest_3_ = bf16[256,256]{1,0:T(8,128)(2,1)S(1)} collective-permute-done((bf16[256,256]{1,0:T(8,128)(2,1)S(1)}, bf16[256,256]{1,0:T(8,128)(2,1)S(1)}, u32[]{:S(2)}, u32[]{:S(2)}) %collective-permute-start.7) | collective-permute-done | bytes 131104 | tf_op jit(solution)/shard_map/ppermute | solution.py:635
  63.0 6.6 %collective-permute-done.8.rest_4_ = bf16[256,256]{1,0:T(8,128)(2,1)S(1)} collective-permute-done((bf16[256,256]{1,0:T(8,128)(2,1)S(1)}, bf16[256,256]{1,0:T(8,128)(2,1)S(1)}, u32[]{:S(2)}, u32[]{:S(2)}) %collective-permute-start.8) | collective-permute-done | bytes 131104 | tf_op jit(solution)/shard_map/ppermute | solution.py:635
  69.6 3.2 %shard_map.117 = (bf16[256,256]{1,0:T(8,128)(2,1)S(1)}, bf16[256,256]{1,0:T(8,128)(2,1)S(1)}) custom-call(s32[2]{0:T(128)S(1)} %pad_add_fusion.place_ref.rank_ref, bf16[256,512]{1,0:T(8,128)(2,1)S(1)} %copy-done.11, bf16[256,512]{1,0:T(8,128)(2,1)S(1)} %copy-done.10, bf16[512,256]{1,0:T(8,128)(2,1)S(1)} %copy-done.9, bf16[512,256]{1,0:T(8,128)(2,1)S(1)} %copy-done.8, ...), custom_call_target="tpu_custom_call" | custom-call | flops 1207959552 | bytes 2621440 | tf_op jit(solution)/shard_map/pallas_call | solution.py:103
  72.9 1.5 %collective-permute-done.10.rest_4_ = bf16[256,256]{1,0:T(8,128)(2,1)S(1)} collective-permute-done((bf16[256,256]{1,0:T(8,128)(2,1)S(1)}, bf16[256,256]{1,0:T(8,128)(2,1)S(1)}, u32[]{:S(2)}, u32[]{:S(2)}) %collective-permute-start.10) | collective-permute-done | bytes 131104 | tf_op jit(solution)/shard_map/ppermute | solution.py:635
  74.3 0.5 collective-permute-done.11.rest_5_
  74.8 3.0 %collective-permute-done.9.rest_3_ = bf16[256,256]{1,0:T(8,128)(2,1)S(1)} collective-permute-done((bf16[256,256]{1,0:T(8,128)(2,1)S(1)}, bf16[256,256]{1,0:T(8,128)(2,1)S(1)}, u32[]{:S(2)}, u32[]{:S(2)}) %collective-permute-start.9) | collective-permute-done | bytes 131104 | tf_op jit(solution)/shard_map/ppermute | solution.py:635
  77.8 1.6 %shard_map.119 = f32[8,1024]{1,0:T(8,128)S(1)} custom-call(s32[2]{0:T(128)S(1)} %pad_add_fusion.place_ref.rank_ref, bf16[3,1024,256]{2,1,0:T(8,128)(2,1)S(1)} %get-tuple-element.21.qkv_ref, bf16[1024,256]{1,0:T(8,128)(2,1)S(1)} %copy-done.2, bf16[3,256,256]{2,1,0:T(8,128)(2,1)S(1)} %get-tuple-element.26.rest_0_, ...), custom_call_target="tpu_custom_call" | custom-call | bytes 786432 | tf_op jit(solution)/shard_map/pallas_call | solution.py:103
  79.4 0.7 collective-permute-start.12
  80.1 3.3 %collective-permute-done.12.ahead_ref = f32[8,1024]{1,0:T(8,128)S(1)} collective-permute-done((f32[8,1024]{1,0:T(8,128)S(1)}, f32[8,1024]{1,0:T(8,128)S(1)}, u32[]{:S(2)}, u32[]{:S(2)}) %collective-permute-start.12) | collective-permute-done | bytes 32800 | tf_op jit(solution)/shard_map/ppermute | solution.py:639
  83.4 7.4 %shard_map.120 = (bf16[1024,256]{1,0:T(8,128)(2,1)}, bf16[3,1024,256]{2,1,0:T(8,128)(2,1)}) custom-call(s32[2]{0:T(128)S(1)} %pad_add_fusion.place_ref.rank_ref, bf16[3,1024,256]{2,1,0:T(8,128)(2,1)S(1)} %get-tuple-element.21.qkv_ref, bf16[1024,256]{1,0:T(8,128)(2,1)S(1)} %copy-done.2, f32[1024,16]{1,0:T(8,128)S(1)} %get-tuple-element.20.cols_ref, ...), custom_call_target="tpu_custom_call" | custom-call | flops 10485760 | bytes 5242880 | tf_op jit(solution)/shard_map/pallas_call | solution.py:103
  (28 shorter events, 0.5 us)
Async XLA Ops:
  0.6 12.5 %copy-start.7 = (s32[16]{0:T(128)S(1)}, s32[16]{0:T(128)}, u32[]{:S(2)}) copy-start(s32[16]{0:T(128)} %lengths_ref.1) | copy-start | bytes 196
  0.7 1.4 %copy-start = (bf16[3,1024,256]{2,1,0:T(8,128)(2,1)S(1)}, bf16[3,1024,256]{2,1,0:T(8,128)(2,1)}, u32[]{:S(2)}) copy-start(bf16[3,1024,256]{2,1,0:T(8,128)(2,1)} %feat_ref.1) | copy-start | bytes 4718596
  2.1 1.0 %copy-start.3 = (bf16[1024,256]{1,0:T(8,128)(2,1)S(1)}, bf16[1024,256]{1,0:T(8,128)(2,1)}, u32[]{:S(2)}) copy-start(bf16[1024,256]{1,0:T(8,128)(2,1)} %filt_ref.7) | copy-start | bytes 1572868
  3.2 0.8 copy-start.5
  4.0 0.7 copy-start.6
  4.7 16.2 %copy-start.1 = (bf16[3,1024,256]{2,1,0:T(8,128)(2,1)S(1)}, bf16[3,1024,256]{2,1,0:T(8,128)(2,1)}, u32[]{:S(2)}) copy-start(bf16[3,1024,256]{2,1,0:T(8,128)(2,1)} %feat_ref.1) | copy-start | bytes 4718596
  4.7 16.2 %copy-start.2 = (bf16[1024,256]{1,0:T(8,128)(2,1)S(1)}, bf16[1024,256]{1,0:T(8,128)(2,1)}, u32[]{:S(2)}) copy-start(bf16[1024,256]{1,0:T(8,128)(2,1)} %dout_ref.5) | copy-start | bytes 1572868
  5.7 23.4 %collective-permute-start.2 = (bf16[256,256]{1,0:T(8,128)(2,1)S(1)}, bf16[256,256]{1,0:T(8,128)(2,1)S(1)}, u32[]{:S(2)}, u32[]{:S(2)}) collective-permute-start(bf16[256,256]{1,0:T(8,128)(2,1)S(1)} %get-tuple-element.23), channel_id=1, source_target_pairs={{0,8},{4,12},{8,0},{12,4},{1,9},{5,13},{9,1},{13,5},{2,10},{6,14},... | collective-permute-start | bytes 393224 | tf_op jit(solution)/shard_map/ppermute | solution.py:635
  9.8 19.3 %collective-permute-start.3 = (bf16[256,256]{1,0:T(8,128)(2,1)S(1)}, bf16[256,256]{1,0:T(8,128)(2,1)S(1)}, u32[]{:S(2)}, u32[]{:S(2)}) collective-permute-start(bf16[256,256]{1,0:T(8,128)(2,1)S(1)} %get-tuple-element.22), channel_id=1, source_target_pairs={{0,12},{4,8},{8,4},{12,0},{1,13},{5,9},{9,5},{13,1},{2,14},{6,10},... | collective-permute-start | bytes 393224 | tf_op jit(solution)/shard_map/ppermute | solution.py:635
  11.1 18.0 %collective-permute-start.1 = (bf16[256,256]{1,0:T(8,128)(2,1)S(1)}, bf16[256,256]{1,0:T(8,128)(2,1)S(1)}, u32[]{:S(2)}, u32[]{:S(2)}) collective-permute-start(bf16[256,256]{1,0:T(8,128)(2,1)S(1)} %get-tuple-element.22), channel_id=1, source_target_pairs={{0,4},{4,0},{8,12},{12,8},{1,5},{5,1},{9,13},{13,9},{2,6},{6,2},{1... | collective-permute-start | bytes 393224 | tf_op jit(solution)/shard_map/ppermute | solution.py:635
  11.4 9.5 %collective-permute-start = (bf16[16,1024]{1,0:T(8,128)(2,1)S(1)}, bf16[16,1024]{1,0:T(8,128)(2,1)S(1)}, u32[]{:S(2)}, u32[]{:S(2)}) collective-permute-start(bf16[16,1024]{1,0:T(8,128)(2,1)S(1)} %get-tuple-element.19), channel_id=1, source_target_pairs={{0,4},{4,8},{8,12},{12,0},{1,5},{5,9},{9,13},{13,1},{2,6},{6,10},{... | collective-permute-start | bytes 98312 | tf_op jit(solution)/shard_map/ppermute | solution.py:639
  20.9 20.4 %copy-start.4 = (bf16[1024,256]{1,0:T(8,128)(2,1)S(1)}, bf16[1024,256]{1,0:T(8,128)(2,1)}, u32[]{:S(2)}) copy-start(bf16[1024,256]{1,0:T(8,128)(2,1)} %filt_ref.7) | copy-start | bytes 1572868
  20.9 20.4 %copy-start.8 = (bf16[512,256]{1,0:T(8,128)(2,1)S(1)}, bf16[512,256]{1,0:T(8,128)(2,1)}, u32[]{:S(2)}) copy-start(bf16[512,256]{1,0:T(8,128)(2,1)} %constant.22.clone.ilo_ref) | copy-start | bytes 786436
  20.9 20.4 %copy-start.9 = (bf16[512,256]{1,0:T(8,128)(2,1)S(1)}, bf16[512,256]{1,0:T(8,128)(2,1)}, u32[]{:S(2)}) copy-start(bf16[512,256]{1,0:T(8,128)(2,1)} %constant.21.clone.ihi_ref) | copy-start | bytes 786436
  20.9 20.4 %copy-start.10 = (bf16[256,512]{1,0:T(8,128)(2,1)S(1)}, bf16[256,512]{1,0:T(8,128)(2,1)}, u32[]{:S(2)}) copy-start(bf16[256,512]{1,0:T(8,128)(2,1)} %constant.20.clone.flo_ref) | copy-start | bytes 786436
  20.9 20.4 %copy-start.11 = (bf16[256,512]{1,0:T(8,128)(2,1)S(1)}, bf16[256,512]{1,0:T(8,128)(2,1)}, u32[]{:S(2)}) copy-start(bf16[256,512]{1,0:T(8,128)(2,1)} %constant.19.clone.fhi_ref) | copy-start | bytes 786436
  26.7 14.5 %collective-permute-start.5 = (bf16[2,512,256]{2,1,0:T(8,128)(2,1)S(1)}, bf16[2,512,256]{2,1,0:T(8,128)(2,1)S(1)}, u32[]{:S(2)}, u32[]{:S(2)}) collective-permute-start(bf16[2,512,256]{2,1,0:T(8,128)(2,1)S(1)} %get-tuple-element.25), channel_id=1, source_target_pairs={{0,4},{4,0},{8,12},{12,8},{1,5},{5,1},{9,13},{13,9},{2,6},{6,2},{1... | collective-permute-start | bytes 1572872 | tf_op jit(solution)/shard_map/ppermute | solution.py:635
  29.2 10.8 %collective-permute-start.4 = (bf16[768,256]{1,0:T(8,128)(2,1)S(1)}, bf16[768,256]{1,0:T(8,128)(2,1)S(1)}, u32[]{:S(2)}, u32[]{:S(2)}) collective-permute-start(bf16[768,256]{1,0:T(8,128)(2,1)S(1)} %pad_maximum_fusion), channel_id=1, source_target_pairs={{0,16},{16,0},{1,17},{17,1},{2,18},{18,2},{3,19},{19,3},{4,20},{20... | collective-permute-start | bytes 1179656 | tf_op jit(solution)/shard_map/ppermute | solution.py:635
  48.7 29.1 %collective-permute-start.6 = (bf16[3,256,256]{2,1,0:T(8,128)(2,1)S(1)}, bf16[3,256,256]{2,1,0:T(8,128)(2,1)S(1)}, u32[]{:S(2)}, u32[]{:S(2)}) collective-permute-start(bf16[3,256,256]{2,1,0:T(8,128)(2,1)S(1)} %get-tuple-element.27), channel_id=1, source_target_pairs={{0,4},{4,0},{8,12},{12,8},{1,5},{5,1},{9,13},{13,9},{2,6},{6,2},{1... | collective-permute-start | bytes 1179656 | tf_op jit(solution)/shard_map/ppermute | solution.py:635
  50.6 12.4 %collective-permute-start.7 = (bf16[256,256]{1,0:T(8,128)(2,1)S(1)}, bf16[256,256]{1,0:T(8,128)(2,1)S(1)}, u32[]{:S(2)}, u32[]{:S(2)}) collective-permute-start(bf16[256,256]{1,0:T(8,128)(2,1)S(1)} %get-tuple-element.28), channel_id=1, source_target_pairs={{0,8},{4,12},{8,0},{12,4},{1,9},{5,13},{9,1},{13,5},{2,10},{6,14},... | collective-permute-start | bytes 393224 | tf_op jit(solution)/shard_map/ppermute | solution.py:635
  52.8 16.8 %collective-permute-start.8 = (bf16[256,256]{1,0:T(8,128)(2,1)S(1)}, bf16[256,256]{1,0:T(8,128)(2,1)S(1)}, u32[]{:S(2)}, u32[]{:S(2)}) collective-permute-start(bf16[256,256]{1,0:T(8,128)(2,1)S(1)} %get-tuple-element.29), channel_id=1, source_target_pairs={{0,12},{4,8},{8,4},{12,0},{1,13},{5,9},{9,5},{13,1},{2,14},{6,10},... | collective-permute-start | bytes 393224 | tf_op jit(solution)/shard_map/ppermute | solution.py:635
  57.1 17.2 %collective-permute-start.10 = (bf16[256,256]{1,0:T(8,128)(2,1)S(1)}, bf16[256,256]{1,0:T(8,128)(2,1)S(1)}, u32[]{:S(2)}, u32[]{:S(2)}) collective-permute-start(bf16[256,256]{1,0:T(8,128)(2,1)S(1)} %get-tuple-element.34), channel_id=1, source_target_pairs={{0,8},{4,12},{8,0},{12,4},{1,9},{5,13},{9,1},{13,5},{2,10},{6,14},... | collective-permute-start | bytes 393224 | tf_op jit(solution)/shard_map/ppermute | solution.py:635
  59.2 15.7 %collective-permute-start.11 = (bf16[256,256]{1,0:T(8,128)(2,1)S(1)}, bf16[256,256]{1,0:T(8,128)(2,1)S(1)}, u32[]{:S(2)}, u32[]{:S(2)}) collective-permute-start(bf16[256,256]{1,0:T(8,128)(2,1)S(1)} %get-tuple-element.35), channel_id=1, source_target_pairs={{0,12},{4,8},{8,4},{12,0},{1,13},{5,9},{9,5},{13,1},{2,14},{6,10},... | collective-permute-start | bytes 393224 | tf_op jit(solution)/shard_map/ppermute | solution.py:635
  72.8 5.0 %collective-permute-start.9 = (bf16[256,256]{1,0:T(8,128)(2,1)S(1)}, bf16[256,256]{1,0:T(8,128)(2,1)S(1)}, u32[]{:S(2)}, u32[]{:S(2)}) collective-permute-start(bf16[256,256]{1,0:T(8,128)(2,1)S(1)} %get-tuple-element.33), channel_id=1, source_target_pairs={{0,4},{4,0},{8,12},{12,8},{1,5},{5,1},{9,13},{13,9},{2,6},{6,2},{1... | collective-permute-start | bytes 393224 | tf_op jit(solution)/shard_map/ppermute | solution.py:635
  79.4 3.9 %collective-permute-start.12 = (f32[8,1024]{1,0:T(8,128)S(1)}, f32[8,1024]{1,0:T(8,128)S(1)}, u32[]{:S(2)}, u32[]{:S(2)}) collective-permute-start(f32[8,1024]{1,0:T(8,128)S(1)} %shard_map.119), channel_id=1, source_target_pairs={{0,12},{4,0},{8,4},{12,8},{1,13},{5,1},{9,5},{13,9},{2,14},{6,2},{... | collective-permute-start | bytes 98312 | tf_op jit(solution)/shard_map/ppermute | solution.py:639

commit v3 on v2

v3 whole, which is shorter than its diff:
```python
import functools
import math

import jax
import jax.numpy as jnp
import numpy as np
from jax import lax
from jax.experimental import pallas as pl
from jax.experimental.pallas import tpu as pltpu
from jax.sharding import PartitionSpec as P

BF16 = jnp.bfloat16
F32 = jnp.float32
VMEM_LIMIT = 24 * 1024 * 1024
SCALARS = pl.BlockSpec(memory_space=pltpu.SMEM)
IN_HBM = pl.BlockSpec(memory_space=pltpu.HBM)
ANYWHERE = pl.BlockSpec(memory_space=pl.ANY)


def split_bf16(table):
    high = table.astype(np.float32).astype(BF16)
    low = (table - high.astype(np.float64)).astype(np.float32).astype(BF16)
    return high, low


def block_tables(span):
    freq = np.concatenate([np.arange(0, span, 2), np.arange(1, span, 2)])
    angle = np.pi * (2 * freq[None, :] + 1) * np.arange(span)[:, None] / (2 * span)
    forward = np.concatenate([np.cos(angle), -np.sin(angle)], axis=1)
    inverse = np.concatenate([np.cos(angle), -np.sin(angle)], axis=1).T / span
    return np.concatenate(split_bf16(forward), axis=0), split_bf16(inverse)[0]


def dot(a, b):
    return jnp.dot(a, b, preferred_element_type=F32)


def estimate(flops, moved):
    return pl.CostEstimate(flops=int(flops), bytes_accessed=int(moved), transcendentals=0)


def offsets_row(lengths_ref, first, span, ahead):
    position = lax.broadcasted_iota(jnp.int32, (8, span), 1) + (first + ahead)

    def step(genome, carry):
        end, start = carry
        end = end + lengths_ref[genome]
        return end, jnp.where(position >= end, end, start)

    begin = (jnp.int32(0), jnp.zeros((8, span), jnp.int32))
    _, start = lax.fori_loop(0, lengths_ref.shape[0], step, begin)
    return position, position - start


class Layout:
    def __init__(self, parts, channels, span):
        self.parts, self.channels, self.span = parts, channels, span
        self.half = parts // 2
        self.size = channels // self.half
        self.sub = self.size // 2


def where_am_i(place_ref, layout):
    rank, group = place_ref[0], place_ref[1]
    side = rank // layout.half
    return side, rank % layout.half, jnp.where(side == 0, 1 - group, group)


def channel_block(place_ref, layout, turn, other):
    _, own, main = where_am_i(place_ref, layout)
    return jnp.bitwise_xor(own, turn) * 2 + jnp.bitwise_xor(main, other)


def fixed(shape):
    return pl.BlockSpec(shape, lambda *args: (0,) * len(shape))


def streamed(body, layout, place, operands, in_specs, outs, out_specs, scratch, grid, cost, aliases=None):
    return pl.pallas_call(
        functools.partial(body, layout),
        out_shape=outs,
        grid_spec=pltpu.PrefetchScalarGridSpec(
            num_scalar_prefetch=1,
            grid=grid,
            in_specs=in_specs,
            out_specs=out_specs,
            scratch_shapes=scratch,
        ),
        input_output_aliases=aliases or {},
        compiler_params=pltpu.CompilerParams(vmem_limit_bytes=VMEM_LIMIT),
        cost_estimate=cost,
    )(place, *operands)


def pack_body(layout, place_ref, feat_ref, filt_ref, halo_ref, *rest):
    filt_out, (tail, turned, sems) = rest[: layout.parts - 1], rest[layout.parts - 1 :]
    span, half, sub = layout.span, layout.half, layout.sub
    copies = [pltpu.make_async_copy(feat_ref.at[:, :, span - 128 : span], tail, sems.at[0])]
    for step in range(1, layout.parts):
        begin = channel_block(place_ref, layout, step % half, step // half) * sub
        source = filt_ref.at[pl.ds(pl.multiple_of(begin, sub), sub), :]
        copies.append(pltpu.make_async_copy(source, filt_out[step - 1], sems.at[step]))
    for copy in copies:
        copy.start()
    turned[...] = jnp.zeros(turned.shape, F32)
    copies[0].wait()
    for which in range(3):
        turned[2 * which : 2 * which + 2, :] = tail[which].astype(F32).T[-2:, :]
    halo_ref[...] = turned[...].astype(BF16)
    for copy in copies[1:]:
        copy.wait()


def pack(layout, place, features, filters):
    channels, span, parts = layout.channels, layout.span, layout.parts
    shapes = [(16, channels)] + [(layout.sub, span)] * (parts - 1)
    found = streamed(
        pack_body,
        layout,
        place,
        (features, filters),
        [IN_HBM, IN_HBM],
        [jax.ShapeDtypeStruct(s, BF16) for s in shapes],
        [fixed(s) for s in shapes],
        [
            pltpu.VMEM((3, channels, 128), BF16),
            pltpu.VMEM((16, channels), F32),
            pltpu.SemaphoreType.DMA((parts,)),
        ],
        (1,),
        estimate(0, 3 * channels * span),
    )
    return found[0], found[1:]


def small_body(layout, place_ref, lengths_ref, taps_ref, skip_ref, keep_ref, cols_ref, turned):
    span = layout.span
    first = place_ref[0] * span
    keep_ref[...] = jnp.zeros(keep_ref.shape, F32)
    _, offset = offsets_row(lengths_ref, first, span, 0)
    for j in (1, 2):
        keep_ref[j - 1 : j, :] = (offset[0:1, :] >= j).astype(F32)
        position, later = offsets_row(lengths_ref, first, span, j)
        inside = (position < layout.parts * span) & (later >= j)
        keep_ref[1 + j : 2 + j, :] = inside[0:1, :].astype(F32)
    turned[...] = jnp.zeros(turned.shape, F32)
    for which in range(3):
        turned[3 * which : 3 * which + 3, :] = taps_ref[which]
    turned[9:10, :] = skip_ref[...]
    cols_ref[...] = turned[...].T


def small(layout, place, lengths, taps, skip):
    channels = layout.channels
    shapes = [(8, layout.span), (channels, 16)]
    return streamed(
        small_body,
        layout,
        place,
        (lengths, taps, skip.reshape(1, channels)),
        [SCALARS, fixed(taps.shape), fixed((1, channels))],
        [jax.ShapeDtypeStruct(s, F32) for s in shapes],
        [fixed(s) for s in shapes],
        [pltpu.VMEM((16, channels), F32)],
        (1,),
        estimate(0, 100 * channels),
    )


def gate_body(other, layout, place_ref, feat_ref, dout_ref, halo_ref, cols_ref, keep_ref, *rest):
    half, rows, span = layout.half, layout.sub, layout.span
    if other:
        main_rest, rest = rest[:half], rest[half + 1 :]
    qkv_ref, rest = rest[0], rest[1:]
    firsts, seconds = rest[:half], rest[half : 2 * half]
    edge, made = rest[2 * half :]
    side, _, _ = where_am_i(place_ref, layout)
    turn = pl.program_id(0)
    base = channel_block(place_ref, layout, turn, other) * rows
    group = min(128, rows)

    @pl.when(turn == 0)
    def _():
        edge[...] = halo_ref[...].astype(F32).T

    keep = keep_ref[0:1, :], keep_ref[1:2, :]
    lane = lax.broadcasted_iota(jnp.int32, (group, span), 1)

    def tile(index, _):
        here = pl.ds(pl.multiple_of(index * group, group), group)
        cols = cols_ref[here, :]
        ends = edge[pl.ds(pl.multiple_of(base + index * group, group), group), :]
        filtered = []
        for which in range(3):
            value = feat_ref[which, here, :].astype(F32)
            two_back = ends[:, 2 * which : 2 * which + 1]
            one_back = ends[:, 2 * which + 1 : 2 * which + 2]
            back = jnp.where(lane == 0, one_back, pltpu.roll(value, 1, 1))
            twice = jnp.where(lane == 0, two_back, jnp.where(lane == 1, one_back, pltpu.roll(value, 2, 1)))
            total = cols[:, 3 * which : 3 * which + 1] * value
            total = total + cols[:, 3 * which + 1 : 3 * which + 2] * back * keep[0]
            total = total + cols[:, 3 * which + 2 : 3 * which + 3] * twice * keep[1]
            rounded = total.astype(BF16)
            qkv_ref[which, here, :] = rounded
            filtered.append(rounded.astype(F32))
        made[0, here, :] = (filtered[1] * filtered[2]).astype(BF16)
        made[1, here, :] = (dout_ref[here, :].astype(F32) * filtered[0]).astype(BF16)
        return 0

    lax.fori_loop(0, rows // group, tile, 0)
    for k in range(half):

        @pl.when(turn == k)
        def _(k=k):
            firsts[k][...] = made[side]
            if other:
                seconds[k][0] = main_rest[k][...]
                seconds[k][1] = made[side]
                seconds[k][2] = made[1 - side]
            else:
                seconds[k][...] = made[1 - side]


def gate(other, layout, place, features, dout, halo, cols, keep, qkv, main_rest):
    half, rows, span, channels = layout.half, layout.sub, layout.span, layout.channels

    def block(turn, place_ref):
        return channel_block(place_ref, layout, turn, other)

    wide = pl.BlockSpec((3, rows, span), lambda *a: (0, block(*a), 0))
    flat = pl.BlockSpec((rows, span), lambda *a: (block(*a), 0))
    columns = pl.BlockSpec((rows, 16), lambda *a: (block(*a), 0))
    shapes = [(rows, span)] * half + [(3, rows, span) if other else (rows, span)] * half
    operands = [features, dout, halo, cols, keep]
    in_specs = [wide, flat, fixed(halo.shape), columns, fixed(keep.shape)]
    if other:
        operands += [*main_rest, qkv]
        in_specs += [fixed((rows, span))] * half + [ANYWHERE]
    found = streamed(
        functools.partial(gate_body, other),
        layout,
        place,
        operands,
        in_specs,
        [jax.ShapeDtypeStruct(features.shape, BF16)] + [jax.ShapeDtypeStruct(s, BF16) for s in shapes],
        [wide] + [fixed(s) for s in shapes],
        [pltpu.VMEM((channels, 16), F32), pltpu.VMEM((2, rows, span), BF16)],
        (half,),
        estimate(15 * channels * span, 9 * channels * span),
        {len(operands): 0} if other else None,
    )
    return found[0], found[1 : 1 + half], found[1 + half :]


def loop(count, body, init):
    if count <= 4:
        for k in range(count):
            init = body(k, init)
        return init
    return lax.fori_loop(0, count, body, init)


def add_product(total, f, x):
    return (total[0] + f[0] * x[0] - f[1] * x[1], total[1] + f[0] * x[1] + f[1] * x[0])


def add_conjugate(total, f, x):
    return (total[0] + f[0] * x[0] + f[1] * x[1], total[1] + f[0] * x[1] - f[1] * x[0])


def turned_sum(spectrum, neighbour, sign):
    half = spectrum[0].shape[1] // 2
    parts = []
    for lanes, flip in ((slice(0, half), sign), (slice(half, None), -sign)):
        n_re, n_im = neighbour[0][:, lanes], neighbour[1][:, lanes]
        s_re, s_im = spectrum[0][:, lanes], spectrum[1][:, lanes]
        parts.append((s_re - n_im, s_im + n_re) if flip > 0 else (s_re + n_im, s_im - n_re))
    return tuple(jnp.concatenate([p[k] for p in parts], axis=1) for k in range(2))


def forward(raw, spec, begin, target, rows, table_ref):
    value = raw[pl.ds(pl.multiple_of(begin, 16), rows), :]
    spec[pl.ds(pl.multiple_of(target, 16), rows), :] = dot(jnp.concatenate([value, value], axis=1), table_ref[...])


def spectrum_at(spec, begin, group, span):
    place = pl.ds(pl.multiple_of(begin, group), group)
    return spec[place, :span], spec[place, span:]


def store_spectrum(ready, begin, value, group, span):
    place = pl.ds(pl.multiple_of(begin, group), group)
    ready[place, :span] = value[0].astype(BF16)
    ready[place, span:] = value[1].astype(BF16)


def own_body(layout, place_ref, cols_ref, forward_ref, inverse_ref, filt_ref, other_ref, *rest):
    parts, half, size, sub, span = layout.parts, layout.half, layout.size, layout.sub, layout.span
    filt_in, rest = rest[: parts - 1], rest[parts - 1 :]
    firsts, seconds, rest = rest[:half], rest[half : 2 * half], rest[2 * half + 1 :]
    returned, later = rest[:half], rest[half : 2 * half]
    raw, spec, ready, back = rest[2 * half :]
    side, own, main = where_am_i(place_ref, layout)
    rank = place_ref[0]
    kind_rows = half * size
    signals = parts * size

    def rows_at(begin, count):
        return pl.ds(pl.multiple_of(begin, sub), count)

    for cls in range(2):
        source = rows_at(jnp.bitwise_xor(main, cls) * sub, sub)
        raw[rows_at(rank * size + cls * sub, sub), :] = filt_ref[source, :]
    for step in range(1, parts):
        begin = jnp.bitwise_xor(rank, step) * size
        raw[rows_at(begin, sub), :] = filt_in[step - 1][...]
        raw[rows_at(begin + sub, sub), :] = other_ref[(step - 1) * sub : step * sub, :]
    for step in range(half):
        block = signals + jnp.bitwise_xor(own, step) * size
        raw[rows_at(block + side * kind_rows, sub), :] = firsts[step][...]
        raw[rows_at(block + (1 - side) * kind_rows, sub), :] = seconds[step][0]
        raw[rows_at(block + side * kind_rows + sub, sub), :] = seconds[step][1]
        raw[rows_at(block + (1 - side) * kind_rows + sub, sub), :] = seconds[step][2]

    def transform(index, _):
        kind, part = index // half, index % half
        begin = jnp.where(kind == 0, 0, signals + (kind - 1) * kind_rows) + part * size
        forward(raw, spec, begin, index * size, size, forward_ref)
        return 0

    lax.fori_loop(0, 3 * half, transform, 0)
    group = 16
    zero = (jnp.zeros((group, span), F32),) * 2

    def products(index, _):
        def read(kind, k):
            return spectrum_at(spec, (kind * half + k) * size + index * group, group, span)

        def store(kind, k, value):
            store_spectrum(ready, (kind * half + k) * size + index * group, value, group, span)

        before = None
        for place in range(half):
            total = loop(place + 1, lambda k, t, p=place: add_product(t, read(0, k), read(1, p - k)), zero)
            store(0, place, total if before is None else turned_sum(total, before, 1))
            before = total
        before = None
        for place in range(half - 1, -1, -1):
            total = loop(half - place, lambda k, t, p=place: add_conjugate(t, read(0, k), read(2, p + k)), zero)
            store(1, place, total if before is None else turned_sum(total, before, -1))
            before = total
        return 0

    lax.fori_loop(0, size // group, products, 0)

    def restore(index, _):
        place = rows_at(index * size, size)
        back[place, :] = dot(ready[place, :], inverse_ref[...])
        return 0

    lax.fori_loop(0, 2 * half, restore, 0)

    def result(kind, cls, part):
        begin = kind * kind_rows + part * size + cls * sub
        direct = raw[rows_at(signals + begin, sub), :].astype(F32)
        skip = cols_ref[rows_at(jnp.bitwise_xor(main, cls) * sub, sub), 9:10]
        return back[rows_at(begin, sub), :] + skip * direct

    for step in range(half):
        part = jnp.bitwise_xor(own, step)
        returned[step][0] = result(side, 0, part).astype(BF16)
        returned[step][1] = result(side, 1, part).astype(BF16)
        returned[step][2] = result(1 - side, 1, part).astype(BF16)
        later[step][...] = result(1 - side, 0, part)


def own_half(layout, place, cols, tables, filters, other, filt, firsts, seconds, after):
    half, size, sub, span, parts = layout.half, layout.size, layout.sub, layout.span, layout.parts
    own_class = lambda step, place_ref: (where_am_i(place_ref, layout)[1], 0)
    shapes = [((3, sub, span), BF16)] * half + [((sub, span), F32)] * half
    rows = 3 * half * size
    found = streamed(
        own_body,
        layout,
        place,
        (cols, *tables, filters, other, *filt, *firsts, *seconds, after),
        [pl.BlockSpec((size, 16), own_class)]
        + [fixed(t.shape) for t in tables]
        + [pl.BlockSpec((size, span), own_class), fixed(other.shape)]
        + [fixed((sub, span))] * (parts - 1 + half)
        + [fixed((3, sub, span))] * half
        + [ANYWHERE],
        [jax.ShapeDtypeStruct(*s) for s in shapes],
        [fixed(s[0]) for s in shapes],
        [
            pltpu.VMEM(((parts + 2 * half) * size, span), BF16),
            pltpu.VMEM((rows, 2 * span), F32),
            pltpu.VMEM((2 * half * size, 2 * span), BF16),
            pltpu.VMEM((2 * half * size, span), F32),
        ],
        (1,),
        estimate(2 * rows * span * 2 * span * 3, 7 * half * size * span * 2),
    )
    return found[:half], found[half:]


def cross_body(arriving, layout, place_ref, forward_ref, inverse_ref, filt_ref, *rest):
    parts, half, sub, span = layout.parts, layout.half, layout.sub, layout.span
    filt_in, rest = rest[: parts - 1], rest[parts - 1 :]
    signal, rest = rest[:half], rest[half:]
    partial, rest = (rest[:half], rest[half:]) if arriving else (None, rest)
    outs = rest[:half]
    raw, spec, ready, back = rest[half:]
    side, own, _ = where_am_i(place_ref, layout)
    rank = place_ref[0]
    block = parts * sub

    def rows_at(begin, count):
        return pl.ds(pl.multiple_of(begin, sub), count)

    raw[rows_at(rank * sub, sub), :] = filt_ref[...]
    for step in range(1, parts):
        raw[rows_at(jnp.bitwise_xor(rank, step) * sub, sub), :] = filt_in[step - 1][...]
    for step in range(half):
        raw[rows_at(block + jnp.bitwise_xor(own, step) * sub, sub), :] = signal[step][...]
    count = (parts + half) * sub
    chunk = math.gcd(count, 512)

    def transform(index, _):
        forward(raw, spec, index * chunk, index * chunk, chunk, forward_ref)
        return 0

    lax.fori_loop(0, count // chunk, transform, 0)
    group = 16
    zero = (jnp.zeros((group, span), F32),) * 2
    from_first = side == (1 if arriving else 0)

    def products(index, ahead):
        def filt(k):
            return spectrum_at(spec, k * sub + index * group, group, span)

        def sig(k):
            return spectrum_at(spec, block + k * sub + index * group, group, span)

        before = None
        if ahead:
            for place in range(half - 1, parts):
                total = loop(half, lambda k, t, p=place: add_product(t, filt(p - k), sig(k)), zero)
                if before is not None:
                    value = turned_sum(total, before, 1)
                    store_spectrum(ready, (place - half) * sub + index * group, value, group, span)
                before = total
        else:
            for place in range(half, -1, -1):
                total = loop(half, lambda k, t, p=place: add_conjugate(t, filt(half + k - p), sig(k)), zero)
                if before is not None:
                    value = turned_sum(total, before, -1)
                    store_spectrum(ready, place * sub + index * group, value, group, span)
                before = total
        return 0

    @pl.when(from_first)
    def _():
        lax.fori_loop(0, sub // group, lambda k, _: products(k, True), 0)

    @pl.when(jnp.logical_not(from_first))
    def _():
        lax.fori_loop(0, sub // group, lambda k, _: products(k, False), 0)

    back[...] = dot(ready[...], inverse_ref[...])
    for step in range(half):
        value = back[rows_at(jnp.bitwise_xor(own, step) * sub, sub), :]
        if arriving:
            value = value + partial[step][...]
        outs[step][...] = value.astype(BF16)


def cross_half(layout, place, tables, filters, filt, signal, partial):
    half, sub, span, parts = layout.half, layout.sub, layout.span, layout.parts
    arriving = partial is not None
    rows = (parts + half) * sub
    main_class = pl.BlockSpec((sub, span), lambda step, place_ref: (channel_block(place_ref, layout, 0, 0), 0))
    return streamed(
        functools.partial(cross_body, arriving),
        layout,
        place,
        (*tables, filters, *filt, *signal, *(partial or ())),
        [fixed(t.shape) for t in tables]
        + [main_class]
        + [fixed((sub, span))] * (parts - 1 + half + (half if arriving else 0)),
        [jax.ShapeDtypeStruct((sub, span), BF16)] * half,
        [fixed((sub, span))] * half,
        [
            pltpu.VMEM((rows, span), BF16),
            pltpu.VMEM((rows, 2 * span), F32),
            pltpu.VMEM((half * sub, 2 * span), BF16),
            pltpu.VMEM((half * sub, span), F32),
        ],
        (1,),
        estimate(2 * rows * span * 2 * span * 3, 10 * half * sub * span * 2),
    )


def first_body(layout, place_ref, qkv_ref, dout_ref, *rest):
    half, sub = layout.half, layout.sub
    returned, completed, crossed = rest[:half], rest[half : 2 * half], rest[2 * half : 3 * half]
    out_ref, grads = rest[3 * half :]
    side, _, _ = where_am_i(place_ref, layout)
    for turn in range(half):
        for other in range(2):
            begin = channel_block(place_ref, layout, turn, other) * sub
            place = pl.ds(pl.multiple_of(begin, sub), sub)
            plain = returned[turn][other].astype(F32)
            if other:
                mixed = returned[turn][2].astype(F32) + crossed[turn][...].astype(F32)
                mixed = mixed.astype(BF16).astype(F32)
            else:
                mixed = completed[turn][...].astype(F32)
            y_out = jnp.where(side == 0, plain, mixed)
            dmixed = jnp.where(side == 0, mixed, plain)
            grads[0, place, :] = dout_ref[place, :].astype(F32) * y_out
            grads[1, place, :] = dmixed * qkv_ref[2, place, :].astype(F32)
            grads[2, place, :] = dmixed * qkv_ref[1, place, :].astype(F32)
    out_ref[...] = jnp.zeros(out_ref.shape, F32)
    for which in range(3):
        out_ref[2 * which : 2 * which + 2, :] = grads[which].T[0:2, :]


def first_grads(layout, place, qkv, dout, returned, completed, crossed):
    half, sub, channels = layout.half, layout.sub, layout.channels
    return streamed(
        first_body,
        layout,
        place,
        (qkv, dout, *returned, *completed, *crossed),
        [fixed((3, channels, 128)), fixed((channels, 128))]
        + [fixed((3, sub, 128))] * half
        + [fixed((sub, 128))] * (2 * half),
        jax.ShapeDtypeStruct((8, channels), F32),
        fixed((8, channels)),
        [pltpu.VMEM((3, channels, 128), F32)],
        (1,),
        estimate(0, 3 * channels * 128 * 2),
    )


def final_body(last, layout, place_ref, qkv_ref, dout_ref, cols_ref, keep_ref, *rest):
    half, rows, span = layout.half, layout.sub, layout.span
    returned, completed, crossed = rest[:half], rest[half : 2 * half], rest[2 * half : 3 * half]
    rest = rest[3 * half :]
    ahead_ref, rest = (rest[0], rest[3:]) if last else (None, rest)
    out_ref, dfeat_ref, edge, moved = rest
    width = 128 if last else span
    written = 128 if last else span - 128
    begin = span - 128 if last else 0
    side, _, _ = where_am_i(place_ref, layout)
    turn, other = pl.program_id(0) // 2, pl.program_id(0) % 2
    base = channel_block(place_ref, layout, turn, other) * rows

    if last:

        @pl.when(pl.program_id(0) == 0)
        def _():
            edge[...] = ahead_ref[...].T

    for k in range(half):

        @pl.when(turn == k)
        def _(k=k):
            moved[side] = returned[k][other]

        @pl.when((turn == k) & (other == 1))
        def _(k=k):
            moved[1 - side] = (returned[k][2].astype(F32) + crossed[k][...].astype(F32)).astype(BF16)

        @pl.when((turn == k) & (other == 0))
        def _(k=k):
            moved[1 - side] = completed[k][...]

    group = min(128, rows)
    lane = lax.broadcasted_iota(jnp.int32, (group, width), 1)
    keep = [keep_ref[j : j + 1, begin : begin + written] for j in (2, 3)]

    def tile(index, _):
        here = pl.ds(pl.multiple_of(index * group, group), group)
        cols = cols_ref[here, :]
        y_out = moved[0, here, :].astype(F32)
        dmixed = moved[1, here, :].astype(F32)
        q_out = qkv_ref[0, here, :].astype(F32) * y_out
        out_ref[here, :] = q_out[:, :written].astype(BF16)
        grads = (
            dout_ref[here, :].astype(F32) * y_out,
            dmixed * qkv_ref[2, here, :].astype(F32),
            dmixed * qkv_ref[1, here, :].astype(F32),
        )
        for which in range(3):
            value = grads[which]
            next_one = pltpu.roll(value, width - 1, 1)
            next_two = pltpu.roll(value, width - 2, 1)
            if last:
                ends = edge[pl.ds(pl.multiple_of(base + index * group, group), group), :]
                first = ends[:, 2 * which : 2 * which + 1]
                second = ends[:, 2 * which + 1 : 2 * which + 2]
                next_one = jnp.where(lane == width - 1, first, next_one)
                next_two = jnp.where(lane == width - 1, second, jnp.where(lane == width - 2, first, next_two))
            total = cols[:, 3 * which : 3 * which + 1] * value[:, :written]
            total = total + cols[:, 3 * which + 1 : 3 * which + 2] * next_one[:, :written] * keep[0]
            total = total + cols[:, 3 * which + 2 : 3 * which + 3] * next_two[:, :written] * keep[1]
            dfeat_ref[which, here, :] = total.astype(BF16)
        return 0

    lax.fori_loop(0, rows // group, tile, 0)


def final(layout, place, qkv, dout, cols, keep, returned, completed, crossed, ahead, earlier):
    half, rows, span, channels = layout.half, layout.sub, layout.span, layout.channels
    last = ahead is not None
    width = 128 if last else span
    written = 128 if last else span - 128
    lanes = span // 128 - 1 if last else 0

    def block(step, place_ref):
        return channel_block(place_ref, layout, step // 2, step % 2)

    def wide(size, index):
        return pl.BlockSpec((3, rows, size), lambda *a: (0, block(*a), index))

    def flat(size, index):
        return pl.BlockSpec((rows, size), lambda *a: (block(*a), index))

    def held(shape):
        return pl.BlockSpec(shape, lambda *a: (0,) * (len(shape) - 1) + (lanes,))

    operands = [qkv, dout, cols, keep, *returned, *completed, *crossed]
    in_specs = (
        [wide(width, lanes), flat(width, lanes), flat(16, 0), fixed(keep.shape)]
        + [held((3, rows, width))] * half
        + [held((rows, width))] * (2 * half)
    )
    aliases = {}
    if last:
        operands += [ahead, *earlier]
        in_specs += [fixed(ahead.shape), ANYWHERE, ANYWHERE]
        aliases = {len(operands) - 1: 0, len(operands): 1}
    return streamed(
        functools.partial(final_body, last),
        layout,
        place,
        operands,
        in_specs,
        [jax.ShapeDtypeStruct((channels, span), BF16), jax.ShapeDtypeStruct((3, channels, span), BF16)],
        [flat(written, lanes), wide(written, lanes)],
        [pltpu.VMEM((channels, 8), F32), pltpu.VMEM((2, rows, width), BF16)],
        (layout.parts,),
        estimate(20 * channels * span, 10 * channels * span),
        aliases,
    )


def swap(value, step, parts, axis="seq"):
    return lax.ppermute(value, axis, [(source, source ^ step) for source in range(parts)])


def around(value, steps, parts):
    return lax.ppermute(value, "seq", [(source, (source + steps) % parts) for source in range(parts)])


def local(features, dout, filters, taps, skip, lengths):
    parts = lax.axis_size("seq")
    _, channels, span = features.shape
    layout = Layout(parts, channels, span)
    half = layout.half
    place = jnp.stack([lax.axis_index("seq"), lax.axis_index("groups")]).astype(jnp.int32)
    tables = [jnp.asarray(t) for t in block_tables(span)]

    halo, filt = pack(layout, place, features, filters)
    halo = around(halo, 1, parts)
    filt = [swap(filt[step - 1], step, parts) for step in range(1, parts)]
    other = swap(jnp.concatenate(filt, axis=0), 1, 2, "groups")
    keep, cols = small(layout, place, lengths, taps, skip)
    qkv, firsts, main_rest = gate(0, layout, place, features, dout, halo, cols, keep, None, None)
    firsts = [firsts[0]] + [swap(firsts[step], step, parts) for step in range(1, half)]
    qkv, cross, seconds = gate(1, layout, place, features, dout, halo, cols, keep, qkv, main_rest)
    seconds = [seconds[0]] + [swap(seconds[step], step, parts) for step in range(1, half)]
    cross = [swap(cross[step], step + half, parts) for step in range(half)]

    sent = cross_half(layout, place, tables, filters, filt, firsts, None)
    crossed = [swap(sent[step], step + half, parts) for step in range(half)]
    returned, later = own_half(layout, place, cols, tables, filters, other, filt, firsts, seconds, sent[0])
    returned = [returned[0]] + [swap(returned[step], step, parts) for step in range(1, half)]
    completed = cross_half(layout, place, tables, filters, filt, cross, later)
    completed = [completed[0]] + [swap(completed[step], step, parts) for step in range(1, half)]

    ahead = around(first_grads(layout, place, qkv, dout, returned, completed, crossed), -1, parts)
    done = final(layout, place, qkv, dout, cols, keep, returned, completed, crossed, None, None)
    return tuple(final(layout, place, qkv, dout, cols, keep, returned, completed, crossed, ahead, done))


def solution(mesh):
    in_specs = (
        P(None, ("chan", "sub"), ("groups", "seq")),
        P(("chan", "sub"), ("groups", "seq")),
        P(("chan", "sub"), "seq"),
        P(None, None, ("chan", "sub")),
        P(("chan", "sub")),
        P("groups"),
    )
    out_specs = (P(("chan", "sub"), ("groups", "seq")), P(None, ("chan", "sub"), ("groups", "seq")))
    return jax.shard_map(local, mesh=mesh, in_specs=in_specs, out_specs=out_specs, check_vma=False)
```

time: 91.1 us -> 94.2 us (1.034)
  starting transfers between devices: 20.4 us -> 24.6 us
  waiting for transfers between devices: 35 us -> 31.4 us
  Pallas kernels: 30.5 us -> 33.8 us
    pallas_call x7 -> x10, Pallas kernels: 29.7 us -> 33.8 us  [streamed(): pl.pallas_call(functools.partial(body, layout), out_shape=outs, grid_spec...]
    ppermute x2, waiting for transfers between devices: 10.1 us -> 6.21 us  [around(): lax.ppermute(value, 'seq', [(source, (source + steps) % parts) for source...]
    ppermute x11 -> x12, starting transfers between devices: 18 us -> 20.5 us  [swap(): lax.ppermute(value, axis, [(source, source ^ step) for source in range(pa...]
    ppermute x2, starting transfers between devices: 2.46 us -> 4.1 us  [around(): lax.ppermute(value, 'seq', [(source, (source + steps) % parts) for source...]
    unnamed x24 -> x20, local copies, waits for them, and re-layouts: 3.97 us -> 3.28 us
    ppermute x11 -> x12, waiting for transfers between devices: 24.9 us -> 25.2 us  [swap(): lax.ppermute(value, axis, [(source, source ^ step) for source in range(pa...]
  transfers between devices with their start and end apart: 13 -> 14, of which waited for: 9 -> 5; matrix products, arithmetic and copies ran while one was open for 0% -> 0% of each run, Pallas kernels for 14% -> 20%
where the time goes in v3:
time: 94.2 us; the launch traced here: 94 us
  Pallas kernels  33.8 us (36%)
  waiting for transfers between devices  31.4 us (33%)
  starting transfers between devices  24.6 us (26%)
  local copies, waits for them, and re-layouts  3.28 us (3%)
    pallas_call x10, Pallas kernels, streamed(): pl.pallas_call(functools.partial(body, layout), out_shape=outs, grid_spec...  33.8 us
    ppermute x12, waiting for transfers between devices, swap(): lax.ppermute(value, axis, [(source, source ^ step) for source in range(pa...  25.2 us
    ppermute x12, starting transfers between devices, swap(): lax.ppermute(value, axis, [(source, source ^ step) for source in range(pa...  20.5 us
    ppermute x2, waiting for transfers between devices, around(): lax.ppermute(value, 'seq', [(source, (source + steps) % parts) for source...  6.21 us
    ppermute x2, starting transfers between devices, around(): lax.ppermute(value, 'seq', [(source, (source + steps) % parts) for source...  4.1 us
    unnamed x20, local copies, waits for them, and re-layouts  3.28 us
  transfers between devices with their start and end apart: 14, of which 5 were waited for; matrix products, arithmetic and copies ran while one was open for 0% of the time, Pallas kernels for 20%

profile of v3, /device:TPU:0, one launch (start us, length us, event | category | flops | bytes accessed | tf_op | source)
XLA Modules:
  0.0 94.0 jit_solution(14199206600618726791)
XLA Ops:
  0.7 0.1 pad_add_fusion.place_ref
  0.7 1.4 %copy-done = bf16[3,1024,256]{2,1,0:T(8,128)(2,1)S(1)} copy-done((bf16[3,1024,256]{2,1,0:T(8,128)(2,1)S(1)}, bf16[3,1024,256]{2,1,0:T(8,128)(2,1)}, u32[]{:S(2)}) %copy-start) | copy-done | bytes 1572888
  2.1 1.0 %copy-done.3 = bf16[1024,256]{1,0:T(8,128)(2,1)S(1)} copy-done((bf16[1024,256]{1,0:T(8,128)(2,1)S(1)}, bf16[1024,256]{1,0:T(8,128)(2,1)}, u32[]{:S(2)}) %copy-start.3) | copy-done | bytes 524312
  3.2 1.5 %shard_map.95 = (bf16[16,1024]{1,0:T(8,128)(2,1)S(1)}, bf16[256,256]{1,0:T(8,128)(2,1)S(1)}, bf16[256,256]{1,0:T(8,128)(2,1)S(1)}, bf16[256,256]{1,0:T(8,128)(2,1)S(1)}) custom-call(s32[2]{0:T(128)S(1)} %pad_add_fusion.place_ref, bf16[3,1024,256]{2,1,0:T(8,128)(2,1)S(1)} %copy-done, bf16[1024,256]{1,0:T(8,128)(2,1)S(1)} %copy-done.3), custom_call_target="tpu_custom_call" | custom-call | bytes 786432 | tf_op jit(solution)/shard_map/pallas_call | solution.py:79
  4.7 3.1 %collective-permute-start.1 = (bf16[256,256]{1,0:T(8,128)(2,1)S(1)}, bf16[256,256]{1,0:T(8,128)(2,1)S(1)}, u32[]{:S(2)}, u32[]{:S(2)}) collective-permute-start(bf16[256,256]{1,0:T(8,128)(2,1)S(1)} %get-tuple-element.35), channel_id=1, source_target_pairs={{0,4},{4,0},{8,12},{12,8},{1,5},{5,1},{9,13},{13,9},{2,6},{6,2},{1... | collective-permute-start | bytes 393224 | tf_op jit(solution)/shard_map/ppermute | solution.py:661
  7.8 2.6 %collective-permute-start.2 = (bf16[256,256]{1,0:T(8,128)(2,1)S(1)}, bf16[256,256]{1,0:T(8,128)(2,1)S(1)}, u32[]{:S(2)}, u32[]{:S(2)}) collective-permute-start(bf16[256,256]{1,0:T(8,128)(2,1)S(1)} %get-tuple-element.36), channel_id=1, source_target_pairs={{0,8},{4,12},{8,0},{12,4},{1,9},{5,13},{9,1},{13,5},{2,10},{6,14},... | collective-permute-start | bytes 393224 | tf_op jit(solution)/shard_map/ppermute | solution.py:661
  10.4 0.9 collective-permute-start
  11.3 0.8 copy-done.5
  12.1 1.6 %shard_map.96 = (f32[8,256]{1,0:T(8,128)S(1)}, f32[1024,16]{1,0:T(8,128)S(1)}) custom-call(s32[2]{0:T(128)S(1)} %pad_add_fusion.place_ref, s32[16]{0:T(128)S(1)} %copy-done.7, f32[3,3,1024]{2,1,0:T(4,128)S(1)} %copy-done.5, f32[1,1024]{1,0:T(1,128)S(1)} %bitcast.3), custom_call_target="tpu_custom_call" | custom-call | bytes 102400 | tf_op jit(solution)/shard_map/pallas_call | solution.py:79
  13.7 6.2 %collective-permute-done.halo_ref = bf16[16,1024]{1,0:T(8,128)(2,1)S(1)} collective-permute-done((bf16[16,1024]{1,0:T(8,128)(2,1)S(1)}, bf16[16,1024]{1,0:T(8,128)(2,1)S(1)}, u32[]{:S(2)}, u32[]{:S(2)}) %collective-permute-start) | collective-permute-done | bytes 32800 | tf_op jit(solution)/shard_map/ppermute | solution.py:665
  19.9 2.9 %shard_map.97 = (bf16[3,1024,256]{2,1,0:T(8,128)(2,1)S(1)}, bf16[256,256]{1,0:T(8,128)(2,1)S(1)}, bf16[256,256]{1,0:T(8,128)(2,1)S(1)}, bf16[256,256]{1,0:T(8,128)(2,1)S(1)}, bf16[256,256]{1,0:T(8,128)(2,1)S(1)}) custom-call(s32[2]{0:T(128)S(1)} %pad_add_fusion.place_ref, bf16[3,1024,256]{2,1,0:T(8,128)(2,1)S(1)} %copy-done.1, ...), custom_call_target="tpu_custom_call" | custom-call | flops 3932160 | bytes 2359296 | tf_op jit(solution)/shard_map/pallas_call | solution.py:79
  22.9 3.0 %shard_map.98 = (bf16[3,1024,256]{2,1,0:T(8,128)(2,1)S(1)}, bf16[256,256]{1,0:T(8,128)(2,1)S(1)}, bf16[256,256]{1,0:T(8,128)(2,1)S(1)}, bf16[3,256,256]{2,1,0:T(8,128)(2,1)S(1)}, bf16[3,256,256]{2,1,0:T(8,128)(2,1)S(1)}) custom-call(s32[2]{0:T(128)S(1)} %pad_add_fusion.place_ref, ...), custom_call_target="tpu_custom_call", output_to_operand_aliasing={{0}: (8, {})} | custom-call | flops 3932160 | bytes 2359296 | tf_op jit(solution)/shard_map/pallas_call | solution.py:79
  25.8 2.6 %collective-permute-start.6 = (bf16[3,256,256]{2,1,0:T(8,128)(2,1)S(1)}, bf16[3,256,256]{2,1,0:T(8,128)(2,1)S(1)}, u32[]{:S(2)}, u32[]{:S(2)}) collective-permute-start(bf16[3,256,256]{2,1,0:T(8,128)(2,1)S(1)} %get-tuple-element.41), channel_id=1, source_target_pairs={{0,4},{4,0},{8,12},{12,8},{1,5},{5,1},{9,13},{13,9},{2,6},{6,2},{1... | collective-permute-start | bytes 1179656 | tf_op jit(solution)/shard_map/ppermute | solution.py:661
  28.5 1.6 %collective-permute-start.4 = (bf16[768,256]{1,0:T(8,128)(2,1)S(1)}, bf16[768,256]{1,0:T(8,128)(2,1)S(1)}, u32[]{:S(2)}, u32[]{:S(2)}) collective-permute-start(bf16[768,256]{1,0:T(8,128)(2,1)S(1)} %pad_maximum_fusion), channel_id=1, source_target_pairs={{0,16},{16,0},{1,17},{17,1},{2,18},{18,2},{3,19},{19,3},{4,20},{20... | collective-permute-start | bytes 1179656 | tf_op jit(solution)/shard_map/ppermute | solution.py:661
  30.1 0.0 collective-permute-start.5
  30.1 9.3 %collective-permute-done.5.rest_4_ = bf16[256,256]{1,0:T(8,128)(2,1)S(1)} collective-permute-done((bf16[256,256]{1,0:T(8,128)(2,1)S(1)}, bf16[256,256]{1,0:T(8,128)(2,1)S(1)}, u32[]{:S(2)}, u32[]{:S(2)}) %collective-permute-start.5) | collective-permute-done | bytes 131104 | tf_op jit(solution)/shard_map/ppermute | solution.py:661
  39.5 2.8 %shard_map.99 = (bf16[256,256]{1,0:T(8,128)(2,1)S(1)}, bf16[256,256]{1,0:T(8,128)(2,1)S(1)}) custom-call(s32[2]{0:T(128)S(1)} %pad_add_fusion.place_ref, bf16[512,512]{1,0:T(8,128)(2,1)S(1)} %copy-done.8, bf16[512,256]{1,0:T(8,128)(2,1)S(1)} %copy-done.9, bf16[1024,256]{1,0:T(8,128)(2,1)S(1)} %copy-done.4, ...), custom_call_target="tpu_custom_call" | custom-call | flops 1207959552 | bytes 2621440 | tf_op jit(solution)/shard_map/pallas_call | solution.py:79
  42.3 5.9 %shard_map.100 = (bf16[3,256,256]{2,1,0:T(8,128)(2,1)S(1)}, bf16[3,256,256]{2,1,0:T(8,128)(2,1)S(1)}, f32[256,256]{1,0:T(8,128)S(1)}, f32[256,256]{1,0:T(8,128)S(1)}) custom-call(s32[2]{0:T(128)S(1)} %pad_add_fusion.place_ref, f32[1024,16]{1,0:T(8,128)S(1)} %get-tuple-element.29.cols_ref, bf16[512,512]{1,0:T(8,128)(2,1)S(1)} %copy-done.8, ...), custom_call_target="tpu_custom_call" | custom-call | flops 2415919104 | bytes 3670016 | tf_op jit(solution)/shard_map/pallas_call | solution.py:79
  48.2 1.8 %collective-permute-start.7 = (bf16[3,256,256]{2,1,0:T(8,128)(2,1)S(1)}, bf16[3,256,256]{2,1,0:T(8,128)(2,1)S(1)}, u32[]{:S(2)}, u32[]{:S(2)}) collective-permute-start(bf16[3,256,256]{2,1,0:T(8,128)(2,1)S(1)} %get-tuple-element.44), channel_id=1, source_target_pairs={{0,4},{4,0},{8,12},{12,8},{1,5},{5,1},{9,13},{13,9},{2,6},{6,2},{1... | collective-permute-start | bytes 1179656 | tf_op jit(solution)/shard_map/ppermute | solution.py:661
  50.1 2.2 %collective-permute-start.8 = (bf16[256,256]{1,0:T(8,128)(2,1)S(1)}, bf16[256,256]{1,0:T(8,128)(2,1)S(1)}, u32[]{:S(2)}, u32[]{:S(2)}) collective-permute-start(bf16[256,256]{1,0:T(8,128)(2,1)S(1)} %get-tuple-element.45), channel_id=1, source_target_pairs={{0,8},{4,12},{8,0},{12,4},{1,9},{5,13},{9,1},{13,5},{2,10},{6,14},... | collective-permute-start | bytes 393224 | tf_op jit(solution)/shard_map/ppermute | solution.py:661
  52.3 1.2 %collective-permute-start.9 = (bf16[256,256]{1,0:T(8,128)(2,1)S(1)}, bf16[256,256]{1,0:T(8,128)(2,1)S(1)}, u32[]{:S(2)}, u32[]{:S(2)}) collective-permute-start(bf16[256,256]{1,0:T(8,128)(2,1)S(1)} %get-tuple-element.46), channel_id=1, source_target_pairs={{0,12},{4,8},{8,4},{12,0},{1,13},{5,9},{9,5},{13,1},{2,14},{6,10},... | collective-permute-start | bytes 393224 | tf_op jit(solution)/shard_map/ppermute | solution.py:661
  53.4 2.0 %collective-permute-start.11 = (bf16[256,256]{1,0:T(8,128)(2,1)S(1)}, bf16[256,256]{1,0:T(8,128)(2,1)S(1)}, u32[]{:S(2)}, u32[]{:S(2)}) collective-permute-start(bf16[256,256]{1,0:T(8,128)(2,1)S(1)} %get-tuple-element.42.rest_7_), channel_id=1, source_target_pairs={{0,8},{4,12},{8,0},{12,4},{1,9},{5,13},{9,1},{13,5},{2,10},{6,14},... | collective-permute-start | bytes 393224 | tf_op jit(solution)/shard_map/ppermute | solution.py:661
  55.5 0.9 collective-permute-start.12
  56.4 6.2 %collective-permute-done.8.rest_3_ = bf16[256,256]{1,0:T(8,128)(2,1)S(1)} collective-permute-done((bf16[256,256]{1,0:T(8,128)(2,1)S(1)}, bf16[256,256]{1,0:T(8,128)(2,1)S(1)}, u32[]{:S(2)}, u32[]{:S(2)}) %collective-permute-start.8) | collective-permute-done | bytes 131104 | tf_op jit(solution)/shard_map/ppermute | solution.py:661
  62.5 6.6 %collective-permute-done.9.rest_4_ = bf16[256,256]{1,0:T(8,128)(2,1)S(1)} collective-permute-done((bf16[256,256]{1,0:T(8,128)(2,1)S(1)}, bf16[256,256]{1,0:T(8,128)(2,1)S(1)}, u32[]{:S(2)}, u32[]{:S(2)}) %collective-permute-start.9) | collective-permute-done | bytes 131104 | tf_op jit(solution)/shard_map/ppermute | solution.py:661
  69.1 2.8 %shard_map.101 = (bf16[256,256]{1,0:T(8,128)(2,1)S(1)}, bf16[256,256]{1,0:T(8,128)(2,1)S(1)}) custom-call(s32[2]{0:T(128)S(1)} %pad_add_fusion.place_ref, bf16[512,512]{1,0:T(8,128)(2,1)S(1)} %copy-done.8, bf16[512,256]{1,0:T(8,128)(2,1)S(1)} %copy-done.9, bf16[1024,256]{1,0:T(8,128)(2,1)S(1)} %copy-done.4, ...), custom_call_target="tpu_custom_call" | custom-call | flops 1207959552 | bytes 2621440 | tf_op jit(solution)/shard_map/pallas_call | solution.py:79
  71.9 2.5 %collective-permute-start.10 = (bf16[256,256]{1,0:T(8,128)(2,1)S(1)}, bf16[256,256]{1,0:T(8,128)(2,1)S(1)}, u32[]{:S(2)}, u32[]{:S(2)}) collective-permute-start(bf16[256,256]{1,0:T(8,128)(2,1)S(1)} %get-tuple-element.50), channel_id=1, source_target_pairs={{0,4},{4,0},{8,12},{12,8},{1,5},{5,1},{9,13},{13,9},{2,6},{6,2},{1... | collective-permute-start | bytes 393224 | tf_op jit(solution)/shard_map/ppermute | solution.py:661
  74.4 3.2 %collective-permute-done.10.rest_3_ = bf16[256,256]{1,0:T(8,128)(2,1)S(1)} collective-permute-done((bf16[256,256]{1,0:T(8,128)(2,1)S(1)}, bf16[256,256]{1,0:T(8,128)(2,1)S(1)}, u32[]{:S(2)}, u32[]{:S(2)}) %collective-permute-start.10) | collective-permute-done | bytes 131104 | tf_op jit(solution)/shard_map/ppermute | solution.py:661
  77.6 1.5 %shard_map.102 = f32[8,1024]{1,0:T(8,128)S(1)} custom-call(s32[2]{0:T(128)S(1)} %pad_add_fusion.place_ref, bf16[3,1024,256]{2,1,0:T(8,128)(2,1)S(1)} %get-tuple-element.34.qkv_ref, bf16[1024,256]{1,0:T(8,128)(2,1)S(1)} %copy-done.2, bf16[3,256,256]{2,1,0:T(8,128)(2,1)S(1)} %get-tuple-element.43.rest_0_, ...), custom_call_target="tpu_custom_call" | custom-call | bytes 786432 | tf_op jit(solution)/shard_map/pallas_call | solution.py:79
  79.1 3.2 %collective-permute-start.13 = (f32[8,1024]{1,0:T(8,128)S(1)}, f32[8,1024]{1,0:T(8,128)S(1)}, u32[]{:S(2)}, u32[]{:S(2)}) collective-permute-start(f32[8,1024]{1,0:T(8,128)S(1)} %shard_map.102), channel_id=1, source_target_pairs={{0,12},{4,0},{8,4},{12,8},{1,13},{5,1},{9,5},{13,9},{2,14},{6,2},{... | collective-permute-start | bytes 98312 | tf_op jit(solution)/shard_map/ppermute | solution.py:665
  82.3 5.6 %shard_map.103 = (bf16[1024,256]{1,0:T(8,128)(2,1)}, bf16[3,1024,256]{2,1,0:T(8,128)(2,1)}) custom-call(s32[2]{0:T(128)S(1)} %pad_add_fusion.place_ref, bf16[3,1024,256]{2,1,0:T(8,128)(2,1)S(1)} %get-tuple-element.34.qkv_ref, bf16[1024,256]{1,0:T(8,128)(2,1)S(1)} %copy-done.2, f32[1024,16]{1,0:T(8,128)S(1)} %get-tuple-element.29.cols_ref, ...), custom_call_target="tpu_custom_call" | custom-call | flops 5242880 | bytes 2621440 | tf_op jit(solution)/shard_map/pallas_call | solution.py:79
  87.9 6.1 %shard_map.104 = (bf16[1024,256]{1,0:T(8,128)(2,1)}, bf16[3,1024,256]{2,1,0:T(8,128)(2,1)}) custom-call(s32[2]{0:T(128)S(1)} %pad_add_fusion.place_ref, bf16[3,1024,256]{2,1,0:T(8,128)(2,1)S(1)} %get-tuple-element.34.qkv_ref, bf16[1024,256]{1,0:T(8,128)(2,1)S(1)} %copy-done.2, ...), custom_call_target="tpu_custom_call", output_to_operand_aliasing={{0}: (12, {}), {1}: (13, {})} | custom-call | flops 5242880 | bytes 2621440 | tf_op jit(solution)/shard_map/pallas_call | solution.py:79
  (28 shorter events, 0.1 us)
Async XLA Ops:
  0.6 10.7 %copy-start.7 = (s32[16]{0:T(128)S(1)}, s32[16]{0:T(128)}, u32[]{:S(2)}) copy-start(s32[16]{0:T(128)} %lengths_ref.1) | copy-start | bytes 196
  0.6 10.7 %copy-start.6 = (f32[1024]{0:T(1024)S(1)}, f32[1024]{0:T(1024)}, u32[]{:S(2)}) copy-start(f32[1024]{0:T(1024)} %param.12) | copy-start | bytes 12292
  0.7 1.4 %copy-start = (bf16[3,1024,256]{2,1,0:T(8,128)(2,1)S(1)}, bf16[3,1024,256]{2,1,0:T(8,128)(2,1)}, u32[]{:S(2)}) copy-start(bf16[3,1024,256]{2,1,0:T(8,128)(2,1)} %feat_ref.5) | copy-start | bytes 4718596
  2.1 1.0 %copy-start.3 = (bf16[1024,256]{1,0:T(8,128)(2,1)S(1)}, bf16[1024,256]{1,0:T(8,128)(2,1)}, u32[]{:S(2)}) copy-start(bf16[1024,256]{1,0:T(8,128)(2,1)} %filt_ref.7) | copy-start | bytes 1572868
  3.2 16.7 %copy-start.1 = (bf16[3,1024,256]{2,1,0:T(8,128)(2,1)S(1)}, bf16[3,1024,256]{2,1,0:T(8,128)(2,1)}, u32[]{:S(2)}) copy-start(bf16[3,1024,256]{2,1,0:T(8,128)(2,1)} %feat_ref.5) | copy-start | bytes 4718596
  3.2 16.7 %copy-start.2 = (bf16[1024,256]{1,0:T(8,128)(2,1)S(1)}, bf16[1024,256]{1,0:T(8,128)(2,1)}, u32[]{:S(2)}) copy-start(bf16[1024,256]{1,0:T(8,128)(2,1)} %dout_ref.9) | copy-start | bytes 1572868
  4.7 23.8 %collective-permute-start.1 = (bf16[256,256]{1,0:T(8,128)(2,1)S(1)}, bf16[256,256]{1,0:T(8,128)(2,1)S(1)}, u32[]{:S(2)}, u32[]{:S(2)}) collective-permute-start(bf16[256,256]{1,0:T(8,128)(2,1)S(1)} %get-tuple-element.35), channel_id=1, source_target_pairs={{0,4},{4,0},{8,12},{12,8},{1,5},{5,1},{9,13},{13,9},{2,6},{6,2},{1... | collective-permute-start | bytes 393224 | tf_op jit(solution)/shard_map/ppermute | solution.py:661
  7.8 20.7 %collective-permute-start.2 = (bf16[256,256]{1,0:T(8,128)(2,1)S(1)}, bf16[256,256]{1,0:T(8,128)(2,1)S(1)}, u32[]{:S(2)}, u32[]{:S(2)}) collective-permute-start(bf16[256,256]{1,0:T(8,128)(2,1)S(1)} %get-tuple-element.36), channel_id=1, source_target_pairs={{0,8},{4,12},{8,0},{12,4},{1,9},{5,13},{9,1},{13,5},{2,10},{6,14},... | collective-permute-start | bytes 393224 | tf_op jit(solution)/shard_map/ppermute | solution.py:661
  10.4 18.1 %collective-permute-start.3 = (bf16[256,256]{1,0:T(8,128)(2,1)S(1)}, bf16[256,256]{1,0:T(8,128)(2,1)S(1)}, u32[]{:S(2)}, u32[]{:S(2)}) collective-permute-start(bf16[256,256]{1,0:T(8,128)(2,1)S(1)} %get-tuple-element.37), channel_id=1, source_target_pairs={{0,12},{4,8},{8,4},{12,0},{1,13},{5,9},{9,5},{13,1},{2,14},{6,10},... | collective-permute-start | bytes 393224 | tf_op jit(solution)/shard_map/ppermute | solution.py:661
  10.4 9.5 %collective-permute-start = (bf16[16,1024]{1,0:T(8,128)(2,1)S(1)}, bf16[16,1024]{1,0:T(8,128)(2,1)S(1)}, u32[]{:S(2)}, u32[]{:S(2)}) collective-permute-start(bf16[16,1024]{1,0:T(8,128)(2,1)S(1)} %get-tuple-element.28), channel_id=1, source_target_pairs={{0,4},{4,8},{8,12},{12,0},{1,5},{5,9},{9,13},{13,1},{2,6},{6,10},{... | collective-permute-start | bytes 98312 | tf_op jit(solution)/shard_map/ppermute | solution.py:665
  11.3 0.8 copy-start.5
  22.8 16.6 %copy-start.4 = (bf16[1024,256]{1,0:T(8,128)(2,1)S(1)}, bf16[1024,256]{1,0:T(8,128)(2,1)}, u32[]{:S(2)}) copy-start(bf16[1024,256]{1,0:T(8,128)(2,1)} %filt_ref.7) | copy-start | bytes 1572868
  22.8 16.6 %copy-start.8 = (bf16[512,512]{1,0:T(8,128)(2,1)S(1)}, bf16[512,512]{1,0:T(8,128)(2,1)}, u32[]{:S(2)}) copy-start(bf16[512,512]{1,0:T(8,128)(2,1)} %constant.15.clone.forward_ref) | copy-start | bytes 1572868
  22.9 16.6 %copy-start.9 = (bf16[512,256]{1,0:T(8,128)(2,1)S(1)}, bf16[512,256]{1,0:T(8,128)(2,1)}, u32[]{:S(2)}) copy-start(bf16[512,256]{1,0:T(8,128)(2,1)} %constant.16.clone.inverse_ref) | copy-start | bytes 786436
  25.8 16.4 %collective-permute-start.6 = (bf16[3,256,256]{2,1,0:T(8,128)(2,1)S(1)}, bf16[3,256,256]{2,1,0:T(8,128)(2,1)S(1)}, u32[]{:S(2)}, u32[]{:S(2)}) collective-permute-start(bf16[3,256,256]{2,1,0:T(8,128)(2,1)S(1)} %get-tuple-element.41), channel_id=1, source_target_pairs={{0,4},{4,0},{8,12},{12,8},{1,5},{5,1},{9,13},{13,9},{2,6},{6,2},{1... | collective-permute-start | bytes 1179656 | tf_op jit(solution)/shard_map/ppermute | solution.py:661
  28.5 13.8 %collective-permute-start.4 = (bf16[768,256]{1,0:T(8,128)(2,1)S(1)}, bf16[768,256]{1,0:T(8,128)(2,1)S(1)}, u32[]{:S(2)}, u32[]{:S(2)}) collective-permute-start(bf16[768,256]{1,0:T(8,128)(2,1)S(1)} %pad_maximum_fusion), channel_id=1, source_target_pairs={{0,16},{16,0},{1,17},{17,1},{2,18},{18,2},{3,19},{19,3},{4,20},{20... | collective-permute-start | bytes 1179656 | tf_op jit(solution)/shard_map/ppermute | solution.py:661
  30.1 9.3 %collective-permute-start.5 = (bf16[256,256]{1,0:T(8,128)(2,1)S(1)}, bf16[256,256]{1,0:T(8,128)(2,1)S(1)}, u32[]{:S(2)}, u32[]{:S(2)}) collective-permute-start(bf16[256,256]{1,0:T(8,128)(2,1)S(1)} %get-tuple-element.39), channel_id=1, source_target_pairs={{0,4},{4,0},{8,12},{12,8},{1,5},{5,1},{9,13},{13,9},{2,6},{6,2},{1... | collective-permute-start | bytes 393224 | tf_op jit(solution)/shard_map/ppermute | solution.py:661
  48.2 29.3 %collective-permute-start.7 = (bf16[3,256,256]{2,1,0:T(8,128)(2,1)S(1)}, bf16[3,256,256]{2,1,0:T(8,128)(2,1)S(1)}, u32[]{:S(2)}, u32[]{:S(2)}) collective-permute-start(bf16[3,256,256]{2,1,0:T(8,128)(2,1)S(1)} %get-tuple-element.44), channel_id=1, source_target_pairs={{0,4},{4,0},{8,12},{12,8},{1,5},{5,1},{9,13},{13,9},{2,6},{6,2},{1... | collective-permute-start | bytes 1179656 | tf_op jit(solution)/shard_map/ppermute | solution.py:661
  50.1 12.4 %collective-permute-start.8 = (bf16[256,256]{1,0:T(8,128)(2,1)S(1)}, bf16[256,256]{1,0:T(8,128)(2,1)S(1)}, u32[]{:S(2)}, u32[]{:S(2)}) collective-permute-start(bf16[256,256]{1,0:T(8,128)(2,1)S(1)} %get-tuple-element.45), channel_id=1, source_target_pairs={{0,8},{4,12},{8,0},{12,4},{1,9},{5,13},{9,1},{13,5},{2,10},{6,14},... | collective-permute-start | bytes 393224 | tf_op jit(solution)/shard_map/ppermute | solution.py:661
  52.3 16.8 %collective-permute-start.9 = (bf16[256,256]{1,0:T(8,128)(2,1)S(1)}, bf16[256,256]{1,0:T(8,128)(2,1)S(1)}, u32[]{:S(2)}, u32[]{:S(2)}) collective-permute-start(bf16[256,256]{1,0:T(8,128)(2,1)S(1)} %get-tuple-element.46), channel_id=1, source_target_pairs={{0,12},{4,8},{8,4},{12,0},{1,13},{5,9},{9,5},{13,1},{2,14},{6,10},... | collective-permute-start | bytes 393224 | tf_op jit(solution)/shard_map/ppermute | solution.py:661
  53.4 21.0 %collective-permute-start.11 = (bf16[256,256]{1,0:T(8,128)(2,1)S(1)}, bf16[256,256]{1,0:T(8,128)(2,1)S(1)}, u32[]{:S(2)}, u32[]{:S(2)}) collective-permute-start(bf16[256,256]{1,0:T(8,128)(2,1)S(1)} %get-tuple-element.42.rest_7_), channel_id=1, source_target_pairs={{0,8},{4,12},{8,0},{12,4},{1,9},{5,13},{9,1},{13,5},{2,10},{6,14},... | collective-permute-start | bytes 393224 | tf_op jit(solution)/shard_map/ppermute | solution.py:661
  55.5 19.0 %collective-permute-start.12 = (bf16[256,256]{1,0:T(8,128)(2,1)S(1)}, bf16[256,256]{1,0:T(8,128)(2,1)S(1)}, u32[]{:S(2)}, u32[]{:S(2)}) collective-permute-start(bf16[256,256]{1,0:T(8,128)(2,1)S(1)} %get-tuple-element.51), channel_id=1, source_target_pairs={{0,12},{4,8},{8,4},{12,0},{1,13},{5,9},{9,5},{13,1},{2,14},{6,10},... | collective-permute-start | bytes 393224 | tf_op jit(solution)/shard_map/ppermute | solution.py:661
  71.9 5.6 %collective-permute-start.10 = (bf16[256,256]{1,0:T(8,128)(2,1)S(1)}, bf16[256,256]{1,0:T(8,128)(2,1)S(1)}, u32[]{:S(2)}, u32[]{:S(2)}) collective-permute-start(bf16[256,256]{1,0:T(8,128)(2,1)S(1)} %get-tuple-element.50), channel_id=1, source_target_pairs={{0,4},{4,0},{8,12},{12,8},{1,5},{5,1},{9,13},{13,9},{2,6},{6,2},{1... | collective-permute-start | bytes 393224 | tf_op jit(solution)/shard_map/ppermute | solution.py:661
  79.1 8.8 %collective-permute-start.13 = (f32[8,1024]{1,0:T(8,128)S(1)}, f32[8,1024]{1,0:T(8,128)S(1)}, u32[]{:S(2)}, u32[]{:S(2)}) collective-permute-start(f32[8,1024]{1,0:T(8,128)S(1)} %shard_map.102), channel_id=1, source_target_pairs={{0,12},{4,0},{8,4},{12,8},{1,13},{5,1},{9,5},{13,9},{2,14},{6,2},{... | collective-permute-start | bytes 98312 | tf_op jit(solution)/shard_map/ppermute | solution.py:665

commit v4 on v3

--- a/solution.py
+++ b/solution.py
@@ -36,7 +36,7 @@
 
 
 def estimate(flops, moved):
-    return pl.CostEstimate(flops=int(flops), bytes_accessed=int(moved), transcendentals=0)
+    return pl.CostEstimate(flops=int(flops) * 16, bytes_accessed=int(moved) * 16, transcendentals=0)
 
 
 def offsets_row(lengths_ref, first, span, ahead):
@@ -92,82 +92,156 @@
     )(place, *operands)
 
 
-def pack_body(layout, place_ref, feat_ref, filt_ref, halo_ref, *rest):
-    filt_out, (tail, turned, sems) = rest[: layout.parts - 1], rest[layout.parts - 1 :]
-    span, half, sub = layout.span, layout.half, layout.sub
-    copies = [pltpu.make_async_copy(feat_ref.at[:, :, span - 128 : span], tail, sems.at[0])]
+def halo_body(layout, place_ref, feat_ref, halo_ref, tail, turned, sem):
+    copy = pltpu.make_async_copy(feat_ref.at[:, :, layout.span - 128 : layout.span], tail, sem)
+    copy.start()
+    turned[...] = jnp.zeros(turned.shape, F32)
+    copy.wait()
+    for which in range(3):
+        turned[2 * which : 2 * which + 2, :] = tail[which].astype(F32).T[-2:, :]
+    halo_ref[...] = turned[...].astype(BF16)
+
+
+def pack_halo(layout, place, features):
+    channels = layout.channels
+    return streamed(
+        halo_body,
+        layout,
+        place,
+        (features,),
+        [IN_HBM],
+        jax.ShapeDtypeStruct((16, channels), BF16),
+        fixed((16, channels)),
+        [pltpu.VMEM((3, channels, 128), BF16), pltpu.VMEM((16, channels), F32), pltpu.SemaphoreType.DMA],
+        (1,),
+        estimate(0, 3 * channels * 128),
+    )
+
+
+def pack_body(layout, place_ref, filt_ref, after_ref, *rest):
+    filt_out, sems = rest[: layout.parts - 1], rest[layout.parts - 1]
+    half, sub = layout.half, layout.sub
+    copies = []
     for step in range(1, layout.parts):
         begin = channel_block(place_ref, layout, step % half, step // half) * sub
         source = filt_ref.at[pl.ds(pl.multiple_of(begin, sub), sub), :]
-        copies.append(pltpu.make_async_copy(source, filt_out[step - 1], sems.at[step]))
+        copies.append(pltpu.make_async_copy(source, filt_out[step - 1], sems.at[step - 1]))
     for copy in copies:
         copy.start()
-    turned[...] = jnp.zeros(turned.shape, F32)
-    copies[0].wait()
-    for which in range(3):
-        turned[2 * which : 2 * which + 2, :] = tail[which].astype(F32).T[-2:, :]
-    halo_ref[...] = turned[...].astype(BF16)
-    for copy in copies[1:]:
+    for copy in copies:
         copy.wait()
 
 
-def pack(layout, place, features, filters):
-    channels, span, parts = layout.channels, layout.span, layout.parts
-    shapes = [(16, channels)] + [(layout.sub, span)] * (parts - 1)
-    found = streamed(
+def pack_filters(layout, place, filters, after):
+    parts = layout.parts
+    shape = (layout.sub, layout.span)
+    return streamed(
         pack_body,
         layout,
         place,
-        (features, filters),
-        [IN_HBM, IN_HBM],
-        [jax.ShapeDtypeStruct(s, BF16) for s in shapes],
-        [fixed(s) for s in shapes],
-        [
-            pltpu.VMEM((3, channels, 128), BF16),
-            pltpu.VMEM((16, channels), F32),
-            pltpu.SemaphoreType.DMA((parts,)),
-        ],
+        (filters, after),
+        [IN_HBM, ANYWHERE],
+        [jax.ShapeDtypeStruct(shape, BF16)] * (parts - 1),
+        [fixed(shape)] * (parts - 1),
+        [pltpu.SemaphoreType.DMA((parts - 1,))],
         (1,),
-        estimate(0, 3 * channels * span),
-    )
-    return found[0], found[1:]
-
-
-def small_body(layout, place_ref, lengths_ref, taps_ref, skip_ref, keep_ref, cols_ref, turned):
+        estimate(0, parts * layout.sub * layout.span),
+    )
+
+
+def lane_table(channel_columns):
+    table = np.zeros((3, channel_columns, 9, 128), np.float32)
+    for column in range(9):
+        table[:, column, column, :] = 1.0
+    return table.reshape(3 * channel_columns, 9 * 128).astype(BF16)
+
+
+def three_parts(value):
+    top = value.astype(BF16).astype(F32)
+    middle = (value - top).astype(BF16).astype(F32)
+    return [top, middle, value - top - middle]
+
+
+def shift_table(rows, first_row, lanes, first_lane, back, keep):
+    row = lax.broadcasted_iota(jnp.int32, (rows, lanes), 0) + first_row
+    lane = lax.broadcasted_iota(jnp.int32, (rows, lanes), 1) + first_lane
+    return jnp.where(row == lane - back, keep, 0.0).astype(BF16)
+
+
+def edge_table(table_rows, lanes, entries):
+    row = lax.broadcasted_iota(jnp.int32, (table_rows, lanes), 0)
+    lane = lax.broadcasted_iota(jnp.int32, (table_rows, lanes), 1)
+    table = jnp.zeros((table_rows, lanes), F32)
+    for rows, where, keep in entries:
+        for own_row in rows:
+            table = jnp.where((row == own_row) & (lane == where), keep, table)
+    return table.astype(BF16)
+
+
+def small_body(layout, place_ref, lengths_ref, taps_ref, skip_ref, cols_ref, split_ref, fwd_ref, fwd_edge_ref, most_ref, last_ref, last_edge_ref, turned):
     span = layout.span
     first = place_ref[0] * span
-    keep_ref[...] = jnp.zeros(keep_ref.shape, F32)
     _, offset = offsets_row(lengths_ref, first, span, 0)
+    keep, keep_back = [], []
     for j in (1, 2):
-        keep_ref[j - 1 : j, :] = (offset[0:1, :] >= j).astype(F32)
+        keep.append((offset[0:1, :] >= j).astype(F32))
         position, later = offsets_row(lengths_ref, first, span, j)
         inside = (position < layout.parts * span) & (later >= j)
-        keep_ref[1 + j : 2 + j, :] = inside[0:1, :].astype(F32)
+        keep_back.append(inside[0:1, :].astype(F32))
+    most = span - 128
+    for j in (0, 1):
+        fwd_ref[:, j * span : (j + 1) * span] = shift_table(span, 0, span, 0, j + 1, keep[j])
+        most_ref[:, j * most : (j + 1) * most] = shift_table(span, 0, most, 0, -j - 1, keep_back[j][:, :most])
+        last_ref[:, j * 128 : (j + 1) * 128] = shift_table(128, most, 128, most, -j - 1, keep_back[j][:, most:])
+    for which in range(3):
+        begin = which * 256
+        two, one = [2 * which], [2 * which + 1]
+        fwd_edge_ref[:, begin : begin + 128] = edge_table(16, 128, [(one, 0, keep[0][:, :128])])
+        fwd_edge_ref[:, begin + 128 : begin + 256] = edge_table(
+            16, 128, [(two, 0, keep[1][:, :128]), (one, 1, keep[1][:, :128])]
+        )
+        near = [2 * which + 8 * k for k in range(3)]
+        far = [2 * which + 1 + 8 * k for k in range(3)]
+        last_edge_ref[:, begin : begin + 128] = edge_table(32, 128, [(near, 127, keep_back[0][:, most:])])
+        last_edge_ref[:, begin + 128 : begin + 256] = edge_table(
+            32, 128, [(far, 127, keep_back[1][:, most:]), (near, 126, keep_back[1][:, most:])]
+        )
     turned[...] = jnp.zeros(turned.shape, F32)
     for which in range(3):
         turned[3 * which : 3 * which + 3, :] = taps_ref[which]
     turned[9:10, :] = skip_ref[...]
-    cols_ref[...] = turned[...].T
+    value = turned[...]
+    cols_ref[...] = value.T
+    split_ref[...] = jnp.concatenate(three_parts(value), axis=0).T.astype(BF16)
 
 
 def small(layout, place, lengths, taps, skip):
-    channels = layout.channels
-    shapes = [(8, layout.span), (channels, 16)]
+    channels, span = layout.channels, layout.span
+    most = span - 128
+    shapes = [
+        ((channels, 16), F32),
+        ((channels, 48), BF16),
+        ((span, 2 * span), BF16),
+        ((16, 768), BF16),
+        ((span, 2 * most), BF16),
+        ((128, 256), BF16),
+        ((32, 768), BF16),
+    ]
     return streamed(
         small_body,
         layout,
         place,
         (lengths, taps, skip.reshape(1, channels)),
         [SCALARS, fixed(taps.shape), fixed((1, channels))],
-        [jax.ShapeDtypeStruct(s, F32) for s in shapes],
-        [fixed(s) for s in shapes],
+        [jax.ShapeDtypeStruct(*s) for s in shapes],
+        [fixed(s[0]) for s in shapes],
         [pltpu.VMEM((16, channels), F32)],
         (1,),
         estimate(0, 100 * channels),
     )
 
 
-def gate_body(other, layout, place_ref, feat_ref, dout_ref, halo_ref, cols_ref, keep_ref, *rest):
+def gate_body(other, layout, place_ref, feat_ref, dout_ref, halo_ref, split_ref, lanes_ref, shift_ref, shift_edge_ref, *rest):
     half, rows, span = layout.half, layout.sub, layout.span
     if other:
         main_rest, rest = rest[:half], rest[half + 1 :]
@@ -181,26 +255,25 @@
 
     @pl.when(turn == 0)
     def _():
-        edge[...] = halo_ref[...].astype(F32).T
-
-    keep = keep_ref[0:1, :], keep_ref[1:2, :]
-    lane = lax.broadcasted_iota(jnp.int32, (group, span), 1)
+        edge[...] = halo_ref[...].astype(F32).T.astype(BF16)
 
     def tile(index, _):
         here = pl.ds(pl.multiple_of(index * group, group), group)
-        cols = cols_ref[here, :]
-        ends = edge[pl.ds(pl.multiple_of(base + index * group, group), group), :]
+        spread = dot(split_ref[here, :], lanes_ref[...])
+        ends = dot(edge[pl.ds(pl.multiple_of(base + index * group, group), group), :], shift_edge_ref[...])
         filtered = []
         for which in range(3):
-            value = feat_ref[which, here, :].astype(F32)
-            two_back = ends[:, 2 * which : 2 * which + 1]
-            one_back = ends[:, 2 * which + 1 : 2 * which + 2]
-            back = jnp.where(lane == 0, one_back, pltpu.roll(value, 1, 1))
-            twice = jnp.where(lane == 0, two_back, jnp.where(lane == 1, one_back, pltpu.roll(value, 2, 1)))
-            total = cols[:, 3 * which : 3 * which + 1] * value
-            total = total + cols[:, 3 * which + 1 : 3 * which + 2] * back * keep[0]
-            total = total + cols[:, 3 * which + 2 : 3 * which + 3] * twice * keep[1]
-            rounded = total.astype(BF16)
+            value = feat_ref[which, here, :]
+            moved = dot(value, shift_ref[...])
+            parts = []
+            for lane in range(0, span, 128):
+                taps = [spread[:, (3 * which + j) * 128 : (3 * which + j + 1) * 128] for j in range(3)]
+                back = [moved[:, j * span + lane : j * span + lane + 128] for j in range(2)]
+                if lane == 0:
+                    back = [back[j] + ends[:, which * 256 + j * 128 : which * 256 + j * 128 + 128] for j in range(2)]
+                total = taps[0] * value[:, lane : lane + 128].astype(F32)
+                parts.append((total + taps[1] * back[0] + taps[2] * back[1]).astype(BF16))
+            rounded = jnp.concatenate(parts, axis=1)
             qkv_ref[which, here, :] = rounded
             filtered.append(rounded.astype(F32))
         made[0, here, :] = (filtered[1] * filtered[2]).astype(BF16)
@@ -221,7 +294,7 @@
                 seconds[k][...] = made[1 - side]
 
 
-def gate(other, layout, place, features, dout, halo, cols, keep, qkv, main_rest):
+def gate(other, layout, place, features, dout, halo, split, lanes, shift, shift_edge, qkv, main_rest):
     half, rows, span, channels = layout.half, layout.sub, layout.span, layout.channels
 
     def block(turn, place_ref):
@@ -229,10 +302,10 @@
 
     wide = pl.BlockSpec((3, rows, span), lambda *a: (0, block(*a), 0))
     flat = pl.BlockSpec((rows, span), lambda *a: (block(*a), 0))
-    columns = pl.BlockSpec((rows, 16), lambda *a: (block(*a), 0))
+    columns = pl.BlockSpec((rows, 48), lambda *a: (block(*a), 0))
     shapes = [(rows, span)] * half + [(3, rows, span) if other else (rows, span)] * half
-    operands = [features, dout, halo, cols, keep]
-    in_specs = [wide, flat, fixed(halo.shape), columns, fixed(keep.shape)]
+    operands = [features, dout, halo, split, lanes, shift, shift_edge]
+    in_specs = [wide, flat, fixed(halo.shape), columns] + [fixed(t.shape) for t in (lanes, shift, shift_edge)]
     if other:
         operands += [*main_rest, qkv]
         in_specs += [fixed((rows, span))] * half + [ANYWHERE]
@@ -244,7 +317,7 @@
         in_specs,
         [jax.ShapeDtypeStruct(features.shape, BF16)] + [jax.ShapeDtypeStruct(s, BF16) for s in shapes],
         [wide] + [fixed(s) for s in shapes],
-        [pltpu.VMEM((channels, 16), F32), pltpu.VMEM((2, rows, span), BF16)],
+        [pltpu.VMEM((channels, 16), BF16), pltpu.VMEM((2, rows, span), BF16)],
         (half,),
         estimate(15 * channels * span, 9 * channels * span),
         {len(operands): 0} if other else None,
@@ -544,15 +617,14 @@
     )
 
 
-def final_body(last, layout, place_ref, qkv_ref, dout_ref, cols_ref, keep_ref, *rest):
+def final_body(last, layout, place_ref, qkv_ref, dout_ref, split_ref, lanes_ref, shift_ref, *rest):
     half, rows, span = layout.half, layout.sub, layout.span
     returned, completed, crossed = rest[:half], rest[half : 2 * half], rest[2 * half : 3 * half]
     rest = rest[3 * half :]
-    ahead_ref, rest = (rest[0], rest[3:]) if last else (None, rest)
+    ahead_ref, edge_ref, rest = (rest[0], rest[1], rest[4:]) if last else (None, None, rest)
     out_ref, dfeat_ref, edge, moved = rest
     width = 128 if last else span
     written = 128 if last else span - 128
-    begin = span - 128 if last else 0
     side, _, _ = where_am_i(place_ref, layout)
     turn, other = pl.program_id(0) // 2, pl.program_id(0) % 2
     base = channel_block(place_ref, layout, turn, other) * rows
@@ -561,7 +633,8 @@
 
         @pl.when(pl.program_id(0) == 0)
         def _():
-            edge[...] = ahead_ref[...].T
+            value = ahead_ref[...]
+            edge[...] = jnp.concatenate(three_parts(value) + [jnp.zeros_like(value)], axis=0).T.astype(BF16)
 
     for k in range(half):
 
@@ -578,41 +651,38 @@
             moved[1 - side] = completed[k][...]
 
     group = min(128, rows)
-    lane = lax.broadcasted_iota(jnp.int32, (group, width), 1)
-    keep = [keep_ref[j : j + 1, begin : begin + written] for j in (2, 3)]
 
     def tile(index, _):
         here = pl.ds(pl.multiple_of(index * group, group), group)
-        cols = cols_ref[here, :]
-        y_out = moved[0, here, :].astype(F32)
-        dmixed = moved[1, here, :].astype(F32)
-        q_out = qkv_ref[0, here, :].astype(F32) * y_out
-        out_ref[here, :] = q_out[:, :written].astype(BF16)
-        grads = (
-            dout_ref[here, :].astype(F32) * y_out,
-            dmixed * qkv_ref[2, here, :].astype(F32),
-            dmixed * qkv_ref[1, here, :].astype(F32),
-        )
-        for which in range(3):
-            value = grads[which]
-            next_one = pltpu.roll(value, width - 1, 1)
-            next_two = pltpu.roll(value, width - 2, 1)
-            if last:
-                ends = edge[pl.ds(pl.multiple_of(base + index * group, group), group), :]
-                first = ends[:, 2 * which : 2 * which + 1]
-                second = ends[:, 2 * which + 1 : 2 * which + 2]
-                next_one = jnp.where(lane == width - 1, first, next_one)
-                next_two = jnp.where(lane == width - 1, second, jnp.where(lane == width - 2, first, next_two))
-            total = cols[:, 3 * which : 3 * which + 1] * value[:, :written]
-            total = total + cols[:, 3 * which + 1 : 3 * which + 2] * next_one[:, :written] * keep[0]
-            total = total + cols[:, 3 * which + 2 : 3 * which + 3] * next_two[:, :written] * keep[1]
-            dfeat_ref[which, here, :] = total.astype(BF16)
+        spread = dot(split_ref[here, :], lanes_ref[...])
+        if last:
+            ends = dot(edge[pl.ds(pl.multiple_of(base + index * group, group), group), :], edge_ref[...])
+        arrays = [moved[0, here, :], moved[1, here, :], dout_ref[here, :], qkv_ref[1, here, :], qkv_ref[2, here, :]]
+        ahead = [dot(a, shift_ref[...]) for a in arrays]
+        query = qkv_ref[0, here, :]
+        for lane in range(0, written, 128):
+
+            def three(a):
+                begins = (lane, lane + written)
+                return [arrays[a][:, lane : lane + 128].astype(F32)] + [ahead[a][:, b : b + 128] for b in begins]
+
+            y_out, dmixed, dout_f, key, value = [three(a) for a in range(5)]
+            lanes = slice(lane, lane + 128)
+            out_ref[here, lanes] = (query[:, lanes].astype(F32) * y_out[0]).astype(BF16)
+            for which, pair in enumerate(((dout_f, y_out), (dmixed, value), (dmixed, key))):
+                grads = [pair[0][j] * pair[1][j] for j in range(3)]
+                if last:
+                    for j in (1, 2):
+                        grads[j] = grads[j] + ends[:, which * 256 + (j - 1) * 128 : which * 256 + j * 128]
+                taps = [spread[:, (3 * which + j) * 128 : (3 * which + j + 1) * 128] for j in range(3)]
+                total = taps[0] * grads[0] + taps[1] * grads[1] + taps[2] * grads[2]
+                dfeat_ref[which, here, lanes] = total.astype(BF16)
         return 0
 
     lax.fori_loop(0, rows // group, tile, 0)
 
 
-def final(layout, place, qkv, dout, cols, keep, returned, completed, crossed, ahead, earlier):
+def final(layout, place, qkv, dout, split, lane_sum, shift, returned, completed, crossed, ahead, edge, earlier):
     half, rows, span, channels = layout.half, layout.sub, layout.span, layout.channels
     last = ahead is not None
     width = 128 if last else span
@@ -631,16 +701,16 @@
     def held(shape):
         return pl.BlockSpec(shape, lambda *a: (0,) * (len(shape) - 1) + (lanes,))
 
-    operands = [qkv, dout, cols, keep, *returned, *completed, *crossed]
+    operands = [qkv, dout, split, lane_sum, shift, *returned, *completed, *crossed]
     in_specs = (
-        [wide(width, lanes), flat(width, lanes), flat(16, 0), fixed(keep.shape)]
+        [wide(width, lanes), flat(width, lanes), flat(48, 0), fixed(lane_sum.shape), fixed(shift.shape)]
         + [held((3, rows, width))] * half
         + [held((rows, width))] * (2 * half)
     )
     aliases = {}
     if last:
-        operands += [ahead, *earlier]
-        in_specs += [fixed(ahead.shape), ANYWHERE, ANYWHERE]
+        operands += [ahead, edge, *earlier]
+        in_specs += [fixed(ahead.shape), fixed(edge.shape), ANYWHERE, ANYWHERE]
         aliases = {len(operands) - 1: 0, len(operands): 1}
     return streamed(
         functools.partial(final_body, last),
@@ -650,7 +720,7 @@
         in_specs,
         [jax.ShapeDtypeStruct((channels, span), BF16), jax.ShapeDtypeStruct((3, channels, span), BF16)],
         [flat(written, lanes), wide(written, lanes)],
-        [pltpu.VMEM((channels, 8), F32), pltpu.VMEM((2, rows, width), BF16)],
+        [pltpu.VMEM((channels, 32), BF16), pltpu.VMEM((2, rows, width), BF16)],
         (layout.parts,),
         estimate(20 * channels * span, 10 * channels * span),
         aliases,
@@ -673,14 +743,17 @@
     place = jnp.stack([lax.axis_index("seq"), lax.axis_index("groups")]).astype(jnp.int32)
     tables = [jnp.asarray(t) for t in block_tables(span)]
 
-    halo, filt = pack(layout, place, features, filters)
-    halo = around(halo, 1, parts)
+    lanes = jnp.asarray(lane_table(16))
+
+    halo = around(pack_halo(layout, place, features), 1, parts)
+    filt = pack_filters(layout, place, filters, halo)
     filt = [swap(filt[step - 1], step, parts) for step in range(1, parts)]
     other = swap(jnp.concatenate(filt, axis=0), 1, 2, "groups")
-    keep, cols = small(layout, place, lengths, taps, skip)
-    qkv, firsts, main_rest = gate(0, layout, place, features, dout, halo, cols, keep, None, None)
+    cols, split, shift, shift_edge, most, last, last_edge = small(layout, place, lengths, taps, skip)
+    first_args = (layout, place, features, dout, halo, split, lanes, shift, shift_edge)
+    qkv, firsts, main_rest = gate(0, *first_args, None, None)
     firsts = [firsts[0]] + [swap(firsts[step], step, parts) for step in range(1, half)]
-    qkv, cross, seconds = gate(1, layout, place, features, dout, halo, cols, keep, qkv, main_rest)
+    qkv, cross, seconds = gate(1, *first_args, qkv, main_rest)
     seconds = [seconds[0]] + [swap(seconds[step], step, parts) for step in range(1, half)]
     cross = [swap(cross[step], step + half, parts) for step in range(half)]
 
@@ -692,8 +765,9 @@
     completed = [completed[0]] + [swap(completed[step], step, parts) for step in range(1, half)]
 
     ahead = around(first_grads(layout, place, qkv, dout, returned, completed, crossed), -1, parts)
-    done = final(layout, place, qkv, dout, cols, keep, returned, completed, crossed, None, None)
-    return tuple(final(layout, place, qkv, dout, cols, keep, returned, completed, crossed, ahead, done))
+    done = final(layout, place, qkv, dout, split, lanes, most, returned, completed, crossed, None, None, None)
+    done = final(layout, place, qkv, dout, split, lanes, last, returned, completed, crossed, ahead, last_edge, done)
+    return tuple(done)
 
 
 def solution(mesh):

time: 94.2 us -> 75.7 us (0.80)
  waiting for transfers between devices: 31.4 us -> 19.1 us
  starting transfers between devices: 24.6 us -> 20.2 us
  Pallas kernels: 33.8 us -> 32 us
    ppermute x12, waiting for transfers between devices: 25.2 us -> 15.2 us  [swap(): lax.ppermute(value, axis, [(source, source ^ step) for source in range(pa...]
    ppermute x12, starting transfers between devices: 20.5 us -> 14.8 us  [swap(): lax.ppermute(value, axis, [(source, source ^ step) for source in range(pa...]
    ppermute x2, waiting for transfers between devices: 6.21 us -> 3.92 us  [around(): lax.ppermute(value, 'seq', [(source, (source + steps) % parts) for source...]
    pallas_call x10 -> x11, Pallas kernels: 33.8 us -> 32 us  [streamed(): pl.pallas_call(functools.partial(body, layout), out_shape=outs, grid_spec...]
    ppermute x2, starting transfers between devices: 4.1 us -> 5.41 us  [around(): lax.ppermute(value, 'seq', [(source, (source + steps) % parts) for source...]
    unnamed x20 -> x22, local copies, waits for them, and re-layouts: 3.28 us -> 3.29 us
  transfers between devices with their start and end apart: 14 -> 14, of which waited for: 5 -> 3; matrix products, arithmetic and copies ran while one was open for 0% -> 0% of each run, Pallas kernels for 20% -> 30%
where the time goes in v4:
time: 75.7 us; the launch traced here: 75.5 us
  Pallas kernels  32 us (42%)
  starting transfers between devices  20.2 us (27%)
  waiting for transfers between devices  19.1 us (25%)
  local copies, waits for them, and re-layouts  3.29 us (4%)
  between operations  0.82 us (1%)
    pallas_call x11, Pallas kernels, streamed(): pl.pallas_call(functools.partial(body, layout), out_shape=outs, grid_spec...  32 us
    ppermute x12, waiting for transfers between devices, swap(): lax.ppermute(value, axis, [(source, source ^ step) for source in range(pa...  15.2 us
    ppermute x12, starting transfers between devices, swap(): lax.ppermute(value, axis, [(source, source ^ step) for source in range(pa...  14.8 us
    ppermute x2, starting transfers between devices, around(): lax.ppermute(value, 'seq', [(source, (source + steps) % parts) for source...  5.41 us
    ppermute x2, waiting for transfers between devices, around(): lax.ppermute(value, 'seq', [(source, (source + steps) % parts) for source...  3.92 us
    unnamed x22, local copies, waits for them, and re-layouts  3.29 us
  transfers between devices with their start and end apart: 14, of which 3 were waited for; matrix products, arithmetic and copies ran while one was open for 0% of the time, Pallas kernels for 30%

profile of v4, /device:TPU:0, one launch (start us, length us, event | category | flops | bytes accessed | tf_op | source)
XLA Modules:
  0.0 75.5 jit_solution(10042168160762563760)
XLA Ops:
  0.7 0.1 pad_add_fusion.place_ref
  0.7 1.4 %copy-done = bf16[3,1024,256]{2,1,0:T(8,128)(2,1)S(1)} copy-done((bf16[3,1024,256]{2,1,0:T(8,128)(2,1)S(1)}, bf16[3,1024,256]{2,1,0:T(8,128)(2,1)}, u32[]{:S(2)}) %copy-start) | copy-done | bytes 1572888
  2.1 1.0 %shard_map.104 = bf16[16,1024]{1,0:T(8,128)(2,1)S(1)} custom-call(s32[2]{0:T(128)S(1)} %pad_add_fusion.place_ref, bf16[3,1024,256]{2,1,0:T(8,128)(2,1)S(1)} %copy-done), custom_call_target="tpu_custom_call" | custom-call | bytes 6291456 | tf_op jit(solution)/shard_map/pallas_call | solution.py:79
  3.1 3.1 %collective-permute-start = (bf16[16,1024]{1,0:T(8,128)(2,1)S(1)}, bf16[16,1024]{1,0:T(8,128)(2,1)S(1)}, u32[]{:S(2)}, u32[]{:S(2)}) collective-permute-start(bf16[16,1024]{1,0:T(8,128)(2,1)S(1)} %shard_map.104), channel_id=1, source_target_pairs={{0,4},{4,8},{8,12},{12,0},{1,5},{5,9},{9,13},{13,1},{2,6},{6,10},{... | collective-permute-start | bytes 98312 | tf_op jit(solution)/shard_map/ppermute | solution.py:735
  6.2 3.9 %collective-permute-done.halo_ref.after_ref = bf16[16,1024]{1,0:T(8,128)(2,1)S(1)} collective-permute-done((bf16[16,1024]{1,0:T(8,128)(2,1)S(1)}, bf16[16,1024]{1,0:T(8,128)(2,1)S(1)}, u32[]{:S(2)}, u32[]{:S(2)}) %collective-permute-start) | collective-permute-done | bytes 32800 | tf_op jit(solution)/shard_map/ppermute | solution.py:735
  10.1 1.0 %copy-done.4 = bf16[1024,256]{1,0:T(8,128)(2,1)S(1)} copy-done((bf16[1024,256]{1,0:T(8,128)(2,1)S(1)}, bf16[1024,256]{1,0:T(8,128)(2,1)}, u32[]{:S(2)}) %copy-start.4) | copy-done | bytes 524312
  11.2 1.1 %shard_map.108 = (bf16[256,256]{1,0:T(8,128)(2,1)S(1)}, bf16[256,256]{1,0:T(8,128)(2,1)S(1)}, bf16[256,256]{1,0:T(8,128)(2,1)S(1)}) custom-call(s32[2]{0:T(128)S(1)} %pad_add_fusion.place_ref, bf16[1024,256]{1,0:T(8,128)(2,1)S(1)} %copy-done.4, bf16[16,1024]{1,0:T(8,128)(2,1)S(1)} %collective-permute-done.halo_ref.after_ref), custom_call_target="tpu_custom_call" | custom-call | bytes 4194304 | tf_op jit(solution)/shard_map/pallas_call | solution.py:79
  12.3 0.1 collective-permute-start.1
  12.3 2.6 %collective-permute-start.2 = (bf16[256,256]{1,0:T(8,128)(2,1)S(1)}, bf16[256,256]{1,0:T(8,128)(2,1)S(1)}, u32[]{:S(2)}, u32[]{:S(2)}) collective-permute-start(bf16[256,256]{1,0:T(8,128)(2,1)S(1)} %get-tuple-element.42), channel_id=1, source_target_pairs={{0,8},{4,12},{8,0},{12,4},{1,9},{5,13},{9,1},{13,5},{2,10},{6,14},... | collective-permute-start | bytes 393224 | tf_op jit(solution)/shard_map/ppermute | solution.py:731
  14.9 1.8 %collective-permute-start.3 = (bf16[256,256]{1,0:T(8,128)(2,1)S(1)}, bf16[256,256]{1,0:T(8,128)(2,1)S(1)}, u32[]{:S(2)}, u32[]{:S(2)}) collective-permute-start(bf16[256,256]{1,0:T(8,128)(2,1)S(1)} %get-tuple-element.43), channel_id=1, source_target_pairs={{0,12},{4,8},{8,4},{12,0},{1,13},{5,9},{9,5},{13,1},{2,14},{6,10},... | collective-permute-start | bytes 393224 | tf_op jit(solution)/shard_map/ppermute | solution.py:731
  16.7 0.8 %copy-done.6 = f32[3,3,1024]{2,1,0:T(4,128)S(1)} copy-done((f32[3,3,1024]{2,1,0:T(4,128)S(1)}, f32[3,3,1024]{2,1,0:T(4,128)}, u32[]{:S(2)}) %copy-start.6) | copy-done | bytes 36888
  17.5 1.8 %shard_map.105 = (f32[1024,16]{1,0:T(8,128)S(1)}, bf16[1024,48]{1,0:T(8,128)(2,1)S(1)}, bf16[256,512]{1,0:T(8,128)(2,1)S(1)}, bf16[16,768]{1,0:T(8,128)(2,1)S(1)...) custom-call(s32[2]{0:T(128)S(1)} %pad_add_fusion.place_ref, ...), custom_call_target="tpu_custom_call" | custom-call | bytes 1638400 | tf_op jit(solution)/shard_map/pallas_call | solution.py:79
  19.3 2.5 %shard_map.106 = (bf16[3,1024,256]{2,1,0:T(8,128)(2,1)S(1)}, bf16[256,256]{1,0:T(8,128)(2,1)S(1)}, bf16[256,256]{1,0:T(8,128)(2,1)S(1)}, bf16[256,256]{1,0:T(8,128)(2,1)S(1)}, bf16[256,256]{1,0:T(8,128)(2,1)S(1)}) custom-call(s32[2]{0:T(128)S(1)} %pad_add_fusion.place_ref, bf16[3,1024,256]{2,1,0:T(8,128)(2,1)S(1)} %copy-done.1, ...), custom_call_target="tpu_custom_call" | custom-call | flops 62914560 | bytes 37748736 | tf_op jit(solution)/shard_map/pallas_call | solution.py:79
  21.9 0.1 collective-permute-start.5
  22.0 0.0 copy-start.9
  22.0 0.0 copy-start.10
  22.0 2.6 %shard_map.107 = (bf16[3,1024,256]{2,1,0:T(8,128)(2,1)S(1)}, bf16[256,256]{1,0:T(8,128)(2,1)S(1)}, bf16[256,256]{1,0:T(8,128)(2,1)S(1)}, bf16[3,256,256]{2,1,0:T(8,128)(2,1)S(1)}, bf16[3,256,256]{2,1,0:T(8,128)(2,1)S(1)}) custom-call(s32[2]{0:T(128)S(1)} %pad_add_fusion.place_ref, ...), custom_call_target="tpu_custom_call", output_to_operand_aliasing={{0}: (10, {})} | custom-call | flops 62914560 | bytes 37748736 | tf_op jit(solution)/shard_map/pallas_call | solution.py:79
  24.6 2.6 %collective-permute-start.8 = (bf16[256,256]{1,0:T(8,128)(2,1)S(1)}, bf16[256,256]{1,0:T(8,128)(2,1)S(1)}, u32[]{:S(2)}, u32[]{:S(2)}) collective-permute-start(bf16[256,256]{1,0:T(8,128)(2,1)S(1)} %get-tuple-element.51), channel_id=1, source_target_pairs={{0,8},{4,12},{8,0},{12,4},{1,9},{5,13},{9,1},{13,5},{2,10},{6,14},... | collective-permute-start | bytes 393224 | tf_op jit(solution)/shard_map/ppermute | solution.py:731
  27.2 1.8 %collective-permute-start.9 = (bf16[256,256]{1,0:T(8,128)(2,1)S(1)}, bf16[256,256]{1,0:T(8,128)(2,1)S(1)}, u32[]{:S(2)}, u32[]{:S(2)}) collective-permute-start(bf16[256,256]{1,0:T(8,128)(2,1)S(1)} %get-tuple-element.52), channel_id=1, source_target_pairs={{0,12},{4,8},{8,4},{12,0},{1,13},{5,9},{9,5},{13,1},{2,14},{6,10},... | collective-permute-start | bytes 393224 | tf_op jit(solution)/shard_map/ppermute | solution.py:731
  29.1 1.8 %collective-permute-start.4 = (bf16[768,256]{1,0:T(8,128)(2,1)S(1)}, bf16[768,256]{1,0:T(8,128)(2,1)S(1)}, u32[]{:S(2)}, u32[]{:S(2)}) collective-permute-start(bf16[768,256]{1,0:T(8,128)(2,1)S(1)} %pad_maximum_fusion), channel_id=1, source_target_pairs={{0,16},{16,0},{1,17},{17,1},{2,18},{18,2},{3,19},{19,3},{4,20},{20... | collective-permute-start | bytes 1179656 | tf_op jit(solution)/shard_map/ppermute | solution.py:731
  30.9 2.8 %shard_map.109 = (bf16[256,256]{1,0:T(8,128)(2,1)S(1)}, bf16[256,256]{1,0:T(8,128)(2,1)S(1)}) custom-call(s32[2]{0:T(128)S(1)} %pad_add_fusion.place_ref, bf16[512,512]{1,0:T(8,128)(2,1)S(1)} %copy-done.9, bf16[512,256]{1,0:T(8,128)(2,1)S(1)} %copy-done.10, bf16[1024,256]{1,0:T(8,128)(2,1)S(1)} %copy-done.5, ...), custom_call_target="tpu_custom_call" | custom-call | flops 19327352832 | bytes 41943040 | tf_op jit(solution)/shard_map/pallas_call | solution.py:79
  33.7 1.9 %collective-permute-start.12 = (bf16[256,256]{1,0:T(8,128)(2,1)S(1)}, bf16[256,256]{1,0:T(8,128)(2,1)S(1)}, u32[]{:S(2)}, u32[]{:S(2)}) collective-permute-start(bf16[256,256]{1,0:T(8,128)(2,1)S(1)} %get-tuple-element.57), channel_id=1, source_target_pairs={{0,12},{4,8},{8,4},{12,0},{1,13},{5,9},{9,5},{13,1},{2,14},{6,10},... | collective-permute-start | bytes 393224 | tf_op jit(solution)/shard_map/ppermute | solution.py:731
  35.6 9.0 %collective-permute-done.6.rest_6_ = bf16[3,256,256]{2,1,0:T(8,128)(2,1)S(1)} collective-permute-done((bf16[3,256,256]{2,1,0:T(8,128)(2,1)S(1)}, bf16[3,256,256]{2,1,0:T(8,128)(2,1)S(1)}, u32[]{:S(2)}, u32[]{:S(2)}) %collective-permute-start.6) | collective-permute-done | bytes 393248 | tf_op jit(solution)/shard_map/ppermute | solution.py:731
  44.6 5.9 %shard_map.110 = (bf16[3,256,256]{2,1,0:T(8,128)(2,1)S(1)}, bf16[3,256,256]{2,1,0:T(8,128)(2,1)S(1)}, f32[256,256]{1,0:T(8,128)S(1)}, f32[256,256]{1,0:T(8,128)S(1)}) custom-call(s32[2]{0:T(128)S(1)} %pad_add_fusion.place_ref, f32[1024,16]{1,0:T(8,128)S(1)} %get-tuple-element.40.cols_ref, bf16[512,512]{1,0:T(8,128)(2,1)S(1)} %copy-done.9, ...), custom_call_target="tpu_custom_call" | custom-call | flops 38654705664 | bytes 58720256 | tf_op jit(solution)/shard_map/pallas_call | solution.py:79
  50.6 0.9 %collective-permute-start.7 = (bf16[3,256,256]{2,1,0:T(8,128)(2,1)S(1)}, bf16[3,256,256]{2,1,0:T(8,128)(2,1)S(1)}, u32[]{:S(2)}, u32[]{:S(2)}) collective-permute-start(bf16[3,256,256]{2,1,0:T(8,128)(2,1)S(1)} %get-tuple-element.50), channel_id=1, source_target_pairs={{0,4},{4,0},{8,12},{12,8},{1,5},{5,1},{9,13},{13,9},{2,6},{6,2},{1... | collective-permute-start | bytes 1179656 | tf_op jit(solution)/shard_map/ppermute | solution.py:731
  51.5 2.8 %shard_map.111 = (bf16[256,256]{1,0:T(8,128)(2,1)S(1)}, bf16[256,256]{1,0:T(8,128)(2,1)S(1)}) custom-call(s32[2]{0:T(128)S(1)} %pad_add_fusion.place_ref, bf16[512,512]{1,0:T(8,128)(2,1)S(1)} %copy-done.9, bf16[512,256]{1,0:T(8,128)(2,1)S(1)} %copy-done.10, bf16[1024,256]{1,0:T(8,128)(2,1)S(1)} %copy-done.5, ...), custom_call_target="tpu_custom_call" | custom-call | flops 19327352832 | bytes 41943040 | tf_op jit(solution)/shard_map/pallas_call | solution.py:79
  54.3 1.2 %collective-permute-start.10 = (bf16[256,256]{1,0:T(8,128)(2,1)S(1)}, bf16[256,256]{1,0:T(8,128)(2,1)S(1)}, u32[]{:S(2)}, u32[]{:S(2)}) collective-permute-start(bf16[256,256]{1,0:T(8,128)(2,1)S(1)} %get-tuple-element.56), channel_id=1, source_target_pairs={{0,4},{4,0},{8,12},{12,8},{1,5},{5,1},{9,13},{13,9},{2,6},{6,2},{1... | collective-permute-start | bytes 393224 | tf_op jit(solution)/shard_map/ppermute | solution.py:731
  55.6 6.1 %collective-permute-done.10.rest_3_ = bf16[256,256]{1,0:T(8,128)(2,1)S(1)} collective-permute-done((bf16[256,256]{1,0:T(8,128)(2,1)S(1)}, bf16[256,256]{1,0:T(8,128)(2,1)S(1)}, u32[]{:S(2)}, u32[]{:S(2)}) %collective-permute-start.10) | collective-permute-done | bytes 131104 | tf_op jit(solution)/shard_map/ppermute | solution.py:731
  61.7 1.5 %shard_map.112 = f32[8,1024]{1,0:T(8,128)S(1)} custom-call(s32[2]{0:T(128)S(1)} %pad_add_fusion.place_ref, bf16[3,1024,256]{2,1,0:T(8,128)(2,1)S(1)} %get-tuple-element.38.qkv_ref, bf16[1024,256]{1,0:T(8,128)(2,1)S(1)} %copy-done.2, bf16[3,256,256]{2,1,0:T(8,128)(2,1)S(1)} %get-tuple-element.49.rest_0_, ...), custom_call_target="tpu_custom_call" | custom-call | bytes 12582912 | tf_op jit(solution)/shard_map/pallas_call | solution.py:79
  63.2 2.3 %collective-permute-start.13 = (f32[8,1024]{1,0:T(8,128)S(1)}, f32[8,1024]{1,0:T(8,128)S(1)}, u32[]{:S(2)}, u32[]{:S(2)}) collective-permute-start(f32[8,1024]{1,0:T(8,128)S(1)} %shard_map.112), channel_id=1, source_target_pairs={{0,12},{4,0},{8,4},{12,8},{1,13},{5,1},{9,5},{13,9},{2,14},{6,2},{... | collective-permute-start | bytes 98312 | tf_op jit(solution)/shard_map/ppermute | solution.py:735
  65.6 4.5 %shard_map.113 = (bf16[1024,256]{1,0:T(8,128)(2,1)}, bf16[3,1024,256]{2,1,0:T(8,128)(2,1)}) custom-call(s32[2]{0:T(128)S(1)} %pad_add_fusion.place_ref, bf16[3,1024,256]{2,1,0:T(8,128)(2,1)S(1)} %get-tuple-element.38.qkv_ref, bf16[1024,256]{1,0:T(8,128)(2,1)S(1)} %copy-done.2, bf16[1024,48]{1,0:T(8,128)(2,1)S(1)} %get-tuple-element.32.split_ref, ...), custom_call_target="tpu_custom_call" | custom-call | flops 83886080 | bytes 41943040 | tf_op jit(solution)/shard_map/pallas_call | solution.py:79
  70.1 5.4 %shard_map.114 = (bf16[1024,256]{1,0:T(8,128)(2,1)}, bf16[3,1024,256]{2,1,0:T(8,128)(2,1)}) custom-call(s32[2]{0:T(128)S(1)} %pad_add_fusion.place_ref, bf16[3,1024,256]{2,1,0:T(8,128)(2,1)S(1)} %get-tuple-element.38.qkv_ref, bf16[1024,256]{1,0:T(8,128)(2,1)S(1)} %copy-done.2, ...), custom_call_target="tpu_custom_call", output_to_operand_aliasing={{0}: (14, {}), {1}: (15, {})} | custom-call | flops 83886080 | bytes 41943040 | tf_op jit(solution)/shard_map/pallas_call | solution.py:79
  (31 shorter events, 0.1 us)
Async XLA Ops:
  0.6 16.1 %copy-start.8 = (s32[16]{0:T(128)S(1)}, s32[16]{0:T(128)}, u32[]{:S(2)}) copy-start(s32[16]{0:T(128)} %lengths_ref.1) | copy-start | bytes 196
  0.6 16.1 %copy-start.7 = (f32[1024]{0:T(1024)S(1)}, f32[1024]{0:T(1024)}, u32[]{:S(2)}) copy-start(f32[1024]{0:T(1024)} %param.13) | copy-start | bytes 12292
  0.7 1.4 %copy-start = (bf16[3,1024,256]{2,1,0:T(8,128)(2,1)S(1)}, bf16[3,1024,256]{2,1,0:T(8,128)(2,1)}, u32[]{:S(2)}) copy-start(bf16[3,1024,256]{2,1,0:T(8,128)(2,1)} %feat_ref.5) | copy-start | bytes 4718596
  2.1 17.2 %copy-start.1 = (bf16[3,1024,256]{2,1,0:T(8,128)(2,1)S(1)}, bf16[3,1024,256]{2,1,0:T(8,128)(2,1)}, u32[]{:S(2)}) copy-start(bf16[3,1024,256]{2,1,0:T(8,128)(2,1)} %feat_ref.5) | copy-start | bytes 4718596
  2.1 17.2 %copy-start.2 = (bf16[1024,256]{1,0:T(8,128)(2,1)S(1)}, bf16[1024,256]{1,0:T(8,128)(2,1)}, u32[]{:S(2)}) copy-start(bf16[1024,256]{1,0:T(8,128)(2,1)} %dout_ref.9) | copy-start | bytes 1572868
  2.1 17.2 %copy-start.3 = (bf16[48,1152]{1,0:T(8,128)(2,1)S(1)}, bf16[48,1152]{1,0:T(8,128)(2,1)}, u32[]{:S(2)}) copy-start(bf16[48,1152]{1,0:T(8,128)(2,1)} %constant.19.clone.lanes_ref) | copy-start | bytes 331780
  3.1 7.0 %collective-permute-start = (bf16[16,1024]{1,0:T(8,128)(2,1)S(1)}, bf16[16,1024]{1,0:T(8,128)(2,1)S(1)}, u32[]{:S(2)}, u32[]{:S(2)}) collective-permute-start(bf16[16,1024]{1,0:T(8,128)(2,1)S(1)} %shard_map.104), channel_id=1, source_target_pairs={{0,4},{4,8},{8,12},{12,0},{1,5},{5,9},{9,13},{13,1},{2,6},{6,10},{... | collective-permute-start | bytes 98312 | tf_op jit(solution)/shard_map/ppermute | solution.py:735
  10.1 1.0 %copy-start.4 = (bf16[1024,256]{1,0:T(8,128)(2,1)S(1)}, bf16[1024,256]{1,0:T(8,128)(2,1)}, u32[]{:S(2)}) copy-start(bf16[1024,256]{1,0:T(8,128)(2,1)} %filt_ref.7) | copy-start | bytes 1572868
  12.3 15.0 %collective-permute-start.1 = (bf16[256,256]{1,0:T(8,128)(2,1)S(1)}, bf16[256,256]{1,0:T(8,128)(2,1)S(1)}, u32[]{:S(2)}, u32[]{:S(2)}) collective-permute-start(bf16[256,256]{1,0:T(8,128)(2,1)S(1)} %get-tuple-element.41), channel_id=1, source_target_pairs={{0,4},{4,0},{8,12},{12,8},{1,5},{5,1},{9,13},{13,9},{2,6},{6,2},{1... | collective-permute-start | bytes 393224 | tf_op jit(solution)/shard_map/ppermute | solution.py:731
  12.3 16.7 %collective-permute-start.2 = (bf16[256,256]{1,0:T(8,128)(2,1)S(1)}, bf16[256,256]{1,0:T(8,128)(2,1)S(1)}, u32[]{:S(2)}, u32[]{:S(2)}) collective-permute-start(bf16[256,256]{1,0:T(8,128)(2,1)S(1)} %get-tuple-element.42), channel_id=1, source_target_pairs={{0,8},{4,12},{8,0},{12,4},{1,9},{5,13},{9,1},{13,5},{2,10},{6,14},... | collective-permute-start | bytes 393224 | tf_op jit(solution)/shard_map/ppermute | solution.py:731
  14.9 14.1 %collective-permute-start.3 = (bf16[256,256]{1,0:T(8,128)(2,1)S(1)}, bf16[256,256]{1,0:T(8,128)(2,1)S(1)}, u32[]{:S(2)}, u32[]{:S(2)}) collective-permute-start(bf16[256,256]{1,0:T(8,128)(2,1)S(1)} %get-tuple-element.43), channel_id=1, source_target_pairs={{0,12},{4,8},{8,4},{12,0},{1,13},{5,9},{9,5},{13,1},{2,14},{6,10},... | collective-permute-start | bytes 393224 | tf_op jit(solution)/shard_map/ppermute | solution.py:731
  16.7 0.8 %copy-start.6 = (f32[3,3,1024]{2,1,0:T(4,128)S(1)}, f32[3,3,1024]{2,1,0:T(4,128)}, u32[]{:S(2)}) copy-start(f32[3,3,1024]{2,1,0:T(4,128)} %taps_ref.1) | copy-start | bytes 110596
  21.9 9.0 %collective-permute-start.5 = (bf16[256,256]{1,0:T(8,128)(2,1)S(1)}, bf16[256,256]{1,0:T(8,128)(2,1)S(1)}, u32[]{:S(2)}, u32[]{:S(2)}) collective-permute-start(bf16[256,256]{1,0:T(8,128)(2,1)S(1)} %get-tuple-element.45), channel_id=1, source_target_pairs={{0,4},{4,0},{8,12},{12,8},{1,5},{5,1},{9,13},{13,9},{2,6},{6,2},{1... | collective-permute-start | bytes 393224 | tf_op jit(solution)/shard_map/ppermute | solution.py:731
  22.0 8.9 %copy-start.5 = (bf16[1024,256]{1,0:T(8,128)(2,1)S(1)}, bf16[1024,256]{1,0:T(8,128)(2,1)}, u32[]{:S(2)}) copy-start(bf16[1024,256]{1,0:T(8,128)(2,1)} %filt_ref.7) | copy-start | bytes 1572868
  22.0 8.9 %copy-start.9 = (bf16[512,512]{1,0:T(8,128)(2,1)S(1)}, bf16[512,512]{1,0:T(8,128)(2,1)}, u32[]{:S(2)}) copy-start(bf16[512,512]{1,0:T(8,128)(2,1)} %constant.17.clone.forward_ref) | copy-start | bytes 1572868
  22.0 8.9 %copy-start.10 = (bf16[512,256]{1,0:T(8,128)(2,1)S(1)}, bf16[512,256]{1,0:T(8,128)(2,1)}, u32[]{:S(2)}) copy-start(bf16[512,256]{1,0:T(8,128)(2,1)} %constant.18.clone.inverse_ref) | copy-start | bytes 786436
  24.6 26.9 %collective-permute-start.8 = (bf16[256,256]{1,0:T(8,128)(2,1)S(1)}, bf16[256,256]{1,0:T(8,128)(2,1)S(1)}, u32[]{:S(2)}, u32[]{:S(2)}) collective-permute-start(bf16[256,256]{1,0:T(8,128)(2,1)S(1)} %get-tuple-element.51), channel_id=1, source_target_pairs={{0,8},{4,12},{8,0},{12,4},{1,9},{5,13},{9,1},{13,5},{2,10},{6,14},... | collective-permute-start | bytes 393224 | tf_op jit(solution)/shard_map/ppermute | solution.py:731
  27.2 24.3 %collective-permute-start.9 = (bf16[256,256]{1,0:T(8,128)(2,1)S(1)}, bf16[256,256]{1,0:T(8,128)(2,1)S(1)}, u32[]{:S(2)}, u32[]{:S(2)}) collective-permute-start(bf16[256,256]{1,0:T(8,128)(2,1)S(1)} %get-tuple-element.52), channel_id=1, source_target_pairs={{0,12},{4,8},{8,4},{12,0},{1,13},{5,9},{9,5},{13,1},{2,14},{6,10},... | collective-permute-start | bytes 393224 | tf_op jit(solution)/shard_map/ppermute | solution.py:731
  29.0 15.6 %collective-permute-start.6 = (bf16[3,256,256]{2,1,0:T(8,128)(2,1)S(1)}, bf16[3,256,256]{2,1,0:T(8,128)(2,1)S(1)}, u32[]{:S(2)}, u32[]{:S(2)}) collective-permute-start(bf16[3,256,256]{2,1,0:T(8,128)(2,1)S(1)} %get-tuple-element.47), channel_id=1, source_target_pairs={{0,4},{4,0},{8,12},{12,8},{1,5},{5,1},{9,13},{13,9},{2,6},{6,2},{1... | collective-permute-start | bytes 1179656 | tf_op jit(solution)/shard_map/ppermute | solution.py:731
  29.1 15.5 %collective-permute-start.4 = (bf16[768,256]{1,0:T(8,128)(2,1)S(1)}, bf16[768,256]{1,0:T(8,128)(2,1)S(1)}, u32[]{:S(2)}, u32[]{:S(2)}) collective-permute-start(bf16[768,256]{1,0:T(8,128)(2,1)S(1)} %pad_maximum_fusion), channel_id=1, source_target_pairs={{0,16},{16,0},{1,17},{17,1},{2,18},{18,2},{3,19},{19,3},{4,20},{20... | collective-permute-start | bytes 1179656 | tf_op jit(solution)/shard_map/ppermute | solution.py:731
  33.7 21.8 %collective-permute-start.12 = (bf16[256,256]{1,0:T(8,128)(2,1)S(1)}, bf16[256,256]{1,0:T(8,128)(2,1)S(1)}, u32[]{:S(2)}, u32[]{:S(2)}) collective-permute-start(bf16[256,256]{1,0:T(8,128)(2,1)S(1)} %get-tuple-element.57), channel_id=1, source_target_pairs={{0,12},{4,8},{8,4},{12,0},{1,13},{5,9},{9,5},{13,1},{2,14},{6,10},... | collective-permute-start | bytes 393224 | tf_op jit(solution)/shard_map/ppermute | solution.py:731
  44.6 11.0 %collective-permute-start.11 = (bf16[256,256]{1,0:T(8,128)(2,1)S(1)}, bf16[256,256]{1,0:T(8,128)(2,1)S(1)}, u32[]{:S(2)}, u32[]{:S(2)}) collective-permute-start(bf16[256,256]{1,0:T(8,128)(2,1)S(1)} %get-tuple-element.48.rest_7_), channel_id=1, source_target_pairs={{0,8},{4,12},{8,0},{12,4},{1,9},{5,13},{9,1},{13,5},{2,10},{6,14},... | collective-permute-start | bytes 393224 | tf_op jit(solution)/shard_map/ppermute | solution.py:731
  50.6 11.1 %collective-permute-start.7 = (bf16[3,256,256]{2,1,0:T(8,128)(2,1)S(1)}, bf16[3,256,256]{2,1,0:T(8,128)(2,1)S(1)}, u32[]{:S(2)}, u32[]{:S(2)}) collective-permute-start(bf16[3,256,256]{2,1,0:T(8,128)(2,1)S(1)} %get-tuple-element.50), channel_id=1, source_target_pairs={{0,4},{4,0},{8,12},{12,8},{1,5},{5,1},{9,13},{13,9},{2,6},{6,2},{1... | collective-permute-start | bytes 1179656 | tf_op jit(solution)/shard_map/ppermute | solution.py:731
  54.3 7.4 %collective-permute-start.10 = (bf16[256,256]{1,0:T(8,128)(2,1)S(1)}, bf16[256,256]{1,0:T(8,128)(2,1)S(1)}, u32[]{:S(2)}, u32[]{:S(2)}) collective-permute-start(bf16[256,256]{1,0:T(8,128)(2,1)S(1)} %get-tuple-element.56), channel_id=1, source_target_pairs={{0,4},{4,0},{8,12},{12,8},{1,5},{5,1},{9,13},{13,9},{2,6},{6,2},{1... | collective-permute-start | bytes 393224 | tf_op jit(solution)/shard_map/ppermute | solution.py:731
  63.2 6.8 %collective-permute-start.13 = (f32[8,1024]{1,0:T(8,128)S(1)}, f32[8,1024]{1,0:T(8,128)S(1)}, u32[]{:S(2)}, u32[]{:S(2)}) collective-permute-start(f32[8,1024]{1,0:T(8,128)S(1)} %shard_map.112), channel_id=1, source_target_pairs={{0,12},{4,0},{8,4},{12,8},{1,13},{5,1},{9,5},{13,9},{2,14},{6,2},{... | collective-permute-start | bytes 98312 | tf_op jit(solution)/shard_map/ppermute | solution.py:735

commit v5 on v0

v5 whole, which is shorter than its diff:
```python
import functools
import math

import jax
import jax.numpy as jnp
import numpy as np
from jax import lax
from jax.experimental import pallas as pl
from jax.experimental.pallas import tpu as pltpu
from jax.sharding import PartitionSpec as P

BF16 = jnp.bfloat16
F32 = jnp.float32
SHARE = 0.5
VMEM_LIMIT = 24 * 1024 * 1024
SCALARS = pl.BlockSpec(memory_space=pltpu.SMEM)
IN_HBM = pl.BlockSpec(memory_space=pltpu.HBM)
HELD = pl.BlockSpec(memory_space=pltpu.VMEM)
ANYWHERE = pl.BlockSpec(memory_space=pl.ANY)


def split_bf16(table):
    high = table.astype(np.float32).astype(BF16)
    low = (table - high.astype(np.float64)).astype(np.float32).astype(BF16)
    return high, low


def block_tables(span):
    freq = np.concatenate([np.arange(0, span, 2), np.arange(1, span, 2)])
    angle = np.pi * (2 * freq[None, :] + 1) * np.arange(span)[:, None] / (2 * span)
    forward = np.concatenate([np.cos(angle), -np.sin(angle)], axis=1)
    inverse = np.concatenate([np.cos(angle), -np.sin(angle)], axis=1).T / span
    return np.concatenate(split_bf16(forward), axis=0), split_bf16(inverse)[0]


def dot(a, b):
    return jnp.dot(a, b, preferred_element_type=F32)


def estimate(time_us):
    return pl.CostEstimate(flops=int(SHARE * time_us * 1e9), bytes_accessed=0, transcendentals=0)


def offsets_row(lengths_ref, first, span, ahead):
    position = lax.broadcasted_iota(jnp.int32, (8, span), 1) + (first + ahead)

    def step(genome, carry):
        end, start = carry
        end = end + lengths_ref[genome]
        return end, jnp.where(position >= end, end, start)

    begin = (jnp.int32(0), jnp.zeros((8, span), jnp.int32))
    _, start = lax.fori_loop(0, lengths_ref.shape[0], step, begin)
    return position, position - start


class Layout:
    def __init__(self, parts, channels, span):
        self.parts, self.channels, self.span = parts, channels, span
        self.half = parts // 2
        self.size = channels // self.half
        self.sub = self.size // 2


def where_am_i(place_ref, layout):
    rank, group = place_ref[0], place_ref[1]
    side = rank // layout.half
    return side, rank % layout.half, jnp.where(side == 0, 1 - group, group)


def channel_block(place_ref, layout, turn, other):
    _, own, main = where_am_i(place_ref, layout)
    return jnp.bitwise_xor(own, turn) * 2 + jnp.bitwise_xor(main, other)


def run(body, layout, place, operands, outs, scratch, cost, in_specs=None, out_specs=None, aliases=None):
    single = not isinstance(outs, list)
    return pl.pallas_call(
        functools.partial(body, layout),
        out_shape=outs,
        in_specs=[SCALARS] + (in_specs or [HELD] * len(operands)),
        out_specs=out_specs or (HELD if single else [HELD] * len(outs)),
        scratch_shapes=scratch,
        input_output_aliases=aliases or {},
        compiler_params=pltpu.CompilerParams(vmem_limit_bytes=VMEM_LIMIT),
        cost_estimate=cost,
    )(place, *operands)


def rows_at(begin, step, count):
    return pl.ds(pl.multiple_of(begin, step), count)


def pack_body(layout, place_ref, feat_hbm, filt_hbm, halo_ref, *rest):
    outs, (tail, turned, sems) = rest[:-3], rest[-3:]
    half, sub = layout.half, layout.sub
    copies = [pltpu.make_async_copy(feat_hbm.at[:, :, pl.ds(layout.span - 128, 128)], tail, sems.at[layout.parts + 1])]
    for step in range(layout.parts + 1):
        turn, other = (step % half, step // half) if step else (0, 0)
        if step == layout.parts:
            turn, other = 0, 1
        begin = channel_block(place_ref, layout, turn, other) * sub
        source = filt_hbm.at[rows_at(begin, sub, sub), :]
        copies.append(pltpu.make_async_copy(source, outs[step], sems.at[step]))
    for copy in copies:
        copy.start()
    turned[...] = jnp.zeros(turned.shape, F32)
    copies[0].wait()
    for which in range(3):
        turned[2 * which : 2 * which + 2, :] = tail[which].astype(F32).T[-2:, :]
    halo_ref[...] = turned[...].astype(BF16)
    for copy in copies[1:]:
        copy.wait()


def pack(layout, place, features, filters):
    parts, sub, span, channels = layout.parts, layout.sub, layout.span, layout.channels
    outs = [jax.ShapeDtypeStruct((16, channels), BF16)] + [jax.ShapeDtypeStruct((sub, span), BF16)] * (parts + 1)
    scratch = [
        pltpu.VMEM((3, channels, 128), BF16),
        pltpu.VMEM((16, channels), F32),
        pltpu.SemaphoreType.DMA((parts + 2,)),
    ]
    found = run(pack_body, layout, place, (features, filters), outs, scratch, estimate(2.0), in_specs=[IN_HBM] * 2)
    return found[0], (found[1], found[1 + parts]), found[2 : 1 + parts]


def three_parts(value):
    top = value.astype(BF16).astype(F32)
    middle = (value - top).astype(BF16).astype(F32)
    return [top, middle, value - top - middle]


def edge_table(table_rows, lanes, entries):
    row = lax.broadcasted_iota(jnp.int32, (table_rows, lanes), 0)
    lane = lax.broadcasted_iota(jnp.int32, (table_rows, lanes), 1)
    table = jnp.zeros((table_rows, lanes), F32)
    for rows, where, keep in entries:
        for own_row in rows:
            table = jnp.where((row == own_row) & (lane == where), keep, table)
    return table.astype(BF16)


def small_body(layout, place_ref, lengths_ref, taps_ref, skip_ref, *rest):
    cols_ref, split_ref, keep_ref, fwd_edge_ref, last_edge_ref, turned, lanes_ref = rest
    span = layout.span
    first = place_ref[0] * span
    _, offset = offsets_row(lengths_ref, first, span, 0)
    keep, keep_back = [], []
    for j in (1, 2):
        keep.append((offset[0:1, :] >= j).astype(F32))
        position, later = offsets_row(lengths_ref, first, span, j)
        inside = (position < layout.parts * span) & (later >= j)
        keep_back.append(inside[0:1, :].astype(F32))
    most = span - 128
    lane = lax.broadcasted_iota(jnp.int32, (1, span), 1)
    keep_ref[...] = jnp.zeros(keep_ref.shape, F32)
    for j in (0, 1):
        keep_ref[j : j + 1, :] = jnp.where(lane > j, keep[j], 0.0)
        keep_ref[2 + j : 3 + j, :] = jnp.where(lane < span - 1 - j, keep_back[j], 0.0)
    for which in range(3):
        begin = which * 256
        two, one = [2 * which], [2 * which + 1]
        fwd_edge_ref[:, begin : begin + 128] = edge_table(16, 128, [(one, 0, keep[0][:, :128])])
        fwd_edge_ref[:, begin + 128 : begin + 256] = edge_table(
            16, 128, [(two, 0, keep[1][:, :128]), (one, 1, keep[1][:, :128])]
        )
        entries = []
        for k, (lane_at, j) in enumerate(((127, 0), (127, 1), (126, 1))):
            entries.append(([3 * which + k + 16 * p for p in range(3)], lane_at, keep_back[j][:, most:]))
        last_edge_ref[:, which * 128 : (which + 1) * 128] = edge_table(48, 128, entries)
    turned[...] = jnp.zeros(turned.shape, F32)
    for which in range(3):
        turned[3 * which : 3 * which + 3, :] = taps_ref[which]
    turned[9:10, :] = skip_ref[...]
    value = turned[...]
    cols_ref[...] = value.T
    split_ref[...] = jnp.concatenate(three_parts(value), axis=0).T.astype(BF16)
    column = lax.broadcasted_iota(jnp.int32, (48, 128), 0) % 16
    for k in range(9):
        lanes_ref[:, k * 128 : (k + 1) * 128] = jnp.where(column == k, 1.0, 0.0).astype(BF16)


def small(layout, place, lengths, taps, skip):
    channels, span = layout.channels, layout.span
    shapes = [
        ((channels, 16), F32),
        ((channels, 48), BF16),
        ((8, span), F32),
        ((16, 768), BF16),
        ((48, 384), BF16),
        ((16, channels), F32),
        ((48, 9 * 128), BF16),
    ]
    return run(
        small_body,
        layout,
        place,
        (lengths, taps, skip.reshape(1, channels)),
        [jax.ShapeDtypeStruct(*s) for s in shapes],
        [],
        estimate(1.2),
        in_specs=[SCALARS, HELD, HELD],
    )


def gate_body(layout, place_ref, feat_hbm, dout_hbm, halo_ref, split_ref, lanes_ref, keep_ref, edge_ref, *rest):
    half, rows, span = layout.half, layout.sub, layout.span
    gated, firsts, cross, seconds = (rest[:4], *(rest[4 + k * half : 4 + (k + 1) * half] for k in range(3)))
    feat_ref, ends_of, spread, ends, sems = rest[4 + 3 * half :]
    side, _, _ = where_am_i(place_ref, layout)
    group = min(32, rows)
    steps = [(turn, other) for other in range(2) for turn in range(half)]
    copies = []
    for k, (turn, other) in enumerate(steps):
        block = rows_at(channel_block(place_ref, layout, turn, other) * rows, rows, rows)
        copies.append(pltpu.make_async_copy(feat_hbm.at[:, block, :], feat_ref.at[k], sems.at[k, 0]))
        copies.append(pltpu.make_async_copy(dout_hbm.at[block, :], gated[2 * other + 1].at[turn], sems.at[k, 1]))
        for copy in copies[-2:]:
            copy.start()
    ends_of[...] = halo_ref[...].astype(F32).T.astype(BF16)
    keep = [keep_ref[j : j + 1, :] for j in range(2)]
    for k, (turn, other) in enumerate(steps):
        block = rows_at(channel_block(place_ref, layout, turn, other) * rows, rows, rows)
        qkv_ref, dout_ref = gated[2 * other : 2 * other + 2]
        spread[...] = dot(split_ref[block, :], lanes_ref[...])
        ends[...] = dot(ends_of[block, :], edge_ref[...])
        for copy in copies[2 * k : 2 * k + 2]:
            copy.wait()

        def tile(index, _, k=k, turn=turn, other=other, qkv_ref=qkv_ref, dout_ref=dout_ref):
            local_rows = rows_at(index * group, group, group)
            filtered = []
            for which in range(3):
                value = feat_ref[k, which, local_rows, :].astype(F32)
                moved = [pltpu.roll(value, j + 1, 1) * keep[j] for j in range(2)]
                taps = [spread[local_rows, (3 * which + j) * 128 : (3 * which + j + 1) * 128] for j in range(3)]
                parts = []
                for lane in range(0, span, 128):
                    back = [moved[j][:, lane : lane + 128] for j in range(2)]
                    if lane == 0:
                        begins = [which * 256 + j * 128 for j in range(2)]
                        back = [back[j] + ends[local_rows, begins[j] : begins[j] + 128] for j in range(2)]
                    total = taps[0] * value[:, lane : lane + 128]
                    parts.append((total + taps[1] * back[0] + taps[2] * back[1]).astype(BF16))
                filtered.append(jnp.concatenate(parts, axis=1))
                qkv_ref[turn, which, local_rows, :] = filtered[-1]
            mixed = filtered[1] * filtered[2]
            grad_in = dout_ref[turn, local_rows, :] * filtered[0]
            first = jnp.where(side == 0, mixed, grad_in)
            second = jnp.where(side == 0, grad_in, mixed)
            pair = seconds[turn] if other else firsts[turn]
            pair[0, local_rows, :] = first
            pair[1, local_rows, :] = second
            if other:
                cross[turn][local_rows, :] = first
            return 0

        lax.fori_loop(0, rows // group, tile, 0, unroll=min(2, rows // group))


def gate(layout, place, features, dout, halo, split, lanes, keep, edge):
    half, rows, span, channels = layout.half, layout.sub, layout.span, layout.channels
    pair = (2, rows, span)
    shapes = [(half, 3, rows, span), (half, rows, span)] * 2 + [pair] * half + [(rows, span)] * half + [pair] * half
    found = run(
        gate_body,
        layout,
        place,
        (features, dout, halo, split, lanes, keep, edge),
        [jax.ShapeDtypeStruct(s, BF16) for s in shapes],
        [
            pltpu.VMEM((2 * half, 3, rows, span), BF16),
            pltpu.VMEM((channels, 16), BF16),
            pltpu.VMEM((rows, 9 * 128), F32),
            pltpu.VMEM((rows, 768), F32),
            pltpu.SemaphoreType.DMA((2 * half, 2)),
        ],
        estimate(5.7),
        in_specs=[IN_HBM] * 2 + [HELD] * 5,
    )
    return found[0:2], found[2:4], found[4 : 4 + half], found[4 + half : 4 + 2 * half], found[4 + 2 * half :]


def loop(count, body, init):
    if count <= 4:
        for k in range(count):
            init = body(k, init)
        return init
    return lax.fori_loop(0, count, body, init)


def add_product(total, f, x):
    return (total[0] + f[0] * x[0] - f[1] * x[1], total[1] + f[0] * x[1] + f[1] * x[0])


def add_conjugate(total, f, x):
    return (total[0] + f[0] * x[0] + f[1] * x[1], total[1] + f[0] * x[1] - f[1] * x[0])


def turned_sum(spectrum, neighbour, sign):
    half = spectrum[0].shape[1] // 2
    parts = []
    for lanes, flip in ((slice(0, half), sign), (slice(half, None), -sign)):
        n_re, n_im = neighbour[0][:, lanes], neighbour[1][:, lanes]
        s_re, s_im = spectrum[0][:, lanes], spectrum[1][:, lanes]
        parts.append((s_re - n_im, s_im + n_re) if flip > 0 else (s_re + n_im, s_im - n_re))
    return tuple(jnp.concatenate([p[k] for p in parts], axis=1) for k in range(2))


def forward(raw, spec, begin, target, rows, table_ref):
    value = raw[pl.ds(pl.multiple_of(begin, 16), rows), :]
    spec[pl.ds(pl.multiple_of(target, 16), rows), :] = dot(jnp.concatenate([value, value], axis=1), table_ref[...])


def spectrum_at(spec, begin, group, span):
    place = pl.ds(pl.multiple_of(begin, group), group)
    return spec[place, :span], spec[place, span:]


def store_spectrum(ready, begin, value, group, span):
    place = pl.ds(pl.multiple_of(begin, group), group)
    ready[place, :span] = value[0].astype(BF16)
    ready[place, span:] = value[1].astype(BF16)


def filter_body(layout, place_ref, forward_ref, filt_ref, *rest):
    parts, sub = layout.parts, layout.sub
    filt_in, (spec, raw) = rest[: parts - 1], rest[parts - 1 :]
    rank = place_ref[0]
    raw[rows_at(rank * sub, sub, sub), :] = filt_ref[...]
    for step in range(1, parts):
        raw[rows_at(jnp.bitwise_xor(rank, step) * sub, sub, sub), :] = filt_in[step - 1][...]
    chunk = math.gcd(parts * sub, 512)

    def transform(index, _):
        forward(raw, spec, index * chunk, index * chunk, chunk, forward_ref)
        return 0

    lax.fori_loop(0, parts * sub // chunk, transform, 0)


def filter_spectra(layout, place, table, own, filt):
    rows, span = layout.parts * layout.sub, layout.span
    return run(
        filter_body,
        layout,
        place,
        (table, own, *filt),
        jax.ShapeDtypeStruct((rows, 2 * span), F32),
        [pltpu.VMEM((rows, span), BF16)],
        estimate(1.5),
    )


def cross_body(layout, place_ref, forward_ref, inverse_ref, known, *rest):
    parts, half, sub, span = layout.parts, layout.half, layout.sub, layout.span
    signal, outs = rest[:half], rest[half : 2 * half]
    spec, raw, ready, back = rest[2 * half :]
    side, own, _ = where_am_i(place_ref, layout)
    for step in range(half):
        raw[rows_at(jnp.bitwise_xor(own, step) * sub, sub, sub), :] = signal[step][0]
    forward(raw, spec, 0, 0, half * sub, forward_ref)
    group = 16
    zero = (jnp.zeros((group, span), F32),) * 2

    def products(index, ahead):
        def filt(k):
            return spectrum_at(known, k * sub + index * group, group, span)

        def sig(k):
            return spectrum_at(spec, k * sub + index * group, group, span)

        before = None
        if ahead:
            for place in range(half - 1, parts):
                total = loop(half, lambda k, t, p=place: add_product(t, filt(p - k), sig(k)), zero)
                if before is not None:
                    value = turned_sum(total, before, 1)
                    store_spectrum(ready, (place - half) * sub + index * group, value, group, span)
                before = total
        else:
            for place in range(half, -1, -1):
                total = loop(half, lambda k, t, p=place: add_conjugate(t, filt(half + k - p), sig(k)), zero)
                if before is not None:
                    value = turned_sum(total, before, -1)
                    store_spectrum(ready, place * sub + index * group, value, group, span)
                before = total
        return 0

    @pl.when(side == 0)
    def _():
        lax.fori_loop(0, sub // group, lambda k, _: products(k, True), 0)

    @pl.when(side == 1)
    def _():
        lax.fori_loop(0, sub // group, lambda k, _: products(k, False), 0)

    back[...] = dot(ready[...], inverse_ref[...])
    for step in range(half):
        outs[step][...] = back[rows_at(jnp.bitwise_xor(own, step) * sub, sub, sub), :].astype(BF16)


def cross_half(layout, place, tables, known, signal):
    half, sub, span = layout.half, layout.sub, layout.span
    rows = half * sub
    found = run(
        cross_body,
        layout,
        place,
        (*tables, known, *signal),
        [jax.ShapeDtypeStruct((sub, span), BF16)] * half + [jax.ShapeDtypeStruct((rows, 2 * span), F32)],
        [
            pltpu.VMEM((rows, span), BF16),
            pltpu.VMEM((rows, 2 * span), BF16),
            pltpu.VMEM((rows, span), F32),
        ],
        estimate(2.0),
    )
    return found[:half], found[half]


def hold_body(layout, place_ref, *refs):
    pass


def hold(layout, place, arrays):
    outs = [jax.ShapeDtypeStruct(a.shape, a.dtype) for a in arrays]
    aliases = {1 + k: k for k in range(len(arrays))}
    return run(hold_body, layout, place, arrays, outs, [], estimate(4.0), aliases=aliases)


def main_body(layout, place_ref, cols_ref, forward_ref, inverse_ref, known, near_spec, *rest):
    parts, half, sub, span = layout.parts, layout.half, layout.sub, layout.span
    firsts, cross, outs = (rest[k * half : (k + 1) * half] for k in range(3))
    raw, spec, ready, back = rest[3 * half :]
    side, own, _ = where_am_i(place_ref, layout)
    block = parts * sub
    for step in range(half):
        place = jnp.bitwise_xor(own, step)
        raw[rows_at((side * half + place) * sub, sub, sub), :] = firsts[step][1]
        raw[rows_at(((1 - side) * half + place) * sub, sub, sub), :] = cross[step][...]
    chunk = math.gcd(block, 512)

    def transform(index, _):
        forward(raw, spec, index * chunk, index * chunk, chunk, forward_ref)
        return 0

    lax.fori_loop(0, block // chunk, transform, 0)
    group = 16
    zero = (jnp.zeros((group, span), F32),) * 2

    def products(index, first_half):
        def filt(k):
            return spectrum_at(known, k * sub + index * group, group, span)

        def near(k):
            return spectrum_at(near_spec, k * sub + index * group, group, span)

        def far(k):
            return spectrum_at(spec, k * sub + index * group, group, span)

        def store(kind, place, value):
            store_spectrum(ready, (kind * half + place) * sub + index * group, value, group, span)

        before = None
        if first_half:
            for place in range(half):
                total = loop(place + 1, lambda k, t, p=place: add_product(t, filt(k), near(p - k)), zero)
                store(0, place, total if before is None else turned_sum(total, before, 1))
                before = total
            before = None
            for place in range(half, -1, -1):
                total = loop(parts - place, lambda k, t, p=place: add_conjugate(t, filt(k), far(p + k)), zero)
                if before is not None:
                    store(1, place, turned_sum(total, before, -1))
                before = total
        else:
            for place in range(half - 1, -1, -1):
                total = loop(half - place, lambda k, t, p=place: add_conjugate(t, filt(k), near(p + k)), zero)
                store(0, place, total if before is None else turned_sum(total, before, -1))
                before = total
            before = None
            for place in range(half - 1, parts):
                total = loop(place + 1, lambda k, t, p=place: add_product(t, filt(k), far(p - k)), zero)
                if before is not None:
                    store(1, place - half, turned_sum(total, before, 1))
                before = total
        return 0

    @pl.when(side == 0)
    def _():
        lax.fori_loop(0, sub // group, lambda k, _: products(k, True), 0)

    @pl.when(side == 1)
    def _():
        lax.fori_loop(0, sub // group, lambda k, _: products(k, False), 0)

    back[...] = dot(ready[...], inverse_ref[...])
    begin = channel_block(place_ref, layout, 0, 0) * sub
    skip = cols_ref[rows_at(begin, sub, sub), 9:10]
    for step in range(half):
        place = jnp.bitwise_xor(own, step)
        for kind in range(2):
            value = back[rows_at((kind * half + place) * sub, sub, sub), :]
            direct = firsts[step][kind].astype(F32)
            outs[step][kind] = (value + skip * direct).astype(BF16)


def main_half(layout, place, cols, tables, known, near, firsts, cross):
    half, sub, span, parts = layout.half, layout.sub, layout.span, layout.parts
    rows = parts * sub
    return run(
        main_body,
        layout,
        place,
        (cols, *tables, known, near, *firsts, *cross),
        [jax.ShapeDtypeStruct((2, sub, span), BF16)] * half,
        [
            pltpu.VMEM((rows, span), BF16),
            pltpu.VMEM((rows, 2 * span), F32),
            pltpu.VMEM((2 * half * sub, 2 * span), BF16),
            pltpu.VMEM((2 * half * sub, span), F32),
        ],
        estimate(3.0),
    )


def other_body(layout, place_ref, cols_ref, forward_ref, inverse_ref, filt_ref, other_ref, *rest):
    parts, half, sub, span = layout.parts, layout.half, layout.sub, layout.span
    seconds, outs = rest[:half], rest[half : 2 * half]
    raw, spec, ready, back = rest[2 * half :]
    side, own, _ = where_am_i(place_ref, layout)
    rank = place_ref[0]
    block, kind_rows = parts * sub, half * sub
    begin = channel_block(place_ref, layout, 0, 1) * sub
    raw[rows_at(rank * sub, sub, sub), :] = filt_ref[...]
    for step in range(1, parts):
        place = rows_at(jnp.bitwise_xor(rank, step) * sub, sub, sub)
        raw[place, :] = other_ref[(step - 1) * sub : step * sub, :]
    for step in range(half):
        place = block + jnp.bitwise_xor(own, step) * sub
        raw[rows_at(place + side * kind_rows, sub, sub), :] = seconds[step][0]
        raw[rows_at(place + (1 - side) * kind_rows, sub, sub), :] = seconds[step][1]

    def transform(kind, _):
        source = jnp.where(kind == 0, 0, block + (kind - 1) * kind_rows)
        forward(raw, spec, source, kind * kind_rows, kind_rows, forward_ref)
        return 0

    lax.fori_loop(0, 3, transform, 0)
    group = 16
    zero = (jnp.zeros((group, span), F32),) * 2

    def products(index, _):
        def read(kind, k):
            return spectrum_at(spec, (kind * half + k) * sub + index * group, group, span)

        def store(kind, k, value):
            store_spectrum(ready, (kind * half + k) * sub + index * group, value, group, span)

        before = None
        for place in range(half):
            total = loop(place + 1, lambda k, t, p=place: add_product(t, read(0, k), read(1, p - k)), zero)
            store(0, place, total if before is None else turned_sum(total, before, 1))
            before = total
        before = None
        for place in range(half - 1, -1, -1):
            total = loop(half - place, lambda k, t, p=place: add_conjugate(t, read(0, k), read(2, p + k)), zero)
            store(1, place, total if before is None else turned_sum(total, before, -1))
            before = total
        return 0

    lax.fori_loop(0, sub // group, products, 0)
    back[...] = dot(ready[...], inverse_ref[...])
    skip = cols_ref[rows_at(begin, sub, sub), 9:10]
    for step in range(half):
        place = jnp.bitwise_xor(own, step) * sub
        for kind in range(2):
            source = jnp.where(side == kind, 0, 1) * kind_rows + place
            value = back[rows_at(source, sub, sub), :]
            direct = seconds[step][kind].astype(F32)
            outs[step][kind] = (value + skip * direct).astype(BF16)


def other_half(layout, place, cols, tables, filters, other, seconds):
    half, sub, span, parts = layout.half, layout.sub, layout.span, layout.parts
    rows = 3 * half * sub
    return run(
        other_body,
        layout,
        place,
        (cols, *tables, filters, other, *seconds),
        [jax.ShapeDtypeStruct((2, sub, span), BF16)] * half,
        [
            pltpu.VMEM(((parts + 2 * half) * sub, span), BF16),
            pltpu.VMEM((rows, 2 * span), F32),
            pltpu.VMEM((2 * half * sub, 2 * span), BF16),
            pltpu.VMEM((2 * half * sub, span), F32),
        ],
        estimate(3.0),
    )


def results(side, found, crossed, here):
    plain, mixed = found[(0, *here)], found[(1, *here)]
    if crossed is not None:
        mixed = (mixed.astype(F32) + crossed[here].astype(F32)).astype(BF16)
    return jnp.where(side == 0, plain, mixed), jnp.where(side == 0, mixed, plain)


def first_body(layout, place_ref, qkv_main, dout_main, qkv_other, dout_other, *refs):
    half, sub = layout.half, layout.sub
    main, rest, crossed = (refs[k * half : (k + 1) * half] for k in range(3))
    out_ref, grads = refs[3 * half :]
    side, _, _ = where_am_i(place_ref, layout)
    for turn in range(half):
        for other in range(2):
            place = rows_at(channel_block(place_ref, layout, turn, other) * sub, sub, sub)
            qkv, dout_ref = (qkv_other, dout_other) if other else (qkv_main, dout_main)
            here = (slice(None), slice(0, 128))
            pair = results(side, (rest if other else main)[turn], crossed[turn] if other else None, here)
            y_out, dmixed = (f.astype(F32) for f in pair)
            grads[0, place, :] = dout_ref[turn, :, 0:128].astype(F32) * y_out
            grads[1, place, :] = dmixed * qkv[turn, 2, :, 0:128].astype(F32)
            grads[2, place, :] = dmixed * qkv[turn, 1, :, 0:128].astype(F32)
    out_ref[...] = jnp.zeros(out_ref.shape, F32)
    for which in range(3):
        out_ref[2 * which : 2 * which + 2, :] = grads[which].T[0:2, :]


def first_grads(layout, place, gated, main, rest, crossed):
    channels = layout.channels
    return run(
        first_body,
        layout,
        place,
        (*gated, *main, *rest, *crossed),
        jax.ShapeDtypeStruct((8, channels), F32),
        [pltpu.VMEM((3, channels, 128), F32)],
        estimate(1.2),
    )


def final_body(other, layout, place_ref, qkv, dout_ref, split_ref, lanes_ref, keep_ref, *refs):
    half, rows, span = layout.half, layout.sub, layout.span
    found, refs = refs[:half], refs[half:]
    crossed, refs = (refs[:half], refs[half + 2 :]) if other else (None, refs)
    out_hbm, dfeat_hbm, partial, out_ref, dfeat_ref, spread, sems = refs
    most = span - 128
    side, _, _ = where_am_i(place_ref, layout)
    group = min(32, rows)
    keep = [keep_ref[2 + j : 3 + j, :] for j in range(2)]
    copies = []
    for turn in range(half):
        base = channel_block(place_ref, layout, turn, other) * rows
        block = rows_at(base, rows, rows)
        spread[...] = dot(split_ref[block, :], lanes_ref[...])

        def tile(index, _, turn=turn):
            local_rows = rows_at(index * group, group, group)
            pair = results(side, found[turn], crossed and crossed[turn], (local_rows, slice(None)))
            out_ref[turn, local_rows, :] = qkv[turn, 0, local_rows, :] * pair[0]
            y_out, dmixed = (f.astype(F32) for f in pair)
            grads = (
                dout_ref[turn, local_rows, :].astype(F32) * y_out,
                dmixed * qkv[turn, 2, local_rows, :].astype(F32),
                dmixed * qkv[turn, 1, local_rows, :].astype(F32),
            )
            for which in range(3):
                ahead = [pltpu.roll(grads[which], span - 1 - j, 1) * keep[j] for j in range(2)]
                taps = [spread[local_rows, (3 * which + j) * 128 : (3 * which + j + 1) * 128] for j in range(3)]
                for lane in range(0, span, 128):
                    total = taps[0] * grads[which][:, lane : lane + 128]
                    total = total + taps[1] * ahead[0][:, lane : lane + 128] + taps[2] * ahead[1][:, lane : lane + 128]
                    if lane == most:
                        partial[turn, which, local_rows, :] = total
                    else:
                        dfeat_ref[turn, which, local_rows, lane : lane + 128] = total.astype(BF16)
            return 0

        lax.fori_loop(0, rows // group, tile, 0, unroll=min(2, rows // group))
        copies.append(pltpu.make_async_copy(out_ref.at[turn], out_hbm.at[block, :], sems.at[turn, 0]))
        copies.append(
            pltpu.make_async_copy(dfeat_ref.at[turn], dfeat_hbm.at[:, block, pl.ds(0, most)], sems.at[turn, 1])
        )
        for copy in copies[-2:]:
            copy.start()
    for copy in copies:
        copy.wait()


def final(other, layout, place, gated, split, lane_sum, keep, found, crossed, earlier):
    half, span, channels, rows = layout.half, layout.span, layout.channels, layout.sub
    operands = [*gated, split, lane_sum, keep, *found]
    in_specs = [HELD] * len(operands)
    aliases = {}
    if other:
        operands += [*crossed, *earlier]
        in_specs += [HELD] * half + [IN_HBM] * 2
        aliases = {len(operands) - 1: 0, len(operands): 1}
    return run(
        functools.partial(final_body, other),
        layout,
        place,
        operands,
        [
            jax.ShapeDtypeStruct((channels, span), BF16),
            jax.ShapeDtypeStruct((3, channels, span), BF16),
            jax.ShapeDtypeStruct((half, 3, rows, 128), F32),
        ],
        [
            pltpu.VMEM((half, rows, span), BF16),
            pltpu.VMEM((half, 3, rows, span - 128), BF16),
            pltpu.VMEM((rows, 9 * 128), F32),
            pltpu.SemaphoreType.DMA((half, 2)),
        ],
        estimate(3.3),
        in_specs=in_specs,
        out_specs=[IN_HBM, IN_HBM, HELD],
        aliases=aliases,
    )


def finish_body(layout, place_ref, ahead_ref, taps_ref, edge_ref, part_main, part_other, dfeat_in, dfeat_hbm, *refs):
    rows_ref, placed, dfeat_ref, sems = refs
    half, rows, span = layout.half, layout.sub, layout.span
    for which in range(3):
        first, second = (ahead_ref[2 * which + k : 2 * which + k + 1, :] for k in range(2))
        one, two = (taps_ref[3 * which + k : 3 * which + k + 1, :] for k in (1, 2))
        for k, value in enumerate((one * first, two * second, two * first)):
            rows_ref[3 * which + k : 3 * which + k + 1, :] = value
    rows_ref[9:16, :] = jnp.zeros((7, layout.channels), F32)
    split = jnp.concatenate(three_parts(rows_ref[...]), axis=0).T.astype(BF16)
    placed[...] = dot(split, edge_ref[...])
    copies = []
    for turn in range(half):
        for other in range(2):
            block = rows_at(channel_block(place_ref, layout, turn, other) * rows, rows, rows)
            partial = part_other if other else part_main
            for which in range(3):
                value = partial[turn, which] + placed[block, which * 128 : (which + 1) * 128]
                dfeat_ref[which, block, :] = value.astype(BF16)
            target = dfeat_hbm.at[:, block, pl.ds(span - 128, 128)]
            copies.append(pltpu.make_async_copy(dfeat_ref.at[:, block, :], target, sems.at[2 * turn + other]))
            copies[-1].start()
    for copy in copies:
        copy.wait()


def finish(layout, place, ahead, taps_rows, edge, partials, dfeat):
    channels = layout.channels
    return run(
        finish_body,
        layout,
        place,
        (ahead, taps_rows, edge, *partials, dfeat),
        jax.ShapeDtypeStruct(dfeat.shape, BF16),
        [
            pltpu.VMEM((16, channels), F32),
            pltpu.VMEM((channels, 384), F32),
            pltpu.VMEM((3, channels, 128), BF16),
            pltpu.SemaphoreType.DMA((layout.parts,)),
        ],
        estimate(1.9),
        in_specs=[HELD] * 5 + [IN_HBM],
        out_specs=IN_HBM,
        aliases={6: 0},
    )


def swap(value, step, parts, axis="seq"):
    return lax.ppermute(value, axis, [(source, source ^ step) for source in range(parts)])


def around(value, steps, parts):
    return lax.ppermute(value, "seq", [(source, (source + steps) % parts) for source in range(parts)])


def local(features, dout, filters, taps, skip, lengths):
    parts = lax.axis_size("seq")
    _, channels, span = features.shape
    layout = Layout(parts, channels, span)
    half = layout.half
    place = jnp.stack([lax.axis_index("seq"), lax.axis_index("groups")]).astype(jnp.int32)
    tables = [jnp.asarray(t) for t in block_tables(span)]

    features, dout, filters = (pltpu.with_memory_space_constraint(a, pltpu.HBM) for a in (features, dout, filters))

    halo, own_filt, filt = pack(layout, place, features, filters)
    halo, filt = lax.optimization_barrier((around(halo, 1, parts), filt))
    filt = [swap(filt[step - 1], step, parts) for step in range(1, parts)]
    other = swap(jnp.concatenate(filt, axis=0), 1, 2, "groups")
    cols, split, keep, first_edge, last_edge, taps_rows, lanes = small(layout, place, lengths, taps, skip)
    gated_main, gated_other, firsts, cross, seconds = gate(
        layout, place, features, dout, halo, split, lanes, keep, first_edge
    )
    firsts = [firsts[0]] + [swap(firsts[step], step, parts) for step in range(1, half)]
    cross = [swap(cross[step], step + half, parts) for step in range(half)]
    seconds = [seconds[0]] + [swap(seconds[step], step, parts) for step in range(1, half)]

    known = filter_spectra(layout, place, tables[0], own_filt[0], filt)
    sent, near = cross_half(layout, place, tables, known, firsts)
    crossed = hold(layout, place, [swap(sent[step], step + half, parts) for step in range(half)])
    main = main_half(layout, place, cols, tables, known, near, firsts, cross)
    main = [main[0]] + [swap(main[step], step, parts) for step in range(1, half)]
    rest = other_half(layout, place, cols, tables, own_filt[1], other, seconds)
    rest = [rest[0]] + [swap(rest[step], step, parts) for step in range(1, half)]

    taken = (split, lanes, keep)
    out, dfeat, part_main = final(0, layout, place, gated_main, *taken, main, None, None)
    first = first_grads(layout, place, (*gated_main, *gated_other), main, rest, crossed)
    ahead = around(first, -1, parts)
    out, dfeat, part_other = final(1, layout, place, gated_other, *taken, rest, crossed, (out, dfeat))
    return out, finish(layout, place, ahead, taps_rows, last_edge, (part_main, part_other), dfeat)


def solution(mesh):
    in_specs = (
        P(None, ("chan", "sub"), ("groups", "seq")),
        P(("chan", "sub"), ("groups", "seq")),
        P(("chan", "sub"), "seq"),
        P(None, None, ("chan", "sub")),
        P(("chan", "sub")),
        P("groups"),
    )
    out_specs = (P(("chan", "sub"), ("groups", "seq")), P(None, ("chan", "sub"), ("groups", "seq")))
    return jax.shard_map(local, mesh=mesh, in_specs=in_specs, out_specs=out_specs, check_vma=False)
```

time: 223 us -> 64 us (0.29); the launches traced: 220 us -> 63.8 us
  matrix products: 84.5 us -> 0 us
  waiting for transfers between devices: 76.4 us -> 10.8 us
  Pallas kernels: 0 us -> 28.9 us
  local copies, waits for them, and re-layouts: 27.4 us -> 0.02 us
  other arithmetic: 14.5 us -> 0.1 us
  starting transfers between devices: 15.5 us -> 23.2 us
    dot_general x30 -> x0, matrix products: 84.5 us -> none  [the longest x3 8.84 us: forward_transform(): jnp.einsum('ckn,nm->ckm', turned_re, col_im, precision=HIGHEST)]
    all_to_all x2 -> x0, waiting for transfers between devices: 71 us -> none  [the longest x1 45.9 us: to_channels(): lax.all_to_all(stacked, 'seq', split_axis=1, concat_axis=2, tiled=True)]
    pallas_call x0 -> x12, Pallas kernels: none -> 28.9 us  [run(): pl.pallas_call(functools.partial(body, layout), out_shape=outs, in_specs=...]
    ppermute x2 -> x14, starting transfers between devices: 6.22 us -> 23.2 us  [the longest x12 18.1 us: swap(): lax.ppermute(value, axis, [(source, source ^ step) for source in range(pa...]
    all_to_all x2 -> x0, starting transfers between devices: 9.25 us -> none  [the longest x1 5.73 us: to_channels(): lax.all_to_all(stacked, 'seq', split_axis=1, concat_axis=2, tiled=True)]
    convert_element_type x6 -> x0, other arithmetic: 8.64 us -> none  [the longest x1 3.92 us: local(): short_backward(grads_ext, taps, offsets_ext).astype(jnp.bfloat16)]
    slice x8 -> x0, local copies, waits for them, and re-layouts: 6.3 us -> none  [the longest x2 3.27 us: local(): ahead = shifted(grads[:, :, :margin], 'seq', -1)]
    ppermute x2 -> x14, waiting for transfers between devices: 5.39 us -> 10.8 us  [the longest x12 8.09 us: swap(): lax.ppermute(value, axis, [(source, source ^ step) for source in range(pa...]
  transfers between devices with their start and end apart: 4 -> 14, of which waited for: 4 -> 5; matrix products, arithmetic and copies ran while one was open for 1% -> 0% of each run, Pallas kernels for 0% -> 37%
where the time goes in v5:
time: 64 us; the launch traced here: 63.8 us
  Pallas kernels  28.9 us (45%)
  starting transfers between devices  23.2 us (36%)
  waiting for transfers between devices  10.8 us (17%)
  between operations  0.76 us (1%)
    pallas_call x12, Pallas kernels, run(): pl.pallas_call(functools.partial(body, layout), out_shape=outs, in_specs=...  28.9 us
    ppermute x12, starting transfers between devices, swap(): lax.ppermute(value, axis, [(source, source ^ step) for source in range(pa...  18.1 us
    ppermute x12, waiting for transfers between devices, swap(): lax.ppermute(value, axis, [(source, source ^ step) for source in range(pa...  8.09 us
    ppermute x2, starting transfers between devices, around(): lax.ppermute(value, 'seq', [(source, (source + steps) % parts) for source...  5.08 us
    ppermute x2, waiting for transfers between devices, around(): lax.ppermute(value, 'seq', [(source, (source + steps) % parts) for source...  2.76 us
  transfers between devices with their start and end apart: 14, of which 5 were waited for; matrix products, arithmetic and copies ran while one was open for 0% of the time, Pallas kernels for 37%

profile of v5, /device:TPU:0, one launch (start us, length us, event | category | flops | bytes accessed | tf_op | source)
XLA Modules:
  0.0 63.8 jit_solution(12797468744720407566)
XLA Ops:
  0.6 0.1 pad_add_fusion.place_ref
  0.7 2.0 %shard_map.95 = (bf16[16,1024]{1,0:T(8,128)(2,1)S(1)}, bf16[256,256]{1,0:T(8,128)(2,1)S(1)}, bf16[256,256]{1,0:T(8,128)(2,1)S(1)}, bf16[256,256]{1,0:T(8,128)(2,...) custom-call(s32[2]{0:T(128)S(1)} %pad_add_fusion.place_ref, bf16[3,1024,256]{2,1,0:T(8,128)(2,1)} %feat_hbm.3, ...), custom_call_target="tpu_custom_call" | custom-call | flops 1000000000 | tf_op jit(solution)/shard_map/pallas_call | solution.py:78
  2.7 3.1 %collective-permute-start = (bf16[16,1024]{1,0:T(8,128)(2,1)S(1)}, bf16[16,1024]{1,0:T(8,128)(2,1)S(1)}, u32[]{:S(2)}, u32[]{:S(2)}) collective-permute-start(bf16[16,1024]{1,0:T(8,128)(2,1)S(1)} %get-tuple-element.44), channel_id=1, source_target_pairs={{0,4},{4,8},{8,12},{12,0},{1,5},{5,9},{9,13},{13,1},{2,6},{6,10},{... | collective-permute-start | bytes 98312 | tf_op jit(solution)/shard_map/ppermute | solution.py:777
  5.8 1.1 %shard_map.96 = (f32[1024,16]{1,0:T(8,128)S(1)}, bf16[1024,48]{1,0:T(8,128)(2,1)S(1)}, f32[8,256]{1,0:T(8,128)S(1)}, bf16[16,768]{1,0:T(8,128)(2,1)S(1)}, bf16[4...) custom-call(s32[2]{0:T(128)S(1)} %pad_add_fusion.place_ref, s32[16]{0:T(128)S(1)} %copy-done.3, ...), custom_call_target="tpu_custom_call" | custom-call | flops 600000000 | tf_op jit(solution)/shard_map/pallas_call | solution.py:78
  7.0 2.8 %collective-permute-done.halo_ref = bf16[16,1024]{1,0:T(8,128)(2,1)S(1)} collective-permute-done((bf16[16,1024]{1,0:T(8,128)(2,1)S(1)}, bf16[16,1024]{1,0:T(8,128)(2,1)S(1)}, u32[]{:S(2)}, u32[]{:S(2)}) %collective-permute-start) | collective-permute-done | bytes 32800 | tf_op jit(solution)/shard_map/ppermute | solution.py:777
  9.7 0.0 collective-permute-start.1
  9.7 2.6 %collective-permute-start.2 = (bf16[256,256]{1,0:T(8,128)(2,1)S(1)}, bf16[256,256]{1,0:T(8,128)(2,1)S(1)}, u32[]{:S(2)}, u32[]{:S(2)}) collective-permute-start(bf16[256,256]{1,0:T(8,128)(2,1)S(1)} %get-tuple-element.58), channel_id=1, source_target_pairs={{0,8},{4,12},{8,0},{12,4},{1,9},{5,13},{9,1},{13,5},{2,10},{6,14},... | collective-permute-start | bytes 393224 | tf_op jit(solution)/shard_map/ppermute | solution.py:773
  12.3 1.8 %collective-permute-start.3 = (bf16[256,256]{1,0:T(8,128)(2,1)S(1)}, bf16[256,256]{1,0:T(8,128)(2,1)S(1)}, u32[]{:S(2)}, u32[]{:S(2)}) collective-permute-start(bf16[256,256]{1,0:T(8,128)(2,1)S(1)} %get-tuple-element.59), channel_id=1, source_target_pairs={{0,12},{4,8},{8,4},{12,0},{1,13},{5,9},{9,5},{13,1},{2,14},{6,10},... | collective-permute-start | bytes 393224 | tf_op jit(solution)/shard_map/ppermute | solution.py:773
  14.1 5.7 %shard_map.97 = (bf16[2,3,256,256]{3,2,1,0:T(8,128)(2,1)S(1)}, bf16[2,256,256]{2,1,0:T(8,128)(2,1)S(1)}, bf16[2,3,256,256]{3,2,1,0:T(8,128)(2,1)S(1)}, bf16[2,25...) custom-call(s32[2]{0:T(128)S(1)} %pad_add_fusion.place_ref, ...), custom_call_target="tpu_custom_call" | custom-call | flops 2849999872 | tf_op jit(solution)/shard_map/pallas_call | solution.py:78
  19.8 0.1 collective-permute-start.7
  19.9 2.2 %collective-permute-done.2.rest_1_ = bf16[256,256]{1,0:T(8,128)(2,1)S(1)} collective-permute-done((bf16[256,256]{1,0:T(8,128)(2,1)S(1)}, bf16[256,256]{1,0:T(8,128)(2,1)S(1)}, u32[]{:S(2)}, u32[]{:S(2)}) %collective-permute-start.2) | collective-permute-done | bytes 131104 | tf_op jit(solution)/shard_map/ppermute | solution.py:773
  22.1 0.0 collective-permute-done.3.rest_2_
  22.1 1.6 %collective-permute-start.4 = (bf16[768,256]{1,0:T(8,128)(2,1)S(1)}, bf16[768,256]{1,0:T(8,128)(2,1)S(1)}, u32[]{:S(2)}, u32[]{:S(2)}) collective-permute-start(bf16[768,256]{1,0:T(8,128)(2,1)S(1)} %pad_maximum_fusion), channel_id=1, source_target_pairs={{0,16},{16,0},{1,17},{17,1},{2,18},{18,2},{3,19},{19,3},{4,20},{20... | collective-permute-start | bytes 1179656 | tf_op jit(solution)/shard_map/ppermute | solution.py:773
  23.7 2.4 %collective-permute-start.10 = (bf16[256,256]{1,0:T(8,128)(2,1)S(1)}, bf16[256,256]{1,0:T(8,128)(2,1)S(1)}, u32[]{:S(2)}, u32[]{:S(2)}) collective-permute-start(bf16[256,256]{1,0:T(8,128)(2,1)S(1)} %get-tuple-element.74), channel_id=1, source_target_pairs={{0,8},{4,12},{8,0},{12,4},{1,9},{5,13},{9,1},{13,5},{2,10},{6,14},... | collective-permute-start | bytes 393224 | tf_op jit(solution)/shard_map/ppermute | solution.py:773
  26.1 1.9 %collective-permute-start.11 = (bf16[256,256]{1,0:T(8,128)(2,1)S(1)}, bf16[256,256]{1,0:T(8,128)(2,1)S(1)}, u32[]{:S(2)}, u32[]{:S(2)}) collective-permute-start(bf16[256,256]{1,0:T(8,128)(2,1)S(1)} %get-tuple-element.75), channel_id=1, source_target_pairs={{0,12},{4,8},{8,4},{12,0},{1,13},{5,9},{9,5},{13,1},{2,14},{6,10},... | collective-permute-start | bytes 393224 | tf_op jit(solution)/shard_map/ppermute | solution.py:773
  28.0 1.4 %shard_map.99.known = f32[1024,512]{1,0:T(8,128)S(1)} custom-call(s32[2]{0:T(128)S(1)} %pad_add_fusion.place_ref, bf16[512,512]{1,0:T(8,128)(2,1)S(1)} %copy-done, bf16[256,256]{1,0:T(8,128)(2,1)S(1)} %get-tuple-element.64.filt_ref, bf16[256,256]{1,0:T(8,128)(2,1)S(1)} %collective-permute-done.1.rest_0_, ...), custom_call_target="tpu_custom_call" | custom-call | flops 750000000 | tf_op jit(solution)/shard_map/pallas_call | solution.py:78
  29.5 0.9 %collective-permute-done.7.rest_1_ = bf16[2,256,256]{2,1,0:T(8,128)(2,1)S(1)} collective-permute-done((bf16[2,256,256]{2,1,0:T(8,128)(2,1)S(1)}, bf16[2,256,256]{2,1,0:T(8,128)(2,1)S(1)}, u32[]{:S(2)}, u32[]{:S(2)}) %collective-permute-start.7) | collective-permute-done | bytes 262176 | tf_op jit(solution)/shard_map/ppermute | solution.py:773
  30.4 2.1 %shard_map.100 = (bf16[256,256]{1,0:T(8,128)(2,1)S(1)}, bf16[256,256]{1,0:T(8,128)(2,1)S(1)}, f32[512,512]{1,0:T(8,128)S(1)}) custom-call(s32[2]{0:T(128)S(1)} %pad_add_fusion.place_ref, bf16[512,512]{1,0:T(8,128)(2,1)S(1)} %copy-done, bf16[512,256]{1,0:T(8,128)(2,1)S(1)} %copy-done.4, f32[1024,512]{1,0:T(8,128)S(1)} %shard_map.99.known, ...), custom_call_target="tpu_custom_call" | custom-call | flops 1000000000 | tf_op jit(solution)/shard_map/pallas_call | solution.py:78
  32.5 1.6 %collective-permute-start.8 = (bf16[256,256]{1,0:T(8,128)(2,1)S(1)}, bf16[256,256]{1,0:T(8,128)(2,1)S(1)}, u32[]{:S(2)}, u32[]{:S(2)}) collective-permute-start(bf16[256,256]{1,0:T(8,128)(2,1)S(1)} %get-tuple-element.67), channel_id=1, source_target_pairs={{0,8},{4,12},{8,0},{12,4},{1,9},{5,13},{9,1},{13,5},{2,10},{6,14},... | collective-permute-start | bytes 393224 | tf_op jit(solution)/shard_map/ppermute | solution.py:773
  34.1 1.3 %collective-permute-done.10.rest_2_ = bf16[256,256]{1,0:T(8,128)(2,1)S(1)} collective-permute-done((bf16[256,256]{1,0:T(8,128)(2,1)S(1)}, bf16[256,256]{1,0:T(8,128)(2,1)S(1)}, u32[]{:S(2)}, u32[]{:S(2)}) %collective-permute-start.10) | collective-permute-done | bytes 131104 | tf_op jit(solution)/shard_map/ppermute | solution.py:773
  35.4 1.9 %collective-permute-start.9 = (bf16[256,256]{1,0:T(8,128)(2,1)S(1)}, bf16[256,256]{1,0:T(8,128)(2,1)S(1)}, u32[]{:S(2)}, u32[]{:S(2)}) collective-permute-start(bf16[256,256]{1,0:T(8,128)(2,1)S(1)} %get-tuple-element.68), channel_id=1, source_target_pairs={{0,12},{4,8},{8,4},{12,0},{1,13},{5,9},{9,5},{13,1},{2,14},{6,10},... | collective-permute-start | bytes 393224 | tf_op jit(solution)/shard_map/ppermute | solution.py:773
  37.3 3.0 %shard_map.102 = (bf16[2,256,256]{2,1,0:T(8,128)(2,1)S(1)}, bf16[2,256,256]{2,1,0:T(8,128)(2,1)S(1)}) custom-call(s32[2]{0:T(128)S(1)} %pad_add_fusion.place_ref, f32[1024,16]{1,0:T(8,128)S(1)} %get-tuple-element.55.cols_ref, bf16[512,512]{1,0:T(8,128)(2,1)S(1)} %copy-done, bf16[512,256]{1,0:T(8,128)(2,1)S(1)} %copy-done.4, ...), custom_call_target="tpu_custom_call" | custom-call | flops 1500000000 | tf_op jit(solution)/shard_map/pallas_call | solution.py:78
  40.3 4.1 %collective-permute-start.12 = (bf16[2,256,256]{2,1,0:T(8,128)(2,1)S(1)}, bf16[2,256,256]{2,1,0:T(8,128)(2,1)S(1)}, u32[]{:S(2)}, u32[]{:S(2)}) collective-permute-start(bf16[2,256,256]{2,1,0:T(8,128)(2,1)S(1)} %get-tuple-element.77), channel_id=1, source_target_pairs={{0,4},{4,0},{8,12},{12,8},{1,5},{5,1},{9,13},{13,9},{2,6},{6,2},{1... | collective-permute-start | bytes 786440 | tf_op jit(solution)/shard_map/ppermute | solution.py:773
  44.5 3.1 %shard_map.98 = (bf16[2,256,256]{2,1,0:T(8,128)(2,1)S(1)}, bf16[2,256,256]{2,1,0:T(8,128)(2,1)S(1)}) custom-call(s32[2]{0:T(128)S(1)} %pad_add_fusion.place_ref, f32[1024,16]{1,0:T(8,128)S(1)} %get-tuple-element.55.cols_ref, bf16[512,512]{1,0:T(8,128)(2,1)S(1)} %copy-done, bf16[512,256]{1,0:T(8,128)(2,1)S(1)} %copy-done.4, ...), custom_call_target="tpu_custom_call" | custom-call | flops 1500000000 | tf_op jit(solution)/shard_map/pallas_call | solution.py:78
  47.5 0.1 collective-permute-start.6
  47.6 0.5 shard_map.101
  48.2 3.7 %collective-permute-done.12.refs_1_ = bf16[2,256,256]{2,1,0:T(8,128)(2,1)S(1)} collective-permute-done((bf16[2,256,256]{2,1,0:T(8,128)(2,1)S(1)}, bf16[2,256,256]{2,1,0:T(8,128)(2,1)S(1)}, u32[]{:S(2)}, u32[]{:S(2)}) %collective-permute-start.12) | collective-permute-done | bytes 262176 | tf_op jit(solution)/shard_map/ppermute | solution.py:773
  51.9 3.3 %shard_map.103 = (bf16[1024,256]{1,0:T(8,128)(2,1)}, bf16[3,1024,256]{2,1,0:T(8,128)(2,1)}, f32[2,3,256,128]{3,2,1,0:T(8,128)S(1)}) custom-call(s32[2]{0:T(128)S(1)} %pad_add_fusion.place_ref, bf16[2,3,256,256]{3,2,1,0:T(8,128)(2,1)S(1)} %get-tuple-element.71.qkv.qkv_main, bf16[2,256,256]{2,1,0:T(8,128)(2,1)S(1)} %get-tuple-element.72.dout_ref.dout_main, ...), custom_call_target="tpu_custom_call" | custom-call | flops 1650000000 | tf_op jit(solution)/shard_map/pallas_call | solution.py:78
  55.3 1.3 %shard_map.105 = f32[8,1024]{1,0:T(8,128)S(1)} custom-call(s32[2]{0:T(128)S(1)} %pad_add_fusion.place_ref, bf16[2,3,256,256]{3,2,1,0:T(8,128)(2,1)S(1)} %get-tuple-element.71.qkv.qkv_main, bf16[2,256,256]{2,1,0:T(8,128)(2,1)S(1)} %get-tuple-element.72.dout_ref.dout_main, bf16[2,3,256,256]{3,2,1,0:T(8,128)(2,1)S(1)} %get-tuple-element.53.qkv.qkv_other, ...), custom_call_target="tpu_custom_call" | custom-call | flops 600000000 | tf_op jit(solution)/shard_map/pallas_call | solution.py:78
  56.5 2.0 %collective-permute-start.13 = (f32[8,1024]{1,0:T(8,128)S(1)}, f32[8,1024]{1,0:T(8,128)S(1)}, u32[]{:S(2)}, u32[]{:S(2)}) collective-permute-start(f32[8,1024]{1,0:T(8,128)S(1)} %shard_map.105), channel_id=1, source_target_pairs={{0,12},{4,0},{8,4},{12,8},{1,13},{5,1},{9,5},{13,9},{2,14},{6,2},{... | collective-permute-start | bytes 98312 | tf_op jit(solution)/shard_map/ppermute | solution.py:777
  58.5 3.4 %shard_map.104 = (bf16[1024,256]{1,0:T(8,128)(2,1)}, bf16[3,1024,256]{2,1,0:T(8,128)(2,1)}, f32[2,3,256,128]{3,2,1,0:T(8,128)S(1)}) custom-call(s32[2]{0:T(128)S(1)} %pad_add_fusion.place_ref, bf16[2,3,256,256]{3,2,1,0:T(8,128)(2,1)S(1)} %get-tuple-element.53.qkv.qkv_other, ...), custom_call_target="tpu_custom_call", output_to_operand_aliasing={{0}: (10, {}), {1}: (11, {})} | custom-call | flops 1650000000 | tf_op jit(solution)/shard_map/pallas_call | solution.py:78
  61.9 1.9 %shard_map.106 = bf16[3,1024,256]{2,1,0:T(8,128)(2,1)} custom-call(s32[2]{0:T(128)S(1)} %pad_add_fusion.place_ref, f32[8,1024]{1,0:T(8,128)S(1)} %collective-permute-done.13.ahead_ref, f32[16,1024]{1,0:T(8,128)S(1)} %get-tuple-element.81.taps_ref, bf16[48,384]{1,0:T(8,128)(2,1)S(1)} %get-tuple-element.82.edge_ref, ...), custom_call_target="tpu_custom_call", output_to_operand_aliasing={{}: (6, {})} | custom-call | flops 950000000 | tf_op jit(solution)/shard_map/pallas_call | solution.py:78
  (20 shorter events, 0.1 us)
Async XLA Ops:
  0.7 5.1 %copy-start.1 = (f32[3,3,1024]{2,1,0:T(4,128)S(1)}, f32[3,3,1024]{2,1,0:T(4,128)}, u32[]{:S(2)}) copy-start(f32[3,3,1024]{2,1,0:T(4,128)} %taps_ref.1) | copy-start | bytes 110596
  0.7 5.1 %copy-start.2 = (f32[1024]{0:T(1024)S(1)}, f32[1024]{0:T(1024)}, u32[]{:S(2)}) copy-start(f32[1024]{0:T(1024)} %param.12) | copy-start | bytes 12292
  0.7 5.1 %copy-start.3 = (s32[16]{0:T(128)S(1)}, s32[16]{0:T(128)}, u32[]{:S(2)}) copy-start(s32[16]{0:T(128)} %lengths_ref.1) | copy-start | bytes 196
  2.7 7.0 %collective-permute-start = (bf16[16,1024]{1,0:T(8,128)(2,1)S(1)}, bf16[16,1024]{1,0:T(8,128)(2,1)S(1)}, u32[]{:S(2)}, u32[]{:S(2)}) collective-permute-start(bf16[16,1024]{1,0:T(8,128)(2,1)S(1)} %get-tuple-element.44), channel_id=1, source_target_pairs={{0,4},{4,8},{8,12},{12,0},{1,5},{5,9},{9,13},{13,1},{2,6},{6,10},{... | collective-permute-start | bytes 98312 | tf_op jit(solution)/shard_map/ppermute | solution.py:777
  9.7 10.2 %collective-permute-start.1 = (bf16[256,256]{1,0:T(8,128)(2,1)S(1)}, bf16[256,256]{1,0:T(8,128)(2,1)S(1)}, u32[]{:S(2)}, u32[]{:S(2)}) collective-permute-start(bf16[256,256]{1,0:T(8,128)(2,1)S(1)} %get-tuple-element.57), channel_id=1, source_target_pairs={{0,4},{4,0},{8,12},{12,8},{1,5},{5,1},{9,13},{13,9},{2,6},{6,2},{1... | collective-permute-start | bytes 393224 | tf_op jit(solution)/shard_map/ppermute | solution.py:773
  9.7 12.3 %collective-permute-start.2 = (bf16[256,256]{1,0:T(8,128)(2,1)S(1)}, bf16[256,256]{1,0:T(8,128)(2,1)S(1)}, u32[]{:S(2)}, u32[]{:S(2)}) collective-permute-start(bf16[256,256]{1,0:T(8,128)(2,1)S(1)} %get-tuple-element.58), channel_id=1, source_target_pairs={{0,8},{4,12},{8,0},{12,4},{1,9},{5,13},{9,1},{13,5},{2,10},{6,14},... | collective-permute-start | bytes 393224 | tf_op jit(solution)/shard_map/ppermute | solution.py:773
  12.3 9.8 %collective-permute-start.3 = (bf16[256,256]{1,0:T(8,128)(2,1)S(1)}, bf16[256,256]{1,0:T(8,128)(2,1)S(1)}, u32[]{:S(2)}, u32[]{:S(2)}) collective-permute-start(bf16[256,256]{1,0:T(8,128)(2,1)S(1)} %get-tuple-element.59), channel_id=1, source_target_pairs={{0,12},{4,8},{8,4},{12,0},{1,13},{5,9},{9,5},{13,1},{2,14},{6,10},... | collective-permute-start | bytes 393224 | tf_op jit(solution)/shard_map/ppermute | solution.py:773
  14.1 13.9 %copy-start = (bf16[512,512]{1,0:T(8,128)(2,1)S(1)}, bf16[512,512]{1,0:T(8,128)(2,1)}, u32[]{:S(2)}) copy-start(bf16[512,512]{1,0:T(8,128)(2,1)} %constant.15.clone.forward_ref) | copy-start | bytes 1572868
  19.8 10.5 %collective-permute-start.7 = (bf16[2,256,256]{2,1,0:T(8,128)(2,1)S(1)}, bf16[2,256,256]{2,1,0:T(8,128)(2,1)S(1)}, u32[]{:S(2)}, u32[]{:S(2)}) collective-permute-start(bf16[2,256,256]{2,1,0:T(8,128)(2,1)S(1)} %get-tuple-element.66), channel_id=1, source_target_pairs={{0,4},{4,0},{8,12},{12,8},{1,5},{5,1},{9,13},{13,9},{2,6},{6,2},{1... | collective-permute-start | bytes 786440 | tf_op jit(solution)/shard_map/ppermute | solution.py:773
  22.1 22.3 %collective-permute-start.4 = (bf16[768,256]{1,0:T(8,128)(2,1)S(1)}, bf16[768,256]{1,0:T(8,128)(2,1)S(1)}, u32[]{:S(2)}, u32[]{:S(2)}) collective-permute-start(bf16[768,256]{1,0:T(8,128)(2,1)S(1)} %pad_maximum_fusion), channel_id=1, source_target_pairs={{0,16},{16,0},{1,17},{17,1},{2,18},{18,2},{3,19},{19,3},{4,20},{20... | collective-permute-start | bytes 1179656 | tf_op jit(solution)/shard_map/ppermute | solution.py:773
  23.7 11.7 %collective-permute-start.10 = (bf16[256,256]{1,0:T(8,128)(2,1)S(1)}, bf16[256,256]{1,0:T(8,128)(2,1)S(1)}, u32[]{:S(2)}, u32[]{:S(2)}) collective-permute-start(bf16[256,256]{1,0:T(8,128)(2,1)S(1)} %get-tuple-element.74), channel_id=1, source_target_pairs={{0,8},{4,12},{8,0},{12,4},{1,9},{5,13},{9,1},{13,5},{2,10},{6,14},... | collective-permute-start | bytes 393224 | tf_op jit(solution)/shard_map/ppermute | solution.py:773
  26.1 11.2 %collective-permute-start.11 = (bf16[256,256]{1,0:T(8,128)(2,1)S(1)}, bf16[256,256]{1,0:T(8,128)(2,1)S(1)}, u32[]{:S(2)}, u32[]{:S(2)}) collective-permute-start(bf16[256,256]{1,0:T(8,128)(2,1)S(1)} %get-tuple-element.75), channel_id=1, source_target_pairs={{0,12},{4,8},{8,4},{12,0},{1,13},{5,9},{9,5},{13,1},{2,14},{6,10},... | collective-permute-start | bytes 393224 | tf_op jit(solution)/shard_map/ppermute | solution.py:773
  28.0 16.4 %collective-permute-start.5 = (bf16[2,256,256]{2,1,0:T(8,128)(2,1)S(1)}, bf16[2,256,256]{2,1,0:T(8,128)(2,1)S(1)}, u32[]{:S(2)}, u32[]{:S(2)}) collective-permute-start(bf16[2,256,256]{2,1,0:T(8,128)(2,1)S(1)} %get-tuple-element.61), channel_id=1, source_target_pairs={{0,4},{4,0},{8,12},{12,8},{1,5},{5,1},{9,13},{13,9},{2,6},{6,2},{1... | collective-permute-start | bytes 786440 | tf_op jit(solution)/shard_map/ppermute | solution.py:773
  28.0 2.4 %copy-start.4 = (bf16[512,256]{1,0:T(8,128)(2,1)S(1)}, bf16[512,256]{1,0:T(8,128)(2,1)}, u32[]{:S(2)}) copy-start(bf16[512,256]{1,0:T(8,128)(2,1)} %constant.16.clone.inverse_ref) | copy-start | bytes 786436
  32.5 15.1 %collective-permute-start.8 = (bf16[256,256]{1,0:T(8,128)(2,1)S(1)}, bf16[256,256]{1,0:T(8,128)(2,1)S(1)}, u32[]{:S(2)}, u32[]{:S(2)}) collective-permute-start(bf16[256,256]{1,0:T(8,128)(2,1)S(1)} %get-tuple-element.67), channel_id=1, source_target_pairs={{0,8},{4,12},{8,0},{12,4},{1,9},{5,13},{9,1},{13,5},{2,10},{6,14},... | collective-permute-start | bytes 393224 | tf_op jit(solution)/shard_map/ppermute | solution.py:773
  35.4 12.2 %collective-permute-start.9 = (bf16[256,256]{1,0:T(8,128)(2,1)S(1)}, bf16[256,256]{1,0:T(8,128)(2,1)S(1)}, u32[]{:S(2)}, u32[]{:S(2)}) collective-permute-start(bf16[256,256]{1,0:T(8,128)(2,1)S(1)} %get-tuple-element.68), channel_id=1, source_target_pairs={{0,12},{4,8},{8,4},{12,0},{1,13},{5,9},{9,5},{13,1},{2,14},{6,10},... | collective-permute-start | bytes 393224 | tf_op jit(solution)/shard_map/ppermute | solution.py:773
  40.3 11.6 %collective-permute-start.12 = (bf16[2,256,256]{2,1,0:T(8,128)(2,1)S(1)}, bf16[2,256,256]{2,1,0:T(8,128)(2,1)S(1)}, u32[]{:S(2)}, u32[]{:S(2)}) collective-permute-start(bf16[2,256,256]{2,1,0:T(8,128)(2,1)S(1)} %get-tuple-element.77), channel_id=1, source_target_pairs={{0,4},{4,0},{8,12},{12,8},{1,5},{5,1},{9,13},{13,9},{2,6},{6,2},{1... | collective-permute-start | bytes 786440 | tf_op jit(solution)/shard_map/ppermute | solution.py:773
  47.5 7.7 %collective-permute-start.6 = (bf16[2,256,256]{2,1,0:T(8,128)(2,1)S(1)}, bf16[2,256,256]{2,1,0:T(8,128)(2,1)S(1)}, u32[]{:S(2)}, u32[]{:S(2)}) collective-permute-start(bf16[2,256,256]{2,1,0:T(8,128)(2,1)S(1)} %get-tuple-element.63), channel_id=1, source_target_pairs={{0,4},{4,0},{8,12},{12,8},{1,5},{5,1},{9,13},{13,9},{2,6},{6,2},{1... | collective-permute-start | bytes 786440 | tf_op jit(solution)/shard_map/ppermute | solution.py:773
  56.5 5.4 %collective-permute-start.13 = (f32[8,1024]{1,0:T(8,128)S(1)}, f32[8,1024]{1,0:T(8,128)S(1)}, u32[]{:S(2)}, u32[]{:S(2)}) collective-permute-start(f32[8,1024]{1,0:T(8,128)S(1)} %shard_map.105), channel_id=1, source_target_pairs={{0,12},{4,0},{8,4},{12,8},{1,13},{5,1},{9,5},{13,9},{2,14},{6,2},{... | collective-permute-start | bytes 98312 | tf_op jit(solution)/shard_map/ppermute | solution.py:777

commit v6 on v5

--- a/solution.py
+++ b/solution.py
@@ -11,7 +11,7 @@
 
 BF16 = jnp.bfloat16
 F32 = jnp.float32
-SHARE = 0.5
+SHARE = 0.6
 VMEM_LIMIT = 24 * 1024 * 1024
 SCALARS = pl.BlockSpec(memory_space=pltpu.SMEM)
 IN_HBM = pl.BlockSpec(memory_space=pltpu.HBM)
@@ -209,7 +209,7 @@
     gated, firsts, cross, seconds = (rest[:4], *(rest[4 + k * half : 4 + (k + 1) * half] for k in range(3)))
     feat_ref, ends_of, spread, ends, sems = rest[4 + 3 * half :]
     side, _, _ = where_am_i(place_ref, layout)
-    group = min(32, rows)
+    group = min(64, rows)
     steps = [(turn, other) for other in range(2) for turn in range(half)]
     copies = []
     for k, (turn, other) in enumerate(steps):
@@ -256,7 +256,7 @@
                 cross[turn][local_rows, :] = first
             return 0
 
-        lax.fori_loop(0, rows // group, tile, 0, unroll=min(2, rows // group))
+        lax.fori_loop(0, rows // group, tile, 0, unroll=rows // group)
 
 
 def gate(layout, place, features, dout, halo, split, lanes, keep, edge):
@@ -276,7 +276,7 @@
             pltpu.VMEM((rows, 768), F32),
             pltpu.SemaphoreType.DMA((2 * half, 2)),
         ],
-        estimate(5.7),
+        estimate(12.0),
         in_specs=[IN_HBM] * 2 + [HELD] * 5,
     )
     return found[0:2], found[2:4], found[4 : 4 + half], found[4 + half : 4 + 2 * half], found[4 + 2 * half :]
@@ -337,7 +337,7 @@
         forward(raw, spec, index * chunk, index * chunk, chunk, forward_ref)
         return 0
 
-    lax.fori_loop(0, parts * sub // chunk, transform, 0)
+    lax.fori_loop(0, parts * sub // chunk, transform, 0, unroll=True)
 
 
 def filter_spectra(layout, place, table, own, filt):
@@ -349,7 +349,7 @@
         (table, own, *filt),
         jax.ShapeDtypeStruct((rows, 2 * span), F32),
         [pltpu.VMEM((rows, span), BF16)],
-        estimate(1.5),
+        estimate(0.3),
     )
 
 
@@ -390,11 +390,11 @@
 
     @pl.when(side == 0)
     def _():
-        lax.fori_loop(0, sub // group, lambda k, _: products(k, True), 0)
+        lax.fori_loop(0, sub // group, lambda k, _: products(k, True), 0, unroll=min(4, sub // group))
 
     @pl.when(side == 1)
     def _():
-        lax.fori_loop(0, sub // group, lambda k, _: products(k, False), 0)
+        lax.fori_loop(0, sub // group, lambda k, _: products(k, False), 0, unroll=min(4, sub // group))
 
     back[...] = dot(ready[...], inverse_ref[...])
     for step in range(half):
@@ -415,7 +415,7 @@
             pltpu.VMEM((rows, 2 * span), BF16),
             pltpu.VMEM((rows, span), F32),
         ],
-        estimate(2.0),
+        estimate(0.3),
     )
     return found[:half], found[half]
 
@@ -424,10 +424,10 @@
     pass
 
 
-def hold(layout, place, arrays):
+def hold(layout, place, arrays, after):
     outs = [jax.ShapeDtypeStruct(a.shape, a.dtype) for a in arrays]
     aliases = {1 + k: k for k in range(len(arrays))}
-    return run(hold_body, layout, place, arrays, outs, [], estimate(4.0), aliases=aliases)
+    return run(hold_body, layout, place, [*arrays, after], outs, [], estimate(4.0), aliases=aliases)
 
 
 def main_body(layout, place_ref, cols_ref, forward_ref, inverse_ref, known, near_spec, *rest):
@@ -446,7 +446,7 @@
         forward(raw, spec, index * chunk, index * chunk, chunk, forward_ref)
         return 0
 
-    lax.fori_loop(0, block // chunk, transform, 0)
+    lax.fori_loop(0, block // chunk, transform, 0, unroll=True)
     group = 16
     zero = (jnp.zeros((group, span), F32),) * 2
 
@@ -490,11 +490,11 @@
 
     @pl.when(side == 0)
     def _():
-        lax.fori_loop(0, sub // group, lambda k, _: products(k, True), 0)
+        lax.fori_loop(0, sub // group, lambda k, _: products(k, True), 0, unroll=min(4, sub // group))
 
     @pl.when(side == 1)
     def _():
-        lax.fori_loop(0, sub // group, lambda k, _: products(k, False), 0)
+        lax.fori_loop(0, sub // group, lambda k, _: products(k, False), 0, unroll=min(4, sub // group))
 
     back[...] = dot(ready[...], inverse_ref[...])
     begin = channel_block(place_ref, layout, 0, 0) * sub
@@ -522,14 +522,14 @@
             pltpu.VMEM((2 * half * sub, 2 * span), BF16),
             pltpu.VMEM((2 * half * sub, span), F32),
         ],
-        estimate(3.0),
+        estimate(10.0),
     )
 
 
 def other_body(layout, place_ref, cols_ref, forward_ref, inverse_ref, filt_ref, other_ref, *rest):
     parts, half, sub, span = layout.parts, layout.half, layout.sub, layout.span
-    seconds, outs = rest[:half], rest[half : 2 * half]
-    raw, spec, ready, back = rest[2 * half :]
+    seconds, early, late = (rest[k * half : (k + 1) * half] for k in range(3))
+    raw, spec, ready, back = rest[3 * half :]
     side, own, _ = where_am_i(place_ref, layout)
     rank = place_ref[0]
     block, kind_rows = parts * sub, half * sub
@@ -548,7 +548,7 @@
         forward(raw, spec, source, kind * kind_rows, kind_rows, forward_ref)
         return 0
 
-    lax.fori_loop(0, 3, transform, 0)
+    lax.fori_loop(0, 3, transform, 0, unroll=True)
     group = 16
     zero = (jnp.zeros((group, span), F32),) * 2
 
@@ -571,7 +571,7 @@
             before = total
         return 0
 
-    lax.fori_loop(0, sub // group, products, 0)
+    lax.fori_loop(0, sub // group, products, 0, unroll=min(4, sub // group))
     back[...] = dot(ready[...], inverse_ref[...])
     skip = cols_ref[rows_at(begin, sub, sub), 9:10]
     for step in range(half):
@@ -580,30 +580,36 @@
             source = jnp.where(side == kind, 0, 1) * kind_rows + place
             value = back[rows_at(source, sub, sub), :]
             direct = seconds[step][kind].astype(F32)
-            outs[step][kind] = (value + skip * direct).astype(BF16)
+            found = (value + skip * direct).astype(BF16)
+            early[step][kind] = found[:, :128]
+            late[step][kind] = found[:, 128:]
 
 
 def other_half(layout, place, cols, tables, filters, other, seconds):
     half, sub, span, parts = layout.half, layout.sub, layout.span, layout.parts
     rows = 3 * half * sub
-    return run(
+    found = run(
         other_body,
         layout,
         place,
         (cols, *tables, filters, other, *seconds),
-        [jax.ShapeDtypeStruct((2, sub, span), BF16)] * half,
+        [jax.ShapeDtypeStruct((2, sub, w), BF16) for w in (128, span - 128) for _ in range(half)],
         [
             pltpu.VMEM(((parts + 2 * half) * sub, span), BF16),
             pltpu.VMEM((rows, 2 * span), F32),
             pltpu.VMEM((2 * half * sub, 2 * span), BF16),
             pltpu.VMEM((2 * half * sub, span), F32),
         ],
-        estimate(3.0),
-    )
+        estimate(8.0),
+    )
+    return found[:half], found[half:]
 
 
 def results(side, found, crossed, here):
-    plain, mixed = found[(0, *here)], found[(1, *here)]
+    if isinstance(found, tuple):
+        plain, mixed = (jnp.concatenate([part[(k, here[0])] for part in found], axis=1) for k in range(2))
+    else:
+        plain, mixed = found[(0, *here)], found[(1, *here)]
     if crossed is not None:
         mixed = (mixed.astype(F32) + crossed[here].astype(F32)).astype(BF16)
     return jnp.where(side == 0, plain, mixed), jnp.where(side == 0, mixed, plain)
@@ -638,18 +644,20 @@
         (*gated, *main, *rest, *crossed),
         jax.ShapeDtypeStruct((8, channels), F32),
         [pltpu.VMEM((3, channels, 128), F32)],
-        estimate(1.2),
+        estimate(6.0),
     )
 
 
 def final_body(other, layout, place_ref, qkv, dout_ref, split_ref, lanes_ref, keep_ref, *refs):
     half, rows, span = layout.half, layout.sub, layout.span
     found, refs = refs[:half], refs[half:]
+    if other:
+        found, refs = list(zip(found, refs[:half])), refs[half:]
     crossed, refs = (refs[:half], refs[half + 2 :]) if other else (None, refs)
     out_hbm, dfeat_hbm, partial, out_ref, dfeat_ref, spread, sems = refs
     most = span - 128
     side, _, _ = where_am_i(place_ref, layout)
-    group = min(32, rows)
+    group = min(64, rows)
     keep = [keep_ref[2 + j : 3 + j, :] for j in range(2)]
     copies = []
     for turn in range(half):
@@ -679,7 +687,7 @@
                         dfeat_ref[turn, which, local_rows, lane : lane + 128] = total.astype(BF16)
             return 0
 
-        lax.fori_loop(0, rows // group, tile, 0, unroll=min(2, rows // group))
+        lax.fori_loop(0, rows // group, tile, 0, unroll=rows // group)
         copies.append(pltpu.make_async_copy(out_ref.at[turn], out_hbm.at[block, :], sems.at[turn, 0]))
         copies.append(
             pltpu.make_async_copy(dfeat_ref.at[turn], dfeat_hbm.at[:, block, pl.ds(0, most)], sems.at[turn, 1])
@@ -788,7 +796,7 @@
     features, dout, filters = (pltpu.with_memory_space_constraint(a, pltpu.HBM) for a in (features, dout, filters))
 
     halo, own_filt, filt = pack(layout, place, features, filters)
-    halo, filt = lax.optimization_barrier((around(halo, 1, parts), filt))
+    halo = around(halo, 1, parts)
     filt = [swap(filt[step - 1], step, parts) for step in range(1, parts)]
     other = swap(jnp.concatenate(filt, axis=0), 1, 2, "groups")
     cols, split, keep, first_edge, last_edge, taps_rows, lanes = small(layout, place, lengths, taps, skip)
@@ -801,17 +809,19 @@
 
     known = filter_spectra(layout, place, tables[0], own_filt[0], filt)
     sent, near = cross_half(layout, place, tables, known, firsts)
-    crossed = hold(layout, place, [swap(sent[step], step + half, parts) for step in range(half)])
+    crossed = [swap(sent[step], step + half, parts) for step in range(half)]
     main = main_half(layout, place, cols, tables, known, near, firsts, cross)
     main = [main[0]] + [swap(main[step], step, parts) for step in range(1, half)]
-    rest = other_half(layout, place, cols, tables, own_filt[1], other, seconds)
-    rest = [rest[0]] + [swap(rest[step], step, parts) for step in range(1, half)]
+    early, late = other_half(layout, place, cols, tables, own_filt[1], other, seconds)
+    crossed = hold(layout, place, crossed, early[0])
+    early = [early[0]] + [swap(early[step], step, parts) for step in range(1, half)]
+    late = [late[0]] + [swap(late[step], step, parts) for step in range(1, half)]
 
     taken = (split, lanes, keep)
     out, dfeat, part_main = final(0, layout, place, gated_main, *taken, main, None, None)
-    first = first_grads(layout, place, (*gated_main, *gated_other), main, rest, crossed)
+    first = first_grads(layout, place, (*gated_main, *gated_other), main, early, crossed)
     ahead = around(first, -1, parts)
-    out, dfeat, part_other = final(1, layout, place, gated_other, *taken, rest, crossed, (out, dfeat))
+    out, dfeat, part_other = final(1, layout, place, gated_other, *taken, [*early, *late], crossed, (out, dfeat))
     return out, finish(layout, place, ahead, taps_rows, last_edge, (part_main, part_other), dfeat)
 
 

time: 64 us -> 58.7 us (0.917)
  Pallas kernels: 28.9 us -> 24.5 us
  starting transfers between devices: 23.2 us -> 21.1 us
  waiting for transfers between devices: 10.8 us -> 12 us
    pallas_call x12, Pallas kernels: 28.9 us -> 24.5 us  [run(): pl.pallas_call(functools.partial(body, layout), out_shape=outs, in_specs=...]
    ppermute x12 -> x13, waiting for transfers between devices: 8.09 us -> 12 us  [swap(): lax.ppermute(value, axis, [(source, source ^ step) for source in range(pa...]
    ppermute x2, waiting for transfers between devices: 2.76 us -> 0.01 us  [around(): lax.ppermute(value, 'seq', [(source, (source + steps) % parts) for source...]
    ppermute x12 -> x13, starting transfers between devices: 18.1 us -> 16.1 us  [swap(): lax.ppermute(value, axis, [(source, source ^ step) for source in range(pa...]
  transfers between devices with their start and end apart: 14 -> 15, of which waited for: 5 -> 5; matrix products, arithmetic and copies ran while one was open for 0% -> 0% of each run, Pallas kernels for 37% -> 35%
where the time goes in v6:
time: 58.7 us; the launch traced here: 58.5 us
  Pallas kernels  24.5 us (42%)
  starting transfers between devices  21.1 us (36%)
  waiting for transfers between devices  12 us (20%)
  between operations  0.78 us (1%)
    pallas_call x12, Pallas kernels, run(): pl.pallas_call(functools.partial(body, layout), out_shape=outs, in_specs=...  24.5 us
    ppermute x13, starting transfers between devices, swap(): lax.ppermute(value, axis, [(source, source ^ step) for source in range(pa...  16.1 us
    ppermute x13, waiting for transfers between devices, swap(): lax.ppermute(value, axis, [(source, source ^ step) for source in range(pa...  12 us
    ppermute x2, starting transfers between devices, around(): lax.ppermute(value, 'seq', [(source, (source + steps) % parts) for source...  4.95 us
  transfers between devices with their start and end apart: 15, of which 5 were waited for; matrix products, arithmetic and copies ran while one was open for 0% of the time, Pallas kernels for 35%

profile of v6, /device:TPU:0, one launch (start us, length us, event | category | flops | bytes accessed | tf_op | source)
XLA Modules:
  0.0 58.5 jit_solution(13661986846512903499)
XLA Ops:
  0.6 0.1 pad_add_fusion.place_ref
  0.7 2.0 %shard_map.95 = (bf16[16,1024]{1,0:T(8,128)(2,1)S(1)}, bf16[256,256]{1,0:T(8,128)(2,1)S(1)}, bf16[256,256]{1,0:T(8,128)(2,1)S(1)}, bf16[256,256]{1,0:T(8,128)(2,...) custom-call(s32[2]{0:T(128)S(1)} %pad_add_fusion.place_ref, bf16[3,1024,256]{2,1,0:T(8,128)(2,1)} %feat_hbm.3, ...), custom_call_target="tpu_custom_call" | custom-call | flops 1200000000 | tf_op jit(solution)/shard_map/pallas_call | solution.py:78
  2.7 3.1 %collective-permute-start = (bf16[16,1024]{1,0:T(8,128)(2,1)S(1)}, bf16[16,1024]{1,0:T(8,128)(2,1)S(1)}, u32[]{:S(2)}, u32[]{:S(2)}) collective-permute-start(bf16[16,1024]{1,0:T(8,128)(2,1)S(1)} %get-tuple-element.42), channel_id=1, source_target_pairs={{0,4},{4,8},{8,12},{12,0},{1,5},{5,9},{9,13},{13,1},{2,6},{6,10},{... | collective-permute-start | bytes 98312 | tf_op jit(solution)/shard_map/ppermute | solution.py:785
  5.8 1.6 %collective-permute-start.1 = (bf16[256,256]{1,0:T(8,128)(2,1)S(1)}, bf16[256,256]{1,0:T(8,128)(2,1)S(1)}, u32[]{:S(2)}, u32[]{:S(2)}) collective-permute-start(bf16[256,256]{1,0:T(8,128)(2,1)S(1)} %get-tuple-element.51), channel_id=1, source_target_pairs={{0,4},{4,0},{8,12},{12,8},{1,5},{5,1},{9,13},{13,9},{2,6},{6,2},{1... | collective-permute-start | bytes 393224 | tf_op jit(solution)/shard_map/ppermute | solution.py:781
  7.4 1.1 %collective-permute-start.2 = (bf16[256,256]{1,0:T(8,128)(2,1)S(1)}, bf16[256,256]{1,0:T(8,128)(2,1)S(1)}, u32[]{:S(2)}, u32[]{:S(2)}) collective-permute-start(bf16[256,256]{1,0:T(8,128)(2,1)S(1)} %get-tuple-element.52), channel_id=1, source_target_pairs={{0,8},{4,12},{8,0},{12,4},{1,9},{5,13},{9,1},{13,5},{2,10},{6,14},... | collective-permute-start | bytes 393224 | tf_op jit(solution)/shard_map/ppermute | solution.py:781
  8.5 1.7 %collective-permute-start.3 = (bf16[256,256]{1,0:T(8,128)(2,1)S(1)}, bf16[256,256]{1,0:T(8,128)(2,1)S(1)}, u32[]{:S(2)}, u32[]{:S(2)}) collective-permute-start(bf16[256,256]{1,0:T(8,128)(2,1)S(1)} %get-tuple-element.53), channel_id=1, source_target_pairs={{0,12},{4,8},{8,4},{12,0},{1,13},{5,9},{9,5},{13,1},{2,14},{6,10},... | collective-permute-start | bytes 393224 | tf_op jit(solution)/shard_map/ppermute | solution.py:781
  10.2 1.1 %shard_map.96 = (f32[1024,16]{1,0:T(8,128)S(1)}, bf16[1024,48]{1,0:T(8,128)(2,1)S(1)}, f32[8,256]{1,0:T(8,128)S(1)}, bf16[16,768]{1,0:T(8,128)(2,1)S(1)}, bf16[4...) custom-call(s32[2]{0:T(128)S(1)} %pad_add_fusion.place_ref, s32[16]{0:T(128)S(1)} %copy-done.4, ...), custom_call_target="tpu_custom_call" | custom-call | flops 720000000 | tf_op jit(solution)/shard_map/pallas_call | solution.py:78
  11.4 4.1 %shard_map.97 = (bf16[2,3,256,256]{3,2,1,0:T(8,128)(2,1)S(1)}, bf16[2,256,256]{2,1,0:T(8,128)(2,1)S(1)}, bf16[2,3,256,256]{3,2,1,0:T(8,128)(2,1)S(1)}, bf16[2,25...) custom-call(s32[2]{0:T(128)S(1)} %pad_add_fusion.place_ref, ...), custom_call_target="tpu_custom_call" | custom-call | flops 7200000000 | tf_op jit(solution)/shard_map/pallas_call | solution.py:78
  15.5 0.8 %collective-permute-start.8 = (bf16[2,256,256]{2,1,0:T(8,128)(2,1)S(1)}, bf16[2,256,256]{2,1,0:T(8,128)(2,1)S(1)}, u32[]{:S(2)}, u32[]{:S(2)}) collective-permute-start(bf16[2,256,256]{2,1,0:T(8,128)(2,1)S(1)} %get-tuple-element.62), channel_id=1, source_target_pairs={{0,4},{4,0},{8,12},{12,8},{1,5},{5,1},{9,13},{13,9},{2,6},{6,2},{1... | collective-permute-start | bytes 786440 | tf_op jit(solution)/shard_map/ppermute | solution.py:781
  16.2 2.0 %collective-permute-start.11 = (bf16[256,256]{1,0:T(8,128)(2,1)S(1)}, bf16[256,256]{1,0:T(8,128)(2,1)S(1)}, u32[]{:S(2)}, u32[]{:S(2)}) collective-permute-start(bf16[256,256]{1,0:T(8,128)(2,1)S(1)} %get-tuple-element.70), channel_id=1, source_target_pairs={{0,8},{4,12},{8,0},{12,4},{1,9},{5,13},{9,1},{13,5},{2,10},{6,14},... | collective-permute-start | bytes 393224 | tf_op jit(solution)/shard_map/ppermute | solution.py:781
  18.2 1.7 %collective-permute-start.12 = (bf16[256,256]{1,0:T(8,128)(2,1)S(1)}, bf16[256,256]{1,0:T(8,128)(2,1)S(1)}, u32[]{:S(2)}, u32[]{:S(2)}) collective-permute-start(bf16[256,256]{1,0:T(8,128)(2,1)S(1)} %get-tuple-element.71), channel_id=1, source_target_pairs={{0,12},{4,8},{8,4},{12,0},{1,13},{5,9},{9,5},{13,1},{2,14},{6,10},... | collective-permute-start | bytes 393224 | tf_op jit(solution)/shard_map/ppermute | solution.py:781
  19.9 0.2 collective-permute-done.2.rest_1_
  20.1 1.6 %collective-permute-start.4 = (bf16[768,256]{1,0:T(8,128)(2,1)S(1)}, bf16[768,256]{1,0:T(8,128)(2,1)S(1)}, u32[]{:S(2)}, u32[]{:S(2)}) collective-permute-start(bf16[768,256]{1,0:T(8,128)(2,1)S(1)} %pad_maximum_fusion), channel_id=1, source_target_pairs={{0,16},{16,0},{1,17},{17,1},{2,18},{18,2},{3,19},{19,3},{4,20},{20... | collective-permute-start | bytes 1179656 | tf_op jit(solution)/shard_map/ppermute | solution.py:781
  21.7 1.3 %shard_map.99.known = f32[1024,512]{1,0:T(8,128)S(1)} custom-call(s32[2]{0:T(128)S(1)} %pad_add_fusion.place_ref, bf16[512,512]{1,0:T(8,128)(2,1)S(1)} %copy-done, bf16[256,256]{1,0:T(8,128)(2,1)S(1)} %get-tuple-element.60.filt_ref, bf16[256,256]{1,0:T(8,128)(2,1)S(1)} %collective-permute-done.1.rest_0_, ...), custom_call_target="tpu_custom_call" | custom-call | flops 180000000 | tf_op jit(solution)/shard_map/pallas_call | solution.py:78
  23.0 6.3 %collective-permute-done.8.rest_1_ = bf16[2,256,256]{2,1,0:T(8,128)(2,1)S(1)} collective-permute-done((bf16[2,256,256]{2,1,0:T(8,128)(2,1)S(1)}, bf16[2,256,256]{2,1,0:T(8,128)(2,1)S(1)}, u32[]{:S(2)}, u32[]{:S(2)}) %collective-permute-start.8) | collective-permute-done | bytes 262176 | tf_op jit(solution)/shard_map/ppermute | solution.py:781
  29.3 2.0 %shard_map.100 = (bf16[256,256]{1,0:T(8,128)(2,1)S(1)}, bf16[256,256]{1,0:T(8,128)(2,1)S(1)}, f32[512,512]{1,0:T(8,128)S(1)}) custom-call(s32[2]{0:T(128)S(1)} %pad_add_fusion.place_ref, bf16[512,512]{1,0:T(8,128)(2,1)S(1)} %copy-done, bf16[512,256]{1,0:T(8,128)(2,1)S(1)} %copy-done.1, f32[1024,512]{1,0:T(8,128)S(1)} %shard_map.99.known, ...), custom_call_target="tpu_custom_call" | custom-call | flops 180000000 | tf_op jit(solution)/shard_map/pallas_call | solution.py:78
  31.4 0.1 collective-permute-start.9
  31.5 3.0 %collective-permute-start.10 = (bf16[256,256]{1,0:T(8,128)(2,1)S(1)}, bf16[256,256]{1,0:T(8,128)(2,1)S(1)}, u32[]{:S(2)}, u32[]{:S(2)}) collective-permute-start(bf16[256,256]{1,0:T(8,128)(2,1)S(1)} %get-tuple-element.64), channel_id=1, source_target_pairs={{0,12},{4,8},{8,4},{12,0},{1,13},{5,9},{9,5},{13,1},{2,14},{6,10},... | collective-permute-start | bytes 393224 | tf_op jit(solution)/shard_map/ppermute | solution.py:781
  34.5 2.8 %shard_map.102 = (bf16[2,256,256]{2,1,0:T(8,128)(2,1)S(1)}, bf16[2,256,256]{2,1,0:T(8,128)(2,1)S(1)}) custom-call(s32[2]{0:T(128)S(1)} %pad_add_fusion.place_ref, f32[1024,16]{1,0:T(8,128)S(1)} %get-tuple-element.49.cols_ref, bf16[512,512]{1,0:T(8,128)(2,1)S(1)} %copy-done, bf16[512,256]{1,0:T(8,128)(2,1)S(1)} %copy-done.1, ...), custom_call_target="tpu_custom_call" | custom-call | flops 6000000000 | tf_op jit(solution)/shard_map/pallas_call | solution.py:78
  37.3 0.6 collective-permute-start.13
  37.8 2.0 %collective-permute-done.5.rest_1_ = bf16[2,256,256]{2,1,0:T(8,128)(2,1)S(1)} collective-permute-done((bf16[2,256,256]{2,1,0:T(8,128)(2,1)S(1)}, bf16[2,256,256]{2,1,0:T(8,128)(2,1)S(1)}, u32[]{:S(2)}, u32[]{:S(2)}) %collective-permute-start.5) | collective-permute-done | bytes 262176 | tf_op jit(solution)/shard_map/ppermute | solution.py:781
  39.8 2.6 %shard_map.98 = (bf16[2,256,128]{2,1,0:T(8,128)(2,1)S(1)}, bf16[2,256,128]{2,1,0:T(8,128)(2,1)S(1)}, bf16[2,256,128]{2,1,0:T(8,128)(2,1)S(1)}, bf16[2,256,128]{2,1,0:T(8,128)(2,1)S(1)}) custom-call(s32[2]{0:T(128)S(1)} %pad_add_fusion.place_ref, f32[1024,16]{1,0:T(8,128)S(1)} %get-tuple-element.49.cols_ref, bf16[512,512]{1,0:T(8,128)(2,1)S(1)} %copy-done, ...), custom_call_target="tpu_custom_call" | custom-call | flops 4800000000 | tf_op jit(solution)/shard_map/pallas_call | solution.py:78
  42.4 0.1 collective-permute-start.6
  42.5 2.0 %collective-permute-start.7 = (bf16[2,256,128]{2,1,0:T(8,128)(2,1)S(1)}, bf16[2,256,128]{2,1,0:T(8,128)(2,1)S(1)}, u32[]{:S(2)}, u32[]{:S(2)}) collective-permute-start(bf16[2,256,128]{2,1,0:T(8,128)(2,1)S(1)} %get-tuple-element.59), channel_id=1, source_target_pairs={{0,4},{4,0},{8,12},{12,8},{1,5},{5,1},{9,13},{13,9},{2,6},{6,2},{1... | collective-permute-start | bytes 393224 | tf_op jit(solution)/shard_map/ppermute | solution.py:781
  44.5 0.5 shard_map.101
  45.1 3.1 %collective-permute-done.13.refs_1_ = bf16[2,256,256]{2,1,0:T(8,128)(2,1)S(1)} collective-permute-done((bf16[2,256,256]{2,1,0:T(8,128)(2,1)S(1)}, bf16[2,256,256]{2,1,0:T(8,128)(2,1)S(1)}, u32[]{:S(2)}, u32[]{:S(2)}) %collective-permute-start.13) | collective-permute-done | bytes 262176 | tf_op jit(solution)/shard_map/ppermute | solution.py:781
  48.2 2.4 %shard_map.103 = (bf16[1024,256]{1,0:T(8,128)(2,1)}, bf16[3,1024,256]{2,1,0:T(8,128)(2,1)}, f32[2,3,256,128]{3,2,1,0:T(8,128)S(1)}) custom-call(s32[2]{0:T(128)S(1)} %pad_add_fusion.place_ref, bf16[2,3,256,256]{3,2,1,0:T(8,128)(2,1)S(1)} %get-tuple-element.67.qkv.qkv_main, bf16[2,256,256]{2,1,0:T(8,128)(2,1)S(1)} %get-tuple-element.68.dout_ref.dout_main, ...), custom_call_target="tpu_custom_call" | custom-call | flops 1980000000 | tf_op jit(solution)/shard_map/pallas_call | solution.py:78
  50.6 0.4 collective-permute-done.6.refs_1_.refs_3_
  51.0 1.2 %shard_map.105 = f32[8,1024]{1,0:T(8,128)S(1)} custom-call(s32[2]{0:T(128)S(1)} %pad_add_fusion.place_ref, bf16[2,3,256,256]{3,2,1,0:T(8,128)(2,1)S(1)} %get-tuple-element.67.qkv.qkv_main, bf16[2,256,256]{2,1,0:T(8,128)(2,1)S(1)} %get-tuple-element.68.dout_ref.dout_main, bf16[2,3,256,256]{3,2,1,0:T(8,128)(2,1)S(1)} %get-tuple-element.47.qkv.qkv_other, ...), custom_call_target="tpu_custom_call" | custom-call | flops 3600000000 | tf_op jit(solution)/shard_map/pallas_call | solution.py:78
  52.3 1.9 %collective-permute-start.14 = (f32[8,1024]{1,0:T(8,128)S(1)}, f32[8,1024]{1,0:T(8,128)S(1)}, u32[]{:S(2)}, u32[]{:S(2)}) collective-permute-start(f32[8,1024]{1,0:T(8,128)S(1)} %shard_map.105), channel_id=1, source_target_pairs={{0,12},{4,0},{8,4},{12,8},{1,13},{5,1},{9,5},{13,9},{2,14},{6,2},{... | collective-permute-start | bytes 98312 | tf_op jit(solution)/shard_map/ppermute | solution.py:785
  54.1 2.4 %shard_map.104 = (bf16[1024,256]{1,0:T(8,128)(2,1)}, bf16[3,1024,256]{2,1,0:T(8,128)(2,1)}, f32[2,3,256,128]{3,2,1,0:T(8,128)S(1)}) custom-call(s32[2]{0:T(128)S(1)} %pad_add_fusion.place_ref, bf16[2,3,256,256]{3,2,1,0:T(8,128)(2,1)S(1)} %get-tuple-element.47.qkv.qkv_other, ...), custom_call_target="tpu_custom_call", output_to_operand_aliasing={{0}: (12, {}), {1}: (13, {})} | custom-call | flops 1980000000 | tf_op jit(solution)/shard_map/pallas_call | solution.py:78
  56.6 1.9 %shard_map.106 = bf16[3,1024,256]{2,1,0:T(8,128)(2,1)} custom-call(s32[2]{0:T(128)S(1)} %pad_add_fusion.place_ref, f32[8,1024]{1,0:T(8,128)S(1)} %collective-permute-done.14.ahead_ref, f32[16,1024]{1,0:T(8,128)S(1)} %get-tuple-element.77.taps_ref, bf16[48,384]{1,0:T(8,128)(2,1)S(1)} %get-tuple-element.78.edge_ref, ...), custom_call_target="tpu_custom_call", output_to_operand_aliasing={{}: (6, {})} | custom-call | flops 1140000000 | tf_op jit(solution)/shard_map/pallas_call | solution.py:78
  (22 shorter events, 0.1 us)
Async XLA Ops:
  0.7 9.5 %copy-start.2 = (f32[3,3,1024]{2,1,0:T(4,128)S(1)}, f32[3,3,1024]{2,1,0:T(4,128)}, u32[]{:S(2)}) copy-start(f32[3,3,1024]{2,1,0:T(4,128)} %taps_ref.1) | copy-start | bytes 110596
  0.7 9.5 %copy-start.3 = (f32[1024]{0:T(1024)S(1)}, f32[1024]{0:T(1024)}, u32[]{:S(2)}) copy-start(f32[1024]{0:T(1024)} %param.12) | copy-start | bytes 12292
  0.7 9.5 %copy-start.4 = (s32[16]{0:T(128)S(1)}, s32[16]{0:T(128)}, u32[]{:S(2)}) copy-start(s32[16]{0:T(128)} %lengths_ref.1) | copy-start | bytes 196
  2.7 8.6 %collective-permute-start = (bf16[16,1024]{1,0:T(8,128)(2,1)S(1)}, bf16[16,1024]{1,0:T(8,128)(2,1)S(1)}, u32[]{:S(2)}, u32[]{:S(2)}) collective-permute-start(bf16[16,1024]{1,0:T(8,128)(2,1)S(1)} %get-tuple-element.42), channel_id=1, source_target_pairs={{0,4},{4,8},{8,12},{12,0},{1,5},{5,9},{9,13},{13,1},{2,6},{6,10},{... | collective-permute-start | bytes 98312 | tf_op jit(solution)/shard_map/ppermute | solution.py:785
  5.8 12.4 %collective-permute-start.1 = (bf16[256,256]{1,0:T(8,128)(2,1)S(1)}, bf16[256,256]{1,0:T(8,128)(2,1)S(1)}, u32[]{:S(2)}, u32[]{:S(2)}) collective-permute-start(bf16[256,256]{1,0:T(8,128)(2,1)S(1)} %get-tuple-element.51), channel_id=1, source_target_pairs={{0,4},{4,0},{8,12},{12,8},{1,5},{5,1},{9,13},{13,9},{2,6},{6,2},{1... | collective-permute-start | bytes 393224 | tf_op jit(solution)/shard_map/ppermute | solution.py:781
  7.4 12.7 %collective-permute-start.2 = (bf16[256,256]{1,0:T(8,128)(2,1)S(1)}, bf16[256,256]{1,0:T(8,128)(2,1)S(1)}, u32[]{:S(2)}, u32[]{:S(2)}) collective-permute-start(bf16[256,256]{1,0:T(8,128)(2,1)S(1)} %get-tuple-element.52), channel_id=1, source_target_pairs={{0,8},{4,12},{8,0},{12,4},{1,9},{5,13},{9,1},{13,5},{2,10},{6,14},... | collective-permute-start | bytes 393224 | tf_op jit(solution)/shard_map/ppermute | solution.py:781
  8.5 11.6 %collective-permute-start.3 = (bf16[256,256]{1,0:T(8,128)(2,1)S(1)}, bf16[256,256]{1,0:T(8,128)(2,1)S(1)}, u32[]{:S(2)}, u32[]{:S(2)}) collective-permute-start(bf16[256,256]{1,0:T(8,128)(2,1)S(1)} %get-tuple-element.53), channel_id=1, source_target_pairs={{0,12},{4,8},{8,4},{12,0},{1,13},{5,9},{9,5},{13,1},{2,14},{6,10},... | collective-permute-start | bytes 393224 | tf_op jit(solution)/shard_map/ppermute | solution.py:781
  11.4 10.3 %copy-start = (bf16[512,512]{1,0:T(8,128)(2,1)S(1)}, bf16[512,512]{1,0:T(8,128)(2,1)}, u32[]{:S(2)}) copy-start(bf16[512,512]{1,0:T(8,128)(2,1)} %constant.15.clone.forward_ref) | copy-start | bytes 1572868
  15.5 13.9 %collective-permute-start.8 = (bf16[2,256,256]{2,1,0:T(8,128)(2,1)S(1)}, bf16[2,256,256]{2,1,0:T(8,128)(2,1)S(1)}, u32[]{:S(2)}, u32[]{:S(2)}) collective-permute-start(bf16[2,256,256]{2,1,0:T(8,128)(2,1)S(1)} %get-tuple-element.62), channel_id=1, source_target_pairs={{0,4},{4,0},{8,12},{12,8},{1,5},{5,1},{9,13},{13,9},{2,6},{6,2},{1... | collective-permute-start | bytes 786440 | tf_op jit(solution)/shard_map/ppermute | solution.py:781
  16.2 15.2 %collective-permute-start.11 = (bf16[256,256]{1,0:T(8,128)(2,1)S(1)}, bf16[256,256]{1,0:T(8,128)(2,1)S(1)}, u32[]{:S(2)}, u32[]{:S(2)}) collective-permute-start(bf16[256,256]{1,0:T(8,128)(2,1)S(1)} %get-tuple-element.70), channel_id=1, source_target_pairs={{0,8},{4,12},{8,0},{12,4},{1,9},{5,13},{9,1},{13,5},{2,10},{6,14},... | collective-permute-start | bytes 393224 | tf_op jit(solution)/shard_map/ppermute | solution.py:781
  18.2 16.2 %collective-permute-start.12 = (bf16[256,256]{1,0:T(8,128)(2,1)S(1)}, bf16[256,256]{1,0:T(8,128)(2,1)S(1)}, u32[]{:S(2)}, u32[]{:S(2)}) collective-permute-start(bf16[256,256]{1,0:T(8,128)(2,1)S(1)} %get-tuple-element.71), channel_id=1, source_target_pairs={{0,12},{4,8},{8,4},{12,0},{1,13},{5,9},{9,5},{13,1},{2,14},{6,10},... | collective-permute-start | bytes 393224 | tf_op jit(solution)/shard_map/ppermute | solution.py:781
  20.1 19.7 %collective-permute-start.5 = (bf16[2,256,256]{2,1,0:T(8,128)(2,1)S(1)}, bf16[2,256,256]{2,1,0:T(8,128)(2,1)S(1)}, u32[]{:S(2)}, u32[]{:S(2)}) collective-permute-start(bf16[2,256,256]{2,1,0:T(8,128)(2,1)S(1)} %get-tuple-element.55), channel_id=1, source_target_pairs={{0,4},{4,0},{8,12},{12,8},{1,5},{5,1},{9,13},{13,9},{2,6},{6,2},{1... | collective-permute-start | bytes 786440 | tf_op jit(solution)/shard_map/ppermute | solution.py:781
  20.1 19.6 %collective-permute-start.4 = (bf16[768,256]{1,0:T(8,128)(2,1)S(1)}, bf16[768,256]{1,0:T(8,128)(2,1)S(1)}, u32[]{:S(2)}, u32[]{:S(2)}) collective-permute-start(bf16[768,256]{1,0:T(8,128)(2,1)S(1)} %pad_maximum_fusion), channel_id=1, source_target_pairs={{0,16},{16,0},{1,17},{17,1},{2,18},{18,2},{3,19},{19,3},{4,20},{20... | collective-permute-start | bytes 1179656 | tf_op jit(solution)/shard_map/ppermute | solution.py:781
  21.7 7.6 %copy-start.1 = (bf16[512,256]{1,0:T(8,128)(2,1)S(1)}, bf16[512,256]{1,0:T(8,128)(2,1)}, u32[]{:S(2)}) copy-start(bf16[512,256]{1,0:T(8,128)(2,1)} %constant.16.clone.inverse_ref) | copy-start | bytes 786436
  31.4 13.2 %collective-permute-start.9 = (bf16[256,256]{1,0:T(8,128)(2,1)S(1)}, bf16[256,256]{1,0:T(8,128)(2,1)S(1)}, u32[]{:S(2)}, u32[]{:S(2)}) collective-permute-start(bf16[256,256]{1,0:T(8,128)(2,1)S(1)} %get-tuple-element.63), channel_id=1, source_target_pairs={{0,8},{4,12},{8,0},{12,4},{1,9},{5,13},{9,1},{13,5},{2,10},{6,14},... | collective-permute-start | bytes 393224 | tf_op jit(solution)/shard_map/ppermute | solution.py:781
  31.5 13.1 %collective-permute-start.10 = (bf16[256,256]{1,0:T(8,128)(2,1)S(1)}, bf16[256,256]{1,0:T(8,128)(2,1)S(1)}, u32[]{:S(2)}, u32[]{:S(2)}) collective-permute-start(bf16[256,256]{1,0:T(8,128)(2,1)S(1)} %get-tuple-element.64), channel_id=1, source_target_pairs={{0,12},{4,8},{8,4},{12,0},{1,13},{5,9},{9,5},{13,1},{2,14},{6,10},... | collective-permute-start | bytes 393224 | tf_op jit(solution)/shard_map/ppermute | solution.py:781
  37.3 10.9 %collective-permute-start.13 = (bf16[2,256,256]{2,1,0:T(8,128)(2,1)S(1)}, bf16[2,256,256]{2,1,0:T(8,128)(2,1)S(1)}, u32[]{:S(2)}, u32[]{:S(2)}) collective-permute-start(bf16[2,256,256]{2,1,0:T(8,128)(2,1)S(1)} %get-tuple-element.73), channel_id=1, source_target_pairs={{0,4},{4,0},{8,12},{12,8},{1,5},{5,1},{9,13},{13,9},{2,6},{6,2},{1... | collective-permute-start | bytes 786440 | tf_op jit(solution)/shard_map/ppermute | solution.py:781
  42.4 8.6 %collective-permute-start.6 = (bf16[2,256,128]{2,1,0:T(8,128)(2,1)S(1)}, bf16[2,256,128]{2,1,0:T(8,128)(2,1)S(1)}, u32[]{:S(2)}, u32[]{:S(2)}) collective-permute-start(bf16[2,256,128]{2,1,0:T(8,128)(2,1)S(1)} %get-tuple-element.57), channel_id=1, source_target_pairs={{0,4},{4,0},{8,12},{12,8},{1,5},{5,1},{9,13},{13,9},{2,6},{6,2},{1... | collective-permute-start | bytes 393224 | tf_op jit(solution)/shard_map/ppermute | solution.py:781
  42.5 11.6 %collective-permute-start.7 = (bf16[2,256,128]{2,1,0:T(8,128)(2,1)S(1)}, bf16[2,256,128]{2,1,0:T(8,128)(2,1)S(1)}, u32[]{:S(2)}, u32[]{:S(2)}) collective-permute-start(bf16[2,256,128]{2,1,0:T(8,128)(2,1)S(1)} %get-tuple-element.59), channel_id=1, source_target_pairs={{0,4},{4,0},{8,12},{12,8},{1,5},{5,1},{9,13},{13,9},{2,6},{6,2},{1... | collective-permute-start | bytes 393224 | tf_op jit(solution)/shard_map/ppermute | solution.py:781
  52.3 4.3 %collective-permute-start.14 = (f32[8,1024]{1,0:T(8,128)S(1)}, f32[8,1024]{1,0:T(8,128)S(1)}, u32[]{:S(2)}, u32[]{:S(2)}) collective-permute-start(f32[8,1024]{1,0:T(8,128)S(1)} %shard_map.105), channel_id=1, source_target_pairs={{0,12},{4,0},{8,4},{12,8},{1,13},{5,1},{9,5},{13,9},{2,14},{6,2},{... | collective-permute-start | bytes 98312 | tf_op jit(solution)/shard_map/ppermute | solution.py:785

commit v7 on v6

--- a/solution.py
+++ b/solution.py
@@ -13,7 +13,6 @@
 F32 = jnp.float32
 SHARE = 0.6
 VMEM_LIMIT = 24 * 1024 * 1024
-SCALARS = pl.BlockSpec(memory_space=pltpu.SMEM)
 IN_HBM = pl.BlockSpec(memory_space=pltpu.HBM)
 HELD = pl.BlockSpec(memory_space=pltpu.VMEM)
 ANYWHERE = pl.BlockSpec(memory_space=pl.ANY)
@@ -43,14 +42,10 @@
 
 def offsets_row(lengths_ref, first, span, ahead):
     position = lax.broadcasted_iota(jnp.int32, (8, span), 1) + (first + ahead)
-
-    def step(genome, carry):
-        end, start = carry
-        end = end + lengths_ref[genome]
-        return end, jnp.where(position >= end, end, start)
-
-    begin = (jnp.int32(0), jnp.zeros((8, span), jnp.int32))
-    _, start = lax.fori_loop(0, lengths_ref.shape[0], step, begin)
+    end, start = jnp.zeros((1, 1), jnp.int32), jnp.zeros((8, span), jnp.int32)
+    for genome in range(lengths_ref.shape[1]):
+        end = end + lengths_ref[:, genome : genome + 1]
+        start = jnp.where(position >= end, end, start)
     return position, position - start
 
 
@@ -73,18 +68,22 @@
     return jnp.bitwise_xor(own, turn) * 2 + jnp.bitwise_xor(main, other)
 
 
-def run(body, layout, place, operands, outs, scratch, cost, in_specs=None, out_specs=None, aliases=None):
+def run(body, layout, operands, outs, scratch, cost, in_specs=None, out_specs=None, aliases=None):
     single = not isinstance(outs, list)
+
+    def kernel(*refs):
+        body(layout, (lax.axis_index("seq"), lax.axis_index("groups")), *refs)
+
     return pl.pallas_call(
-        functools.partial(body, layout),
+        kernel,
         out_shape=outs,
-        in_specs=[SCALARS] + (in_specs or [HELD] * len(operands)),
+        in_specs=in_specs or [HELD] * len(operands),
         out_specs=out_specs or (HELD if single else [HELD] * len(outs)),
         scratch_shapes=scratch,
         input_output_aliases=aliases or {},
         compiler_params=pltpu.CompilerParams(vmem_limit_bytes=VMEM_LIMIT),
         cost_estimate=cost,
-    )(place, *operands)
+    )(*operands)
 
 
 def rows_at(begin, step, count):
@@ -113,7 +112,7 @@
         copy.wait()
 
 
-def pack(layout, place, features, filters):
+def pack(layout, features, filters):
     parts, sub, span, channels = layout.parts, layout.sub, layout.span, layout.channels
     outs = [jax.ShapeDtypeStruct((16, channels), BF16)] + [jax.ShapeDtypeStruct((sub, span), BF16)] * (parts + 1)
     scratch = [
@@ -121,7 +120,7 @@
         pltpu.VMEM((16, channels), F32),
         pltpu.SemaphoreType.DMA((parts + 2,)),
     ]
-    found = run(pack_body, layout, place, (features, filters), outs, scratch, estimate(2.0), in_specs=[IN_HBM] * 2)
+    found = run(pack_body, layout, (features, filters), outs, scratch, estimate(2.0), in_specs=[IN_HBM] * 2)
     return found[0], (found[1], found[1 + parts]), found[2 : 1 + parts]
 
 
@@ -141,8 +140,8 @@
     return table.astype(BF16)
 
 
-def small_body(layout, place_ref, lengths_ref, taps_ref, skip_ref, *rest):
-    cols_ref, split_ref, keep_ref, fwd_edge_ref, last_edge_ref, turned, lanes_ref = rest
+def fill_tables(layout, place_ref, lengths_ref, taps_ref, skip_ref, fwd_edge_ref, *rest):
+    cols_ref, split_ref, keep_ref, last_edge_ref, turned, lanes_ref = rest
     span = layout.span
     first = place_ref[0] * span
     _, offset = offsets_row(lengths_ref, first, span, 0)
@@ -181,33 +180,23 @@
         lanes_ref[:, k * 128 : (k + 1) * 128] = jnp.where(column == k, 1.0, 0.0).astype(BF16)
 
 
-def small(layout, place, lengths, taps, skip):
-    channels, span = layout.channels, layout.span
-    shapes = [
+def table_shapes(layout):
+    channels = layout.channels
+    return [
         ((channels, 16), F32),
         ((channels, 48), BF16),
-        ((8, span), F32),
-        ((16, 768), BF16),
+        ((8, layout.span), F32),
         ((48, 384), BF16),
         ((16, channels), F32),
         ((48, 9 * 128), BF16),
     ]
-    return run(
-        small_body,
-        layout,
-        place,
-        (lengths, taps, skip.reshape(1, channels)),
-        [jax.ShapeDtypeStruct(*s) for s in shapes],
-        [],
-        estimate(1.2),
-        in_specs=[SCALARS, HELD, HELD],
-    )
-
-
-def gate_body(layout, place_ref, feat_hbm, dout_hbm, halo_ref, split_ref, lanes_ref, keep_ref, edge_ref, *rest):
+
+
+def gate_body(layout, place_ref, feat_hbm, dout_hbm, halo_ref, lengths_ref, taps_ref, skip_ref, *rest):
     half, rows, span = layout.half, layout.sub, layout.span
-    gated, firsts, cross, seconds = (rest[:4], *(rest[4 + k * half : 4 + (k + 1) * half] for k in range(3)))
-    feat_ref, ends_of, spread, ends, sems = rest[4 + 3 * half :]
+    gated, firsts, trails, cross, seconds = (rest[:4], *(rest[4 + k * half : 4 + (k + 1) * half] for k in range(4)))
+    tables, (feat_ref, ends_of, spread, ends, edge_ref, sems) = rest[4 + 4 * half : 10 + 4 * half], rest[10 + 4 * half :]
+    _, split_ref, keep_ref, _, _, lanes_ref = tables
     side, _, _ = where_am_i(place_ref, layout)
     group = min(64, rows)
     steps = [(turn, other) for other in range(2) for turn in range(half)]
@@ -218,6 +207,7 @@
         copies.append(pltpu.make_async_copy(dout_hbm.at[block, :], gated[2 * other + 1].at[turn], sems.at[k, 1]))
         for copy in copies[-2:]:
             copy.start()
+    fill_tables(layout, place_ref, lengths_ref, taps_ref, skip_ref, edge_ref, *tables)
     ends_of[...] = halo_ref[...].astype(F32).T.astype(BF16)
     keep = [keep_ref[j : j + 1, :] for j in range(2)]
     for k, (turn, other) in enumerate(steps):
@@ -249,37 +239,39 @@
             grad_in = dout_ref[turn, local_rows, :] * filtered[0]
             first = jnp.where(side == 0, mixed, grad_in)
             second = jnp.where(side == 0, grad_in, mixed)
-            pair = seconds[turn] if other else firsts[turn]
-            pair[0, local_rows, :] = first
-            pair[1, local_rows, :] = second
             if other:
+                seconds[turn][0, local_rows, :] = first
+                seconds[turn][1, local_rows, :] = second
                 cross[turn][local_rows, :] = first
+            else:
+                firsts[turn][local_rows, :] = first
+                trails[turn][local_rows, :] = second
             return 0
 
         lax.fori_loop(0, rows // group, tile, 0, unroll=rows // group)
 
 
-def gate(layout, place, features, dout, halo, split, lanes, keep, edge):
+def gate(layout, features, dout, halo, lengths, taps, skip):
     half, rows, span, channels = layout.half, layout.sub, layout.span, layout.channels
     pair = (2, rows, span)
-    shapes = [(half, 3, rows, span), (half, rows, span)] * 2 + [pair] * half + [(rows, span)] * half + [pair] * half
+    shapes = [(half, 3, rows, span), (half, rows, span)] * 2 + [(rows, span)] * (3 * half) + [pair] * half
     found = run(
         gate_body,
         layout,
-        place,
-        (features, dout, halo, split, lanes, keep, edge),
-        [jax.ShapeDtypeStruct(s, BF16) for s in shapes],
+        (features, dout, halo, lengths.reshape(1, -1), taps, skip.reshape(1, channels)),
+        [jax.ShapeDtypeStruct(s, BF16) for s in shapes] + [jax.ShapeDtypeStruct(*s) for s in table_shapes(layout)],
         [
             pltpu.VMEM((2 * half, 3, rows, span), BF16),
             pltpu.VMEM((channels, 16), BF16),
             pltpu.VMEM((rows, 9 * 128), F32),
             pltpu.VMEM((rows, 768), F32),
+            pltpu.VMEM((16, 768), BF16),
             pltpu.SemaphoreType.DMA((2 * half, 2)),
         ],
         estimate(12.0),
-        in_specs=[IN_HBM] * 2 + [HELD] * 5,
+        in_specs=[IN_HBM] * 2 + [HELD] * 4,
     )
-    return found[0:2], found[2:4], found[4 : 4 + half], found[4 + half : 4 + 2 * half], found[4 + 2 * half :]
+    return found[0:2], found[2:4], *(found[4 + k * half : 4 + (k + 1) * half] for k in range(4)), found[4 + 4 * half :]
 
 
 def loop(count, body, init):
@@ -324,42 +316,25 @@
     ready[place, span:] = value[1].astype(BF16)
 
 
-def filter_body(layout, place_ref, forward_ref, filt_ref, *rest):
-    parts, sub = layout.parts, layout.sub
-    filt_in, (spec, raw) = rest[: parts - 1], rest[parts - 1 :]
+def cross_body(layout, place_ref, forward_ref, inverse_ref, filt_ref, *rest):
+    parts, half, sub, span = layout.parts, layout.half, layout.sub, layout.span
+    filt_in, rest = rest[: parts - 1], rest[parts - 1 :]
+    signal, outs = rest[:half], rest[half : 2 * half]
+    known, spec, filt_raw, raw, ready, back = rest[2 * half :]
     rank = place_ref[0]
-    raw[rows_at(rank * sub, sub, sub), :] = filt_ref[...]
+    filt_raw[rows_at(rank * sub, sub, sub), :] = filt_ref[...]
     for step in range(1, parts):
-        raw[rows_at(jnp.bitwise_xor(rank, step) * sub, sub, sub), :] = filt_in[step - 1][...]
+        filt_raw[rows_at(jnp.bitwise_xor(rank, step) * sub, sub, sub), :] = filt_in[step - 1][...]
     chunk = math.gcd(parts * sub, 512)
 
     def transform(index, _):
-        forward(raw, spec, index * chunk, index * chunk, chunk, forward_ref)
+        forward(filt_raw, known, index * chunk, index * chunk, chunk, forward_ref)
         return 0
 
     lax.fori_loop(0, parts * sub // chunk, transform, 0, unroll=True)
-
-
-def filter_spectra(layout, place, table, own, filt):
-    rows, span = layout.parts * layout.sub, layout.span
-    return run(
-        filter_body,
-        layout,
-        place,
-        (table, own, *filt),
-        jax.ShapeDtypeStruct((rows, 2 * span), F32),
-        [pltpu.VMEM((rows, span), BF16)],
-        estimate(0.3),
-    )
-
-
-def cross_body(layout, place_ref, forward_ref, inverse_ref, known, *rest):
-    parts, half, sub, span = layout.parts, layout.half, layout.sub, layout.span
-    signal, outs = rest[:half], rest[half : 2 * half]
-    spec, raw, ready, back = rest[2 * half :]
     side, own, _ = where_am_i(place_ref, layout)
     for step in range(half):
-        raw[rows_at(jnp.bitwise_xor(own, step) * sub, sub, sub), :] = signal[step][0]
+        raw[rows_at(jnp.bitwise_xor(own, step) * sub, sub, sub), :] = signal[step][...]
     forward(raw, spec, 0, 0, half * sub, forward_ref)
     group = 16
     zero = (jnp.zeros((group, span), F32),) * 2
@@ -401,44 +376,46 @@
         outs[step][...] = back[rows_at(jnp.bitwise_xor(own, step) * sub, sub, sub), :].astype(BF16)
 
 
-def cross_half(layout, place, tables, known, signal):
+def cross_half(layout, tables, own, filt, signal):
     half, sub, span = layout.half, layout.sub, layout.span
+    all_rows = layout.parts * sub
     rows = half * sub
     found = run(
         cross_body,
         layout,
-        place,
-        (*tables, known, *signal),
-        [jax.ShapeDtypeStruct((sub, span), BF16)] * half + [jax.ShapeDtypeStruct((rows, 2 * span), F32)],
+        (*tables, own, *filt, *signal),
+        [jax.ShapeDtypeStruct((sub, span), BF16)] * half
+        + [jax.ShapeDtypeStruct((r, 2 * span), F32) for r in (all_rows, rows)],
         [
+            pltpu.VMEM((all_rows, span), BF16),
             pltpu.VMEM((rows, span), BF16),
             pltpu.VMEM((rows, 2 * span), BF16),
             pltpu.VMEM((rows, span), F32),
         ],
         estimate(0.3),
     )
-    return found[:half], found[half]
+    return found[:half], found[half], found[half + 1]
 
 
 def hold_body(layout, place_ref, *refs):
     pass
 
 
-def hold(layout, place, arrays, after):
+def hold(layout, arrays, after):
     outs = [jax.ShapeDtypeStruct(a.shape, a.dtype) for a in arrays]
-    aliases = {1 + k: k for k in range(len(arrays))}
-    return run(hold_body, layout, place, [*arrays, after], outs, [], estimate(4.0), aliases=aliases)
+    aliases = {k: k for k in range(len(arrays))}
+    return run(hold_body, layout, [*arrays, after], outs, [], estimate(4.0), aliases=aliases)
 
 
 def main_body(layout, place_ref, cols_ref, forward_ref, inverse_ref, known, near_spec, *rest):
     parts, half, sub, span = layout.parts, layout.half, layout.sub, layout.span
-    firsts, cross, outs = (rest[k * half : (k + 1) * half] for k in range(3))
-    raw, spec, ready, back = rest[3 * half :]
+    firsts, trails, cross, outs = (rest[k * half : (k + 1) * half] for k in range(4))
+    raw, spec, ready, back = rest[4 * half :]
     side, own, _ = where_am_i(place_ref, layout)
     block = parts * sub
     for step in range(half):
         place = jnp.bitwise_xor(own, step)
-        raw[rows_at((side * half + place) * sub, sub, sub), :] = firsts[step][1]
+        raw[rows_at((side * half + place) * sub, sub, sub), :] = trails[step][...]
         raw[rows_at(((1 - side) * half + place) * sub, sub, sub), :] = cross[step][...]
     chunk = math.gcd(block, 512)
 
@@ -503,18 +480,17 @@
         place = jnp.bitwise_xor(own, step)
         for kind in range(2):
             value = back[rows_at((kind * half + place) * sub, sub, sub), :]
-            direct = firsts[step][kind].astype(F32)
+            direct = (trails if kind else firsts)[step][...].astype(F32)
             outs[step][kind] = (value + skip * direct).astype(BF16)
 
 
-def main_half(layout, place, cols, tables, known, near, firsts, cross):
+def main_half(layout, cols, tables, known, near, firsts, trails, cross):
     half, sub, span, parts = layout.half, layout.sub, layout.span, layout.parts
     rows = parts * sub
     return run(
         main_body,
         layout,
-        place,
-        (cols, *tables, known, near, *firsts, *cross),
+        (cols, *tables, known, near, *firsts, *trails, *cross),
         [jax.ShapeDtypeStruct((2, sub, span), BF16)] * half,
         [
             pltpu.VMEM((rows, span), BF16),
@@ -585,13 +561,12 @@
             late[step][kind] = found[:, 128:]
 
 
-def other_half(layout, place, cols, tables, filters, other, seconds):
+def other_half(layout, cols, tables, filters, other, seconds):
     half, sub, span, parts = layout.half, layout.sub, layout.span, layout.parts
     rows = 3 * half * sub
     found = run(
         other_body,
         layout,
-        place,
         (cols, *tables, filters, other, *seconds),
         [jax.ShapeDtypeStruct((2, sub, w), BF16) for w in (128, span - 128) for _ in range(half)],
         [
@@ -635,12 +610,11 @@
         out_ref[2 * which : 2 * which + 2, :] = grads[which].T[0:2, :]
 
 
-def first_grads(layout, place, gated, main, rest, crossed):
+def first_grads(layout, gated, main, rest, crossed):
     channels = layout.channels
     return run(
         first_body,
         layout,
-        place,
         (*gated, *main, *rest, *crossed),
         jax.ShapeDtypeStruct((8, channels), F32),
         [pltpu.VMEM((3, channels, 128), F32)],
@@ -648,27 +622,30 @@
     )
 
 
-def final_body(other, layout, place_ref, qkv, dout_ref, split_ref, lanes_ref, keep_ref, *refs):
-    half, rows, span = layout.half, layout.sub, layout.span
-    found, refs = refs[:half], refs[half:]
-    if other:
-        found, refs = list(zip(found, refs[:half])), refs[half:]
-    crossed, refs = (refs[:half], refs[half + 2 :]) if other else (None, refs)
+def final_body(blocks, chained, layout, place_ref, qkv_main, dout_main, qkv_other, dout_other, split_ref, lanes_ref, keep_ref, *refs):
+    rows, span = layout.sub, layout.span
+    found = []
+    for _, other in blocks:
+        count = 3 if other else 1
+        found.append(refs[:count])
+        refs = refs[count:]
+    refs = refs[1 + 2 * chained :]
     out_hbm, dfeat_hbm, partial, out_ref, dfeat_ref, spread, sems = refs
     most = span - 128
     side, _, _ = where_am_i(place_ref, layout)
     group = min(64, rows)
     keep = [keep_ref[2 + j : 3 + j, :] for j in range(2)]
     copies = []
-    for turn in range(half):
-        base = channel_block(place_ref, layout, turn, other) * rows
-        block = rows_at(base, rows, rows)
+    for k, (turn, other) in enumerate(blocks):
+        block = rows_at(channel_block(place_ref, layout, turn, other) * rows, rows, rows)
+        qkv, dout_ref = (qkv_other, dout_other) if other else (qkv_main, dout_main)
+        source, crossed = (found[k][:2], found[k][2]) if other else (found[k][0], None)
         spread[...] = dot(split_ref[block, :], lanes_ref[...])
 
-        def tile(index, _, turn=turn):
+        def tile(index, _, k=k, turn=turn, qkv=qkv, dout_ref=dout_ref, source=source, crossed=crossed):
             local_rows = rows_at(index * group, group, group)
-            pair = results(side, found[turn], crossed and crossed[turn], (local_rows, slice(None)))
-            out_ref[turn, local_rows, :] = qkv[turn, 0, local_rows, :] * pair[0]
+            pair = results(side, source, crossed, (local_rows, slice(None)))
+            out_ref[k, local_rows, :] = qkv[turn, 0, local_rows, :] * pair[0]
             y_out, dmixed = (f.astype(F32) for f in pair)
             grads = (
                 dout_ref[turn, local_rows, :].astype(F32) * y_out,
@@ -682,57 +659,59 @@
                     total = taps[0] * grads[which][:, lane : lane + 128]
                     total = total + taps[1] * ahead[0][:, lane : lane + 128] + taps[2] * ahead[1][:, lane : lane + 128]
                     if lane == most:
-                        partial[turn, which, local_rows, :] = total
+                        partial[k, which, local_rows, :] = total
                     else:
-                        dfeat_ref[turn, which, local_rows, lane : lane + 128] = total.astype(BF16)
+                        dfeat_ref[k, which, local_rows, lane : lane + 128] = total.astype(BF16)
             return 0
 
         lax.fori_loop(0, rows // group, tile, 0, unroll=rows // group)
-        copies.append(pltpu.make_async_copy(out_ref.at[turn], out_hbm.at[block, :], sems.at[turn, 0]))
-        copies.append(
-            pltpu.make_async_copy(dfeat_ref.at[turn], dfeat_hbm.at[:, block, pl.ds(0, most)], sems.at[turn, 1])
-        )
+        copies.append(pltpu.make_async_copy(out_ref.at[k], out_hbm.at[block, :], sems.at[k, 0]))
+        copies.append(pltpu.make_async_copy(dfeat_ref.at[k], dfeat_hbm.at[:, block, pl.ds(0, most)], sems.at[k, 1]))
         for copy in copies[-2:]:
             copy.start()
     for copy in copies:
         copy.wait()
 
 
-def final(other, layout, place, gated, split, lane_sum, keep, found, crossed, earlier):
-    half, span, channels, rows = layout.half, layout.span, layout.channels, layout.sub
-    operands = [*gated, split, lane_sum, keep, *found]
-    in_specs = [HELD] * len(operands)
+def final(blocks, layout, gated, shared, found, after, earlier):
+    span, channels, rows, count = layout.span, layout.channels, layout.sub, len(blocks)
+    operands = [*gated, *shared]
+    for turn, other in blocks:
+        main, early, late, crossed = (f[turn] for f in found)
+        operands += [early, late, crossed] if other else [main]
+    in_specs = [HELD] * len(operands) + [ANYWHERE]
+    operands.append(after)
     aliases = {}
-    if other:
-        operands += [*crossed, *earlier]
-        in_specs += [HELD] * half + [IN_HBM] * 2
-        aliases = {len(operands) - 1: 0, len(operands): 1}
+    if earlier:
+        operands += earlier
+        in_specs += [IN_HBM] * 2
+        aliases = {len(operands) - 2: 0, len(operands) - 1: 1}
     return run(
-        functools.partial(final_body, other),
+        functools.partial(final_body, blocks, bool(earlier)),
         layout,
-        place,
         operands,
         [
             jax.ShapeDtypeStruct((channels, span), BF16),
             jax.ShapeDtypeStruct((3, channels, span), BF16),
-            jax.ShapeDtypeStruct((half, 3, rows, 128), F32),
+            jax.ShapeDtypeStruct((count, 3, rows, 128), F32),
         ],
         [
-            pltpu.VMEM((half, rows, span), BF16),
-            pltpu.VMEM((half, 3, rows, span - 128), BF16),
+            pltpu.VMEM((count, rows, span), BF16),
+            pltpu.VMEM((count, 3, rows, span - 128), BF16),
             pltpu.VMEM((rows, 9 * 128), F32),
-            pltpu.SemaphoreType.DMA((half, 2)),
+            pltpu.SemaphoreType.DMA((count, 2)),
         ],
-        estimate(3.3),
+        estimate(1.2 * count),
         in_specs=in_specs,
         out_specs=[IN_HBM, IN_HBM, HELD],
         aliases=aliases,
     )
 
 
-def finish_body(layout, place_ref, ahead_ref, taps_ref, edge_ref, part_main, part_other, dfeat_in, dfeat_hbm, *refs):
-    rows_ref, placed, dfeat_ref, sems = refs
-    half, rows, span = layout.half, layout.sub, layout.span
+def finish_body(lists, layout, place_ref, ahead_ref, taps_ref, edge_ref, *refs):
+    partials, refs = refs[: len(lists)], refs[len(lists) + 1 :]
+    dfeat_hbm, rows_ref, placed, dfeat_ref, sems = refs
+    rows, span = layout.sub, layout.span
     for which in range(3):
         first, second = (ahead_ref[2 * which + k : 2 * which + k + 1, :] for k in range(2))
         one, two = (taps_ref[3 * which + k : 3 * which + k + 1, :] for k in (1, 2))
@@ -742,26 +721,24 @@
     split = jnp.concatenate(three_parts(rows_ref[...]), axis=0).T.astype(BF16)
     placed[...] = dot(split, edge_ref[...])
     copies = []
-    for turn in range(half):
-        for other in range(2):
+    for blocks, partial in zip(lists, partials):
+        for k, (turn, other) in enumerate(blocks):
             block = rows_at(channel_block(place_ref, layout, turn, other) * rows, rows, rows)
-            partial = part_other if other else part_main
             for which in range(3):
-                value = partial[turn, which] + placed[block, which * 128 : (which + 1) * 128]
+                value = partial[k, which] + placed[block, which * 128 : (which + 1) * 128]
                 dfeat_ref[which, block, :] = value.astype(BF16)
             target = dfeat_hbm.at[:, block, pl.ds(span - 128, 128)]
-            copies.append(pltpu.make_async_copy(dfeat_ref.at[:, block, :], target, sems.at[2 * turn + other]))
+            copies.append(pltpu.make_async_copy(dfeat_ref.at[:, block, :], target, sems.at[len(copies)]))
             copies[-1].start()
     for copy in copies:
         copy.wait()
 
 
-def finish(layout, place, ahead, taps_rows, edge, partials, dfeat):
+def finish(lists, layout, ahead, taps_rows, edge, partials, dfeat):
     channels = layout.channels
     return run(
-        finish_body,
+        functools.partial(finish_body, lists),
         layout,
-        place,
         (ahead, taps_rows, edge, *partials, dfeat),
         jax.ShapeDtypeStruct(dfeat.shape, BF16),
         [
@@ -771,9 +748,9 @@
             pltpu.SemaphoreType.DMA((layout.parts,)),
         ],
         estimate(1.9),
-        in_specs=[HELD] * 5 + [IN_HBM],
+        in_specs=[HELD] * (3 + len(lists)) + [IN_HBM],
         out_specs=IN_HBM,
-        aliases={6: 0},
+        aliases={3 + len(lists): 0},
     )
 
 
@@ -790,39 +767,43 @@
     _, channels, span = features.shape
     layout = Layout(parts, channels, span)
     half = layout.half
-    place = jnp.stack([lax.axis_index("seq"), lax.axis_index("groups")]).astype(jnp.int32)
     tables = [jnp.asarray(t) for t in block_tables(span)]
 
     features, dout, filters = (pltpu.with_memory_space_constraint(a, pltpu.HBM) for a in (features, dout, filters))
 
-    halo, own_filt, filt = pack(layout, place, features, filters)
+    halo, own_filt, filt = pack(layout, features, filters)
     halo = around(halo, 1, parts)
     filt = [swap(filt[step - 1], step, parts) for step in range(1, parts)]
     other = swap(jnp.concatenate(filt, axis=0), 1, 2, "groups")
-    cols, split, keep, first_edge, last_edge, taps_rows, lanes = small(layout, place, lengths, taps, skip)
-    gated_main, gated_other, firsts, cross, seconds = gate(
-        layout, place, features, dout, halo, split, lanes, keep, first_edge
+    gated_main, gated_other, firsts, trails, cross, seconds, shared = gate(
+        layout, features, dout, halo, lengths, taps, skip
     )
+    cols, split, keep, last_edge, taps_rows, lanes = shared
     firsts = [firsts[0]] + [swap(firsts[step], step, parts) for step in range(1, half)]
+    trails = [trails[0]] + [swap(trails[step], step, parts) for step in range(1, half)]
     cross = [swap(cross[step], step + half, parts) for step in range(half)]
     seconds = [seconds[0]] + [swap(seconds[step], step, parts) for step in range(1, half)]
 
-    known = filter_spectra(layout, place, tables[0], own_filt[0], filt)
-    sent, near = cross_half(layout, place, tables, known, firsts)
+    sent, known, near = cross_half(layout, tables, own_filt[0], filt, firsts)
     crossed = [swap(sent[step], step + half, parts) for step in range(half)]
-    main = main_half(layout, place, cols, tables, known, near, firsts, cross)
+    main = main_half(layout, cols, tables, known, near, firsts, trails, cross)
     main = [main[0]] + [swap(main[step], step, parts) for step in range(1, half)]
-    early, late = other_half(layout, place, cols, tables, own_filt[1], other, seconds)
-    crossed = hold(layout, place, crossed, early[0])
+    early, late = other_half(layout, cols, tables, own_filt[1], other, seconds)
+    crossed = hold(layout, crossed, early[0])
     early = [early[0]] + [swap(early[step], step, parts) for step in range(1, half)]
     late = [late[0]] + [swap(late[step], step, parts) for step in range(1, half)]
 
-    taken = (split, lanes, keep)
-    out, dfeat, part_main = final(0, layout, place, gated_main, *taken, main, None, None)
-    first = first_grads(layout, place, (*gated_main, *gated_other), main, early, crossed)
-    ahead = around(first, -1, parts)
-    out, dfeat, part_other = final(1, layout, place, gated_other, *taken, [*early, *late], crossed, (out, dfeat))
-    return out, finish(layout, place, ahead, taps_rows, last_edge, (part_main, part_other), dfeat)
+    gated = (*gated_main, *gated_other)
+    found = (main, early, late, crossed)
+    shared = (split, lanes, keep)
+    lists = [[(0, 0), (0, 1)], [(turn, 0) for turn in range(1, half)], [(turn, 1) for turn in range(1, half)]]
+    ahead = around(first_grads(layout, gated, main, early, crossed), -1, parts)
+    done, partials, after = (), [], crossed[0]
+    for blocks in lists:
+        *done, partial = final(blocks, layout, gated, shared, found, after, done)
+        partials.append(partial)
+        after = partial
+    return done[0], finish(lists, layout, ahead, taps_rows, last_edge, partials, done[1])
 
 
 def solution(mesh):

time: 58.7 us -> 56 us (0.954)
  Pallas kernels: 24.5 us -> 18.2 us
  starting transfers between devices: 21.1 us -> 24.2 us
  waiting for transfers between devices: 12 us -> 12.6 us
    pallas_call x12 -> x11, Pallas kernels: 24.5 us -> 18.2 us  [run(): pl.pallas_call(kernel, out_shape=outs, in_specs=in_specs or [HELD] * len(...]
    ppermute x13 -> x14, starting transfers between devices: 16.1 us -> 19.2 us  [swap(): lax.ppermute(value, axis, [(source, source ^ step) for source in range(pa...]
    ppermute x2, waiting for transfers between devices: 0.01 us -> 0.73 us  [around(): lax.ppermute(value, 'seq', [(source, (source + steps) % parts) for source...]
    ppermute x13 -> x14, waiting for transfers between devices: 12 us -> 11.9 us  [swap(): lax.ppermute(value, axis, [(source, source ^ step) for source in range(pa...]
  transfers between devices with their start and end apart: 15 -> 16, of which waited for: 5 -> 8; matrix products, arithmetic and copies ran while one was open for 0% -> 0% of each run, Pallas kernels for 35% -> 27%
where the time goes in v7:
time: 56 us; the launch traced here: 55.8 us
  starting transfers between devices  24.2 us (43%)
  Pallas kernels  18.2 us (32%)
  waiting for transfers between devices  12.6 us (22%)
  between operations  0.77 us (1%)
    ppermute x14, starting transfers between devices, swap(): lax.ppermute(value, axis, [(source, source ^ step) for source in range(pa...  19.2 us
    pallas_call x11, Pallas kernels, run(): pl.pallas_call(kernel, out_shape=outs, in_specs=in_specs or [HELD] * len(...  18.2 us
    ppermute x14, waiting for transfers between devices, swap(): lax.ppermute(value, axis, [(source, source ^ step) for source in range(pa...  11.9 us
    ppermute x2, starting transfers between devices, around(): lax.ppermute(value, 'seq', [(source, (source + steps) % parts) for source...  5.04 us
  transfers between devices with their start and end apart: 16, of which 8 were waited for; matrix products, arithmetic and copies ran while one was open for 0% of the time, Pallas kernels for 27%

profile of v7, /device:TPU:0, one launch (start us, length us, event | category | flops | bytes accessed | tf_op | source)
XLA Modules:
  0.0 55.8 jit_solution(11100619204092675778)
XLA Ops:
  0.7 1.5 %shard_map.95 = (bf16[16,1024]{1,0:T(8,128)(2,1)S(1)}, bf16[256,256]{1,0:T(8,128)(2,1)S(1)}, bf16[256,256]{1,0:T(8,128)(2,1)S(1)}, bf16[256,256]{1,0:T(8,128)(2,...) custom-call(bf16[3,1024,256]{2,1,0:T(8,128)(2,1)} %refs_0_.4, bf16[1024,256]{1,0:T(8,128)(2,1)} %refs_1_.5), custom_call_target="tpu_custom_call" | custom-call | flops 1200000000 | tf_op jit(solution)/shard_map/pallas_call | solution.py:77
  2.2 3.1 %collective-permute-start = (bf16[16,1024]{1,0:T(8,128)(2,1)S(1)}, bf16[16,1024]{1,0:T(8,128)(2,1)S(1)}, u32[]{:S(2)}, u32[]{:S(2)}) collective-permute-start(bf16[16,1024]{1,0:T(8,128)(2,1)S(1)} %get-tuple-element.47), channel_id=1, source_target_pairs={{0,4},{4,8},{8,12},{12,0},{1,5},{5,9},{9,13},{13,1},{2,6},{6,10},{... | collective-permute-start | bytes 98312 | tf_op jit(solution)/shard_map/ppermute | solution.py:762
  5.2 1.6 %collective-permute-start.1 = (bf16[256,256]{1,0:T(8,128)(2,1)S(1)}, bf16[256,256]{1,0:T(8,128)(2,1)S(1)}, u32[]{:S(2)}, u32[]{:S(2)}) collective-permute-start(bf16[256,256]{1,0:T(8,128)(2,1)S(1)} %get-tuple-element.57), channel_id=1, source_target_pairs={{0,4},{4,0},{8,12},{12,8},{1,5},{5,1},{9,13},{13,9},{2,6},{6,2},{1... | collective-permute-start | bytes 393224 | tf_op jit(solution)/shard_map/ppermute | solution.py:758
  6.8 1.1 %collective-permute-start.2 = (bf16[256,256]{1,0:T(8,128)(2,1)S(1)}, bf16[256,256]{1,0:T(8,128)(2,1)S(1)}, u32[]{:S(2)}, u32[]{:S(2)}) collective-permute-start(bf16[256,256]{1,0:T(8,128)(2,1)S(1)} %get-tuple-element.58), channel_id=1, source_target_pairs={{0,8},{4,12},{8,0},{12,4},{1,9},{5,13},{9,1},{13,5},{2,10},{6,14},... | collective-permute-start | bytes 393224 | tf_op jit(solution)/shard_map/ppermute | solution.py:758
  7.9 1.7 %collective-permute-start.3 = (bf16[256,256]{1,0:T(8,128)(2,1)S(1)}, bf16[256,256]{1,0:T(8,128)(2,1)S(1)}, u32[]{:S(2)}, u32[]{:S(2)}) collective-permute-start(bf16[256,256]{1,0:T(8,128)(2,1)S(1)} %get-tuple-element.59), channel_id=1, source_target_pairs={{0,12},{4,8},{8,4},{12,0},{1,13},{5,9},{9,5},{13,1},{2,14},{6,10},... | collective-permute-start | bytes 393224 | tf_op jit(solution)/shard_map/ppermute | solution.py:758
  9.7 3.8 %shard_map.96 = (bf16[2,3,256,256]{3,2,1,0:T(8,128)(2,1)S(1)}, bf16[2,256,256]{2,1,0:T(8,128)(2,1)S(1)}, bf16[2,3,256,256]{3,2,1,0:T(8,128)(2,1)S(1)}, bf16[2,25...) custom-call(bf16[3,1024,256]{2,1,0:T(8,128)(2,1)} %refs_0_.4, ...), custom_call_target="tpu_custom_call" | custom-call | flops 7200000000 | tf_op jit(solution)/shard_map/pallas_call | solution.py:77
  13.5 0.7 %collective-permute-start.8 = (bf16[256,256]{1,0:T(8,128)(2,1)S(1)}, bf16[256,256]{1,0:T(8,128)(2,1)S(1)}, u32[]{:S(2)}, u32[]{:S(2)}) collective-permute-start(bf16[256,256]{1,0:T(8,128)(2,1)S(1)} %get-tuple-element.66), channel_id=1, source_target_pairs={{0,4},{4,0},{8,12},{12,8},{1,5},{5,1},{9,13},{13,9},{2,6},{6,2},{1... | collective-permute-start | bytes 393224 | tf_op jit(solution)/shard_map/ppermute | solution.py:758
  14.2 1.3 %collective-permute-start.11 = (bf16[256,256]{1,0:T(8,128)(2,1)S(1)}, bf16[256,256]{1,0:T(8,128)(2,1)S(1)}, u32[]{:S(2)}, u32[]{:S(2)}) collective-permute-start(bf16[256,256]{1,0:T(8,128)(2,1)S(1)} %get-tuple-element.74), channel_id=1, source_target_pairs={{0,4},{4,0},{8,12},{12,8},{1,5},{5,1},{9,13},{13,9},{2,6},{6,2},{1... | collective-permute-start | bytes 393224 | tf_op jit(solution)/shard_map/ppermute | solution.py:758
  15.6 1.7 %collective-permute-start.12 = (bf16[256,256]{1,0:T(8,128)(2,1)S(1)}, bf16[256,256]{1,0:T(8,128)(2,1)S(1)}, u32[]{:S(2)}, u32[]{:S(2)}) collective-permute-start(bf16[256,256]{1,0:T(8,128)(2,1)S(1)} %get-tuple-element.75), channel_id=1, source_target_pairs={{0,8},{4,12},{8,0},{12,4},{1,9},{5,13},{9,1},{13,5},{2,10},{6,14},... | collective-permute-start | bytes 393224 | tf_op jit(solution)/shard_map/ppermute | solution.py:758
  17.3 2.3 %collective-permute-done.2.refs_4_ = bf16[256,256]{1,0:T(8,128)(2,1)S(1)} collective-permute-done((bf16[256,256]{1,0:T(8,128)(2,1)S(1)}, bf16[256,256]{1,0:T(8,128)(2,1)S(1)}, u32[]{:S(2)}, u32[]{:S(2)}) %collective-permute-start.2) | collective-permute-done | bytes 131104 | tf_op jit(solution)/shard_map/ppermute | solution.py:758
  19.5 2.1 %collective-permute-start.13 = (bf16[256,256]{1,0:T(8,128)(2,1)S(1)}, bf16[256,256]{1,0:T(8,128)(2,1)S(1)}, u32[]{:S(2)}, u32[]{:S(2)}) collective-permute-start(bf16[256,256]{1,0:T(8,128)(2,1)S(1)} %get-tuple-element.76), channel_id=1, source_target_pairs={{0,12},{4,8},{8,4},{12,0},{1,13},{5,9},{9,5},{13,1},{2,14},{6,10},... | collective-permute-start | bytes 393224 | tf_op jit(solution)/shard_map/ppermute | solution.py:758
  21.6 1.6 %collective-permute-start.5 = (bf16[2,256,256]{2,1,0:T(8,128)(2,1)S(1)}, bf16[2,256,256]{2,1,0:T(8,128)(2,1)S(1)}, u32[]{:S(2)}, u32[]{:S(2)}) collective-permute-start(bf16[2,256,256]{2,1,0:T(8,128)(2,1)S(1)} %get-tuple-element.61), channel_id=1, source_target_pairs={{0,4},{4,0},{8,12},{12,8},{1,5},{5,1},{9,13},{13,9},{2,6},{6,2},{1... | collective-permute-start | bytes 786440 | tf_op jit(solution)/shard_map/ppermute | solution.py:758
  23.3 1.5 %collective-permute-start.4 = (bf16[768,256]{1,0:T(8,128)(2,1)S(1)}, bf16[768,256]{1,0:T(8,128)(2,1)S(1)}, u32[]{:S(2)}, u32[]{:S(2)}) collective-permute-start(bf16[768,256]{1,0:T(8,128)(2,1)S(1)} %pad_maximum_fusion), channel_id=1, source_target_pairs={{0,16},{16,0},{1,17},{17,1},{2,18},{18,2},{3,19},{19,3},{4,20},{20... | collective-permute-start | bytes 1179656 | tf_op jit(solution)/shard_map/ppermute | solution.py:758
  24.8 2.1 %shard_map.98 = (bf16[256,256]{1,0:T(8,128)(2,1)S(1)}, bf16[256,256]{1,0:T(8,128)(2,1)S(1)}, f32[1024,512]{1,0:T(8,128)S(1)}, f32[512,512]{1,0:T(8,128)S(1)}) custom-call(bf16[512,512]{1,0:T(8,128)(2,1)S(1)} %copy-done, bf16[512,256]{1,0:T(8,128)(2,1)S(1)} %copy-done.1, bf16[256,256]{1,0:T(8,128)(2,1)S(1)} %get-tuple-element.64.refs_2_, ...), custom_call_target="tpu_custom_call" | custom-call | flops 180000000 | tf_op jit(solution)/shard_map/pallas_call | solution.py:77
  27.0 1.6 %collective-permute-done.11.refs_8_ = bf16[256,256]{1,0:T(8,128)(2,1)S(1)} collective-permute-done((bf16[256,256]{1,0:T(8,128)(2,1)S(1)}, bf16[256,256]{1,0:T(8,128)(2,1)S(1)}, u32[]{:S(2)}, u32[]{:S(2)}) %collective-permute-start.11) | collective-permute-done | bytes 131104 | tf_op jit(solution)/shard_map/ppermute | solution.py:758
  28.5 2.2 %collective-permute-done.12.refs_9_ = bf16[256,256]{1,0:T(8,128)(2,1)S(1)} collective-permute-done((bf16[256,256]{1,0:T(8,128)(2,1)S(1)}, bf16[256,256]{1,0:T(8,128)(2,1)S(1)}, u32[]{:S(2)}, u32[]{:S(2)}) %collective-permute-start.12) | collective-permute-done | bytes 131104 | tf_op jit(solution)/shard_map/ppermute | solution.py:758
  30.8 2.1 %collective-permute-start.10 = (bf16[256,256]{1,0:T(8,128)(2,1)S(1)}, bf16[256,256]{1,0:T(8,128)(2,1)S(1)}, u32[]{:S(2)}, u32[]{:S(2)}) collective-permute-start(bf16[256,256]{1,0:T(8,128)(2,1)S(1)} %get-tuple-element.68), channel_id=1, source_target_pairs={{0,12},{4,8},{8,4},{12,0},{1,13},{5,9},{9,5},{13,1},{2,14},{6,10},... | collective-permute-start | bytes 393224 | tf_op jit(solution)/shard_map/ppermute | solution.py:758
  32.9 2.3 %shard_map.100 = (bf16[2,256,256]{2,1,0:T(8,128)(2,1)S(1)}, bf16[2,256,256]{2,1,0:T(8,128)(2,1)S(1)}) custom-call(f32[1024,16]{1,0:T(8,128)S(1)} %get-tuple-element.55.refs_0_, bf16[512,512]{1,0:T(8,128)(2,1)S(1)} %copy-done, bf16[512,256]{1,0:T(8,128)(2,1)S(1)} %copy-done.1, f32[1024,512]{1,0:T(8,128)S(1)} %get-tuple-element.71.refs_3_, ...), custom_call_target="tpu_custom_call" | custom-call | flops 6000000000 | tf_op jit(solution)/shard_map/pallas_call | solution.py:77
  35.2 1.6 %collective-permute-start.14 = (bf16[2,256,256]{2,1,0:T(8,128)(2,1)S(1)}, bf16[2,256,256]{2,1,0:T(8,128)(2,1)S(1)}, u32[]{:S(2)}, u32[]{:S(2)}) collective-permute-start(bf16[2,256,256]{2,1,0:T(8,128)(2,1)S(1)} %get-tuple-element.77), channel_id=1, source_target_pairs={{0,4},{4,0},{8,12},{12,8},{1,5},{5,1},{9,13},{13,9},{2,6},{6,2},{1... | collective-permute-start | bytes 786440 | tf_op jit(solution)/shard_map/ppermute | solution.py:758
  36.8 2.9 %collective-permute-done.5.refs_6_ = bf16[2,256,256]{2,1,0:T(8,128)(2,1)S(1)} collective-permute-done((bf16[2,256,256]{2,1,0:T(8,128)(2,1)S(1)}, bf16[2,256,256]{2,1,0:T(8,128)(2,1)S(1)}, u32[]{:S(2)}, u32[]{:S(2)}) %collective-permute-start.5) | collective-permute-done | bytes 262176 | tf_op jit(solution)/shard_map/ppermute | solution.py:758
  39.7 2.1 %shard_map.97 = (bf16[2,256,128]{2,1,0:T(8,128)(2,1)S(1)}, bf16[2,256,128]{2,1,0:T(8,128)(2,1)S(1)}, bf16[2,256,128]{2,1,0:T(8,128)(2,1)S(1)}, bf16[2,256,128]{2,1,0:T(8,128)(2,1)S(1)}) custom-call(f32[1024,16]{1,0:T(8,128)S(1)} %get-tuple-element.55.refs_0_, bf16[512,512]{1,0:T(8,128)(2,1)S(1)} %copy-done, bf16[512,256]{1,0:T(8,128)(2,1)S(1)} %copy-done.1, ...), custom_call_target="tpu_custom_call" | custom-call | flops 4800000000 | tf_op jit(solution)/shard_map/pallas_call | solution.py:77
  41.8 0.1 collective-permute-start.6
  41.9 2.0 %collective-permute-start.7 = (bf16[2,256,128]{2,1,0:T(8,128)(2,1)S(1)}, bf16[2,256,128]{2,1,0:T(8,128)(2,1)S(1)}, u32[]{:S(2)}, u32[]{:S(2)}) collective-permute-start(bf16[2,256,128]{2,1,0:T(8,128)(2,1)S(1)} %get-tuple-element.63), channel_id=1, source_target_pairs={{0,4},{4,0},{8,12},{12,8},{1,5},{5,1},{9,13},{13,9},{2,6},{6,2},{1... | collective-permute-start | bytes 393224 | tf_op jit(solution)/shard_map/ppermute | solution.py:758
  43.9 1.8 %shard_map.101 = (bf16[1024,256]{1,0:T(8,128)(2,1)}, bf16[3,1024,256]{2,1,0:T(8,128)(2,1)}, f32[2,3,256,128]{3,2,1,0:T(8,128)S(1)}) custom-call(bf16[2,3,256,256]{3,2,1,0:T(8,128)(2,1)S(1)} %get-tuple-element.48.refs_0_, bf16[2,256,256]{2,1,0:T(8,128)(2,1)S(1)} %get-tuple-element.49.refs_1_, bf16[2,3,256,256]{3,2,1,0:T(8,128)(2,1)S(1)} %get-tuple-element.50.refs_2_, ...), custom_call_target="tpu_custom_call" | custom-call | flops 1440000000 | tf_op jit(solution)/shard_map/pallas_call | solution.py:77
  45.8 1.2 %collective-permute-done.14.refs_7_.refs_5_ = bf16[2,256,256]{2,1,0:T(8,128)(2,1)S(1)} collective-permute-done((bf16[2,256,256]{2,1,0:T(8,128)(2,1)S(1)}, bf16[2,256,256]{2,1,0:T(8,128)(2,1)S(1)}, u32[]{:S(2)}, u32[]{:S(2)}) %collective-permute-start.14) | collective-permute-done | bytes 262176 | tf_op jit(solution)/shard_map/ppermute | solution.py:758
  47.0 1.2 %shard_map.102 = (bf16[1024,256]{1,0:T(8,128)(2,1)}, bf16[3,1024,256]{2,1,0:T(8,128)(2,1)}, f32[1,3,256,128]{3,2,1,0:T(8,128)S(1)}) custom-call(bf16[2,3,256,256]{3,2,1,0:T(8,128)(2,1)S(1)} %get-tuple-element.48.refs_0_, bf16[2,256,256]{2,1,0:T(8,128)(2,1)S(1)} %get-tuple-element.49.refs_1_, ...), custom_call_target="tpu_custom_call", output_to_operand_aliasing={{0}: (9, {}), {1}: (10, {})} | custom-call | flops 720000000 | tf_op jit(solution)/shard_map/pallas_call | solution.py:77
  48.3 1.6 %collective-permute-done.6.refs_7_ = bf16[2,256,128]{2,1,0:T(8,128)(2,1)S(1)} collective-permute-done((bf16[2,256,128]{2,1,0:T(8,128)(2,1)S(1)}, bf16[2,256,128]{2,1,0:T(8,128)(2,1)S(1)}, u32[]{:S(2)}, u32[]{:S(2)}) %collective-permute-start.6) | collective-permute-done | bytes 131104 | tf_op jit(solution)/shard_map/ppermute | solution.py:758
  49.8 0.7 %shard_map.104 = f32[8,1024]{1,0:T(8,128)S(1)} custom-call(bf16[2,3,256,256]{3,2,1,0:T(8,128)(2,1)S(1)} %get-tuple-element.48.refs_0_, bf16[2,256,256]{2,1,0:T(8,128)(2,1)S(1)} %get-tuple-element.49.refs_1_, bf16[2,3,256,256]{3,2,1,0:T(8,128)(2,1)S(1)} %get-tuple-element.50.refs_2_, bf16[2,256,256]{2,1,0:T(8,128)(2,1)S(1)} %get-tuple-element.51.refs_3_, ...), custom_call_target="tpu_custom_call" | custom-call | flops 3600000000 | tf_op jit(solution)/shard_map/pallas_call | solution.py:77
  50.5 2.0 %collective-permute-start.15 = (f32[8,1024]{1,0:T(8,128)S(1)}, f32[8,1024]{1,0:T(8,128)S(1)}, u32[]{:S(2)}, u32[]{:S(2)}) collective-permute-start(f32[8,1024]{1,0:T(8,128)S(1)} %shard_map.104), channel_id=1, source_target_pairs={{0,12},{4,0},{8,4},{12,8},{1,13},{5,1},{9,5},{13,9},{2,14},{6,2},{... | collective-permute-start | bytes 98312 | tf_op jit(solution)/shard_map/ppermute | solution.py:762
  52.5 1.2 %shard_map.103 = (bf16[1024,256]{1,0:T(8,128)(2,1)}, bf16[3,1024,256]{2,1,0:T(8,128)(2,1)}, f32[1,3,256,128]{3,2,1,0:T(8,128)S(1)}) custom-call(bf16[2,3,256,256]{3,2,1,0:T(8,128)(2,1)S(1)} %get-tuple-element.48.refs_0_, bf16[2,256,256]{2,1,0:T(8,128)(2,1)S(1)} %get-tuple-element.49.refs_1_, ...), custom_call_target="tpu_custom_call", output_to_operand_aliasing={{0}: (11, {}), {1}: (12, {})} | custom-call | flops 720000000 | tf_op jit(solution)/shard_map/pallas_call | solution.py:77
  53.7 0.7 %collective-permute-done.15.refs_0_ = f32[8,1024]{1,0:T(8,128)S(1)} collective-permute-done((f32[8,1024]{1,0:T(8,128)S(1)}, f32[8,1024]{1,0:T(8,128)S(1)}, u32[]{:S(2)}, u32[]{:S(2)}) %collective-permute-start.15) | collective-permute-done | bytes 32800 | tf_op jit(solution)/shard_map/ppermute | solution.py:762
  54.5 1.4 %shard_map.105 = bf16[3,1024,256]{2,1,0:T(8,128)(2,1)} custom-call(f32[8,1024]{1,0:T(8,128)S(1)} %collective-permute-done.15.refs_0_, f32[16,1024]{1,0:T(8,128)S(1)} %get-tuple-element.88.refs_1_, bf16[48,384]{1,0:T(8,128)(2,1)S(1)} %get-tuple-element.89.refs_2_, ...), custom_call_target="tpu_custom_call", output_to_operand_aliasing={{}: (6, {})} | custom-call | flops 1140000000 | tf_op jit(solution)/shard_map/pallas_call | solution.py:77
  (22 shorter events, 0.1 us)
Async XLA Ops:
  0.6 9.0 %copy-start.4 = (s32[16]{0:T(128)S(1)}, s32[16]{0:T(128)}, u32[]{:S(2)}) copy-start(s32[16]{0:T(128)} %param.13) | copy-start | bytes 196
  0.6 9.0 %copy-start.3 = (f32[1024]{0:T(1024)S(1)}, f32[1024]{0:T(1024)}, u32[]{:S(2)}) copy-start(f32[1024]{0:T(1024)} %param.12) | copy-start | bytes 12292
  0.7 9.0 %copy-start.2 = (f32[3,3,1024]{2,1,0:T(4,128)S(1)}, f32[3,3,1024]{2,1,0:T(4,128)}, u32[]{:S(2)}) copy-start(f32[3,3,1024]{2,1,0:T(4,128)} %refs_4_.1) | copy-start | bytes 110596
  2.2 7.5 %collective-permute-start = (bf16[16,1024]{1,0:T(8,128)(2,1)S(1)}, bf16[16,1024]{1,0:T(8,128)(2,1)S(1)}, u32[]{:S(2)}, u32[]{:S(2)}) collective-permute-start(bf16[16,1024]{1,0:T(8,128)(2,1)S(1)} %get-tuple-element.47), channel_id=1, source_target_pairs={{0,4},{4,8},{8,12},{12,0},{1,5},{5,9},{9,13},{13,1},{2,6},{6,10},{... | collective-permute-start | bytes 98312 | tf_op jit(solution)/shard_map/ppermute | solution.py:762
  5.2 10.3 %collective-permute-start.1 = (bf16[256,256]{1,0:T(8,128)(2,1)S(1)}, bf16[256,256]{1,0:T(8,128)(2,1)S(1)}, u32[]{:S(2)}, u32[]{:S(2)}) collective-permute-start(bf16[256,256]{1,0:T(8,128)(2,1)S(1)} %get-tuple-element.57), channel_id=1, source_target_pairs={{0,4},{4,0},{8,12},{12,8},{1,5},{5,1},{9,13},{13,9},{2,6},{6,2},{1... | collective-permute-start | bytes 393224 | tf_op jit(solution)/shard_map/ppermute | solution.py:758
  6.8 12.7 %collective-permute-start.2 = (bf16[256,256]{1,0:T(8,128)(2,1)S(1)}, bf16[256,256]{1,0:T(8,128)(2,1)S(1)}, u32[]{:S(2)}, u32[]{:S(2)}) collective-permute-start(bf16[256,256]{1,0:T(8,128)(2,1)S(1)} %get-tuple-element.58), channel_id=1, source_target_pairs={{0,8},{4,12},{8,0},{12,4},{1,9},{5,13},{9,1},{13,5},{2,10},{6,14},... | collective-permute-start | bytes 393224 | tf_op jit(solution)/shard_map/ppermute | solution.py:758
  7.9 13.7 %collective-permute-start.3 = (bf16[256,256]{1,0:T(8,128)(2,1)S(1)}, bf16[256,256]{1,0:T(8,128)(2,1)S(1)}, u32[]{:S(2)}, u32[]{:S(2)}) collective-permute-start(bf16[256,256]{1,0:T(8,128)(2,1)S(1)} %get-tuple-element.59), channel_id=1, source_target_pairs={{0,12},{4,8},{8,4},{12,0},{1,13},{5,9},{9,5},{13,1},{2,14},{6,10},... | collective-permute-start | bytes 393224 | tf_op jit(solution)/shard_map/ppermute | solution.py:758
  9.7 15.2 %copy-start = (bf16[512,512]{1,0:T(8,128)(2,1)S(1)}, bf16[512,512]{1,0:T(8,128)(2,1)}, u32[]{:S(2)}) copy-start(bf16[512,512]{1,0:T(8,128)(2,1)} %constant.4.clone.refs_1_.refs_0_) | copy-start | bytes 1572868
  9.7 15.2 %copy-start.1 = (bf16[512,256]{1,0:T(8,128)(2,1)S(1)}, bf16[512,256]{1,0:T(8,128)(2,1)}, u32[]{:S(2)}) copy-start(bf16[512,256]{1,0:T(8,128)(2,1)} %constant.5.clone.refs_2_.refs_1_) | copy-start | bytes 786436
  13.5 9.8 %collective-permute-start.8 = (bf16[256,256]{1,0:T(8,128)(2,1)S(1)}, bf16[256,256]{1,0:T(8,128)(2,1)S(1)}, u32[]{:S(2)}, u32[]{:S(2)}) collective-permute-start(bf16[256,256]{1,0:T(8,128)(2,1)S(1)} %get-tuple-element.66), channel_id=1, source_target_pairs={{0,4},{4,0},{8,12},{12,8},{1,5},{5,1},{9,13},{13,9},{2,6},{6,2},{1... | collective-permute-start | bytes 393224 | tf_op jit(solution)/shard_map/ppermute | solution.py:758
  14.2 14.3 %collective-permute-start.11 = (bf16[256,256]{1,0:T(8,128)(2,1)S(1)}, bf16[256,256]{1,0:T(8,128)(2,1)S(1)}, u32[]{:S(2)}, u32[]{:S(2)}) collective-permute-start(bf16[256,256]{1,0:T(8,128)(2,1)S(1)} %get-tuple-element.74), channel_id=1, source_target_pairs={{0,4},{4,0},{8,12},{12,8},{1,5},{5,1},{9,13},{13,9},{2,6},{6,2},{1... | collective-permute-start | bytes 393224 | tf_op jit(solution)/shard_map/ppermute | solution.py:758
  15.6 15.2 %collective-permute-start.12 = (bf16[256,256]{1,0:T(8,128)(2,1)S(1)}, bf16[256,256]{1,0:T(8,128)(2,1)S(1)}, u32[]{:S(2)}, u32[]{:S(2)}) collective-permute-start(bf16[256,256]{1,0:T(8,128)(2,1)S(1)} %get-tuple-element.75), channel_id=1, source_target_pairs={{0,8},{4,12},{8,0},{12,4},{1,9},{5,13},{9,1},{13,5},{2,10},{6,14},... | collective-permute-start | bytes 393224 | tf_op jit(solution)/shard_map/ppermute | solution.py:758
  19.5 13.3 %collective-permute-start.13 = (bf16[256,256]{1,0:T(8,128)(2,1)S(1)}, bf16[256,256]{1,0:T(8,128)(2,1)S(1)}, u32[]{:S(2)}, u32[]{:S(2)}) collective-permute-start(bf16[256,256]{1,0:T(8,128)(2,1)S(1)} %get-tuple-element.76), channel_id=1, source_target_pairs={{0,12},{4,8},{8,4},{12,0},{1,13},{5,9},{9,5},{13,1},{2,14},{6,10},... | collective-permute-start | bytes 393224 | tf_op jit(solution)/shard_map/ppermute | solution.py:758
  21.6 18.1 %collective-permute-start.5 = (bf16[2,256,256]{2,1,0:T(8,128)(2,1)S(1)}, bf16[2,256,256]{2,1,0:T(8,128)(2,1)S(1)}, u32[]{:S(2)}, u32[]{:S(2)}) collective-permute-start(bf16[2,256,256]{2,1,0:T(8,128)(2,1)S(1)} %get-tuple-element.61), channel_id=1, source_target_pairs={{0,4},{4,0},{8,12},{12,8},{1,5},{5,1},{9,13},{13,9},{2,6},{6,2},{1... | collective-permute-start | bytes 786440 | tf_op jit(solution)/shard_map/ppermute | solution.py:758
  23.3 16.4 %collective-permute-start.4 = (bf16[768,256]{1,0:T(8,128)(2,1)S(1)}, bf16[768,256]{1,0:T(8,128)(2,1)S(1)}, u32[]{:S(2)}, u32[]{:S(2)}) collective-permute-start(bf16[768,256]{1,0:T(8,128)(2,1)S(1)} %pad_maximum_fusion), channel_id=1, source_target_pairs={{0,16},{16,0},{1,17},{17,1},{2,18},{18,2},{3,19},{19,3},{4,20},{20... | collective-permute-start | bytes 1179656 | tf_op jit(solution)/shard_map/ppermute | solution.py:758
  28.5 15.4 %collective-permute-start.9 = (bf16[256,256]{1,0:T(8,128)(2,1)S(1)}, bf16[256,256]{1,0:T(8,128)(2,1)S(1)}, u32[]{:S(2)}, u32[]{:S(2)}) collective-permute-start(bf16[256,256]{1,0:T(8,128)(2,1)S(1)} %get-tuple-element.67), channel_id=1, source_target_pairs={{0,8},{4,12},{8,0},{12,4},{1,9},{5,13},{9,1},{13,5},{2,10},{6,14},... | collective-permute-start | bytes 393224 | tf_op jit(solution)/shard_map/ppermute | solution.py:758
  30.8 13.2 %collective-permute-start.10 = (bf16[256,256]{1,0:T(8,128)(2,1)S(1)}, bf16[256,256]{1,0:T(8,128)(2,1)S(1)}, u32[]{:S(2)}, u32[]{:S(2)}) collective-permute-start(bf16[256,256]{1,0:T(8,128)(2,1)S(1)} %get-tuple-element.68), channel_id=1, source_target_pairs={{0,12},{4,8},{8,4},{12,0},{1,13},{5,9},{9,5},{13,1},{2,14},{6,10},... | collective-permute-start | bytes 393224 | tf_op jit(solution)/shard_map/ppermute | solution.py:758
  35.2 11.9 %collective-permute-start.14 = (bf16[2,256,256]{2,1,0:T(8,128)(2,1)S(1)}, bf16[2,256,256]{2,1,0:T(8,128)(2,1)S(1)}, u32[]{:S(2)}, u32[]{:S(2)}) collective-permute-start(bf16[2,256,256]{2,1,0:T(8,128)(2,1)S(1)} %get-tuple-element.77), channel_id=1, source_target_pairs={{0,4},{4,0},{8,12},{12,8},{1,5},{5,1},{9,13},{13,9},{2,6},{6,2},{1... | collective-permute-start | bytes 786440 | tf_op jit(solution)/shard_map/ppermute | solution.py:758
  41.8 8.0 %collective-permute-start.6 = (bf16[2,256,128]{2,1,0:T(8,128)(2,1)S(1)}, bf16[2,256,128]{2,1,0:T(8,128)(2,1)S(1)}, u32[]{:S(2)}, u32[]{:S(2)}) collective-permute-start(bf16[2,256,128]{2,1,0:T(8,128)(2,1)S(1)} %get-tuple-element.62), channel_id=1, source_target_pairs={{0,4},{4,0},{8,12},{12,8},{1,5},{5,1},{9,13},{13,9},{2,6},{6,2},{1... | collective-permute-start | bytes 393224 | tf_op jit(solution)/shard_map/ppermute | solution.py:758
  41.9 10.6 %collective-permute-start.7 = (bf16[2,256,128]{2,1,0:T(8,128)(2,1)S(1)}, bf16[2,256,128]{2,1,0:T(8,128)(2,1)S(1)}, u32[]{:S(2)}, u32[]{:S(2)}) collective-permute-start(bf16[2,256,128]{2,1,0:T(8,128)(2,1)S(1)} %get-tuple-element.63), channel_id=1, source_target_pairs={{0,4},{4,0},{8,12},{12,8},{1,5},{5,1},{9,13},{13,9},{2,6},{6,2},{1... | collective-permute-start | bytes 393224 | tf_op jit(solution)/shard_map/ppermute | solution.py:758
  50.5 3.9 %collective-permute-start.15 = (f32[8,1024]{1,0:T(8,128)S(1)}, f32[8,1024]{1,0:T(8,128)S(1)}, u32[]{:S(2)}, u32[]{:S(2)}) collective-permute-start(f32[8,1024]{1,0:T(8,128)S(1)} %shard_map.104), channel_id=1, source_target_pairs={{0,12},{4,0},{8,4},{12,8},{1,13},{5,1},{9,5},{13,9},{2,14},{6,2},{... | collective-permute-start | bytes 98312 | tf_op jit(solution)/shard_map/ppermute | solution.py:762

commit v8 on v7

--- a/solution.py
+++ b/solution.py
@@ -11,6 +11,7 @@
 
 BF16 = jnp.bfloat16
 F32 = jnp.float32
+GATE_MAIN, GATE_OTHER = 6.0, 1.0
 SHARE = 0.6
 VMEM_LIMIT = 24 * 1024 * 1024
 IN_HBM = pl.BlockSpec(memory_space=pltpu.HBM)
@@ -192,37 +193,42 @@
     ]
 
 
-def gate_body(layout, place_ref, feat_hbm, dout_hbm, halo_ref, lengths_ref, taps_ref, skip_ref, *rest):
+def gate_body(other, layout, place_ref, feat_hbm, dout_hbm, *rest):
     half, rows, span = layout.half, layout.sub, layout.span
-    gated, firsts, trails, cross, seconds = (rest[:4], *(rest[4 + k * half : 4 + (k + 1) * half] for k in range(4)))
-    tables, (feat_ref, ends_of, spread, ends, edge_ref, sems) = rest[4 + 4 * half : 10 + 4 * half], rest[10 + 4 * half :]
-    _, split_ref, keep_ref, _, _, lanes_ref = tables
+    given, rest = (rest[:5], rest[5:]) if other else (rest[:4], rest[4:])
+    qkv_ref, dout_ref, firsts, seconds = rest[0], rest[1], rest[2 : 2 + half], rest[2 + half : 2 + 2 * half]
+    rest = rest[2 + 2 * half :]
+    feat_ref, spread, ends, sems = rest[-4:]
     side, _, _ = where_am_i(place_ref, layout)
     group = min(64, rows)
-    steps = [(turn, other) for other in range(2) for turn in range(half)]
     copies = []
-    for k, (turn, other) in enumerate(steps):
+    for turn in range(half):
         block = rows_at(channel_block(place_ref, layout, turn, other) * rows, rows, rows)
-        copies.append(pltpu.make_async_copy(feat_hbm.at[:, block, :], feat_ref.at[k], sems.at[k, 0]))
-        copies.append(pltpu.make_async_copy(dout_hbm.at[block, :], gated[2 * other + 1].at[turn], sems.at[k, 1]))
+        copies.append(pltpu.make_async_copy(feat_hbm.at[:, block, :], feat_ref.at[turn], sems.at[turn, 0]))
+        copies.append(pltpu.make_async_copy(dout_hbm.at[block, :], dout_ref.at[turn], sems.at[turn, 1]))
         for copy in copies[-2:]:
             copy.start()
-    fill_tables(layout, place_ref, lengths_ref, taps_ref, skip_ref, edge_ref, *tables)
-    ends_of[...] = halo_ref[...].astype(F32).T.astype(BF16)
+    if other:
+        split_ref, keep_ref, lanes_ref, edge_ref, ends_of = given
+    else:
+        halo_ref, lengths_ref, taps_ref, skip_ref = given
+        tables, edge_ref, ends_of = rest[:6], rest[6], rest[7]
+        _, split_ref, keep_ref, _, _, lanes_ref = tables
+        fill_tables(layout, place_ref, lengths_ref, taps_ref, skip_ref, edge_ref, *tables)
+        ends_of[...] = halo_ref[...].astype(F32).T.astype(BF16)
     keep = [keep_ref[j : j + 1, :] for j in range(2)]
-    for k, (turn, other) in enumerate(steps):
+    for turn in range(half):
         block = rows_at(channel_block(place_ref, layout, turn, other) * rows, rows, rows)
-        qkv_ref, dout_ref = gated[2 * other : 2 * other + 2]
         spread[...] = dot(split_ref[block, :], lanes_ref[...])
         ends[...] = dot(ends_of[block, :], edge_ref[...])
-        for copy in copies[2 * k : 2 * k + 2]:
+        for copy in copies[2 * turn : 2 * turn + 2]:
             copy.wait()
 
-        def tile(index, _, k=k, turn=turn, other=other, qkv_ref=qkv_ref, dout_ref=dout_ref):
+        def tile(index, _, turn=turn):
             local_rows = rows_at(index * group, group, group)
             filtered = []
             for which in range(3):
-                value = feat_ref[k, which, local_rows, :].astype(F32)
+                value = feat_ref[turn, which, local_rows, :].astype(F32)
                 moved = [pltpu.roll(value, j + 1, 1) * keep[j] for j in range(2)]
                 taps = [spread[local_rows, (3 * which + j) * 128 : (3 * which + j + 1) * 128] for j in range(3)]
                 parts = []
@@ -239,39 +245,40 @@
             grad_in = dout_ref[turn, local_rows, :] * filtered[0]
             first = jnp.where(side == 0, mixed, grad_in)
             second = jnp.where(side == 0, grad_in, mixed)
+            firsts[turn][local_rows, :] = first
             if other:
                 seconds[turn][0, local_rows, :] = first
                 seconds[turn][1, local_rows, :] = second
-                cross[turn][local_rows, :] = first
             else:
-                firsts[turn][local_rows, :] = first
-                trails[turn][local_rows, :] = second
+                seconds[turn][local_rows, :] = second
             return 0
 
         lax.fori_loop(0, rows // group, tile, 0, unroll=rows // group)
 
 
-def gate(layout, features, dout, halo, lengths, taps, skip):
+def gate(other, layout, features, dout, *given):
     half, rows, span, channels = layout.half, layout.sub, layout.span, layout.channels
-    pair = (2, rows, span)
-    shapes = [(half, 3, rows, span), (half, rows, span)] * 2 + [(rows, span)] * (3 * half) + [pair] * half
+    shapes = [(half, 3, rows, span), (half, rows, span)] + [(rows, span)] * half
+    shapes += [(2, rows, span) if other else (rows, span)] * half
+    outs = [jax.ShapeDtypeStruct(s, BF16) for s in shapes]
+    if not other:
+        more = table_shapes(layout) + [((16, 768), BF16), ((channels, 16), BF16)]
+        outs += [jax.ShapeDtypeStruct(*s) for s in more]
     found = run(
-        gate_body,
+        functools.partial(gate_body, other),
         layout,
-        (features, dout, halo, lengths.reshape(1, -1), taps, skip.reshape(1, channels)),
-        [jax.ShapeDtypeStruct(s, BF16) for s in shapes] + [jax.ShapeDtypeStruct(*s) for s in table_shapes(layout)],
+        (features, dout, *given),
+        outs,
         [
-            pltpu.VMEM((2 * half, 3, rows, span), BF16),
-            pltpu.VMEM((channels, 16), BF16),
+            pltpu.VMEM((half, 3, rows, span), BF16),
             pltpu.VMEM((rows, 9 * 128), F32),
             pltpu.VMEM((rows, 768), F32),
-            pltpu.VMEM((16, 768), BF16),
-            pltpu.SemaphoreType.DMA((2 * half, 2)),
+            pltpu.SemaphoreType.DMA((half, 2)),
         ],
-        estimate(12.0),
-        in_specs=[IN_HBM] * 2 + [HELD] * 4,
+        estimate(GATE_OTHER if other else GATE_MAIN),
+        in_specs=[IN_HBM] * 2 + [HELD] * len(given),
     )
-    return found[0:2], found[2:4], *(found[4 + k * half : 4 + (k + 1) * half] for k in range(4)), found[4 + 4 * half :]
+    return found[0:2], found[2 : 2 + half], found[2 + half : 2 + 2 * half], found[2 + 2 * half :]
 
 
 def loop(count, body, init):
@@ -398,13 +405,14 @@
 
 
 def hold_body(layout, place_ref, *refs):
-    pass
+    count = (len(refs) - 1) // 2
+    for source, target in zip(refs[:count], refs[count + 1 :]):
+        target[...] = source[...]
 
 
 def hold(layout, arrays, after):
     outs = [jax.ShapeDtypeStruct(a.shape, a.dtype) for a in arrays]
-    aliases = {k: k for k in range(len(arrays))}
-    return run(hold_body, layout, [*arrays, after], outs, [], estimate(4.0), aliases=aliases)
+    return run(hold_body, layout, [*arrays, after], outs, [], estimate(4.0), in_specs=[HELD] * len(arrays) + [ANYWHERE])
 
 
 def main_body(layout, place_ref, cols_ref, forward_ref, inverse_ref, known, near_spec, *rest):
@@ -775,10 +783,10 @@
     halo = around(halo, 1, parts)
     filt = [swap(filt[step - 1], step, parts) for step in range(1, parts)]
     other = swap(jnp.concatenate(filt, axis=0), 1, 2, "groups")
-    gated_main, gated_other, firsts, trails, cross, seconds, shared = gate(
-        layout, features, dout, halo, lengths, taps, skip
-    )
-    cols, split, keep, last_edge, taps_rows, lanes = shared
+    first_given = (halo, lengths.reshape(1, -1), taps, skip.reshape(1, channels))
+    gated_main, firsts, trails, shared = gate(0, layout, features, dout, *first_given)
+    cols, split, keep, last_edge, taps_rows, lanes, first_edge, ends_of = shared
+    gated_other, cross, seconds, _ = gate(1, layout, features, dout, split, keep, lanes, first_edge, ends_of)
     firsts = [firsts[0]] + [swap(firsts[step], step, parts) for step in range(1, half)]
     trails = [trails[0]] + [swap(trails[step], step, parts) for step in range(1, half)]
     cross = [swap(cross[step], step + half, parts) for step in range(half)]

time: 56 us -> 55.7 us (level)
  waiting for transfers between devices: 12.6 us -> 10.1 us
  Pallas kernels: 18.2 us -> 19.4 us
  starting transfers between devices: 24.2 us -> 25.2 us
    ppermute x14, waiting for transfers between devices: 11.9 us -> 9.56 us  [swap(): lax.ppermute(value, axis, [(source, source ^ step) for source in range(pa...]
    pallas_call x11 -> x12, Pallas kernels: 18.2 us -> 19.4 us  [run(): pl.pallas_call(kernel, out_shape=outs, in_specs=in_specs or [HELD] * len(...]
    ppermute x14, starting transfers between devices: 19.2 us -> 20 us  [swap(): lax.ppermute(value, axis, [(source, source ^ step) for source in range(pa...]
  transfers between devices with their start and end apart: 16 -> 16, of which waited for: 8 -> 7; matrix products, arithmetic and copies ran while one was open for 0% -> 0% of each run, Pallas kernels for 27% -> 30%
where the time goes in v8:
time: 55.7 us; the launch traced here: 55.6 us
  starting transfers between devices  25.2 us (45%)
  Pallas kernels  19.4 us (35%)
  waiting for transfers between devices  10.1 us (18%)
  between operations  0.78 us (1%)
    ppermute x14, starting transfers between devices, swap(): lax.ppermute(value, axis, [(source, source ^ step) for source in range(pa...  20 us
    pallas_call x12, Pallas kernels, run(): pl.pallas_call(kernel, out_shape=outs, in_specs=in_specs or [HELD] * len(...  19.4 us
    ppermute x14, waiting for transfers between devices, swap(): lax.ppermute(value, axis, [(source, source ^ step) for source in range(pa...  9.56 us
    ppermute x2, starting transfers between devices, around(): lax.ppermute(value, 'seq', [(source, (source + steps) % parts) for source...  5.21 us
  transfers between devices with their start and end apart: 16, of which 7 were waited for; matrix products, arithmetic and copies ran while one was open for 0% of the time, Pallas kernels for 30%

profile of v8, /device:TPU:0, one launch (start us, length us, event | category | flops | bytes accessed | tf_op | source)
XLA Modules:
  0.0 55.6 jit_solution(4750125374154613677)
XLA Ops:
  0.7 1.5 %shard_map.95 = (bf16[16,1024]{1,0:T(8,128)(2,1)S(1)}, bf16[256,256]{1,0:T(8,128)(2,1)S(1)}, bf16[256,256]{1,0:T(8,128)(2,1)S(1)}, bf16[256,256]{1,0:T(8,128)(2,...) custom-call(bf16[3,1024,256]{2,1,0:T(8,128)(2,1)} %refs_0_.6, bf16[1024,256]{1,0:T(8,128)(2,1)} %refs_1_.6), custom_call_target="tpu_custom_call" | custom-call | flops 1200000000 | tf_op jit(solution)/shard_map/pallas_call | solution.py:78
  2.2 3.1 %collective-permute-start = (bf16[16,1024]{1,0:T(8,128)(2,1)S(1)}, bf16[16,1024]{1,0:T(8,128)(2,1)S(1)}, u32[]{:S(2)}, u32[]{:S(2)}) collective-permute-start(bf16[16,1024]{1,0:T(8,128)(2,1)S(1)} %get-tuple-element.49), channel_id=1, source_target_pairs={{0,4},{4,8},{8,12},{12,0},{1,5},{5,9},{9,13},{13,1},{2,6},{6,10},{... | collective-permute-start | bytes 98312 | tf_op jit(solution)/shard_map/ppermute | solution.py:770
  5.2 1.6 %collective-permute-start.1 = (bf16[256,256]{1,0:T(8,128)(2,1)S(1)}, bf16[256,256]{1,0:T(8,128)(2,1)S(1)}, u32[]{:S(2)}, u32[]{:S(2)}) collective-permute-start(bf16[256,256]{1,0:T(8,128)(2,1)S(1)} %get-tuple-element.61), channel_id=1, source_target_pairs={{0,4},{4,0},{8,12},{12,8},{1,5},{5,1},{9,13},{13,9},{2,6},{6,2},{1... | collective-permute-start | bytes 393224 | tf_op jit(solution)/shard_map/ppermute | solution.py:766
  6.8 1.1 %collective-permute-start.2 = (bf16[256,256]{1,0:T(8,128)(2,1)S(1)}, bf16[256,256]{1,0:T(8,128)(2,1)S(1)}, u32[]{:S(2)}, u32[]{:S(2)}) collective-permute-start(bf16[256,256]{1,0:T(8,128)(2,1)S(1)} %get-tuple-element.62), channel_id=1, source_target_pairs={{0,8},{4,12},{8,0},{12,4},{1,9},{5,13},{9,1},{13,5},{2,10},{6,14},... | collective-permute-start | bytes 393224 | tf_op jit(solution)/shard_map/ppermute | solution.py:766
  7.9 1.7 %collective-permute-start.3 = (bf16[256,256]{1,0:T(8,128)(2,1)S(1)}, bf16[256,256]{1,0:T(8,128)(2,1)S(1)}, u32[]{:S(2)}, u32[]{:S(2)}) collective-permute-start(bf16[256,256]{1,0:T(8,128)(2,1)S(1)} %get-tuple-element.63), channel_id=1, source_target_pairs={{0,12},{4,8},{8,4},{12,0},{1,13},{5,9},{9,5},{13,1},{2,14},{6,10},... | collective-permute-start | bytes 393224 | tf_op jit(solution)/shard_map/ppermute | solution.py:766
  9.7 2.6 %shard_map.96 = (bf16[2,3,256,256]{3,2,1,0:T(8,128)(2,1)S(1)}, bf16[2,256,256]{2,1,0:T(8,128)(2,1)S(1)}, bf16[256,256]{1,0:T(8,128)(2,1)S(1)}, bf16[256,256]{1,0...) custom-call(bf16[3,1024,256]{2,1,0:T(8,128)(2,1)} %refs_0_.6, ...), custom_call_target="tpu_custom_call" | custom-call | flops 3600000000 | tf_op jit(solution)/shard_map/pallas_call | solution.py:78
  12.3 0.7 %collective-permute-start.8 = (bf16[256,256]{1,0:T(8,128)(2,1)S(1)}, bf16[256,256]{1,0:T(8,128)(2,1)S(1)}, u32[]{:S(2)}, u32[]{:S(2)}) collective-permute-start(bf16[256,256]{1,0:T(8,128)(2,1)S(1)} %get-tuple-element.70), channel_id=1, source_target_pairs={{0,4},{4,0},{8,12},{12,8},{1,5},{5,1},{9,13},{13,9},{2,6},{6,2},{1... | collective-permute-start | bytes 393224 | tf_op jit(solution)/shard_map/ppermute | solution.py:766
  13.0 1.4 %collective-permute-start.11 = (bf16[256,256]{1,0:T(8,128)(2,1)S(1)}, bf16[256,256]{1,0:T(8,128)(2,1)S(1)}, u32[]{:S(2)}, u32[]{:S(2)}) collective-permute-start(bf16[256,256]{1,0:T(8,128)(2,1)S(1)} %get-tuple-element.78), channel_id=1, source_target_pairs={{0,4},{4,0},{8,12},{12,8},{1,5},{5,1},{9,13},{13,9},{2,6},{6,2},{1... | collective-permute-start | bytes 393224 | tf_op jit(solution)/shard_map/ppermute | solution.py:766
  14.4 2.3 %shard_map.97 = (bf16[2,3,256,256]{3,2,1,0:T(8,128)(2,1)S(1)}, bf16[2,256,256]{2,1,0:T(8,128)(2,1)S(1)}, bf16[256,256]{1,0:T(8,128)(2,1)S(1)}, bf16[256,256]{1,0...) custom-call(bf16[3,1024,256]{2,1,0:T(8,128)(2,1)} %refs_0_.6, ...), custom_call_target="tpu_custom_call" | custom-call | flops 600000000 | tf_op jit(solution)/shard_map/pallas_call | solution.py:78
  16.8 1.8 %collective-permute-start.12 = (bf16[256,256]{1,0:T(8,128)(2,1)S(1)}, bf16[256,256]{1,0:T(8,128)(2,1)S(1)}, u32[]{:S(2)}, u32[]{:S(2)}) collective-permute-start(bf16[256,256]{1,0:T(8,128)(2,1)S(1)} %get-tuple-element.79), channel_id=1, source_target_pairs={{0,8},{4,12},{8,0},{12,4},{1,9},{5,13},{9,1},{13,5},{2,10},{6,14},... | collective-permute-start | bytes 393224 | tf_op jit(solution)/shard_map/ppermute | solution.py:766
  18.5 1.0 %collective-permute-done.2.refs_4_ = bf16[256,256]{1,0:T(8,128)(2,1)S(1)} collective-permute-done((bf16[256,256]{1,0:T(8,128)(2,1)S(1)}, bf16[256,256]{1,0:T(8,128)(2,1)S(1)}, u32[]{:S(2)}, u32[]{:S(2)}) %collective-permute-start.2) | collective-permute-done | bytes 131104 | tf_op jit(solution)/shard_map/ppermute | solution.py:766
  19.5 2.1 %collective-permute-start.13 = (bf16[256,256]{1,0:T(8,128)(2,1)S(1)}, bf16[256,256]{1,0:T(8,128)(2,1)S(1)}, u32[]{:S(2)}, u32[]{:S(2)}) collective-permute-start(bf16[256,256]{1,0:T(8,128)(2,1)S(1)} %get-tuple-element.80), channel_id=1, source_target_pairs={{0,12},{4,8},{8,4},{12,0},{1,13},{5,9},{9,5},{13,1},{2,14},{6,10},... | collective-permute-start | bytes 393224 | tf_op jit(solution)/shard_map/ppermute | solution.py:766
  21.6 1.6 %collective-permute-start.5 = (bf16[2,256,256]{2,1,0:T(8,128)(2,1)S(1)}, bf16[2,256,256]{2,1,0:T(8,128)(2,1)S(1)}, u32[]{:S(2)}, u32[]{:S(2)}) collective-permute-start(bf16[2,256,256]{2,1,0:T(8,128)(2,1)S(1)} %get-tuple-element.65), channel_id=1, source_target_pairs={{0,4},{4,0},{8,12},{12,8},{1,5},{5,1},{9,13},{13,9},{2,6},{6,2},{1... | collective-permute-start | bytes 786440 | tf_op jit(solution)/shard_map/ppermute | solution.py:766
  23.3 1.6 %collective-permute-start.4 = (bf16[768,256]{1,0:T(8,128)(2,1)S(1)}, bf16[768,256]{1,0:T(8,128)(2,1)S(1)}, u32[]{:S(2)}, u32[]{:S(2)}) collective-permute-start(bf16[768,256]{1,0:T(8,128)(2,1)S(1)} %pad_maximum_fusion), channel_id=1, source_target_pairs={{0,16},{16,0},{1,17},{17,1},{2,18},{18,2},{3,19},{19,3},{4,20},{20... | collective-permute-start | bytes 1179656 | tf_op jit(solution)/shard_map/ppermute | solution.py:766
  24.8 2.1 %shard_map.99 = (bf16[256,256]{1,0:T(8,128)(2,1)S(1)}, bf16[256,256]{1,0:T(8,128)(2,1)S(1)}, f32[1024,512]{1,0:T(8,128)S(1)}, f32[512,512]{1,0:T(8,128)S(1)}) custom-call(bf16[512,512]{1,0:T(8,128)(2,1)S(1)} %copy-done, bf16[512,256]{1,0:T(8,128)(2,1)S(1)} %copy-done.1, bf16[256,256]{1,0:T(8,128)(2,1)S(1)} %get-tuple-element.68.refs_2_, ...), custom_call_target="tpu_custom_call" | custom-call | flops 180000000 | tf_op jit(solution)/shard_map/pallas_call | solution.py:78
  27.3 0.7 %collective-permute-start.9 = (bf16[256,256]{1,0:T(8,128)(2,1)S(1)}, bf16[256,256]{1,0:T(8,128)(2,1)S(1)}, u32[]{:S(2)}, u32[]{:S(2)}) collective-permute-start(bf16[256,256]{1,0:T(8,128)(2,1)S(1)} %get-tuple-element.71), channel_id=1, source_target_pairs={{0,8},{4,12},{8,0},{12,4},{1,9},{5,13},{9,1},{13,5},{2,10},{6,14},... | collective-permute-start | bytes 393224 | tf_op jit(solution)/shard_map/ppermute | solution.py:766
  28.0 2.8 %collective-permute-done.12.refs_9_ = bf16[256,256]{1,0:T(8,128)(2,1)S(1)} collective-permute-done((bf16[256,256]{1,0:T(8,128)(2,1)S(1)}, bf16[256,256]{1,0:T(8,128)(2,1)S(1)}, u32[]{:S(2)}, u32[]{:S(2)}) %collective-permute-start.12) | collective-permute-done | bytes 131104 | tf_op jit(solution)/shard_map/ppermute | solution.py:766
  30.8 2.1 %collective-permute-start.10 = (bf16[256,256]{1,0:T(8,128)(2,1)S(1)}, bf16[256,256]{1,0:T(8,128)(2,1)S(1)}, u32[]{:S(2)}, u32[]{:S(2)}) collective-permute-start(bf16[256,256]{1,0:T(8,128)(2,1)S(1)} %get-tuple-element.72), channel_id=1, source_target_pairs={{0,12},{4,8},{8,4},{12,0},{1,13},{5,9},{9,5},{13,1},{2,14},{6,10},... | collective-permute-start | bytes 393224 | tf_op jit(solution)/shard_map/ppermute | solution.py:766
  32.9 2.3 %shard_map.101 = (bf16[2,256,256]{2,1,0:T(8,128)(2,1)S(1)}, bf16[2,256,256]{2,1,0:T(8,128)(2,1)S(1)}) custom-call(f32[1024,16]{1,0:T(8,128)S(1)} %get-tuple-element.59.refs_0_, bf16[512,512]{1,0:T(8,128)(2,1)S(1)} %copy-done, bf16[512,256]{1,0:T(8,128)(2,1)S(1)} %copy-done.1, f32[1024,512]{1,0:T(8,128)S(1)} %get-tuple-element.75.refs_3_, ...), custom_call_target="tpu_custom_call" | custom-call | flops 6000000000 | tf_op jit(solution)/shard_map/pallas_call | solution.py:78
  35.2 1.6 %collective-permute-start.14 = (bf16[2,256,256]{2,1,0:T(8,128)(2,1)S(1)}, bf16[2,256,256]{2,1,0:T(8,128)(2,1)S(1)}, u32[]{:S(2)}, u32[]{:S(2)}) collective-permute-start(bf16[2,256,256]{2,1,0:T(8,128)(2,1)S(1)} %get-tuple-element.81), channel_id=1, source_target_pairs={{0,4},{4,0},{8,12},{12,8},{1,5},{5,1},{9,13},{13,9},{2,6},{6,2},{1... | collective-permute-start | bytes 786440 | tf_op jit(solution)/shard_map/ppermute | solution.py:766
  36.8 1.7 %collective-permute-done.5.refs_6_ = bf16[2,256,256]{2,1,0:T(8,128)(2,1)S(1)} collective-permute-done((bf16[2,256,256]{2,1,0:T(8,128)(2,1)S(1)}, bf16[2,256,256]{2,1,0:T(8,128)(2,1)S(1)}, u32[]{:S(2)}, u32[]{:S(2)}) %collective-permute-start.5) | collective-permute-done | bytes 262176 | tf_op jit(solution)/shard_map/ppermute | solution.py:766
  38.5 2.1 %shard_map.98 = (bf16[2,256,128]{2,1,0:T(8,128)(2,1)S(1)}, bf16[2,256,128]{2,1,0:T(8,128)(2,1)S(1)}, bf16[2,256,128]{2,1,0:T(8,128)(2,1)S(1)}, bf16[2,256,128]{2,1,0:T(8,128)(2,1)S(1)}) custom-call(f32[1024,16]{1,0:T(8,128)S(1)} %get-tuple-element.59.refs_0_, bf16[512,512]{1,0:T(8,128)(2,1)S(1)} %copy-done, bf16[512,256]{1,0:T(8,128)(2,1)S(1)} %copy-done.1, ...), custom_call_target="tpu_custom_call" | custom-call | flops 4800000000 | tf_op jit(solution)/shard_map/pallas_call | solution.py:78
  40.7 2.0 %collective-permute-start.7 = (bf16[2,256,128]{2,1,0:T(8,128)(2,1)S(1)}, bf16[2,256,128]{2,1,0:T(8,128)(2,1)S(1)}, u32[]{:S(2)}, u32[]{:S(2)}) collective-permute-start(bf16[2,256,128]{2,1,0:T(8,128)(2,1)S(1)} %get-tuple-element.67), channel_id=1, source_target_pairs={{0,4},{4,0},{8,12},{12,8},{1,5},{5,1},{9,13},{13,9},{2,6},{6,2},{1... | collective-permute-start | bytes 393224 | tf_op jit(solution)/shard_map/ppermute | solution.py:766
  42.7 1.8 %shard_map.102 = (bf16[1024,256]{1,0:T(8,128)(2,1)}, bf16[3,1024,256]{2,1,0:T(8,128)(2,1)}, f32[2,3,256,128]{3,2,1,0:T(8,128)S(1)}) custom-call(bf16[2,3,256,256]{3,2,1,0:T(8,128)(2,1)S(1)} %get-tuple-element.50.refs_0_, bf16[2,256,256]{2,1,0:T(8,128)(2,1)S(1)} %get-tuple-element.51.refs_1_, bf16[2,3,256,256]{3,2,1,0:T(8,128)(2,1)S(1)} %get-tuple-element.57.refs_2_, ...), custom_call_target="tpu_custom_call" | custom-call | flops 1440000000 | tf_op jit(solution)/shard_map/pallas_call | solution.py:78
  44.6 2.2 %collective-permute-done.14.refs_7_.refs_5_ = bf16[2,256,256]{2,1,0:T(8,128)(2,1)S(1)} collective-permute-done((bf16[2,256,256]{2,1,0:T(8,128)(2,1)S(1)}, bf16[2,256,256]{2,1,0:T(8,128)(2,1)S(1)}, u32[]{:S(2)}, u32[]{:S(2)}) %collective-permute-start.14) | collective-permute-done | bytes 262176 | tf_op jit(solution)/shard_map/ppermute | solution.py:766
  46.7 1.2 %shard_map.103 = (bf16[1024,256]{1,0:T(8,128)(2,1)}, bf16[3,1024,256]{2,1,0:T(8,128)(2,1)}, f32[1,3,256,128]{3,2,1,0:T(8,128)S(1)}) custom-call(bf16[2,3,256,256]{3,2,1,0:T(8,128)(2,1)S(1)} %get-tuple-element.50.refs_0_, bf16[2,256,256]{2,1,0:T(8,128)(2,1)S(1)} %get-tuple-element.51.refs_1_, ...), custom_call_target="tpu_custom_call", output_to_operand_aliasing={{0}: (9, {}), {1}: (10, {})} | custom-call | flops 720000000 | tf_op jit(solution)/shard_map/pallas_call | solution.py:78
  48.0 1.6 %collective-permute-done.6.refs_7_ = bf16[2,256,128]{2,1,0:T(8,128)(2,1)S(1)} collective-permute-done((bf16[2,256,128]{2,1,0:T(8,128)(2,1)S(1)}, bf16[2,256,128]{2,1,0:T(8,128)(2,1)S(1)}, u32[]{:S(2)}, u32[]{:S(2)}) %collective-permute-start.6) | collective-permute-done | bytes 131104 | tf_op jit(solution)/shard_map/ppermute | solution.py:766
  49.5 0.7 %shard_map.105 = f32[8,1024]{1,0:T(8,128)S(1)} custom-call(bf16[2,3,256,256]{3,2,1,0:T(8,128)(2,1)S(1)} %get-tuple-element.50.refs_0_, bf16[2,256,256]{2,1,0:T(8,128)(2,1)S(1)} %get-tuple-element.51.refs_1_, bf16[2,3,256,256]{3,2,1,0:T(8,128)(2,1)S(1)} %get-tuple-element.57.refs_2_, bf16[2,256,256]{2,1,0:T(8,128)(2,1)S(1)} %get-tuple-element.58.refs_3_, ...), custom_call_target="tpu_custom_call" | custom-call | flops 3600000000 | tf_op jit(solution)/shard_map/pallas_call | solution.py:78
  50.2 2.1 %collective-permute-start.15 = (f32[8,1024]{1,0:T(8,128)S(1)}, f32[8,1024]{1,0:T(8,128)S(1)}, u32[]{:S(2)}, u32[]{:S(2)}) collective-permute-start(f32[8,1024]{1,0:T(8,128)S(1)} %shard_map.105), channel_id=1, source_target_pairs={{0,12},{4,0},{8,4},{12,8},{1,13},{5,1},{9,5},{13,9},{2,14},{6,2},{... | collective-permute-start | bytes 98312 | tf_op jit(solution)/shard_map/ppermute | solution.py:770
  52.4 1.2 %shard_map.104 = (bf16[1024,256]{1,0:T(8,128)(2,1)}, bf16[3,1024,256]{2,1,0:T(8,128)(2,1)}, f32[1,3,256,128]{3,2,1,0:T(8,128)S(1)}) custom-call(bf16[2,3,256,256]{3,2,1,0:T(8,128)(2,1)S(1)} %get-tuple-element.50.refs_0_, bf16[2,256,256]{2,1,0:T(8,128)(2,1)S(1)} %get-tuple-element.51.refs_1_, ...), custom_call_target="tpu_custom_call", output_to_operand_aliasing={{0}: (11, {}), {1}: (12, {})} | custom-call | flops 720000000 | tf_op jit(solution)/shard_map/pallas_call | solution.py:78
  53.6 0.6 collective-permute-done.15.refs_0_
  54.2 1.4 %shard_map.106 = bf16[3,1024,256]{2,1,0:T(8,128)(2,1)} custom-call(f32[8,1024]{1,0:T(8,128)S(1)} %collective-permute-done.15.refs_0_, f32[16,1024]{1,0:T(8,128)S(1)} %get-tuple-element.92.refs_1_, bf16[48,384]{1,0:T(8,128)(2,1)S(1)} %get-tuple-element.93.refs_2_, ...), custom_call_target="tpu_custom_call", output_to_operand_aliasing={{}: (6, {})} | custom-call | flops 1140000000 | tf_op jit(solution)/shard_map/pallas_call | solution.py:78
  (23 shorter events, 0.5 us)
Async XLA Ops:
  0.6 9.0 %copy-start.4 = (s32[16]{0:T(128)S(1)}, s32[16]{0:T(128)}, u32[]{:S(2)}) copy-start(s32[16]{0:T(128)} %param.13) | copy-start | bytes 196
  0.6 9.0 %copy-start.3 = (f32[1024]{0:T(1024)S(1)}, f32[1024]{0:T(1024)}, u32[]{:S(2)}) copy-start(f32[1024]{0:T(1024)} %param.12) | copy-start | bytes 12292
  0.7 9.0 %copy-start.2 = (f32[3,3,1024]{2,1,0:T(4,128)S(1)}, f32[3,3,1024]{2,1,0:T(4,128)}, u32[]{:S(2)}) copy-start(f32[3,3,1024]{2,1,0:T(4,128)} %refs_4_.1) | copy-start | bytes 110596
  2.2 7.5 %collective-permute-start = (bf16[16,1024]{1,0:T(8,128)(2,1)S(1)}, bf16[16,1024]{1,0:T(8,128)(2,1)S(1)}, u32[]{:S(2)}, u32[]{:S(2)}) collective-permute-start(bf16[16,1024]{1,0:T(8,128)(2,1)S(1)} %get-tuple-element.49), channel_id=1, source_target_pairs={{0,4},{4,8},{8,12},{12,0},{1,5},{5,9},{9,13},{13,1},{2,6},{6,10},{... | collective-permute-start | bytes 98312 | tf_op jit(solution)/shard_map/ppermute | solution.py:770
  5.2 11.5 %collective-permute-start.1 = (bf16[256,256]{1,0:T(8,128)(2,1)S(1)}, bf16[256,256]{1,0:T(8,128)(2,1)S(1)}, u32[]{:S(2)}, u32[]{:S(2)}) collective-permute-start(bf16[256,256]{1,0:T(8,128)(2,1)S(1)} %get-tuple-element.61), channel_id=1, source_target_pairs={{0,4},{4,0},{8,12},{12,8},{1,5},{5,1},{9,13},{13,9},{2,6},{6,2},{1... | collective-permute-start | bytes 393224 | tf_op jit(solution)/shard_map/ppermute | solution.py:766
  6.8 12.7 %collective-permute-start.2 = (bf16[256,256]{1,0:T(8,128)(2,1)S(1)}, bf16[256,256]{1,0:T(8,128)(2,1)S(1)}, u32[]{:S(2)}, u32[]{:S(2)}) collective-permute-start(bf16[256,256]{1,0:T(8,128)(2,1)S(1)} %get-tuple-element.62), channel_id=1, source_target_pairs={{0,8},{4,12},{8,0},{12,4},{1,9},{5,13},{9,1},{13,5},{2,10},{6,14},... | collective-permute-start | bytes 393224 | tf_op jit(solution)/shard_map/ppermute | solution.py:766
  7.9 13.7 %collective-permute-start.3 = (bf16[256,256]{1,0:T(8,128)(2,1)S(1)}, bf16[256,256]{1,0:T(8,128)(2,1)S(1)}, u32[]{:S(2)}, u32[]{:S(2)}) collective-permute-start(bf16[256,256]{1,0:T(8,128)(2,1)S(1)} %get-tuple-element.63), channel_id=1, source_target_pairs={{0,12},{4,8},{8,4},{12,0},{1,13},{5,9},{9,5},{13,1},{2,14},{6,10},... | collective-permute-start | bytes 393224 | tf_op jit(solution)/shard_map/ppermute | solution.py:766
  12.3 11.0 %collective-permute-start.8 = (bf16[256,256]{1,0:T(8,128)(2,1)S(1)}, bf16[256,256]{1,0:T(8,128)(2,1)S(1)}, u32[]{:S(2)}, u32[]{:S(2)}) collective-permute-start(bf16[256,256]{1,0:T(8,128)(2,1)S(1)} %get-tuple-element.70), channel_id=1, source_target_pairs={{0,4},{4,0},{8,12},{12,8},{1,5},{5,1},{9,13},{13,9},{2,6},{6,2},{1... | collective-permute-start | bytes 393224 | tf_op jit(solution)/shard_map/ppermute | solution.py:766
  13.0 14.2 %collective-permute-start.11 = (bf16[256,256]{1,0:T(8,128)(2,1)S(1)}, bf16[256,256]{1,0:T(8,128)(2,1)S(1)}, u32[]{:S(2)}, u32[]{:S(2)}) collective-permute-start(bf16[256,256]{1,0:T(8,128)(2,1)S(1)} %get-tuple-element.78), channel_id=1, source_target_pairs={{0,4},{4,0},{8,12},{12,8},{1,5},{5,1},{9,13},{13,9},{2,6},{6,2},{1... | collective-permute-start | bytes 393224 | tf_op jit(solution)/shard_map/ppermute | solution.py:766
  14.4 10.5 %copy-start = (bf16[512,512]{1,0:T(8,128)(2,1)S(1)}, bf16[512,512]{1,0:T(8,128)(2,1)}, u32[]{:S(2)}) copy-start(bf16[512,512]{1,0:T(8,128)(2,1)} %constant.4.clone.refs_1_.refs_0_) | copy-start | bytes 1572868
  14.4 10.5 %copy-start.1 = (bf16[512,256]{1,0:T(8,128)(2,1)S(1)}, bf16[512,256]{1,0:T(8,128)(2,1)}, u32[]{:S(2)}) copy-start(bf16[512,256]{1,0:T(8,128)(2,1)} %constant.5.clone.refs_2_.refs_1_) | copy-start | bytes 786436
  16.8 14.0 %collective-permute-start.12 = (bf16[256,256]{1,0:T(8,128)(2,1)S(1)}, bf16[256,256]{1,0:T(8,128)(2,1)S(1)}, u32[]{:S(2)}, u32[]{:S(2)}) collective-permute-start(bf16[256,256]{1,0:T(8,128)(2,1)S(1)} %get-tuple-element.79), channel_id=1, source_target_pairs={{0,8},{4,12},{8,0},{12,4},{1,9},{5,13},{9,1},{13,5},{2,10},{6,14},... | collective-permute-start | bytes 393224 | tf_op jit(solution)/shard_map/ppermute | solution.py:766
  19.5 13.3 %collective-permute-start.13 = (bf16[256,256]{1,0:T(8,128)(2,1)S(1)}, bf16[256,256]{1,0:T(8,128)(2,1)S(1)}, u32[]{:S(2)}, u32[]{:S(2)}) collective-permute-start(bf16[256,256]{1,0:T(8,128)(2,1)S(1)} %get-tuple-element.80), channel_id=1, source_target_pairs={{0,12},{4,8},{8,4},{12,0},{1,13},{5,9},{9,5},{13,1},{2,14},{6,10},... | collective-permute-start | bytes 393224 | tf_op jit(solution)/shard_map/ppermute | solution.py:766
  21.6 16.9 %collective-permute-start.5 = (bf16[2,256,256]{2,1,0:T(8,128)(2,1)S(1)}, bf16[2,256,256]{2,1,0:T(8,128)(2,1)S(1)}, u32[]{:S(2)}, u32[]{:S(2)}) collective-permute-start(bf16[2,256,256]{2,1,0:T(8,128)(2,1)S(1)} %get-tuple-element.65), channel_id=1, source_target_pairs={{0,4},{4,0},{8,12},{12,8},{1,5},{5,1},{9,13},{13,9},{2,6},{6,2},{1... | collective-permute-start | bytes 786440 | tf_op jit(solution)/shard_map/ppermute | solution.py:766
  23.3 15.3 %collective-permute-start.4 = (bf16[768,256]{1,0:T(8,128)(2,1)S(1)}, bf16[768,256]{1,0:T(8,128)(2,1)S(1)}, u32[]{:S(2)}, u32[]{:S(2)}) collective-permute-start(bf16[768,256]{1,0:T(8,128)(2,1)S(1)} %pad_maximum_fusion), channel_id=1, source_target_pairs={{0,16},{16,0},{1,17},{17,1},{2,18},{18,2},{3,19},{19,3},{4,20},{20... | collective-permute-start | bytes 1179656 | tf_op jit(solution)/shard_map/ppermute | solution.py:766
  27.3 15.4 %collective-permute-start.9 = (bf16[256,256]{1,0:T(8,128)(2,1)S(1)}, bf16[256,256]{1,0:T(8,128)(2,1)S(1)}, u32[]{:S(2)}, u32[]{:S(2)}) collective-permute-start(bf16[256,256]{1,0:T(8,128)(2,1)S(1)} %get-tuple-element.71), channel_id=1, source_target_pairs={{0,8},{4,12},{8,0},{12,4},{1,9},{5,13},{9,1},{13,5},{2,10},{6,14},... | collective-permute-start | bytes 393224 | tf_op jit(solution)/shard_map/ppermute | solution.py:766
  30.8 11.9 %collective-permute-start.10 = (bf16[256,256]{1,0:T(8,128)(2,1)S(1)}, bf16[256,256]{1,0:T(8,128)(2,1)S(1)}, u32[]{:S(2)}, u32[]{:S(2)}) collective-permute-start(bf16[256,256]{1,0:T(8,128)(2,1)S(1)} %get-tuple-element.72), channel_id=1, source_target_pairs={{0,12},{4,8},{8,4},{12,0},{1,13},{5,9},{9,5},{13,1},{2,14},{6,10},... | collective-permute-start | bytes 393224 | tf_op jit(solution)/shard_map/ppermute | solution.py:766
  35.2 11.6 %collective-permute-start.14 = (bf16[2,256,256]{2,1,0:T(8,128)(2,1)S(1)}, bf16[2,256,256]{2,1,0:T(8,128)(2,1)S(1)}, u32[]{:S(2)}, u32[]{:S(2)}) collective-permute-start(bf16[2,256,256]{2,1,0:T(8,128)(2,1)S(1)} %get-tuple-element.81), channel_id=1, source_target_pairs={{0,4},{4,0},{8,12},{12,8},{1,5},{5,1},{9,13},{13,9},{2,6},{6,2},{1... | collective-permute-start | bytes 786440 | tf_op jit(solution)/shard_map/ppermute | solution.py:766
  40.6 8.9 %collective-permute-start.6 = (bf16[2,256,128]{2,1,0:T(8,128)(2,1)S(1)}, bf16[2,256,128]{2,1,0:T(8,128)(2,1)S(1)}, u32[]{:S(2)}, u32[]{:S(2)}) collective-permute-start(bf16[2,256,128]{2,1,0:T(8,128)(2,1)S(1)} %get-tuple-element.66), channel_id=1, source_target_pairs={{0,4},{4,0},{8,12},{12,8},{1,5},{5,1},{9,13},{13,9},{2,6},{6,2},{1... | collective-permute-start | bytes 393224 | tf_op jit(solution)/shard_map/ppermute | solution.py:766
  40.7 11.7 %collective-permute-start.7 = (bf16[2,256,128]{2,1,0:T(8,128)(2,1)S(1)}, bf16[2,256,128]{2,1,0:T(8,128)(2,1)S(1)}, u32[]{:S(2)}, u32[]{:S(2)}) collective-permute-start(bf16[2,256,128]{2,1,0:T(8,128)(2,1)S(1)} %get-tuple-element.67), channel_id=1, source_target_pairs={{0,4},{4,0},{8,12},{12,8},{1,5},{5,1},{9,13},{13,9},{2,6},{6,2},{1... | collective-permute-start | bytes 393224 | tf_op jit(solution)/shard_map/ppermute | solution.py:766
  50.2 3.9 %collective-permute-start.15 = (f32[8,1024]{1,0:T(8,128)S(1)}, f32[8,1024]{1,0:T(8,128)S(1)}, u32[]{:S(2)}, u32[]{:S(2)}) collective-permute-start(f32[8,1024]{1,0:T(8,128)S(1)} %shard_map.105), channel_id=1, source_target_pairs={{0,12},{4,0},{8,4},{12,8},{1,13},{5,1},{9,5},{13,9},{2,14},{6,2},{... | collective-permute-start | bytes 98312 | tf_op jit(solution)/shard_map/ppermute | solution.py:770

commit v9 on v8

--- a/solution.py
+++ b/solution.py
@@ -510,9 +510,17 @@
     )
 
 
+def pick_first(value):
+    row = lax.broadcasted_iota(jnp.int32, (16, 128), 0)
+    lane = lax.broadcasted_iota(jnp.int32, (16, 128), 1)
+    table = jnp.where((row == lane) & (row < 2), 1.0, 0.0).astype(BF16)
+    dims = (((1,), (1,)), ((), ()))
+    return lax.dot_general(table, value, dims, preferred_element_type=F32).astype(BF16)
+
+
 def other_body(layout, place_ref, cols_ref, forward_ref, inverse_ref, filt_ref, other_ref, *rest):
     parts, half, sub, span = layout.parts, layout.half, layout.sub, layout.span
-    seconds, early, late = (rest[k * half : (k + 1) * half] for k in range(3))
+    seconds, leads, outs = (rest[k * half : (k + 1) * half] for k in range(3))
     raw, spec, ready, back = rest[3 * half :]
     side, own, _ = where_am_i(place_ref, layout)
     rank = place_ref[0]
@@ -565,8 +573,8 @@
             value = back[rows_at(source, sub, sub), :]
             direct = seconds[step][kind].astype(F32)
             found = (value + skip * direct).astype(BF16)
-            early[step][kind] = found[:, :128]
-            late[step][kind] = found[:, 128:]
+            outs[step][kind] = found
+            leads[step][kind] = pick_first(found[:, :128])
 
 
 def other_half(layout, cols, tables, filters, other, seconds):
@@ -576,7 +584,7 @@
         other_body,
         layout,
         (cols, *tables, filters, other, *seconds),
-        [jax.ShapeDtypeStruct((2, sub, w), BF16) for w in (128, span - 128) for _ in range(half)],
+        [jax.ShapeDtypeStruct((2, 16, sub), BF16)] * half + [jax.ShapeDtypeStruct((2, sub, span), BF16)] * half,
         [
             pltpu.VMEM(((parts + 2 * half) * sub, span), BF16),
             pltpu.VMEM((rows, 2 * span), F32),
@@ -588,13 +596,9 @@
     return found[:half], found[half:]
 
 
-def results(side, found, crossed, here):
-    if isinstance(found, tuple):
-        plain, mixed = (jnp.concatenate([part[(k, here[0])] for part in found], axis=1) for k in range(2))
-    else:
-        plain, mixed = found[(0, *here)], found[(1, *here)]
+def results(side, plain, mixed, crossed):
     if crossed is not None:
-        mixed = (mixed.astype(F32) + crossed[here].astype(F32)).astype(BF16)
+        mixed = (mixed.astype(F32) + crossed.astype(F32)).astype(BF16)
     return jnp.where(side == 0, plain, mixed), jnp.where(side == 0, mixed, plain)
 
 
@@ -607,8 +611,13 @@
         for other in range(2):
             place = rows_at(channel_block(place_ref, layout, turn, other) * sub, sub, sub)
             qkv, dout_ref = (qkv_other, dout_other) if other else (qkv_main, dout_main)
-            here = (slice(None), slice(0, 128))
-            pair = results(side, (rest if other else main)[turn], crossed[turn] if other else None, here)
+            source = (rest if other else main)[turn]
+            if other and turn:
+                fill = jnp.zeros((112, sub), F32)
+                pair = [jnp.concatenate([source[k].astype(F32), fill], axis=0).T.astype(BF16) for k in range(2)]
+            else:
+                pair = [source[k, :, 0:128] for k in range(2)]
+            pair = results(side, *pair, crossed[turn][:, 0:128] if other else None)
             y_out, dmixed = (f.astype(F32) for f in pair)
             grads[0, place, :] = dout_ref[turn, :, 0:128].astype(F32) * y_out
             grads[1, place, :] = dmixed * qkv[turn, 2, :, 0:128].astype(F32)
@@ -634,7 +643,7 @@
     rows, span = layout.sub, layout.span
     found = []
     for _, other in blocks:
-        count = 3 if other else 1
+        count = 2 if other else 1
         found.append(refs[:count])
         refs = refs[count:]
     refs = refs[1 + 2 * chained :]
@@ -647,12 +656,13 @@
     for k, (turn, other) in enumerate(blocks):
         block = rows_at(channel_block(place_ref, layout, turn, other) * rows, rows, rows)
         qkv, dout_ref = (qkv_other, dout_other) if other else (qkv_main, dout_main)
-        source, crossed = (found[k][:2], found[k][2]) if other else (found[k][0], None)
+        source, crossed = found[k] if other else (found[k][0], None)
         spread[...] = dot(split_ref[block, :], lanes_ref[...])
 
         def tile(index, _, k=k, turn=turn, qkv=qkv, dout_ref=dout_ref, source=source, crossed=crossed):
             local_rows = rows_at(index * group, group, group)
-            pair = results(side, source, crossed, (local_rows, slice(None)))
+            pair = [source[kind, local_rows, :] for kind in range(2)]
+            pair = results(side, *pair, None if crossed is None else crossed[local_rows, :])
             out_ref[k, local_rows, :] = qkv[turn, 0, local_rows, :] * pair[0]
             y_out, dmixed = (f.astype(F32) for f in pair)
             grads = (
@@ -685,8 +695,8 @@
     span, channels, rows, count = layout.span, layout.channels, layout.sub, len(blocks)
     operands = [*gated, *shared]
     for turn, other in blocks:
-        main, early, late, crossed = (f[turn] for f in found)
-        operands += [early, late, crossed] if other else [main]
+        main, rest, crossed = (f[turn] for f in found)
+        operands += [rest, crossed] if other else [main]
     in_specs = [HELD] * len(operands) + [ANYWHERE]
     operands.append(after)
     aliases = {}
@@ -796,16 +806,16 @@
     crossed = [swap(sent[step], step + half, parts) for step in range(half)]
     main = main_half(layout, cols, tables, known, near, firsts, trails, cross)
     main = [main[0]] + [swap(main[step], step, parts) for step in range(1, half)]
-    early, late = other_half(layout, cols, tables, own_filt[1], other, seconds)
-    crossed = hold(layout, crossed, early[0])
-    early = [early[0]] + [swap(early[step], step, parts) for step in range(1, half)]
-    late = [late[0]] + [swap(late[step], step, parts) for step in range(1, half)]
+    leads, rest = other_half(layout, cols, tables, own_filt[1], other, seconds)
+    crossed = hold(layout, crossed, leads[0])
+    leads = [swap(leads[step], step, parts) for step in range(1, half)]
+    rest = [rest[0]] + [swap(rest[step], step, parts) for step in range(1, half)]
 
     gated = (*gated_main, *gated_other)
-    found = (main, early, late, crossed)
+    found = (main, rest, crossed)
     shared = (split, lanes, keep)
     lists = [[(0, 0), (0, 1)], [(turn, 0) for turn in range(1, half)], [(turn, 1) for turn in range(1, half)]]
-    ahead = around(first_grads(layout, gated, main, early, crossed), -1, parts)
+    ahead = around(first_grads(layout, gated, main, [rest[0], *leads], crossed), -1, parts)
     done, partials, after = (), [], crossed[0]
     for blocks in lists:
         *done, partial = final(blocks, layout, gated, shared, found, after, done)

time: 55.7 us -> 54.5 us (0.978)
  waiting for transfers between devices: 10.1 us -> 8.53 us
    ppermute x14, waiting for transfers between devices: 9.56 us -> 8.53 us  [swap(): lax.ppermute(value, axis, [(source, source ^ step) for source in range(pa...]
  transfers between devices with their start and end apart: 16 -> 16, of which waited for: 7 -> 6; matrix products, arithmetic and copies ran while one was open for 0% -> 0% of each run, Pallas kernels for 30% -> 31%
where the time goes in v9:
time: 54.5 us; the launch traced here: 54.3 us
  starting transfers between devices  25.2 us (46%)
  Pallas kernels  19.8 us (36%)
  waiting for transfers between devices  8.53 us (16%)
  between operations  0.79 us (1%)
    ppermute x14, starting transfers between devices, swap(): lax.ppermute(value, axis, [(source, source ^ step) for source in range(pa...  20 us
    pallas_call x12, Pallas kernels, run(): pl.pallas_call(kernel, out_shape=outs, in_specs=in_specs or [HELD] * len(...  19.8 us
    ppermute x14, waiting for transfers between devices, swap(): lax.ppermute(value, axis, [(source, source ^ step) for source in range(pa...  8.53 us
    ppermute x2, starting transfers between devices, around(): lax.ppermute(value, 'seq', [(source, (source + steps) % parts) for source...  5.21 us
  transfers between devices with their start and end apart: 16, of which 6 were waited for; matrix products, arithmetic and copies ran while one was open for 0% of the time, Pallas kernels for 31%

profile of v9, /device:TPU:0, one launch (start us, length us, event | category | flops | bytes accessed | tf_op | source)
XLA Modules:
  0.0 54.3 jit_solution(16626628687676576561)
XLA Ops:
  0.7 1.5 %shard_map.95 = (bf16[16,1024]{1,0:T(8,128)(2,1)S(1)}, bf16[256,256]{1,0:T(8,128)(2,1)S(1)}, bf16[256,256]{1,0:T(8,128)(2,1)S(1)}, bf16[256,256]{1,0:T(8,128)(2,...) custom-call(bf16[3,1024,256]{2,1,0:T(8,128)(2,1)} %refs_0_.6, bf16[1024,256]{1,0:T(8,128)(2,1)} %refs_1_.6), custom_call_target="tpu_custom_call" | custom-call | flops 1200000000 | tf_op jit(solution)/shard_map/pallas_call | solution.py:78
  2.2 3.1 %collective-permute-start = (bf16[16,1024]{1,0:T(8,128)(2,1)S(1)}, bf16[16,1024]{1,0:T(8,128)(2,1)S(1)}, u32[]{:S(2)}, u32[]{:S(2)}) collective-permute-start(bf16[16,1024]{1,0:T(8,128)(2,1)S(1)} %get-tuple-element.49), channel_id=1, source_target_pairs={{0,4},{4,8},{8,12},{12,0},{1,5},{5,9},{9,13},{13,1},{2,6},{6,10},{... | collective-permute-start | bytes 98312 | tf_op jit(solution)/shard_map/ppermute | solution.py:780
  5.2 1.6 %collective-permute-start.1 = (bf16[256,256]{1,0:T(8,128)(2,1)S(1)}, bf16[256,256]{1,0:T(8,128)(2,1)S(1)}, u32[]{:S(2)}, u32[]{:S(2)}) collective-permute-start(bf16[256,256]{1,0:T(8,128)(2,1)S(1)} %get-tuple-element.61), channel_id=1, source_target_pairs={{0,4},{4,0},{8,12},{12,8},{1,5},{5,1},{9,13},{13,9},{2,6},{6,2},{1... | collective-permute-start | bytes 393224 | tf_op jit(solution)/shard_map/ppermute | solution.py:776
  6.8 1.1 %collective-permute-start.2 = (bf16[256,256]{1,0:T(8,128)(2,1)S(1)}, bf16[256,256]{1,0:T(8,128)(2,1)S(1)}, u32[]{:S(2)}, u32[]{:S(2)}) collective-permute-start(bf16[256,256]{1,0:T(8,128)(2,1)S(1)} %get-tuple-element.62), channel_id=1, source_target_pairs={{0,8},{4,12},{8,0},{12,4},{1,9},{5,13},{9,1},{13,5},{2,10},{6,14},... | collective-permute-start | bytes 393224 | tf_op jit(solution)/shard_map/ppermute | solution.py:776
  7.9 1.7 %collective-permute-start.3 = (bf16[256,256]{1,0:T(8,128)(2,1)S(1)}, bf16[256,256]{1,0:T(8,128)(2,1)S(1)}, u32[]{:S(2)}, u32[]{:S(2)}) collective-permute-start(bf16[256,256]{1,0:T(8,128)(2,1)S(1)} %get-tuple-element.63), channel_id=1, source_target_pairs={{0,12},{4,8},{8,4},{12,0},{1,13},{5,9},{9,5},{13,1},{2,14},{6,10},... | collective-permute-start | bytes 393224 | tf_op jit(solution)/shard_map/ppermute | solution.py:776
  9.7 2.6 %shard_map.96 = (bf16[2,3,256,256]{3,2,1,0:T(8,128)(2,1)S(1)}, bf16[2,256,256]{2,1,0:T(8,128)(2,1)S(1)}, bf16[256,256]{1,0:T(8,128)(2,1)S(1)}, bf16[256,256]{1,0...) custom-call(bf16[3,1024,256]{2,1,0:T(8,128)(2,1)} %refs_0_.6, ...), custom_call_target="tpu_custom_call" | custom-call | flops 3600000000 | tf_op jit(solution)/shard_map/pallas_call | solution.py:78
  12.3 0.7 %collective-permute-start.7 = (bf16[256,256]{1,0:T(8,128)(2,1)S(1)}, bf16[256,256]{1,0:T(8,128)(2,1)S(1)}, u32[]{:S(2)}, u32[]{:S(2)}) collective-permute-start(bf16[256,256]{1,0:T(8,128)(2,1)S(1)} %get-tuple-element.69), channel_id=1, source_target_pairs={{0,4},{4,0},{8,12},{12,8},{1,5},{5,1},{9,13},{13,9},{2,6},{6,2},{1... | collective-permute-start | bytes 393224 | tf_op jit(solution)/shard_map/ppermute | solution.py:776
  13.0 1.4 %collective-permute-start.10 = (bf16[256,256]{1,0:T(8,128)(2,1)S(1)}, bf16[256,256]{1,0:T(8,128)(2,1)S(1)}, u32[]{:S(2)}, u32[]{:S(2)}) collective-permute-start(bf16[256,256]{1,0:T(8,128)(2,1)S(1)} %get-tuple-element.77), channel_id=1, source_target_pairs={{0,4},{4,0},{8,12},{12,8},{1,5},{5,1},{9,13},{13,9},{2,6},{6,2},{1... | collective-permute-start | bytes 393224 | tf_op jit(solution)/shard_map/ppermute | solution.py:776
  14.4 2.3 %shard_map.97 = (bf16[2,3,256,256]{3,2,1,0:T(8,128)(2,1)S(1)}, bf16[2,256,256]{2,1,0:T(8,128)(2,1)S(1)}, bf16[256,256]{1,0:T(8,128)(2,1)S(1)}, bf16[256,256]{1,0...) custom-call(bf16[3,1024,256]{2,1,0:T(8,128)(2,1)} %refs_0_.6, ...), custom_call_target="tpu_custom_call" | custom-call | flops 600000000 | tf_op jit(solution)/shard_map/pallas_call | solution.py:78
  16.8 1.8 %collective-permute-start.11 = (bf16[256,256]{1,0:T(8,128)(2,1)S(1)}, bf16[256,256]{1,0:T(8,128)(2,1)S(1)}, u32[]{:S(2)}, u32[]{:S(2)}) collective-permute-start(bf16[256,256]{1,0:T(8,128)(2,1)S(1)} %get-tuple-element.78), channel_id=1, source_target_pairs={{0,8},{4,12},{8,0},{12,4},{1,9},{5,13},{9,1},{13,5},{2,10},{6,14},... | collective-permute-start | bytes 393224 | tf_op jit(solution)/shard_map/ppermute | solution.py:776
  18.5 1.0 %collective-permute-done.2.refs_4_ = bf16[256,256]{1,0:T(8,128)(2,1)S(1)} collective-permute-done((bf16[256,256]{1,0:T(8,128)(2,1)S(1)}, bf16[256,256]{1,0:T(8,128)(2,1)S(1)}, u32[]{:S(2)}, u32[]{:S(2)}) %collective-permute-start.2) | collective-permute-done | bytes 131104 | tf_op jit(solution)/shard_map/ppermute | solution.py:776
  19.5 2.1 %collective-permute-start.12 = (bf16[256,256]{1,0:T(8,128)(2,1)S(1)}, bf16[256,256]{1,0:T(8,128)(2,1)S(1)}, u32[]{:S(2)}, u32[]{:S(2)}) collective-permute-start(bf16[256,256]{1,0:T(8,128)(2,1)S(1)} %get-tuple-element.79), channel_id=1, source_target_pairs={{0,12},{4,8},{8,4},{12,0},{1,13},{5,9},{9,5},{13,1},{2,14},{6,10},... | collective-permute-start | bytes 393224 | tf_op jit(solution)/shard_map/ppermute | solution.py:776
  21.6 1.6 %collective-permute-start.5 = (bf16[2,256,256]{2,1,0:T(8,128)(2,1)S(1)}, bf16[2,256,256]{2,1,0:T(8,128)(2,1)S(1)}, u32[]{:S(2)}, u32[]{:S(2)}) collective-permute-start(bf16[2,256,256]{2,1,0:T(8,128)(2,1)S(1)} %get-tuple-element.65), channel_id=1, source_target_pairs={{0,4},{4,0},{8,12},{12,8},{1,5},{5,1},{9,13},{13,9},{2,6},{6,2},{1... | collective-permute-start | bytes 786440 | tf_op jit(solution)/shard_map/ppermute | solution.py:776
  23.3 1.6 %collective-permute-start.4 = (bf16[768,256]{1,0:T(8,128)(2,1)S(1)}, bf16[768,256]{1,0:T(8,128)(2,1)S(1)}, u32[]{:S(2)}, u32[]{:S(2)}) collective-permute-start(bf16[768,256]{1,0:T(8,128)(2,1)S(1)} %pad_maximum_fusion), channel_id=1, source_target_pairs={{0,16},{16,0},{1,17},{17,1},{2,18},{18,2},{3,19},{19,3},{4,20},{20... | collective-permute-start | bytes 1179656 | tf_op jit(solution)/shard_map/ppermute | solution.py:776
  24.8 2.1 %shard_map.99 = (bf16[256,256]{1,0:T(8,128)(2,1)S(1)}, bf16[256,256]{1,0:T(8,128)(2,1)S(1)}, f32[1024,512]{1,0:T(8,128)S(1)}, f32[512,512]{1,0:T(8,128)S(1)}) custom-call(bf16[512,512]{1,0:T(8,128)(2,1)S(1)} %copy-done, bf16[512,256]{1,0:T(8,128)(2,1)S(1)} %copy-done.1, bf16[256,256]{1,0:T(8,128)(2,1)S(1)} %get-tuple-element.67.refs_2_, ...), custom_call_target="tpu_custom_call" | custom-call | flops 180000000 | tf_op jit(solution)/shard_map/pallas_call | solution.py:78
  27.0 0.3 collective-permute-done.10.refs_8_
  27.3 0.7 %collective-permute-start.8 = (bf16[256,256]{1,0:T(8,128)(2,1)S(1)}, bf16[256,256]{1,0:T(8,128)(2,1)S(1)}, u32[]{:S(2)}, u32[]{:S(2)}) collective-permute-start(bf16[256,256]{1,0:T(8,128)(2,1)S(1)} %get-tuple-element.70), channel_id=1, source_target_pairs={{0,8},{4,12},{8,0},{12,4},{1,9},{5,13},{9,1},{13,5},{2,10},{6,14},... | collective-permute-start | bytes 393224 | tf_op jit(solution)/shard_map/ppermute | solution.py:776
  28.0 2.8 %collective-permute-done.11.refs_9_ = bf16[256,256]{1,0:T(8,128)(2,1)S(1)} collective-permute-done((bf16[256,256]{1,0:T(8,128)(2,1)S(1)}, bf16[256,256]{1,0:T(8,128)(2,1)S(1)}, u32[]{:S(2)}, u32[]{:S(2)}) %collective-permute-start.11) | collective-permute-done | bytes 131104 | tf_op jit(solution)/shard_map/ppermute | solution.py:776
  30.8 2.1 %collective-permute-start.9 = (bf16[256,256]{1,0:T(8,128)(2,1)S(1)}, bf16[256,256]{1,0:T(8,128)(2,1)S(1)}, u32[]{:S(2)}, u32[]{:S(2)}) collective-permute-start(bf16[256,256]{1,0:T(8,128)(2,1)S(1)} %get-tuple-element.71), channel_id=1, source_target_pairs={{0,12},{4,8},{8,4},{12,0},{1,13},{5,9},{9,5},{13,1},{2,14},{6,10},... | collective-permute-start | bytes 393224 | tf_op jit(solution)/shard_map/ppermute | solution.py:776
  32.9 2.3 %shard_map.101 = (bf16[2,256,256]{2,1,0:T(8,128)(2,1)S(1)}, bf16[2,256,256]{2,1,0:T(8,128)(2,1)S(1)}) custom-call(f32[1024,16]{1,0:T(8,128)S(1)} %get-tuple-element.59.refs_0_, bf16[512,512]{1,0:T(8,128)(2,1)S(1)} %copy-done, bf16[512,256]{1,0:T(8,128)(2,1)S(1)} %copy-done.1, f32[1024,512]{1,0:T(8,128)S(1)} %get-tuple-element.74.refs_3_, ...), custom_call_target="tpu_custom_call" | custom-call | flops 6000000000 | tf_op jit(solution)/shard_map/pallas_call | solution.py:78
  35.2 1.6 %collective-permute-start.13 = (bf16[2,256,256]{2,1,0:T(8,128)(2,1)S(1)}, bf16[2,256,256]{2,1,0:T(8,128)(2,1)S(1)}, u32[]{:S(2)}, u32[]{:S(2)}) collective-permute-start(bf16[2,256,256]{2,1,0:T(8,128)(2,1)S(1)} %get-tuple-element.80), channel_id=1, source_target_pairs={{0,4},{4,0},{8,12},{12,8},{1,5},{5,1},{9,13},{13,9},{2,6},{6,2},{1... | collective-permute-start | bytes 786440 | tf_op jit(solution)/shard_map/ppermute | solution.py:776
  36.8 1.7 %collective-permute-done.5.refs_6_ = bf16[2,256,256]{2,1,0:T(8,128)(2,1)S(1)} collective-permute-done((bf16[2,256,256]{2,1,0:T(8,128)(2,1)S(1)}, bf16[2,256,256]{2,1,0:T(8,128)(2,1)S(1)}, u32[]{:S(2)}, u32[]{:S(2)}) %collective-permute-start.5) | collective-permute-done | bytes 262176 | tf_op jit(solution)/shard_map/ppermute | solution.py:776
  38.5 2.4 %shard_map.98 = (bf16[2,16,256]{2,1,0:T(8,128)(2,1)S(1)}, bf16[2,16,256]{2,1,0:T(8,128)(2,1)S(1)}, bf16[2,256,256]{2,1,0:T(8,128)(2,1)S(1)}, bf16[2,256,256]{2,1,0:T(8,128)(2,1)S(1)}) custom-call(f32[1024,16]{1,0:T(8,128)S(1)} %get-tuple-element.59.refs_0_, bf16[512,512]{1,0:T(8,128)(2,1)S(1)} %copy-done, bf16[512,256]{1,0:T(8,128)(2,1)S(1)} %copy-done.1, ...), custom_call_target="tpu_custom_call" | custom-call | flops 4800000000 | tf_op jit(solution)/shard_map/pallas_call | solution.py:78
  40.9 2.0 %collective-permute-start.6 = (bf16[2,256,256]{2,1,0:T(8,128)(2,1)S(1)}, bf16[2,256,256]{2,1,0:T(8,128)(2,1)S(1)}, u32[]{:S(2)}, u32[]{:S(2)}) collective-permute-start(bf16[2,256,256]{2,1,0:T(8,128)(2,1)S(1)} %get-tuple-element.66), channel_id=1, source_target_pairs={{0,4},{4,0},{8,12},{12,8},{1,5},{5,1},{9,13},{13,9},{2,6},{6,2},{1... | collective-permute-start | bytes 786440 | tf_op jit(solution)/shard_map/ppermute | solution.py:776
  43.0 1.8 %shard_map.102 = (bf16[1024,256]{1,0:T(8,128)(2,1)}, bf16[3,1024,256]{2,1,0:T(8,128)(2,1)}, f32[2,3,256,128]{3,2,1,0:T(8,128)S(1)}) custom-call(bf16[2,3,256,256]{3,2,1,0:T(8,128)(2,1)S(1)} %get-tuple-element.50.refs_0_, bf16[2,256,256]{2,1,0:T(8,128)(2,1)S(1)} %get-tuple-element.51.refs_1_, bf16[2,3,256,256]{3,2,1,0:T(8,128)(2,1)S(1)} %get-tuple-element.57.refs_2_, ...), custom_call_target="tpu_custom_call" | custom-call | flops 1440000000 | tf_op jit(solution)/shard_map/pallas_call | solution.py:78
  44.9 1.9 %collective-permute-done.13.refs_7_.refs_5_ = bf16[2,256,256]{2,1,0:T(8,128)(2,1)S(1)} collective-permute-done((bf16[2,256,256]{2,1,0:T(8,128)(2,1)S(1)}, bf16[2,256,256]{2,1,0:T(8,128)(2,1)S(1)}, u32[]{:S(2)}, u32[]{:S(2)}) %collective-permute-start.13) | collective-permute-done | bytes 262176 | tf_op jit(solution)/shard_map/ppermute | solution.py:776
  46.7 1.2 %shard_map.103 = (bf16[1024,256]{1,0:T(8,128)(2,1)}, bf16[3,1024,256]{2,1,0:T(8,128)(2,1)}, f32[1,3,256,128]{3,2,1,0:T(8,128)S(1)}) custom-call(bf16[2,3,256,256]{3,2,1,0:T(8,128)(2,1)S(1)} %get-tuple-element.50.refs_0_, bf16[2,256,256]{2,1,0:T(8,128)(2,1)S(1)} %get-tuple-element.51.refs_1_, ...), custom_call_target="tpu_custom_call", output_to_operand_aliasing={{0}: (9, {}), {1}: (10, {})} | custom-call | flops 720000000 | tf_op jit(solution)/shard_map/pallas_call | solution.py:78
  48.0 0.8 %shard_map.105 = f32[8,1024]{1,0:T(8,128)S(1)} custom-call(bf16[2,3,256,256]{3,2,1,0:T(8,128)(2,1)S(1)} %get-tuple-element.50.refs_0_, bf16[2,256,256]{2,1,0:T(8,128)(2,1)S(1)} %get-tuple-element.51.refs_1_, bf16[2,3,256,256]{3,2,1,0:T(8,128)(2,1)S(1)} %get-tuple-element.57.refs_2_, bf16[2,256,256]{2,1,0:T(8,128)(2,1)S(1)} %get-tuple-element.58.refs_3_, ...), custom_call_target="tpu_custom_call" | custom-call | flops 3600000000 | tf_op jit(solution)/shard_map/pallas_call | solution.py:78
  48.8 2.1 %collective-permute-start.15 = (f32[8,1024]{1,0:T(8,128)S(1)}, f32[8,1024]{1,0:T(8,128)S(1)}, u32[]{:S(2)}, u32[]{:S(2)}) collective-permute-start(f32[8,1024]{1,0:T(8,128)S(1)} %shard_map.105), channel_id=1, source_target_pairs={{0,12},{4,0},{8,4},{12,8},{1,13},{5,1},{9,5},{13,9},{2,14},{6,2},{... | collective-permute-start | bytes 98312 | tf_op jit(solution)/shard_map/ppermute | solution.py:780
  50.9 0.8 %collective-permute-done.6.refs_7_ = bf16[2,256,256]{2,1,0:T(8,128)(2,1)S(1)} collective-permute-done((bf16[2,256,256]{2,1,0:T(8,128)(2,1)S(1)}, bf16[2,256,256]{2,1,0:T(8,128)(2,1)S(1)}, u32[]{:S(2)}, u32[]{:S(2)}) %collective-permute-start.6) | collective-permute-done | bytes 262176 | tf_op jit(solution)/shard_map/ppermute | solution.py:776
  51.7 1.2 %shard_map.104 = (bf16[1024,256]{1,0:T(8,128)(2,1)}, bf16[3,1024,256]{2,1,0:T(8,128)(2,1)}, f32[1,3,256,128]{3,2,1,0:T(8,128)S(1)}) custom-call(bf16[2,3,256,256]{3,2,1,0:T(8,128)(2,1)S(1)} %get-tuple-element.50.refs_0_, bf16[2,256,256]{2,1,0:T(8,128)(2,1)S(1)} %get-tuple-element.51.refs_1_, ...), custom_call_target="tpu_custom_call", output_to_operand_aliasing={{0}: (10, {}), {1}: (11, {})} | custom-call | flops 720000000 | tf_op jit(solution)/shard_map/pallas_call | solution.py:78
  52.9 1.4 %shard_map.106 = bf16[3,1024,256]{2,1,0:T(8,128)(2,1)} custom-call(f32[8,1024]{1,0:T(8,128)S(1)} %collective-permute-done.15.refs_0_, f32[16,1024]{1,0:T(8,128)S(1)} %get-tuple-element.92.refs_1_, bf16[48,384]{1,0:T(8,128)(2,1)S(1)} %get-tuple-element.93.refs_2_, ...), custom_call_target="tpu_custom_call", output_to_operand_aliasing={{}: (6, {})} | custom-call | flops 1140000000 | tf_op jit(solution)/shard_map/pallas_call | solution.py:78
  (23 shorter events, 0.1 us)
Async XLA Ops:
  0.6 9.0 %copy-start.4 = (s32[16]{0:T(128)S(1)}, s32[16]{0:T(128)}, u32[]{:S(2)}) copy-start(s32[16]{0:T(128)} %param.13) | copy-start | bytes 196
  0.6 9.0 %copy-start.3 = (f32[1024]{0:T(1024)S(1)}, f32[1024]{0:T(1024)}, u32[]{:S(2)}) copy-start(f32[1024]{0:T(1024)} %param.12) | copy-start | bytes 12292
  0.7 9.0 %copy-start.2 = (f32[3,3,1024]{2,1,0:T(4,128)S(1)}, f32[3,3,1024]{2,1,0:T(4,128)}, u32[]{:S(2)}) copy-start(f32[3,3,1024]{2,1,0:T(4,128)} %refs_4_.1) | copy-start | bytes 110596
  2.2 7.5 %collective-permute-start = (bf16[16,1024]{1,0:T(8,128)(2,1)S(1)}, bf16[16,1024]{1,0:T(8,128)(2,1)S(1)}, u32[]{:S(2)}, u32[]{:S(2)}) collective-permute-start(bf16[16,1024]{1,0:T(8,128)(2,1)S(1)} %get-tuple-element.49), channel_id=1, source_target_pairs={{0,4},{4,8},{8,12},{12,0},{1,5},{5,9},{9,13},{13,1},{2,6},{6,10},{... | collective-permute-start | bytes 98312 | tf_op jit(solution)/shard_map/ppermute | solution.py:780
  5.2 11.5 %collective-permute-start.1 = (bf16[256,256]{1,0:T(8,128)(2,1)S(1)}, bf16[256,256]{1,0:T(8,128)(2,1)S(1)}, u32[]{:S(2)}, u32[]{:S(2)}) collective-permute-start(bf16[256,256]{1,0:T(8,128)(2,1)S(1)} %get-tuple-element.61), channel_id=1, source_target_pairs={{0,4},{4,0},{8,12},{12,8},{1,5},{5,1},{9,13},{13,9},{2,6},{6,2},{1... | collective-permute-start | bytes 393224 | tf_op jit(solution)/shard_map/ppermute | solution.py:776
  6.8 12.7 %collective-permute-start.2 = (bf16[256,256]{1,0:T(8,128)(2,1)S(1)}, bf16[256,256]{1,0:T(8,128)(2,1)S(1)}, u32[]{:S(2)}, u32[]{:S(2)}) collective-permute-start(bf16[256,256]{1,0:T(8,128)(2,1)S(1)} %get-tuple-element.62), channel_id=1, source_target_pairs={{0,8},{4,12},{8,0},{12,4},{1,9},{5,13},{9,1},{13,5},{2,10},{6,14},... | collective-permute-start | bytes 393224 | tf_op jit(solution)/shard_map/ppermute | solution.py:776
  7.9 13.7 %collective-permute-start.3 = (bf16[256,256]{1,0:T(8,128)(2,1)S(1)}, bf16[256,256]{1,0:T(8,128)(2,1)S(1)}, u32[]{:S(2)}, u32[]{:S(2)}) collective-permute-start(bf16[256,256]{1,0:T(8,128)(2,1)S(1)} %get-tuple-element.63), channel_id=1, source_target_pairs={{0,12},{4,8},{8,4},{12,0},{1,13},{5,9},{9,5},{13,1},{2,14},{6,10},... | collective-permute-start | bytes 393224 | tf_op jit(solution)/shard_map/ppermute | solution.py:776
  12.3 11.0 %collective-permute-start.7 = (bf16[256,256]{1,0:T(8,128)(2,1)S(1)}, bf16[256,256]{1,0:T(8,128)(2,1)S(1)}, u32[]{:S(2)}, u32[]{:S(2)}) collective-permute-start(bf16[256,256]{1,0:T(8,128)(2,1)S(1)} %get-tuple-element.69), channel_id=1, source_target_pairs={{0,4},{4,0},{8,12},{12,8},{1,5},{5,1},{9,13},{13,9},{2,6},{6,2},{1... | collective-permute-start | bytes 393224 | tf_op jit(solution)/shard_map/ppermute | solution.py:776
  13.0 14.2 %collective-permute-start.10 = (bf16[256,256]{1,0:T(8,128)(2,1)S(1)}, bf16[256,256]{1,0:T(8,128)(2,1)S(1)}, u32[]{:S(2)}, u32[]{:S(2)}) collective-permute-start(bf16[256,256]{1,0:T(8,128)(2,1)S(1)} %get-tuple-element.77), channel_id=1, source_target_pairs={{0,4},{4,0},{8,12},{12,8},{1,5},{5,1},{9,13},{13,9},{2,6},{6,2},{1... | collective-permute-start | bytes 393224 | tf_op jit(solution)/shard_map/ppermute | solution.py:776
  14.4 10.5 %copy-start = (bf16[512,512]{1,0:T(8,128)(2,1)S(1)}, bf16[512,512]{1,0:T(8,128)(2,1)}, u32[]{:S(2)}) copy-start(bf16[512,512]{1,0:T(8,128)(2,1)} %constant.4.clone.refs_1_.refs_0_) | copy-start | bytes 1572868
  14.4 10.5 %copy-start.1 = (bf16[512,256]{1,0:T(8,128)(2,1)S(1)}, bf16[512,256]{1,0:T(8,128)(2,1)}, u32[]{:S(2)}) copy-start(bf16[512,256]{1,0:T(8,128)(2,1)} %constant.5.clone.refs_2_.refs_1_) | copy-start | bytes 786436
  16.8 14.0 %collective-permute-start.11 = (bf16[256,256]{1,0:T(8,128)(2,1)S(1)}, bf16[256,256]{1,0:T(8,128)(2,1)S(1)}, u32[]{:S(2)}, u32[]{:S(2)}) collective-permute-start(bf16[256,256]{1,0:T(8,128)(2,1)S(1)} %get-tuple-element.78), channel_id=1, source_target_pairs={{0,8},{4,12},{8,0},{12,4},{1,9},{5,13},{9,1},{13,5},{2,10},{6,14},... | collective-permute-start | bytes 393224 | tf_op jit(solution)/shard_map/ppermute | solution.py:776
  19.5 13.3 %collective-permute-start.12 = (bf16[256,256]{1,0:T(8,128)(2,1)S(1)}, bf16[256,256]{1,0:T(8,128)(2,1)S(1)}, u32[]{:S(2)}, u32[]{:S(2)}) collective-permute-start(bf16[256,256]{1,0:T(8,128)(2,1)S(1)} %get-tuple-element.79), channel_id=1, source_target_pairs={{0,12},{4,8},{8,4},{12,0},{1,13},{5,9},{9,5},{13,1},{2,14},{6,10},... | collective-permute-start | bytes 393224 | tf_op jit(solution)/shard_map/ppermute | solution.py:776
  21.6 16.9 %collective-permute-start.5 = (bf16[2,256,256]{2,1,0:T(8,128)(2,1)S(1)}, bf16[2,256,256]{2,1,0:T(8,128)(2,1)S(1)}, u32[]{:S(2)}, u32[]{:S(2)}) collective-permute-start(bf16[2,256,256]{2,1,0:T(8,128)(2,1)S(1)} %get-tuple-element.65), channel_id=1, source_target_pairs={{0,4},{4,0},{8,12},{12,8},{1,5},{5,1},{9,13},{13,9},{2,6},{6,2},{1... | collective-permute-start | bytes 786440 | tf_op jit(solution)/shard_map/ppermute | solution.py:776
  23.3 15.3 %collective-permute-start.4 = (bf16[768,256]{1,0:T(8,128)(2,1)S(1)}, bf16[768,256]{1,0:T(8,128)(2,1)S(1)}, u32[]{:S(2)}, u32[]{:S(2)}) collective-permute-start(bf16[768,256]{1,0:T(8,128)(2,1)S(1)} %pad_maximum_fusion), channel_id=1, source_target_pairs={{0,16},{16,0},{1,17},{17,1},{2,18},{18,2},{3,19},{19,3},{4,20},{20... | collective-permute-start | bytes 1179656 | tf_op jit(solution)/shard_map/ppermute | solution.py:776
  27.3 15.7 %collective-permute-start.8 = (bf16[256,256]{1,0:T(8,128)(2,1)S(1)}, bf16[256,256]{1,0:T(8,128)(2,1)S(1)}, u32[]{:S(2)}, u32[]{:S(2)}) collective-permute-start(bf16[256,256]{1,0:T(8,128)(2,1)S(1)} %get-tuple-element.70), channel_id=1, source_target_pairs={{0,8},{4,12},{8,0},{12,4},{1,9},{5,13},{9,1},{13,5},{2,10},{6,14},... | collective-permute-start | bytes 393224 | tf_op jit(solution)/shard_map/ppermute | solution.py:776
  30.8 12.2 %collective-permute-start.9 = (bf16[256,256]{1,0:T(8,128)(2,1)S(1)}, bf16[256,256]{1,0:T(8,128)(2,1)S(1)}, u32[]{:S(2)}, u32[]{:S(2)}) collective-permute-start(bf16[256,256]{1,0:T(8,128)(2,1)S(1)} %get-tuple-element.71), channel_id=1, source_target_pairs={{0,12},{4,8},{8,4},{12,0},{1,13},{5,9},{9,5},{13,1},{2,14},{6,10},... | collective-permute-start | bytes 393224 | tf_op jit(solution)/shard_map/ppermute | solution.py:776
  35.2 11.6 %collective-permute-start.13 = (bf16[2,256,256]{2,1,0:T(8,128)(2,1)S(1)}, bf16[2,256,256]{2,1,0:T(8,128)(2,1)S(1)}, u32[]{:S(2)}, u32[]{:S(2)}) collective-permute-start(bf16[2,256,256]{2,1,0:T(8,128)(2,1)S(1)} %get-tuple-element.80), channel_id=1, source_target_pairs={{0,4},{4,0},{8,12},{12,8},{1,5},{5,1},{9,13},{13,9},{2,6},{6,2},{1... | collective-permute-start | bytes 786440 | tf_op jit(solution)/shard_map/ppermute | solution.py:776
  40.9 7.1 %collective-permute-start.14 = (bf16[2,16,256]{2,1,0:T(8,128)(2,1)S(1)}, bf16[2,16,256]{2,1,0:T(8,128)(2,1)S(1)}, u32[]{:S(2)}, u32[]{:S(2)}) collective-permute-start(bf16[2,16,256]{2,1,0:T(8,128)(2,1)S(1)} %get-tuple-element.91), channel_id=1, source_target_pairs={{0,4},{4,0},{8,12},{12,8},{1,5},{5,1},{9,13},{13,9},{2,6},{6,2},{1... | collective-permute-start | bytes 49160 | tf_op jit(solution)/shard_map/ppermute | solution.py:776
  40.9 10.7 %collective-permute-start.6 = (bf16[2,256,256]{2,1,0:T(8,128)(2,1)S(1)}, bf16[2,256,256]{2,1,0:T(8,128)(2,1)S(1)}, u32[]{:S(2)}, u32[]{:S(2)}) collective-permute-start(bf16[2,256,256]{2,1,0:T(8,128)(2,1)S(1)} %get-tuple-element.66), channel_id=1, source_target_pairs={{0,4},{4,0},{8,12},{12,8},{1,5},{5,1},{9,13},{13,9},{2,6},{6,2},{1... | collective-permute-start | bytes 786440 | tf_op jit(solution)/shard_map/ppermute | solution.py:776
  48.8 4.2 %collective-permute-start.15 = (f32[8,1024]{1,0:T(8,128)S(1)}, f32[8,1024]{1,0:T(8,128)S(1)}, u32[]{:S(2)}, u32[]{:S(2)}) collective-permute-start(f32[8,1024]{1,0:T(8,128)S(1)} %shard_map.105), channel_id=1, source_target_pairs={{0,12},{4,0},{8,4},{12,8},{1,13},{5,1},{9,5},{13,9},{2,14},{6,2},{... | collective-permute-start | bytes 98312 | tf_op jit(solution)/shard_map/ppermute | solution.py:780

commit v10 on v9

--- a/solution.py
+++ b/solution.py
@@ -11,7 +11,7 @@
 
 BF16 = jnp.bfloat16
 F32 = jnp.float32
-GATE_MAIN, GATE_OTHER = 6.0, 1.0
+GATE_MAIN, GATE_OTHER = 6.0, 6.0
 SHARE = 0.6
 VMEM_LIMIT = 24 * 1024 * 1024
 IN_HBM = pl.BlockSpec(memory_space=pltpu.HBM)
@@ -196,8 +196,9 @@
 def gate_body(other, layout, place_ref, feat_hbm, dout_hbm, *rest):
     half, rows, span = layout.half, layout.sub, layout.span
     given, rest = (rest[:5], rest[5:]) if other else (rest[:4], rest[4:])
-    qkv_ref, dout_ref, firsts, seconds = rest[0], rest[1], rest[2 : 2 + half], rest[2 + half : 2 + 2 * half]
-    rest = rest[2 + 2 * half :]
+    qkv_ref, dout_ref, pairs, rest = rest[0], rest[1], rest[2 : 2 + half], rest[2 + half :]
+    if other:
+        cross, rest = rest[:half], rest[half:]
     feat_ref, spread, ends, sems = rest[-4:]
     side, _, _ = where_am_i(place_ref, layout)
     group = min(64, rows)
@@ -245,12 +246,10 @@
             grad_in = dout_ref[turn, local_rows, :] * filtered[0]
             first = jnp.where(side == 0, mixed, grad_in)
             second = jnp.where(side == 0, grad_in, mixed)
-            firsts[turn][local_rows, :] = first
+            pairs[turn][0, local_rows, :] = first
+            pairs[turn][1, local_rows, :] = second
             if other:
-                seconds[turn][0, local_rows, :] = first
-                seconds[turn][1, local_rows, :] = second
-            else:
-                seconds[turn][local_rows, :] = second
+                cross[turn][local_rows, :] = first
             return 0
 
         lax.fori_loop(0, rows // group, tile, 0, unroll=rows // group)
@@ -258,8 +257,8 @@
 
 def gate(other, layout, features, dout, *given):
     half, rows, span, channels = layout.half, layout.sub, layout.span, layout.channels
-    shapes = [(half, 3, rows, span), (half, rows, span)] + [(rows, span)] * half
-    shapes += [(2, rows, span) if other else (rows, span)] * half
+    shapes = [(half, 3, rows, span), (half, rows, span)] + [(2, rows, span)] * half
+    shapes += [(rows, span)] * half if other else []
     outs = [jax.ShapeDtypeStruct(s, BF16) for s in shapes]
     if not other:
         more = table_shapes(layout) + [((16, 768), BF16), ((channels, 16), BF16)]
@@ -278,7 +277,7 @@
         estimate(GATE_OTHER if other else GATE_MAIN),
         in_specs=[IN_HBM] * 2 + [HELD] * len(given),
     )
-    return found[0:2], found[2 : 2 + half], found[2 + half : 2 + 2 * half], found[2 + 2 * half :]
+    return found[0:2], found[2 : 2 + half], found[2 + half :]
 
 
 def loop(count, body, init):
@@ -341,7 +340,7 @@
     lax.fori_loop(0, parts * sub // chunk, transform, 0, unroll=True)
     side, own, _ = where_am_i(place_ref, layout)
     for step in range(half):
-        raw[rows_at(jnp.bitwise_xor(own, step) * sub, sub, sub), :] = signal[step][...]
+        raw[rows_at(jnp.bitwise_xor(own, step) * sub, sub, sub), :] = signal[step][0]
     forward(raw, spec, 0, 0, half * sub, forward_ref)
     group = 16
     zero = (jnp.zeros((group, span), F32),) * 2
@@ -417,13 +416,13 @@
 
 def main_body(layout, place_ref, cols_ref, forward_ref, inverse_ref, known, near_spec, *rest):
     parts, half, sub, span = layout.parts, layout.half, layout.sub, layout.span
-    firsts, trails, cross, outs = (rest[k * half : (k + 1) * half] for k in range(4))
-    raw, spec, ready, back = rest[4 * half :]
+    firsts, cross, outs = (rest[k * half : (k + 1) * half] for k in range(3))
+    raw, spec, ready, back = rest[3 * half :]
     side, own, _ = where_am_i(place_ref, layout)
     block = parts * sub
     for step in range(half):
         place = jnp.bitwise_xor(own, step)
-        raw[rows_at((side * half + place) * sub, sub, sub), :] = trails[step][...]
+        raw[rows_at((side * half + place) * sub, sub, sub), :] = firsts[step][1]
         raw[rows_at(((1 - side) * half + place) * sub, sub, sub), :] = cross[step][...]
     chunk = math.gcd(block, 512)
 
@@ -488,17 +487,17 @@
         place = jnp.bitwise_xor(own, step)
         for kind in range(2):
             value = back[rows_at((kind * half + place) * sub, sub, sub), :]
-            direct = (trails if kind else firsts)[step][...].astype(F32)
+            direct = firsts[step][kind].astype(F32)
             outs[step][kind] = (value + skip * direct).astype(BF16)
 
 
-def main_half(layout, cols, tables, known, near, firsts, trails, cross):
+def main_half(layout, cols, tables, known, near, firsts, cross):
     half, sub, span, parts = layout.half, layout.sub, layout.span, layout.parts
     rows = parts * sub
     return run(
         main_body,
         layout,
-        (cols, *tables, known, near, *firsts, *trails, *cross),
+        (cols, *tables, known, near, *firsts, *cross),
         [jax.ShapeDtypeStruct((2, sub, span), BF16)] * half,
         [
             pltpu.VMEM((rows, span), BF16),
@@ -794,17 +793,16 @@
     filt = [swap(filt[step - 1], step, parts) for step in range(1, parts)]
     other = swap(jnp.concatenate(filt, axis=0), 1, 2, "groups")
     first_given = (halo, lengths.reshape(1, -1), taps, skip.reshape(1, channels))
-    gated_main, firsts, trails, shared = gate(0, layout, features, dout, *first_given)
+    gated_main, firsts, shared = gate(0, layout, features, dout, *first_given)
     cols, split, keep, last_edge, taps_rows, lanes, first_edge, ends_of = shared
-    gated_other, cross, seconds, _ = gate(1, layout, features, dout, split, keep, lanes, first_edge, ends_of)
+    gated_other, seconds, cross = gate(1, layout, features, dout, split, keep, lanes, first_edge, ends_of)
     firsts = [firsts[0]] + [swap(firsts[step], step, parts) for step in range(1, half)]
-    trails = [trails[0]] + [swap(trails[step], step, parts) for step in range(1, half)]
     cross = [swap(cross[step], step + half, parts) for step in range(half)]
     seconds = [seconds[0]] + [swap(seconds[step], step, parts) for step in range(1, half)]
 
     sent, known, near = cross_half(layout, tables, own_filt[0], filt, firsts)
     crossed = [swap(sent[step], step + half, parts) for step in range(half)]
-    main = main_half(layout, cols, tables, known, near, firsts, trails, cross)
+    main = main_half(layout, cols, tables, known, near, firsts, cross)
     main = [main[0]] + [swap(main[step], step, parts) for step in range(1, half)]
     leads, rest = other_half(layout, cols, tables, own_filt[1], other, seconds)
     crossed = hold(layout, crossed, leads[0])

time: 54.5 us -> 54.5 us (level)
  waiting for transfers between devices: 8.53 us -> 12.3 us
  starting transfers between devices: 25.2 us -> 21.5 us
    ppermute x14 -> x13, waiting for transfers between devices: 8.53 us -> 12.3 us  [swap(): lax.ppermute(value, axis, [(source, source ^ step) for source in range(pa...]
    ppermute x14 -> x13, starting transfers between devices: 20 us -> 16.3 us  [swap(): lax.ppermute(value, axis, [(source, source ^ step) for source in range(pa...]
  transfers between devices with their start and end apart: 16 -> 15, of which waited for: 6 -> 6; matrix products, arithmetic and copies ran while one was open for 0% -> 0% of each run, Pallas kernels for 31% -> 31%
where the time goes in v10:
time: 54.5 us; the launch traced here: 54.3 us
  starting transfers between devices  21.5 us (39%)
  Pallas kernels  19.7 us (36%)
  waiting for transfers between devices  12.3 us (23%)
  between operations  0.78 us (1%)
    pallas_call x12, Pallas kernels, run(): pl.pallas_call(kernel, out_shape=outs, in_specs=in_specs or [HELD] * len(...  19.7 us
    ppermute x13, starting transfers between devices, swap(): lax.ppermute(value, axis, [(source, source ^ step) for source in range(pa...  16.3 us
    ppermute x13, waiting for transfers between devices, swap(): lax.ppermute(value, axis, [(source, source ^ step) for source in range(pa...  12.3 us
    ppermute x2, starting transfers between devices, around(): lax.ppermute(value, 'seq', [(source, (source + steps) % parts) for source...  5.17 us
  transfers between devices with their start and end apart: 15, of which 6 were waited for; matrix products, arithmetic and copies ran while one was open for 0% of the time, Pallas kernels for 31%

profile of v10, /device:TPU:0, one launch (start us, length us, event | category | flops | bytes accessed | tf_op | source)
XLA Modules:
  0.0 54.3 jit_solution(7822316634613960378)
XLA Ops:
  0.7 1.5 %shard_map.95 = (bf16[16,1024]{1,0:T(8,128)(2,1)S(1)}, bf16[256,256]{1,0:T(8,128)(2,1)S(1)}, bf16[256,256]{1,0:T(8,128)(2,1)S(1)}, bf16[256,256]{1,0:T(8,128)(2,...) custom-call(bf16[3,1024,256]{2,1,0:T(8,128)(2,1)} %refs_0_.6, bf16[1024,256]{1,0:T(8,128)(2,1)} %refs_1_.6), custom_call_target="tpu_custom_call" | custom-call | flops 1200000000 | tf_op jit(solution)/shard_map/pallas_call | solution.py:78
  2.2 3.1 %collective-permute-start = (bf16[16,1024]{1,0:T(8,128)(2,1)S(1)}, bf16[16,1024]{1,0:T(8,128)(2,1)S(1)}, u32[]{:S(2)}, u32[]{:S(2)}) collective-permute-start(bf16[16,1024]{1,0:T(8,128)(2,1)S(1)} %get-tuple-element.47), channel_id=1, source_target_pairs={{0,4},{4,8},{8,12},{12,0},{1,5},{5,9},{9,13},{13,1},{2,6},{6,10},{... | collective-permute-start | bytes 98312 | tf_op jit(solution)/shard_map/ppermute | solution.py:779
  5.2 1.6 %collective-permute-start.1 = (bf16[256,256]{1,0:T(8,128)(2,1)S(1)}, bf16[256,256]{1,0:T(8,128)(2,1)S(1)}, u32[]{:S(2)}, u32[]{:S(2)}) collective-permute-start(bf16[256,256]{1,0:T(8,128)(2,1)S(1)} %get-tuple-element.59), channel_id=1, source_target_pairs={{0,4},{4,0},{8,12},{12,8},{1,5},{5,1},{9,13},{13,9},{2,6},{6,2},{1... | collective-permute-start | bytes 393224 | tf_op jit(solution)/shard_map/ppermute | solution.py:775
  6.8 1.1 %collective-permute-start.2 = (bf16[256,256]{1,0:T(8,128)(2,1)S(1)}, bf16[256,256]{1,0:T(8,128)(2,1)S(1)}, u32[]{:S(2)}, u32[]{:S(2)}) collective-permute-start(bf16[256,256]{1,0:T(8,128)(2,1)S(1)} %get-tuple-element.60), channel_id=1, source_target_pairs={{0,8},{4,12},{8,0},{12,4},{1,9},{5,13},{9,1},{13,5},{2,10},{6,14},... | collective-permute-start | bytes 393224 | tf_op jit(solution)/shard_map/ppermute | solution.py:775
  7.9 1.7 %collective-permute-start.3 = (bf16[256,256]{1,0:T(8,128)(2,1)S(1)}, bf16[256,256]{1,0:T(8,128)(2,1)S(1)}, u32[]{:S(2)}, u32[]{:S(2)}) collective-permute-start(bf16[256,256]{1,0:T(8,128)(2,1)S(1)} %get-tuple-element.61), channel_id=1, source_target_pairs={{0,12},{4,8},{8,4},{12,0},{1,13},{5,9},{9,5},{13,1},{2,14},{6,10},... | collective-permute-start | bytes 393224 | tf_op jit(solution)/shard_map/ppermute | solution.py:775
  9.6 0.0 collective-permute-done.refs_2_
  9.7 2.6 %shard_map.96 = (bf16[2,3,256,256]{3,2,1,0:T(8,128)(2,1)S(1)}, bf16[2,256,256]{2,1,0:T(8,128)(2,1)S(1)}, bf16[2,256,256]{2,1,0:T(8,128)(2,1)S(1)}, bf16[2,256,25...) custom-call(bf16[3,1024,256]{2,1,0:T(8,128)(2,1)} %refs_0_.6, ...), custom_call_target="tpu_custom_call" | custom-call | flops 3600000000 | tf_op jit(solution)/shard_map/pallas_call | solution.py:78
  12.3 0.8 %collective-permute-start.7 = (bf16[2,256,256]{2,1,0:T(8,128)(2,1)S(1)}, bf16[2,256,256]{2,1,0:T(8,128)(2,1)S(1)}, u32[]{:S(2)}, u32[]{:S(2)}) collective-permute-start(bf16[2,256,256]{2,1,0:T(8,128)(2,1)S(1)} %get-tuple-element.67), channel_id=1, source_target_pairs={{0,4},{4,0},{8,12},{12,8},{1,5},{5,1},{9,13},{13,9},{2,6},{6,2},{1... | collective-permute-start | bytes 786440 | tf_op jit(solution)/shard_map/ppermute | solution.py:775
  13.0 2.4 %shard_map.97 = (bf16[2,3,256,256]{3,2,1,0:T(8,128)(2,1)S(1)}, bf16[2,256,256]{2,1,0:T(8,128)(2,1)S(1)}, bf16[2,256,256]{2,1,0:T(8,128)(2,1)S(1)}, bf16[2,256,25...) custom-call(bf16[3,1024,256]{2,1,0:T(8,128)(2,1)} %refs_0_.6, ...), custom_call_target="tpu_custom_call" | custom-call | flops 3600000000 | tf_op jit(solution)/shard_map/pallas_call | solution.py:78
  15.4 2.0 %collective-permute-start.10 = (bf16[256,256]{1,0:T(8,128)(2,1)S(1)}, bf16[256,256]{1,0:T(8,128)(2,1)S(1)}, u32[]{:S(2)}, u32[]{:S(2)}) collective-permute-start(bf16[256,256]{1,0:T(8,128)(2,1)S(1)} %get-tuple-element.74), channel_id=1, source_target_pairs={{0,8},{4,12},{8,0},{12,4},{1,9},{5,13},{9,1},{13,5},{2,10},{6,14},... | collective-permute-start | bytes 393224 | tf_op jit(solution)/shard_map/ppermute | solution.py:775
  17.4 1.7 %collective-permute-start.11 = (bf16[256,256]{1,0:T(8,128)(2,1)S(1)}, bf16[256,256]{1,0:T(8,128)(2,1)S(1)}, u32[]{:S(2)}, u32[]{:S(2)}) collective-permute-start(bf16[256,256]{1,0:T(8,128)(2,1)S(1)} %get-tuple-element.75), channel_id=1, source_target_pairs={{0,12},{4,8},{8,4},{12,0},{1,13},{5,9},{9,5},{13,1},{2,14},{6,10},... | collective-permute-start | bytes 393224 | tf_op jit(solution)/shard_map/ppermute | solution.py:775
  19.2 0.4 collective-permute-done.2.refs_4_
  19.6 1.6 %collective-permute-start.4 = (bf16[768,256]{1,0:T(8,128)(2,1)S(1)}, bf16[768,256]{1,0:T(8,128)(2,1)S(1)}, u32[]{:S(2)}, u32[]{:S(2)}) collective-permute-start(bf16[768,256]{1,0:T(8,128)(2,1)S(1)} %pad_maximum_fusion), channel_id=1, source_target_pairs={{0,16},{16,0},{1,17},{17,1},{2,18},{18,2},{3,19},{19,3},{4,20},{20... | collective-permute-start | bytes 1179656 | tf_op jit(solution)/shard_map/ppermute | solution.py:775
  21.2 6.1 %collective-permute-done.7.refs_7_.refs_6_ = bf16[2,256,256]{2,1,0:T(8,128)(2,1)S(1)} collective-permute-done((bf16[2,256,256]{2,1,0:T(8,128)(2,1)S(1)}, bf16[2,256,256]{2,1,0:T(8,128)(2,1)S(1)}, u32[]{:S(2)}, u32[]{:S(2)}) %collective-permute-start.7) | collective-permute-done | bytes 262176 | tf_op jit(solution)/shard_map/ppermute | solution.py:775
  27.3 2.1 %shard_map.99 = (bf16[256,256]{1,0:T(8,128)(2,1)S(1)}, bf16[256,256]{1,0:T(8,128)(2,1)S(1)}, f32[1024,512]{1,0:T(8,128)S(1)}, f32[512,512]{1,0:T(8,128)S(1)}) custom-call(bf16[512,512]{1,0:T(8,128)(2,1)S(1)} %copy-done, bf16[512,256]{1,0:T(8,128)(2,1)S(1)} %copy-done.1, bf16[256,256]{1,0:T(8,128)(2,1)S(1)} %get-tuple-element.65.refs_2_, ...), custom_call_target="tpu_custom_call" | custom-call | flops 180000000 | tf_op jit(solution)/shard_map/pallas_call | solution.py:78
  29.4 0.1 collective-permute-start.8
  29.5 1.3 %collective-permute-done.10.refs_7_ = bf16[256,256]{1,0:T(8,128)(2,1)S(1)} collective-permute-done((bf16[256,256]{1,0:T(8,128)(2,1)S(1)}, bf16[256,256]{1,0:T(8,128)(2,1)S(1)}, u32[]{:S(2)}, u32[]{:S(2)}) %collective-permute-start.10) | collective-permute-done | bytes 131104 | tf_op jit(solution)/shard_map/ppermute | solution.py:775
  30.8 2.1 %collective-permute-start.9 = (bf16[256,256]{1,0:T(8,128)(2,1)S(1)}, bf16[256,256]{1,0:T(8,128)(2,1)S(1)}, u32[]{:S(2)}, u32[]{:S(2)}) collective-permute-start(bf16[256,256]{1,0:T(8,128)(2,1)S(1)} %get-tuple-element.69), channel_id=1, source_target_pairs={{0,12},{4,8},{8,4},{12,0},{1,13},{5,9},{9,5},{13,1},{2,14},{6,10},... | collective-permute-start | bytes 393224 | tf_op jit(solution)/shard_map/ppermute | solution.py:775
  32.9 2.3 %shard_map.101 = (bf16[2,256,256]{2,1,0:T(8,128)(2,1)S(1)}, bf16[2,256,256]{2,1,0:T(8,128)(2,1)S(1)}) custom-call(f32[1024,16]{1,0:T(8,128)S(1)} %get-tuple-element.57.refs_0_, bf16[512,512]{1,0:T(8,128)(2,1)S(1)} %copy-done, bf16[512,256]{1,0:T(8,128)(2,1)S(1)} %copy-done.1, f32[1024,512]{1,0:T(8,128)S(1)} %get-tuple-element.72.refs_3_, ...), custom_call_target="tpu_custom_call" | custom-call | flops 6000000000 | tf_op jit(solution)/shard_map/pallas_call | solution.py:78
  35.2 1.6 %collective-permute-start.12 = (bf16[2,256,256]{2,1,0:T(8,128)(2,1)S(1)}, bf16[2,256,256]{2,1,0:T(8,128)(2,1)S(1)}, u32[]{:S(2)}, u32[]{:S(2)}) collective-permute-start(bf16[2,256,256]{2,1,0:T(8,128)(2,1)S(1)} %get-tuple-element.76), channel_id=1, source_target_pairs={{0,4},{4,0},{8,12},{12,8},{1,5},{5,1},{9,13},{13,9},{2,6},{6,2},{1... | collective-permute-start | bytes 786440 | tf_op jit(solution)/shard_map/ppermute | solution.py:775
  36.8 1.6 %collective-permute-done.5.refs_6_ = bf16[2,256,256]{2,1,0:T(8,128)(2,1)S(1)} collective-permute-done((bf16[2,256,256]{2,1,0:T(8,128)(2,1)S(1)}, bf16[2,256,256]{2,1,0:T(8,128)(2,1)S(1)}, u32[]{:S(2)}, u32[]{:S(2)}) %collective-permute-start.5) | collective-permute-done | bytes 262176 | tf_op jit(solution)/shard_map/ppermute | solution.py:775
  38.4 2.4 %shard_map.98 = (bf16[2,16,256]{2,1,0:T(8,128)(2,1)S(1)}, bf16[2,16,256]{2,1,0:T(8,128)(2,1)S(1)}, bf16[2,256,256]{2,1,0:T(8,128)(2,1)S(1)}, bf16[2,256,256]{2,1,0:T(8,128)(2,1)S(1)}) custom-call(f32[1024,16]{1,0:T(8,128)S(1)} %get-tuple-element.57.refs_0_, bf16[512,512]{1,0:T(8,128)(2,1)S(1)} %copy-done, bf16[512,256]{1,0:T(8,128)(2,1)S(1)} %copy-done.1, ...), custom_call_target="tpu_custom_call" | custom-call | flops 4800000000 | tf_op jit(solution)/shard_map/pallas_call | solution.py:78
  40.8 0.0 collective-permute-start.13
  40.8 2.0 %collective-permute-start.6 = (bf16[2,256,256]{2,1,0:T(8,128)(2,1)S(1)}, bf16[2,256,256]{2,1,0:T(8,128)(2,1)S(1)}, u32[]{:S(2)}, u32[]{:S(2)}) collective-permute-start(bf16[2,256,256]{2,1,0:T(8,128)(2,1)S(1)} %get-tuple-element.64), channel_id=1, source_target_pairs={{0,4},{4,0},{8,12},{12,8},{1,5},{5,1},{9,13},{13,9},{2,6},{6,2},{1... | collective-permute-start | bytes 786440 | tf_op jit(solution)/shard_map/ppermute | solution.py:775
  42.9 1.9 %shard_map.102 = (bf16[1024,256]{1,0:T(8,128)(2,1)}, bf16[3,1024,256]{2,1,0:T(8,128)(2,1)}, f32[2,3,256,128]{3,2,1,0:T(8,128)S(1)}) custom-call(bf16[2,3,256,256]{3,2,1,0:T(8,128)(2,1)S(1)} %get-tuple-element.48.refs_0_, bf16[2,256,256]{2,1,0:T(8,128)(2,1)S(1)} %get-tuple-element.49.refs_1_, bf16[2,3,256,256]{3,2,1,0:T(8,128)(2,1)S(1)} %get-tuple-element.55.refs_2_, ...), custom_call_target="tpu_custom_call" | custom-call | flops 1440000000 | tf_op jit(solution)/shard_map/pallas_call | solution.py:78
  44.7 2.4 %collective-permute-done.13.refs_7_ = bf16[2,16,256]{2,1,0:T(8,128)(2,1)S(1)} collective-permute-done((bf16[2,16,256]{2,1,0:T(8,128)(2,1)S(1)}, bf16[2,16,256]{2,1,0:T(8,128)(2,1)S(1)}, u32[]{:S(2)}, u32[]{:S(2)}) %collective-permute-start.13) | collective-permute-done | bytes 16416 | tf_op jit(solution)/shard_map/ppermute | solution.py:775
  47.1 0.8 %shard_map.105 = f32[8,1024]{1,0:T(8,128)S(1)} custom-call(bf16[2,3,256,256]{3,2,1,0:T(8,128)(2,1)S(1)} %get-tuple-element.48.refs_0_, bf16[2,256,256]{2,1,0:T(8,128)(2,1)S(1)} %get-tuple-element.49.refs_1_, bf16[2,3,256,256]{3,2,1,0:T(8,128)(2,1)S(1)} %get-tuple-element.55.refs_2_, bf16[2,256,256]{2,1,0:T(8,128)(2,1)S(1)} %get-tuple-element.56.refs_3_, ...), custom_call_target="tpu_custom_call" | custom-call | flops 3600000000 | tf_op jit(solution)/shard_map/pallas_call | solution.py:78
  47.9 2.1 %collective-permute-start.14 = (f32[8,1024]{1,0:T(8,128)S(1)}, f32[8,1024]{1,0:T(8,128)S(1)}, u32[]{:S(2)}, u32[]{:S(2)}) collective-permute-start(f32[8,1024]{1,0:T(8,128)S(1)} %shard_map.105), channel_id=1, source_target_pairs={{0,12},{4,0},{8,4},{12,8},{1,13},{5,1},{9,5},{13,9},{2,14},{6,2},{... | collective-permute-start | bytes 98312 | tf_op jit(solution)/shard_map/ppermute | solution.py:779
  50.0 1.2 %shard_map.103 = (bf16[1024,256]{1,0:T(8,128)(2,1)}, bf16[3,1024,256]{2,1,0:T(8,128)(2,1)}, f32[1,3,256,128]{3,2,1,0:T(8,128)S(1)}) custom-call(bf16[2,3,256,256]{3,2,1,0:T(8,128)(2,1)S(1)} %get-tuple-element.48.refs_0_, bf16[2,256,256]{2,1,0:T(8,128)(2,1)S(1)} %get-tuple-element.49.refs_1_, ...), custom_call_target="tpu_custom_call", output_to_operand_aliasing={{0}: (9, {}), {1}: (10, {})} | custom-call | flops 720000000 | tf_op jit(solution)/shard_map/pallas_call | solution.py:78
  51.2 0.4 collective-permute-done.6.refs_7_
  51.7 1.2 %shard_map.104 = (bf16[1024,256]{1,0:T(8,128)(2,1)}, bf16[3,1024,256]{2,1,0:T(8,128)(2,1)}, f32[1,3,256,128]{3,2,1,0:T(8,128)S(1)}) custom-call(bf16[2,3,256,256]{3,2,1,0:T(8,128)(2,1)S(1)} %get-tuple-element.48.refs_0_, bf16[2,256,256]{2,1,0:T(8,128)(2,1)S(1)} %get-tuple-element.49.refs_1_, ...), custom_call_target="tpu_custom_call", output_to_operand_aliasing={{0}: (10, {}), {1}: (11, {})} | custom-call | flops 720000000 | tf_op jit(solution)/shard_map/pallas_call | solution.py:78
  52.9 1.4 %shard_map.106 = bf16[3,1024,256]{2,1,0:T(8,128)(2,1)} custom-call(f32[8,1024]{1,0:T(8,128)S(1)} %collective-permute-done.14.refs_0_, f32[16,1024]{1,0:T(8,128)S(1)} %get-tuple-element.88.refs_1_, bf16[48,384]{1,0:T(8,128)(2,1)S(1)} %get-tuple-element.89.refs_2_, ...), custom_call_target="tpu_custom_call", output_to_operand_aliasing={{}: (6, {})} | custom-call | flops 1140000000 | tf_op jit(solution)/shard_map/pallas_call | solution.py:78
  (21 shorter events, 0.1 us)
Async XLA Ops:
  0.6 9.0 %copy-start.4 = (s32[16]{0:T(128)S(1)}, s32[16]{0:T(128)}, u32[]{:S(2)}) copy-start(s32[16]{0:T(128)} %param.13) | copy-start | bytes 196
  0.6 9.0 %copy-start.3 = (f32[1024]{0:T(1024)S(1)}, f32[1024]{0:T(1024)}, u32[]{:S(2)}) copy-start(f32[1024]{0:T(1024)} %param.12) | copy-start | bytes 12292
  0.7 9.0 %copy-start.2 = (f32[3,3,1024]{2,1,0:T(4,128)S(1)}, f32[3,3,1024]{2,1,0:T(4,128)}, u32[]{:S(2)}) copy-start(f32[3,3,1024]{2,1,0:T(4,128)} %refs_4_.1) | copy-start | bytes 110596
  2.2 7.5 %collective-permute-start = (bf16[16,1024]{1,0:T(8,128)(2,1)S(1)}, bf16[16,1024]{1,0:T(8,128)(2,1)S(1)}, u32[]{:S(2)}, u32[]{:S(2)}) collective-permute-start(bf16[16,1024]{1,0:T(8,128)(2,1)S(1)} %get-tuple-element.47), channel_id=1, source_target_pairs={{0,4},{4,8},{8,12},{12,0},{1,5},{5,9},{9,13},{13,1},{2,6},{6,10},{... | collective-permute-start | bytes 98312 | tf_op jit(solution)/shard_map/ppermute | solution.py:779
  5.2 12.2 %collective-permute-start.1 = (bf16[256,256]{1,0:T(8,128)(2,1)S(1)}, bf16[256,256]{1,0:T(8,128)(2,1)S(1)}, u32[]{:S(2)}, u32[]{:S(2)}) collective-permute-start(bf16[256,256]{1,0:T(8,128)(2,1)S(1)} %get-tuple-element.59), channel_id=1, source_target_pairs={{0,4},{4,0},{8,12},{12,8},{1,5},{5,1},{9,13},{13,9},{2,6},{6,2},{1... | collective-permute-start | bytes 393224 | tf_op jit(solution)/shard_map/ppermute | solution.py:775
  6.8 12.7 %collective-permute-start.2 = (bf16[256,256]{1,0:T(8,128)(2,1)S(1)}, bf16[256,256]{1,0:T(8,128)(2,1)S(1)}, u32[]{:S(2)}, u32[]{:S(2)}) collective-permute-start(bf16[256,256]{1,0:T(8,128)(2,1)S(1)} %get-tuple-element.60), channel_id=1, source_target_pairs={{0,8},{4,12},{8,0},{12,4},{1,9},{5,13},{9,1},{13,5},{2,10},{6,14},... | collective-permute-start | bytes 393224 | tf_op jit(solution)/shard_map/ppermute | solution.py:775
  7.9 11.6 %collective-permute-start.3 = (bf16[256,256]{1,0:T(8,128)(2,1)S(1)}, bf16[256,256]{1,0:T(8,128)(2,1)S(1)}, u32[]{:S(2)}, u32[]{:S(2)}) collective-permute-start(bf16[256,256]{1,0:T(8,128)(2,1)S(1)} %get-tuple-element.61), channel_id=1, source_target_pairs={{0,12},{4,8},{8,4},{12,0},{1,13},{5,9},{9,5},{13,1},{2,14},{6,10},... | collective-permute-start | bytes 393224 | tf_op jit(solution)/shard_map/ppermute | solution.py:775
  12.3 15.0 %collective-permute-start.7 = (bf16[2,256,256]{2,1,0:T(8,128)(2,1)S(1)}, bf16[2,256,256]{2,1,0:T(8,128)(2,1)S(1)}, u32[]{:S(2)}, u32[]{:S(2)}) collective-permute-start(bf16[2,256,256]{2,1,0:T(8,128)(2,1)S(1)} %get-tuple-element.67), channel_id=1, source_target_pairs={{0,4},{4,0},{8,12},{12,8},{1,5},{5,1},{9,13},{13,9},{2,6},{6,2},{1... | collective-permute-start | bytes 786440 | tf_op jit(solution)/shard_map/ppermute | solution.py:775
  13.0 14.2 %copy-start = (bf16[512,512]{1,0:T(8,128)(2,1)S(1)}, bf16[512,512]{1,0:T(8,128)(2,1)}, u32[]{:S(2)}) copy-start(bf16[512,512]{1,0:T(8,128)(2,1)} %constant.4.clone.refs_1_.refs_0_) | copy-start | bytes 1572868
  13.0 14.2 %copy-start.1 = (bf16[512,256]{1,0:T(8,128)(2,1)S(1)}, bf16[512,256]{1,0:T(8,128)(2,1)}, u32[]{:S(2)}) copy-start(bf16[512,256]{1,0:T(8,128)(2,1)} %constant.5.clone.refs_2_.refs_1_) | copy-start | bytes 786436
  15.4 15.4 %collective-permute-start.10 = (bf16[256,256]{1,0:T(8,128)(2,1)S(1)}, bf16[256,256]{1,0:T(8,128)(2,1)S(1)}, u32[]{:S(2)}, u32[]{:S(2)}) collective-permute-start(bf16[256,256]{1,0:T(8,128)(2,1)S(1)} %get-tuple-element.74), channel_id=1, source_target_pairs={{0,8},{4,12},{8,0},{12,4},{1,9},{5,13},{9,1},{13,5},{2,10},{6,14},... | collective-permute-start | bytes 393224 | tf_op jit(solution)/shard_map/ppermute | solution.py:775
  17.4 15.4 %collective-permute-start.11 = (bf16[256,256]{1,0:T(8,128)(2,1)S(1)}, bf16[256,256]{1,0:T(8,128)(2,1)S(1)}, u32[]{:S(2)}, u32[]{:S(2)}) collective-permute-start(bf16[256,256]{1,0:T(8,128)(2,1)S(1)} %get-tuple-element.75), channel_id=1, source_target_pairs={{0,12},{4,8},{8,4},{12,0},{1,13},{5,9},{9,5},{13,1},{2,14},{6,10},... | collective-permute-start | bytes 393224 | tf_op jit(solution)/shard_map/ppermute | solution.py:775
  19.5 18.9 %collective-permute-start.5 = (bf16[2,256,256]{2,1,0:T(8,128)(2,1)S(1)}, bf16[2,256,256]{2,1,0:T(8,128)(2,1)S(1)}, u32[]{:S(2)}, u32[]{:S(2)}) collective-permute-start(bf16[2,256,256]{2,1,0:T(8,128)(2,1)S(1)} %get-tuple-element.63), channel_id=1, source_target_pairs={{0,4},{4,0},{8,12},{12,8},{1,5},{5,1},{9,13},{13,9},{2,6},{6,2},{1... | collective-permute-start | bytes 786440 | tf_op jit(solution)/shard_map/ppermute | solution.py:775
  19.6 18.8 %collective-permute-start.4 = (bf16[768,256]{1,0:T(8,128)(2,1)S(1)}, bf16[768,256]{1,0:T(8,128)(2,1)S(1)}, u32[]{:S(2)}, u32[]{:S(2)}) collective-permute-start(bf16[768,256]{1,0:T(8,128)(2,1)S(1)} %pad_maximum_fusion), channel_id=1, source_target_pairs={{0,16},{16,0},{1,17},{17,1},{2,18},{18,2},{3,19},{19,3},{4,20},{20... | collective-permute-start | bytes 1179656 | tf_op jit(solution)/shard_map/ppermute | solution.py:775
  29.4 13.5 %collective-permute-start.8 = (bf16[256,256]{1,0:T(8,128)(2,1)S(1)}, bf16[256,256]{1,0:T(8,128)(2,1)S(1)}, u32[]{:S(2)}, u32[]{:S(2)}) collective-permute-start(bf16[256,256]{1,0:T(8,128)(2,1)S(1)} %get-tuple-element.68), channel_id=1, source_target_pairs={{0,8},{4,12},{8,0},{12,4},{1,9},{5,13},{9,1},{13,5},{2,10},{6,14},... | collective-permute-start | bytes 393224 | tf_op jit(solution)/shard_map/ppermute | solution.py:775
  30.8 12.1 %collective-permute-start.9 = (bf16[256,256]{1,0:T(8,128)(2,1)S(1)}, bf16[256,256]{1,0:T(8,128)(2,1)S(1)}, u32[]{:S(2)}, u32[]{:S(2)}) collective-permute-start(bf16[256,256]{1,0:T(8,128)(2,1)S(1)} %get-tuple-element.69), channel_id=1, source_target_pairs={{0,12},{4,8},{8,4},{12,0},{1,13},{5,9},{9,5},{13,1},{2,14},{6,10},... | collective-permute-start | bytes 393224 | tf_op jit(solution)/shard_map/ppermute | solution.py:775
  35.2 12.0 %collective-permute-start.12 = (bf16[2,256,256]{2,1,0:T(8,128)(2,1)S(1)}, bf16[2,256,256]{2,1,0:T(8,128)(2,1)S(1)}, u32[]{:S(2)}, u32[]{:S(2)}) collective-permute-start(bf16[2,256,256]{2,1,0:T(8,128)(2,1)S(1)} %get-tuple-element.76), channel_id=1, source_target_pairs={{0,4},{4,0},{8,12},{12,8},{1,5},{5,1},{9,13},{13,9},{2,6},{6,2},{1... | collective-permute-start | bytes 786440 | tf_op jit(solution)/shard_map/ppermute | solution.py:775
  40.8 6.3 %collective-permute-start.13 = (bf16[2,16,256]{2,1,0:T(8,128)(2,1)S(1)}, bf16[2,16,256]{2,1,0:T(8,128)(2,1)S(1)}, u32[]{:S(2)}, u32[]{:S(2)}) collective-permute-start(bf16[2,16,256]{2,1,0:T(8,128)(2,1)S(1)} %get-tuple-element.87), channel_id=1, source_target_pairs={{0,4},{4,0},{8,12},{12,8},{1,5},{5,1},{9,13},{13,9},{2,6},{6,2},{1... | collective-permute-start | bytes 49160 | tf_op jit(solution)/shard_map/ppermute | solution.py:775
  40.8 10.8 %collective-permute-start.6 = (bf16[2,256,256]{2,1,0:T(8,128)(2,1)S(1)}, bf16[2,256,256]{2,1,0:T(8,128)(2,1)S(1)}, u32[]{:S(2)}, u32[]{:S(2)}) collective-permute-start(bf16[2,256,256]{2,1,0:T(8,128)(2,1)S(1)} %get-tuple-element.64), channel_id=1, source_target_pairs={{0,4},{4,0},{8,12},{12,8},{1,5},{5,1},{9,13},{13,9},{2,6},{6,2},{1... | collective-permute-start | bytes 786440 | tf_op jit(solution)/shard_map/ppermute | solution.py:775
  47.9 5.0 %collective-permute-start.14 = (f32[8,1024]{1,0:T(8,128)S(1)}, f32[8,1024]{1,0:T(8,128)S(1)}, u32[]{:S(2)}, u32[]{:S(2)}) collective-permute-start(f32[8,1024]{1,0:T(8,128)S(1)} %shard_map.105), channel_id=1, source_target_pairs={{0,12},{4,0},{8,4},{12,8},{1,13},{5,1},{9,5},{13,9},{2,14},{6,2},{... | collective-permute-start | bytes 98312 | tf_op jit(solution)/shard_map/ppermute | solution.py:779

commit v11 on v10

--- a/solution.py
+++ b/solution.py
@@ -638,7 +638,7 @@
     )
 
 
-def final_body(blocks, chained, layout, place_ref, qkv_main, dout_main, qkv_other, dout_other, split_ref, lanes_ref, keep_ref, *refs):
+def final_body(blocks, chained, layout, place_ref, qkv_main, dout_main, qkv_other, dout_other, split_ref, lanes_ref, keep_ref, *refs, wait=True):
     rows, span = layout.sub, layout.span
     found = []
     for _, other in blocks:
@@ -686,6 +686,8 @@
         copies.append(pltpu.make_async_copy(dfeat_ref.at[k], dfeat_hbm.at[:, block, pl.ds(0, most)], sems.at[k, 1]))
         for copy in copies[-2:]:
             copy.start()
+    if not wait:
+        return copies
     for copy in copies:
         copy.wait()
 
@@ -751,23 +753,45 @@
         copy.wait()
 
 
-def finish(lists, layout, ahead, taps_rows, edge, partials, dfeat):
-    channels = layout.channels
+def last_body(lists, layout, place_ref, *refs):
+    count = 7 + 2 * len(lists[-1])
+    given, refs = refs[:count], refs[count:]
+    edge, partials, earlier, outs, refs = refs[:3], refs[3:5], refs[5:7], refs[7:9], refs[9:]
+    scratch, partial = refs[1:5], refs[0]
+    copies = final_body(lists[-1], True, layout, place_ref, *given, None, *earlier, *outs, partial, *scratch, wait=False)
+    finish_body(lists, layout, place_ref, *edge, *partials, partial, None, outs[1], *refs[5:])
+    for copy in copies:
+        copy.wait()
+
+
+def last(lists, layout, gated, shared, found, edge, partials, earlier):
+    span, channels, rows, count = layout.span, layout.channels, layout.sub, len(lists[-1])
+    operands = [*gated, *shared]
+    for turn, _ in lists[-1]:
+        operands += [found[1][turn], found[2][turn]]
+    operands += [*edge, *partials]
+    in_specs = [HELD] * len(operands) + [IN_HBM] * 2
+    operands += earlier
     return run(
-        functools.partial(finish_body, lists),
+        functools.partial(last_body, lists),
         layout,
-        (ahead, taps_rows, edge, *partials, dfeat),
-        jax.ShapeDtypeStruct(dfeat.shape, BF16),
+        operands,
+        [jax.ShapeDtypeStruct((channels, span), BF16), jax.ShapeDtypeStruct((3, channels, span), BF16)],
         [
+            pltpu.VMEM((count, 3, rows, 128), F32),
+            pltpu.VMEM((count, rows, span), BF16),
+            pltpu.VMEM((count, 3, rows, span - 128), BF16),
+            pltpu.VMEM((rows, 9 * 128), F32),
+            pltpu.SemaphoreType.DMA((count, 2)),
             pltpu.VMEM((16, channels), F32),
             pltpu.VMEM((channels, 384), F32),
             pltpu.VMEM((3, channels, 128), BF16),
             pltpu.SemaphoreType.DMA((layout.parts,)),
         ],
-        estimate(1.9),
-        in_specs=[HELD] * (3 + len(lists)) + [IN_HBM],
-        out_specs=IN_HBM,
-        aliases={3 + len(lists): 0},
+        estimate(3.0),
+        in_specs=in_specs,
+        out_specs=[IN_HBM, IN_HBM],
+        aliases={len(operands) - 2: 0, len(operands) - 1: 1},
     )
 
 
@@ -815,11 +839,11 @@
     lists = [[(0, 0), (0, 1)], [(turn, 0) for turn in range(1, half)], [(turn, 1) for turn in range(1, half)]]
     ahead = around(first_grads(layout, gated, main, [rest[0], *leads], crossed), -1, parts)
     done, partials, after = (), [], crossed[0]
-    for blocks in lists:
+    for blocks in lists[:2]:
         *done, partial = final(blocks, layout, gated, shared, found, after, done)
         partials.append(partial)
         after = partial
-    return done[0], finish(lists, layout, ahead, taps_rows, last_edge, partials, done[1])
+    return tuple(last(lists, layout, gated, shared, found, (ahead, taps_rows, last_edge), partials, done))
 
 
 def solution(mesh):

time: 54.5 us -> 54.2 us (level)
    ppermute x2, waiting for transfers between devices: 0.01 us -> 0.79 us  [around(): lax.ppermute(value, 'seq', [(source, (source + steps) % parts) for source...]
    pallas_call x12 -> x11, Pallas kernels: 19.7 us -> 19.2 us  [run(): pl.pallas_call(kernel, out_shape=outs, in_specs=in_specs or [HELD] * len(...]
  transfers between devices with their start and end apart: 15 -> 15, of which waited for: 6 -> 6; matrix products, arithmetic and copies ran while one was open for 0% -> 0% of each run, Pallas kernels for 31% -> 29%
where the time goes in v11:
time: 54.2 us; the launch traced here: 54.1 us
  starting transfers between devices  21.5 us (40%)
  Pallas kernels  19.2 us (35%)
  waiting for transfers between devices  12.6 us (23%)
  between operations  0.76 us (1%)
    pallas_call x11, Pallas kernels, run(): pl.pallas_call(kernel, out_shape=outs, in_specs=in_specs or [HELD] * len(...  19.2 us
    ppermute x13, starting transfers between devices, swap(): lax.ppermute(value, axis, [(source, source ^ step) for source in range(pa...  16.3 us
    ppermute x13, waiting for transfers between devices, swap(): lax.ppermute(value, axis, [(source, source ^ step) for source in range(pa...  11.8 us
    ppermute x2, starting transfers between devices, around(): lax.ppermute(value, 'seq', [(source, (source + steps) % parts) for source...  5.17 us
  transfers between devices with their start and end apart: 15, of which 6 were waited for; matrix products, arithmetic and copies ran while one was open for 0% of the time, Pallas kernels for 29%

profile of v11, /device:TPU:0, one launch (start us, length us, event | category | flops | bytes accessed | tf_op | source)
XLA Modules:
  0.0 54.1 jit_solution(14592808408538598109)
XLA Ops:
  0.7 1.5 %shard_map.95 = (bf16[16,1024]{1,0:T(8,128)(2,1)S(1)}, bf16[256,256]{1,0:T(8,128)(2,1)S(1)}, bf16[256,256]{1,0:T(8,128)(2,1)S(1)}, bf16[256,256]{1,0:T(8,128)(2,...) custom-call(bf16[3,1024,256]{2,1,0:T(8,128)(2,1)} %refs_0_.6, bf16[1024,256]{1,0:T(8,128)(2,1)} %refs_1_.6), custom_call_target="tpu_custom_call" | custom-call | flops 1200000000 | tf_op jit(solution)/shard_map/pallas_call | solution.py:78
  2.2 3.1 %collective-permute-start = (bf16[16,1024]{1,0:T(8,128)(2,1)S(1)}, bf16[16,1024]{1,0:T(8,128)(2,1)S(1)}, u32[]{:S(2)}, u32[]{:S(2)}) collective-permute-start(bf16[16,1024]{1,0:T(8,128)(2,1)S(1)} %get-tuple-element.44), channel_id=1, source_target_pairs={{0,4},{4,8},{8,12},{12,0},{1,5},{5,9},{9,13},{13,1},{2,6},{6,10},{... | collective-permute-start | bytes 98312 | tf_op jit(solution)/shard_map/ppermute | solution.py:803
  5.2 1.6 %collective-permute-start.1 = (bf16[256,256]{1,0:T(8,128)(2,1)S(1)}, bf16[256,256]{1,0:T(8,128)(2,1)S(1)}, u32[]{:S(2)}, u32[]{:S(2)}) collective-permute-start(bf16[256,256]{1,0:T(8,128)(2,1)S(1)} %get-tuple-element.56), channel_id=1, source_target_pairs={{0,4},{4,0},{8,12},{12,8},{1,5},{5,1},{9,13},{13,9},{2,6},{6,2},{1... | collective-permute-start | bytes 393224 | tf_op jit(solution)/shard_map/ppermute | solution.py:799
  6.8 1.1 %collective-permute-start.2 = (bf16[256,256]{1,0:T(8,128)(2,1)S(1)}, bf16[256,256]{1,0:T(8,128)(2,1)S(1)}, u32[]{:S(2)}, u32[]{:S(2)}) collective-permute-start(bf16[256,256]{1,0:T(8,128)(2,1)S(1)} %get-tuple-element.57), channel_id=1, source_target_pairs={{0,8},{4,12},{8,0},{12,4},{1,9},{5,13},{9,1},{13,5},{2,10},{6,14},... | collective-permute-start | bytes 393224 | tf_op jit(solution)/shard_map/ppermute | solution.py:799
  7.9 1.7 %collective-permute-start.3 = (bf16[256,256]{1,0:T(8,128)(2,1)S(1)}, bf16[256,256]{1,0:T(8,128)(2,1)S(1)}, u32[]{:S(2)}, u32[]{:S(2)}) collective-permute-start(bf16[256,256]{1,0:T(8,128)(2,1)S(1)} %get-tuple-element.58), channel_id=1, source_target_pairs={{0,12},{4,8},{8,4},{12,0},{1,13},{5,9},{9,5},{13,1},{2,14},{6,10},... | collective-permute-start | bytes 393224 | tf_op jit(solution)/shard_map/ppermute | solution.py:799
  9.7 2.6 %shard_map.96 = (bf16[2,3,256,256]{3,2,1,0:T(8,128)(2,1)S(1)}, bf16[2,256,256]{2,1,0:T(8,128)(2,1)S(1)}, bf16[2,256,256]{2,1,0:T(8,128)(2,1)S(1)}, bf16[2,256,25...) custom-call(bf16[3,1024,256]{2,1,0:T(8,128)(2,1)} %refs_0_.6, ...), custom_call_target="tpu_custom_call" | custom-call | flops 3600000000 | tf_op jit(solution)/shard_map/pallas_call | solution.py:78
  12.3 0.8 %collective-permute-start.7 = (bf16[2,256,256]{2,1,0:T(8,128)(2,1)S(1)}, bf16[2,256,256]{2,1,0:T(8,128)(2,1)S(1)}, u32[]{:S(2)}, u32[]{:S(2)}) collective-permute-start(bf16[2,256,256]{2,1,0:T(8,128)(2,1)S(1)} %get-tuple-element.64), channel_id=1, source_target_pairs={{0,4},{4,0},{8,12},{12,8},{1,5},{5,1},{9,13},{13,9},{2,6},{6,2},{1... | collective-permute-start | bytes 786440 | tf_op jit(solution)/shard_map/ppermute | solution.py:799
  13.0 2.4 %shard_map.97 = (bf16[2,3,256,256]{3,2,1,0:T(8,128)(2,1)S(1)}, bf16[2,256,256]{2,1,0:T(8,128)(2,1)S(1)}, bf16[2,256,256]{2,1,0:T(8,128)(2,1)S(1)}, bf16[2,256,25...) custom-call(bf16[3,1024,256]{2,1,0:T(8,128)(2,1)} %refs_0_.6, ...), custom_call_target="tpu_custom_call" | custom-call | flops 3600000000 | tf_op jit(solution)/shard_map/pallas_call | solution.py:78
  15.4 2.0 %collective-permute-start.10 = (bf16[256,256]{1,0:T(8,128)(2,1)S(1)}, bf16[256,256]{1,0:T(8,128)(2,1)S(1)}, u32[]{:S(2)}, u32[]{:S(2)}) collective-permute-start(bf16[256,256]{1,0:T(8,128)(2,1)S(1)} %get-tuple-element.71), channel_id=1, source_target_pairs={{0,8},{4,12},{8,0},{12,4},{1,9},{5,13},{9,1},{13,5},{2,10},{6,14},... | collective-permute-start | bytes 393224 | tf_op jit(solution)/shard_map/ppermute | solution.py:799
  17.4 0.0 collective-permute-done.1.refs_3_
  17.4 1.7 %collective-permute-start.11 = (bf16[256,256]{1,0:T(8,128)(2,1)S(1)}, bf16[256,256]{1,0:T(8,128)(2,1)S(1)}, u32[]{:S(2)}, u32[]{:S(2)}) collective-permute-start(bf16[256,256]{1,0:T(8,128)(2,1)S(1)} %get-tuple-element.72), channel_id=1, source_target_pairs={{0,12},{4,8},{8,4},{12,0},{1,13},{5,9},{9,5},{13,1},{2,14},{6,10},... | collective-permute-start | bytes 393224 | tf_op jit(solution)/shard_map/ppermute | solution.py:799
  19.2 0.4 collective-permute-done.2.refs_4_
  19.5 0.0 collective-permute-start.5
  19.6 1.6 %collective-permute-start.4 = (bf16[768,256]{1,0:T(8,128)(2,1)S(1)}, bf16[768,256]{1,0:T(8,128)(2,1)S(1)}, u32[]{:S(2)}, u32[]{:S(2)}) collective-permute-start(bf16[768,256]{1,0:T(8,128)(2,1)S(1)} %pad_maximum_fusion), channel_id=1, source_target_pairs={{0,16},{16,0},{1,17},{17,1},{2,18},{18,2},{3,19},{19,3},{4,20},{20... | collective-permute-start | bytes 1179656 | tf_op jit(solution)/shard_map/ppermute | solution.py:799
  21.2 6.1 %collective-permute-done.7.refs_7_.refs_6_ = bf16[2,256,256]{2,1,0:T(8,128)(2,1)S(1)} collective-permute-done((bf16[2,256,256]{2,1,0:T(8,128)(2,1)S(1)}, bf16[2,256,256]{2,1,0:T(8,128)(2,1)S(1)}, u32[]{:S(2)}, u32[]{:S(2)}) %collective-permute-start.7) | collective-permute-done | bytes 262176 | tf_op jit(solution)/shard_map/ppermute | solution.py:799
  27.3 2.1 %shard_map.99 = (bf16[256,256]{1,0:T(8,128)(2,1)S(1)}, bf16[256,256]{1,0:T(8,128)(2,1)S(1)}, f32[1024,512]{1,0:T(8,128)S(1)}, f32[512,512]{1,0:T(8,128)S(1)}) custom-call(bf16[512,512]{1,0:T(8,128)(2,1)S(1)} %copy-done, bf16[512,256]{1,0:T(8,128)(2,1)S(1)} %copy-done.1, bf16[256,256]{1,0:T(8,128)(2,1)S(1)} %get-tuple-element.62.refs_2_, ...), custom_call_target="tpu_custom_call" | custom-call | flops 180000000 | tf_op jit(solution)/shard_map/pallas_call | solution.py:78
  29.4 0.1 collective-permute-start.8
  29.5 1.3 %collective-permute-done.10.refs_7_ = bf16[256,256]{1,0:T(8,128)(2,1)S(1)} collective-permute-done((bf16[256,256]{1,0:T(8,128)(2,1)S(1)}, bf16[256,256]{1,0:T(8,128)(2,1)S(1)}, u32[]{:S(2)}, u32[]{:S(2)}) %collective-permute-start.10) | collective-permute-done | bytes 131104 | tf_op jit(solution)/shard_map/ppermute | solution.py:799
  30.8 2.1 %collective-permute-start.9 = (bf16[256,256]{1,0:T(8,128)(2,1)S(1)}, bf16[256,256]{1,0:T(8,128)(2,1)S(1)}, u32[]{:S(2)}, u32[]{:S(2)}) collective-permute-start(bf16[256,256]{1,0:T(8,128)(2,1)S(1)} %get-tuple-element.66), channel_id=1, source_target_pairs={{0,12},{4,8},{8,4},{12,0},{1,13},{5,9},{9,5},{13,1},{2,14},{6,10},... | collective-permute-start | bytes 393224 | tf_op jit(solution)/shard_map/ppermute | solution.py:799
  32.9 2.3 %shard_map.101 = (bf16[2,256,256]{2,1,0:T(8,128)(2,1)S(1)}, bf16[2,256,256]{2,1,0:T(8,128)(2,1)S(1)}) custom-call(f32[1024,16]{1,0:T(8,128)S(1)} %get-tuple-element.54.refs_0_, bf16[512,512]{1,0:T(8,128)(2,1)S(1)} %copy-done, bf16[512,256]{1,0:T(8,128)(2,1)S(1)} %copy-done.1, f32[1024,512]{1,0:T(8,128)S(1)} %get-tuple-element.69.refs_3_, ...), custom_call_target="tpu_custom_call" | custom-call | flops 6000000000 | tf_op jit(solution)/shard_map/pallas_call | solution.py:78
  35.1 1.6 %collective-permute-start.12 = (bf16[2,256,256]{2,1,0:T(8,128)(2,1)S(1)}, bf16[2,256,256]{2,1,0:T(8,128)(2,1)S(1)}, u32[]{:S(2)}, u32[]{:S(2)}) collective-permute-start(bf16[2,256,256]{2,1,0:T(8,128)(2,1)S(1)} %get-tuple-element.74), channel_id=1, source_target_pairs={{0,4},{4,0},{8,12},{12,8},{1,5},{5,1},{9,13},{13,9},{2,6},{6,2},{1... | collective-permute-start | bytes 786440 | tf_op jit(solution)/shard_map/ppermute | solution.py:799
  36.8 1.6 %collective-permute-done.5.refs_6_ = bf16[2,256,256]{2,1,0:T(8,128)(2,1)S(1)} collective-permute-done((bf16[2,256,256]{2,1,0:T(8,128)(2,1)S(1)}, bf16[2,256,256]{2,1,0:T(8,128)(2,1)S(1)}, u32[]{:S(2)}, u32[]{:S(2)}) %collective-permute-start.5) | collective-permute-done | bytes 262176 | tf_op jit(solution)/shard_map/ppermute | solution.py:799
  38.4 2.4 %shard_map.98 = (bf16[2,16,256]{2,1,0:T(8,128)(2,1)S(1)}, bf16[2,16,256]{2,1,0:T(8,128)(2,1)S(1)}, bf16[2,256,256]{2,1,0:T(8,128)(2,1)S(1)}, bf16[2,256,256]{2,1,0:T(8,128)(2,1)S(1)}) custom-call(f32[1024,16]{1,0:T(8,128)S(1)} %get-tuple-element.54.refs_0_, bf16[512,512]{1,0:T(8,128)(2,1)S(1)} %copy-done, bf16[512,256]{1,0:T(8,128)(2,1)S(1)} %copy-done.1, ...), custom_call_target="tpu_custom_call" | custom-call | flops 4800000000 | tf_op jit(solution)/shard_map/pallas_call | solution.py:78
  40.8 0.0 collective-permute-start.13
  40.8 2.0 %collective-permute-start.6 = (bf16[2,256,256]{2,1,0:T(8,128)(2,1)S(1)}, bf16[2,256,256]{2,1,0:T(8,128)(2,1)S(1)}, u32[]{:S(2)}, u32[]{:S(2)}) collective-permute-start(bf16[2,256,256]{2,1,0:T(8,128)(2,1)S(1)} %get-tuple-element.61), channel_id=1, source_target_pairs={{0,4},{4,0},{8,12},{12,8},{1,5},{5,1},{9,13},{13,9},{2,6},{6,2},{1... | collective-permute-start | bytes 786440 | tf_op jit(solution)/shard_map/ppermute | solution.py:799
  42.9 1.9 %shard_map.103 = (bf16[1024,256]{1,0:T(8,128)(2,1)}, bf16[3,1024,256]{2,1,0:T(8,128)(2,1)}, f32[2,3,256,128]{3,2,1,0:T(8,128)S(1)}) custom-call(bf16[2,3,256,256]{3,2,1,0:T(8,128)(2,1)S(1)} %get-tuple-element.45.refs_0_, bf16[2,256,256]{2,1,0:T(8,128)(2,1)S(1)} %get-tuple-element.46.refs_1_, bf16[2,3,256,256]{3,2,1,0:T(8,128)(2,1)S(1)} %get-tuple-element.52.refs_2_, ...), custom_call_target="tpu_custom_call" | custom-call | flops 1440000000 | tf_op jit(solution)/shard_map/pallas_call | solution.py:78
  44.8 2.4 %collective-permute-done.13.refs_7_ = bf16[2,16,256]{2,1,0:T(8,128)(2,1)S(1)} collective-permute-done((bf16[2,16,256]{2,1,0:T(8,128)(2,1)S(1)}, bf16[2,16,256]{2,1,0:T(8,128)(2,1)S(1)}, u32[]{:S(2)}, u32[]{:S(2)}) %collective-permute-start.13) | collective-permute-done | bytes 16416 | tf_op jit(solution)/shard_map/ppermute | solution.py:799
  47.1 0.8 %shard_map.102 = f32[8,1024]{1,0:T(8,128)S(1)} custom-call(bf16[2,3,256,256]{3,2,1,0:T(8,128)(2,1)S(1)} %get-tuple-element.45.refs_0_, bf16[2,256,256]{2,1,0:T(8,128)(2,1)S(1)} %get-tuple-element.46.refs_1_, bf16[2,3,256,256]{3,2,1,0:T(8,128)(2,1)S(1)} %get-tuple-element.52.refs_2_, bf16[2,256,256]{2,1,0:T(8,128)(2,1)S(1)} %get-tuple-element.53.refs_3_, ...), custom_call_target="tpu_custom_call" | custom-call | flops 3600000000 | tf_op jit(solution)/shard_map/pallas_call | solution.py:78
  47.9 2.1 %collective-permute-start.14 = (f32[8,1024]{1,0:T(8,128)S(1)}, f32[8,1024]{1,0:T(8,128)S(1)}, u32[]{:S(2)}, u32[]{:S(2)}) collective-permute-start(f32[8,1024]{1,0:T(8,128)S(1)} %shard_map.102), channel_id=1, source_target_pairs={{0,12},{4,0},{8,4},{12,8},{1,13},{5,1},{9,5},{13,9},{2,14},{6,2},{... | collective-permute-start | bytes 98312 | tf_op jit(solution)/shard_map/ppermute | solution.py:803
  50.0 1.2 %shard_map.104 = (bf16[1024,256]{1,0:T(8,128)(2,1)}, bf16[3,1024,256]{2,1,0:T(8,128)(2,1)}, f32[1,3,256,128]{3,2,1,0:T(8,128)S(1)}) custom-call(bf16[2,3,256,256]{3,2,1,0:T(8,128)(2,1)S(1)} %get-tuple-element.45.refs_0_, bf16[2,256,256]{2,1,0:T(8,128)(2,1)S(1)} %get-tuple-element.46.refs_1_, ...), custom_call_target="tpu_custom_call", output_to_operand_aliasing={{0}: (9, {}), {1}: (10, {})} | custom-call | flops 720000000 | tf_op jit(solution)/shard_map/pallas_call | solution.py:78
  51.2 0.8 %collective-permute-done.14.refs_9_ = f32[8,1024]{1,0:T(8,128)S(1)} collective-permute-done((f32[8,1024]{1,0:T(8,128)S(1)}, f32[8,1024]{1,0:T(8,128)S(1)}, u32[]{:S(2)}, u32[]{:S(2)}) %collective-permute-start.14) | collective-permute-done | bytes 32800 | tf_op jit(solution)/shard_map/ppermute | solution.py:803
  52.0 2.0 %shard_map.105 = (bf16[1024,256]{1,0:T(8,128)(2,1)}, bf16[3,1024,256]{2,1,0:T(8,128)(2,1)}) custom-call(bf16[2,3,256,256]{3,2,1,0:T(8,128)(2,1)S(1)} %get-tuple-element.45.refs_0_, bf16[2,256,256]{2,1,0:T(8,128)(2,1)S(1)} %get-tuple-element.46.refs_1_, ...), custom_call_target="tpu_custom_call", output_to_operand_aliasing={{0}: (14, {}), {1}: (15, {})} | custom-call | flops 1800000000 | tf_op jit(solution)/shard_map/pallas_call | solution.py:78
  (20 shorter events, 0.1 us)
Async XLA Ops:
  0.6 9.0 %copy-start.4 = (s32[16]{0:T(128)S(1)}, s32[16]{0:T(128)}, u32[]{:S(2)}) copy-start(s32[16]{0:T(128)} %param.13) | copy-start | bytes 196
  0.6 9.0 %copy-start.3 = (f32[1024]{0:T(1024)S(1)}, f32[1024]{0:T(1024)}, u32[]{:S(2)}) copy-start(f32[1024]{0:T(1024)} %param.12) | copy-start | bytes 12292
  0.7 9.0 %copy-start.2 = (f32[3,3,1024]{2,1,0:T(4,128)S(1)}, f32[3,3,1024]{2,1,0:T(4,128)}, u32[]{:S(2)}) copy-start(f32[3,3,1024]{2,1,0:T(4,128)} %refs_4_.1) | copy-start | bytes 110596
  2.2 7.5 %collective-permute-start = (bf16[16,1024]{1,0:T(8,128)(2,1)S(1)}, bf16[16,1024]{1,0:T(8,128)(2,1)S(1)}, u32[]{:S(2)}, u32[]{:S(2)}) collective-permute-start(bf16[16,1024]{1,0:T(8,128)(2,1)S(1)} %get-tuple-element.44), channel_id=1, source_target_pairs={{0,4},{4,8},{8,12},{12,0},{1,5},{5,9},{9,13},{13,1},{2,6},{6,10},{... | collective-permute-start | bytes 98312 | tf_op jit(solution)/shard_map/ppermute | solution.py:803
  5.2 12.2 %collective-permute-start.1 = (bf16[256,256]{1,0:T(8,128)(2,1)S(1)}, bf16[256,256]{1,0:T(8,128)(2,1)S(1)}, u32[]{:S(2)}, u32[]{:S(2)}) collective-permute-start(bf16[256,256]{1,0:T(8,128)(2,1)S(1)} %get-tuple-element.56), channel_id=1, source_target_pairs={{0,4},{4,0},{8,12},{12,8},{1,5},{5,1},{9,13},{13,9},{2,6},{6,2},{1... | collective-permute-start | bytes 393224 | tf_op jit(solution)/shard_map/ppermute | solution.py:799
  6.8 12.7 %collective-permute-start.2 = (bf16[256,256]{1,0:T(8,128)(2,1)S(1)}, bf16[256,256]{1,0:T(8,128)(2,1)S(1)}, u32[]{:S(2)}, u32[]{:S(2)}) collective-permute-start(bf16[256,256]{1,0:T(8,128)(2,1)S(1)} %get-tuple-element.57), channel_id=1, source_target_pairs={{0,8},{4,12},{8,0},{12,4},{1,9},{5,13},{9,1},{13,5},{2,10},{6,14},... | collective-permute-start | bytes 393224 | tf_op jit(solution)/shard_map/ppermute | solution.py:799
  7.9 11.6 %collective-permute-start.3 = (bf16[256,256]{1,0:T(8,128)(2,1)S(1)}, bf16[256,256]{1,0:T(8,128)(2,1)S(1)}, u32[]{:S(2)}, u32[]{:S(2)}) collective-permute-start(bf16[256,256]{1,0:T(8,128)(2,1)S(1)} %get-tuple-element.58), channel_id=1, source_target_pairs={{0,12},{4,8},{8,4},{12,0},{1,13},{5,9},{9,5},{13,1},{2,14},{6,10},... | collective-permute-start | bytes 393224 | tf_op jit(solution)/shard_map/ppermute | solution.py:799
  12.3 15.0 %collective-permute-start.7 = (bf16[2,256,256]{2,1,0:T(8,128)(2,1)S(1)}, bf16[2,256,256]{2,1,0:T(8,128)(2,1)S(1)}, u32[]{:S(2)}, u32[]{:S(2)}) collective-permute-start(bf16[2,256,256]{2,1,0:T(8,128)(2,1)S(1)} %get-tuple-element.64), channel_id=1, source_target_pairs={{0,4},{4,0},{8,12},{12,8},{1,5},{5,1},{9,13},{13,9},{2,6},{6,2},{1... | collective-permute-start | bytes 786440 | tf_op jit(solution)/shard_map/ppermute | solution.py:799
  13.0 14.2 %copy-start = (bf16[512,512]{1,0:T(8,128)(2,1)S(1)}, bf16[512,512]{1,0:T(8,128)(2,1)}, u32[]{:S(2)}) copy-start(bf16[512,512]{1,0:T(8,128)(2,1)} %constant.4.clone.refs_1_.refs_0_) | copy-start | bytes 1572868
  13.0 14.2 %copy-start.1 = (bf16[512,256]{1,0:T(8,128)(2,1)S(1)}, bf16[512,256]{1,0:T(8,128)(2,1)}, u32[]{:S(2)}) copy-start(bf16[512,256]{1,0:T(8,128)(2,1)} %constant.5.clone.refs_2_.refs_1_) | copy-start | bytes 786436
  15.4 15.4 %collective-permute-start.10 = (bf16[256,256]{1,0:T(8,128)(2,1)S(1)}, bf16[256,256]{1,0:T(8,128)(2,1)S(1)}, u32[]{:S(2)}, u32[]{:S(2)}) collective-permute-start(bf16[256,256]{1,0:T(8,128)(2,1)S(1)} %get-tuple-element.71), channel_id=1, source_target_pairs={{0,8},{4,12},{8,0},{12,4},{1,9},{5,13},{9,1},{13,5},{2,10},{6,14},... | collective-permute-start | bytes 393224 | tf_op jit(solution)/shard_map/ppermute | solution.py:799
  17.4 15.4 %collective-permute-start.11 = (bf16[256,256]{1,0:T(8,128)(2,1)S(1)}, bf16[256,256]{1,0:T(8,128)(2,1)S(1)}, u32[]{:S(2)}, u32[]{:S(2)}) collective-permute-start(bf16[256,256]{1,0:T(8,128)(2,1)S(1)} %get-tuple-element.72), channel_id=1, source_target_pairs={{0,12},{4,8},{8,4},{12,0},{1,13},{5,9},{9,5},{13,1},{2,14},{6,10},... | collective-permute-start | bytes 393224 | tf_op jit(solution)/shard_map/ppermute | solution.py:799
  19.5 18.9 %collective-permute-start.5 = (bf16[2,256,256]{2,1,0:T(8,128)(2,1)S(1)}, bf16[2,256,256]{2,1,0:T(8,128)(2,1)S(1)}, u32[]{:S(2)}, u32[]{:S(2)}) collective-permute-start(bf16[2,256,256]{2,1,0:T(8,128)(2,1)S(1)} %get-tuple-element.60), channel_id=1, source_target_pairs={{0,4},{4,0},{8,12},{12,8},{1,5},{5,1},{9,13},{13,9},{2,6},{6,2},{1... | collective-permute-start | bytes 786440 | tf_op jit(solution)/shard_map/ppermute | solution.py:799
  19.6 18.8 %collective-permute-start.4 = (bf16[768,256]{1,0:T(8,128)(2,1)S(1)}, bf16[768,256]{1,0:T(8,128)(2,1)S(1)}, u32[]{:S(2)}, u32[]{:S(2)}) collective-permute-start(bf16[768,256]{1,0:T(8,128)(2,1)S(1)} %pad_maximum_fusion), channel_id=1, source_target_pairs={{0,16},{16,0},{1,17},{17,1},{2,18},{18,2},{3,19},{19,3},{4,20},{20... | collective-permute-start | bytes 1179656 | tf_op jit(solution)/shard_map/ppermute | solution.py:799
  29.4 13.5 %collective-permute-start.8 = (bf16[256,256]{1,0:T(8,128)(2,1)S(1)}, bf16[256,256]{1,0:T(8,128)(2,1)S(1)}, u32[]{:S(2)}, u32[]{:S(2)}) collective-permute-start(bf16[256,256]{1,0:T(8,128)(2,1)S(1)} %get-tuple-element.65), channel_id=1, source_target_pairs={{0,8},{4,12},{8,0},{12,4},{1,9},{5,13},{9,1},{13,5},{2,10},{6,14},... | collective-permute-start | bytes 393224 | tf_op jit(solution)/shard_map/ppermute | solution.py:799
  30.8 12.1 %collective-permute-start.9 = (bf16[256,256]{1,0:T(8,128)(2,1)S(1)}, bf16[256,256]{1,0:T(8,128)(2,1)S(1)}, u32[]{:S(2)}, u32[]{:S(2)}) collective-permute-start(bf16[256,256]{1,0:T(8,128)(2,1)S(1)} %get-tuple-element.66), channel_id=1, source_target_pairs={{0,12},{4,8},{8,4},{12,0},{1,13},{5,9},{9,5},{13,1},{2,14},{6,10},... | collective-permute-start | bytes 393224 | tf_op jit(solution)/shard_map/ppermute | solution.py:799
  35.1 12.0 %collective-permute-start.12 = (bf16[2,256,256]{2,1,0:T(8,128)(2,1)S(1)}, bf16[2,256,256]{2,1,0:T(8,128)(2,1)S(1)}, u32[]{:S(2)}, u32[]{:S(2)}) collective-permute-start(bf16[2,256,256]{2,1,0:T(8,128)(2,1)S(1)} %get-tuple-element.74), channel_id=1, source_target_pairs={{0,4},{4,0},{8,12},{12,8},{1,5},{5,1},{9,13},{13,9},{2,6},{6,2},{1... | collective-permute-start | bytes 786440 | tf_op jit(solution)/shard_map/ppermute | solution.py:799
  40.8 6.3 %collective-permute-start.13 = (bf16[2,16,256]{2,1,0:T(8,128)(2,1)S(1)}, bf16[2,16,256]{2,1,0:T(8,128)(2,1)S(1)}, u32[]{:S(2)}, u32[]{:S(2)}) collective-permute-start(bf16[2,16,256]{2,1,0:T(8,128)(2,1)S(1)} %get-tuple-element.76), channel_id=1, source_target_pairs={{0,4},{4,0},{8,12},{12,8},{1,5},{5,1},{9,13},{13,9},{2,6},{6,2},{1... | collective-permute-start | bytes 49160 | tf_op jit(solution)/shard_map/ppermute | solution.py:799
  40.8 11.2 %collective-permute-start.6 = (bf16[2,256,256]{2,1,0:T(8,128)(2,1)S(1)}, bf16[2,256,256]{2,1,0:T(8,128)(2,1)S(1)}, u32[]{:S(2)}, u32[]{:S(2)}) collective-permute-start(bf16[2,256,256]{2,1,0:T(8,128)(2,1)S(1)} %get-tuple-element.61), channel_id=1, source_target_pairs={{0,4},{4,0},{8,12},{12,8},{1,5},{5,1},{9,13},{13,9},{2,6},{6,2},{1... | collective-permute-start | bytes 786440 | tf_op jit(solution)/shard_map/ppermute | solution.py:799
  47.9 4.1 %collective-permute-start.14 = (f32[8,1024]{1,0:T(8,128)S(1)}, f32[8,1024]{1,0:T(8,128)S(1)}, u32[]{:S(2)}, u32[]{:S(2)}) collective-permute-start(f32[8,1024]{1,0:T(8,128)S(1)} %shard_map.102), channel_id=1, source_target_pairs={{0,12},{4,0},{8,4},{12,8},{1,13},{5,1},{9,5},{13,9},{2,14},{6,2},{... | collective-permute-start | bytes 98312 | tf_op jit(solution)/shard_map/ppermute | solution.py:803
